TPU v7x, 256 devices: a whole 4x4x8 slice. The times are simulated.
256 devices in a mesh: freq: 8 (over x, core), aux: 32 (over y, z).
Axes of the slice: x: 4, y: 4, z: 8, core: 2. Of those that a mesh axis runs over, the one named last changes fastest.
Arguments:
- screened: bfloat16 [16, 4096, 4096], P('freq', 'aux'), may hold values from -0.09375 to 0.09375
- grid_weights: float32 [16], replicated, may hold values from 0.2 to 0.5
- greens: float32 [16, 16], replicated, may hold values from 0.2 to 2
- three_state: bfloat16 [4096, 16, 128], P('aux'), may hold values from -6 to 6
- three_orbital: bfloat16 [4096, 16, 512], P('aux'), may hold values from -0.0234375 to 0.0234375
- block_ids: int32 [64, 8], P('aux'), may hold values from 0 to 7, each once within a row
- block_counts: int32 [64], P('aux'), may hold values from 1 to 8
- owners: int32 [32], replicated, may hold values from 0 to 31, each once
Outputs:
- self_energy: float32 [16, 512, 128], P('freq', 'aux')
Inputs may be any that keep to these rules, and one draw needn't show every extreme that they name: `block_ids`: each row lists all 8 orbital blocks once, in a drawn order. `owners`: each device of aux owns exactly one orbital row block.
All inputs are finite; a program needn't handle non-finite values.
Results may differ from a plain program's by a relative error of at most 0.011.
Values may be sent and summed in bfloat16 or wider, within the bound.
No kernel may reach another device: no remote copies, remote signals or barrier semaphores. Data moves between devices by JAX's collectives and lax.ppermute only.
A program may use at most 128 MiB of HBM per device.

v0:
```python
import jax
import jax.numpy as jnp
from jax import lax
from jax.sharding import PartitionSpec as P


def cosine_table(grid_weights, count):
    steps_t = jnp.arange(count, dtype=jnp.float32)
    return grid_weights[None, :] * jnp.cos(
        jnp.pi * (steps_t[:, None] + 0.5) * steps_t[None, :] / count
    )


def product(operand, piece):
    upper = operand.astype(jnp.bfloat16)
    lower = (operand - upper.astype(jnp.float32)).astype(jnp.bfloat16)
    first = jnp.einsum("tpq,qx->tpx", upper, piece, preferred_element_type=jnp.float32)
    return first + jnp.einsum("tpq,qx->tpx", lower, piece, preferred_element_type=jnp.float32)


def shards(
    screened, grid_weights, greens, three_state, three_orbital, block_ids, block_counts, owners
):
    freq_count = lax.axis_size("freq")
    aux_count = lax.axis_size("aux")
    local_times, rows, width = screened.shape
    total_times = local_times * freq_count
    table = cosine_table(grid_weights, total_times)
    states = three_state.shape[1]
    targets = three_state.shape[2]
    flat_state = three_state.reshape(rows, states * targets)
    pieces = lax.all_to_all(screened, "freq", split_axis=2, concat_axis=0, tiled=True)
    timed = jnp.einsum(
        "tj,jpq->tpq", table, pieces.astype(jnp.float32), precision=lax.Precision.HIGHEST
    )
    operand = lax.all_to_all(timed, "freq", split_axis=0, concat_axis=2, tiled=True)
    contracted = product(operand, lax.all_gather(flat_state, "aux", axis=0, tiled=True))
    own_greens = lax.dynamic_slice_in_dim(
        greens, lax.axis_index("freq") * local_times, local_times, 0
    )
    scaled = (
        contracted.reshape(local_times, rows, states, targets) * own_greens[:, None, :, None]
    ).astype(jnp.bfloat16)
    block_count, slot_count = block_ids.shape
    orbitals = three_orbital.shape[2]
    block_width = orbitals // slot_count
    row_block = rows // block_count
    slot_index = jnp.arange(slot_count, dtype=jnp.int32)
    onehot = (
        (block_ids[:, :, None] == slot_index[None, None, :])
        & (slot_index[None, :, None] < block_counts[:, None, None])
    ).astype(jnp.bfloat16)
    values = three_orbital.reshape(block_count, row_block, states, slot_count, block_width)
    dense_orbital = jnp.einsum(
        "bsn,brksc->brknc", onehot, values, preferred_element_type=jnp.float32
    )
    dense_orbital = dense_orbital.reshape(rows * states, orbitals).astype(jnp.bfloat16)
    partial_value = jnp.einsum(
        "rn,trm->tnm",
        dense_orbital,
        scaled.reshape(local_times, rows * states, targets),
        preferred_element_type=jnp.float32,
    )
    inverse = jnp.argsort(owners)
    partial_value = jnp.take(
        partial_value.reshape(local_times, aux_count, orbitals // aux_count, targets),
        inverse,
        axis=1,
    )
    partial_value = partial_value.reshape(local_times, orbitals, targets)
    return lax.psum_scatter(partial_value, "aux", scatter_dimension=1, tiled=True)


def solution(mesh):
    return jax.shard_map(
        shards,
        mesh=mesh,
        in_specs=(
            P("freq", "aux", None),
            P(),
            P(),
            P("aux", None, None),
            P("aux", None, None),
            P("aux", None),
            P("aux"),
            P(),
        ),
        out_specs=P("freq", "aux", None),
        check_vma=False,
    )
```

profile of v0, /device:TPU:32, one launch (start us, length us, event | category | flops | bytes accessed | tf_op | source)
XLA Modules:
  0.0 398.6 jit_solution(5469521270729638254)
XLA Ops:
  6.5 2.0 copy.35
  8.6 6.2 %copy.22 = bf16[2,128,4096]{1,0,2:T(2,128)(2,1)} copy(bf16[2,128,4096]{2,1,0:T(8,128)(2,1)} %param.8) | data formatting | bytes 4194304 | tf_op args[0]
  14.7 4.3 %all-to-all-start = ((bf16[2,128,4096]{1,0,2:T(2,128)(2,1)}), bf16[2,128,4096]{1,0,2:T(2,128)(2,1)S(1)}, u32[]{:S(2)}, u32[]{:S(2)}) async-start(bf16[2,128,4096]{1,0,2:T(2,128)(2,1)} %copy.22), calls=%async_computation | async-start | bytes 4194304 | tf_op jit(solution)/shard_map/all_to_all | solution.py:32
  19.0 27.2 %all-to-all-done = bf16[2,128,4096]{1,0,2:T(2,128)(2,1)S(1)} async-done(((bf16[2,128,4096]{1,0,2:T(2,128)(2,1)}), bf16[2,128,4096]{1,0,2:T(2,128)(2,1)S(1)}, u32[]{:S(2)}, u32[]{:S(2)}) %all-to-all-start) | async-done | bytes 2097184 | tf_op jit(solution)/shard_map/all_to_all | solution.py:32
  46.2 5.6 %copy.23 = bf16[2,128,8,512]{3,0,2,1:T(2,128)(2,1)} copy(bf16[2,128,8,512]{1,0,3,2:T(2,128)(2,1)S(1)} %bitcast.48) | data formatting | bytes 4194304 | tf_op jit(solution)/shard_map/all_to_all | solution.py:32
  51.8 2.8 all_to_all.29
  54.6 1.9 fusion.15
  56.5 4.4 %copy.24 = f32[16,128,512]{2,1,0:T(8,128)} copy(f32[16,128,512]{2,0,1:T(8,128)S(1)} %fusion.15) | data formatting | bytes 8388608 | tf_op jit(solution)/shard_map/tj,jpq->tpq/dot_general | solution.py:33
  60.9 4.6 %all-to-all-start.1 = ((f32[16,128,512]{2,1,0:T(8,128)}), f32[16,128,512]{2,1,0:T(8,128)}, u32[]{:S(2)}, u32[]{:S(2)}) async-start(f32[16,128,512]{2,1,0:T(8,128)} %copy.24), calls=%async_computation.1 | async-start | bytes 8388608 | tf_op jit(solution)/shard_map/all_to_all | solution.py:36
  66.5 1.5 mul.58
  68.0 6.3 %reshape.61 = bf16[2,64,16,8,64]{4,3,2,1,0:T(8,128)(2,1)} reshape(bf16[128,16,512]{2,1,0:T(8,128)(2,1)} %param.12) | data formatting | bytes 4194304 | tf_op jit(solution)/shard_map/reshape | solution.py:53
  74.4 5.4 %convert_bitcast_fusion = bf16[2,64,16,8,64]{4,3,2,1,0:T(8,128)(2,1)} fusion(bf16[2,64,16,8,64]{4,3,2,1,0:T(8,128)(2,1)} %reshape.61, s32[2,8]{1,0:T(2,128)S(1)} %copy-done.4, pred[2,8]{1,0:T(4,128)(4,1)S(1)} %iota_compare_fusion.1), kind=kOutput, calls=%fused_computation.6 | convolution fusion | flops 17826048 | bytes 4194384 | tf_op jit(solution)/shard_map/bsn,brksc->brknc/dot_general | solution.py:54
  79.8 5.4 %reshape.75 = bf16[2048,512,1]{1,0,2:T(8,128)(2,1)S(1)} reshape(bf16[2,64,16,8,64]{4,3,2,1,0:T(8,128)(2,1)} %convert_bitcast_fusion) | data formatting | bytes 4194304 | tf_op jit(solution)/shard_map/convert_element_type | solution.py:57
  85.2 1.6 sort.17
  87.0 28.1 %all-to-all-done.1 = f32[16,128,512]{2,1,0:T(8,128)} async-done(((f32[16,128,512]{2,1,0:T(8,128)}), f32[16,128,512]{2,1,0:T(8,128)}, u32[]{:S(2)}, u32[]{:S(2)}) %all-to-all-start.1) | async-done | bytes 4194336 | tf_op jit(solution)/shard_map/all_to_all | solution.py:36
  115.1 6.9 %copy.34 = f32[8,2,128,512]{3,0,2,1:T(8,128)} copy(f32[8,2,128,512]{3,2,1,0:T(8,128)} %bitcast.3) | data formatting | bytes 8388608 | tf_op jit(solution)/shard_map/all_to_all | solution.py:36
  122.1 5.0 %all_to_all.33 = f32[2,128,4096]{2,1,0:T(8,128)} reshape(f32[2,128,8,512]{3,2,1,0:T(8,128)} %bitcast.47) | data formatting | bytes 8388608 | tf_op jit(solution)/shard_map/all_to_all | solution.py:36
  127.1 24.3 %all-gather.2.cloned.1.call-done = bf16[4096,2048]{1,0:T(8,128)(2,1)} async-done(((bf16[128,2048]{1,0:T(8,128)(2,1)}), bf16[4096,2048]{1,0:T(8,128)(2,1)}) %all-gather.2.cloned.1.call-update) | async-done | bytes 16777232 | tf_op jit(solution)/shard_map/all_gather | solution.py:37
  151.4 12.8 %fusion = f32[2,128,2048]{2,1,0:T(8,128)S(1)} fusion(bf16[4096,2048]{1,0:T(8,128)(2,1)} %all-gather.2.cloned.1.call-done, f32[2,128,4096]{2,1,0:T(8,128)} %all_to_all.33), kind=kOutput, calls=%fused_computation.1 | convolution fusion | flops 4299161600 | bytes 23068672 | tf_op jit(solution)/shard_map/tpq,qx->tpx/dot_general | solution.py:18
  164.2 9.6 %fusion.10 = bf16[2,128,2048]{2,1,0:T(8,128)(2,1)} fusion(f32[2,128,2048]{2,1,0:T(8,128)S(1)} %copy-done.3, f32[2,128,2048]{2,1,0:T(8,128)S(1)} %fusion, bf16[4096,2048]{1,0:T(8,128)(2,1)} %all-gather.2.cloned.1.call-done, f32[2,128,4096]{2,1,0:T(8,128)S(1)} %copy-done.2), kind=kOutput, calls=%fused_computation.10 | convolution fusion | flops 4297588736 | bytes 26214400 | tf_op jit(solution)/shard_map/tpq,qx->tpx/dot_general | solution.py:17
  173.8 1.6 convert_element_type.31
  175.3 1.5 convolution_bitcast_fusion
  176.9 1.2 copy.27
  179.7 212.1 %reduce-scatter.2.cloned.1.call-done = f32[2,16,128]{2,1,0:T(8,128)} async-done(((f32[2,512,128]{2,1,0:T(8,128)}), f32[2,16,128]{2,1,0:T(8,128)}) %reduce-scatter.2.cloned.1.call-update) | async-done | bytes 16400 | tf_op jit(solution)/shard_map/reduce_scatter | solution.py:71
  (35 shorter events, 2.8 us)
Async XLA Ops:
  6.5 59.2 %copy-start = (f32[16,16]{1,0:T(8,128)S(1)}, f32[16,16]{1,0:T(8,128)}, u32[]{:S(2)}) copy-start(f32[16,16]{1,0:T(8,128)} %param.10) | copy-start | bytes 3076
  6.5 144.9 %all-gather.2.cloned.1.call-start = ((), (), s32[]{:S(2)}) async-start(), calls=%async_computation.3 | async-start | bytes 17301504 | tf_op jit(solution)/shard_map/all_gather | solution.py:37
  14.7 31.5 %all-to-all-start = ((bf16[2,128,4096]{1,0,2:T(2,128)(2,1)}), bf16[2,128,4096]{1,0,2:T(2,128)(2,1)S(1)}, u32[]{:S(2)}, u32[]{:S(2)}) async-start(bf16[2,128,4096]{1,0,2:T(2,128)(2,1)} %copy.22), calls=%async_computation | async-start | bytes 4194304 | tf_op jit(solution)/shard_map/all_to_all | solution.py:32
  51.8 2.8 copy-start.5
  60.9 54.2 %all-to-all-start.1 = ((f32[16,128,512]{2,1,0:T(8,128)}), f32[16,128,512]{2,1,0:T(8,128)}, u32[]{:S(2)}, u32[]{:S(2)}) async-start(f32[16,128,512]{2,1,0:T(8,128)} %copy.24), calls=%async_computation.1 | async-start | bytes 8388608 | tf_op jit(solution)/shard_map/all_to_all | solution.py:36
  65.5 326.3 %reduce-scatter.2.cloned.1.call-start = ((), (), s32[]{:S(2)}) async-start(), calls=%async_computation.4 | async-start | bytes 540672 | tf_op jit(solution)/shard_map/reduce_scatter | solution.py:71
  68.0 6.3 %copy-start.6 = (s32[2]{0:T(128)S(1)}, s32[2]{0:T(128)}, u32[]{:S(2)}) copy-start(s32[2]{0:T(128)} %param.14) | copy-start | bytes 28
  68.0 6.4 %copy-start.4 = (s32[2,8]{1,0:T(2,128)S(1)}, s32[2,8]{1,0:T(2,128)}, u32[]{:S(2)}) copy-start(s32[2,8]{1,0:T(2,128)} %param.13) | copy-start | bytes 196
  79.8 5.5 %copy-start.7 = (s32[32]{0:T(128)S(1)}, s32[32]{0:T(128)}, u32[]{:S(2)}) copy-start(s32[32]{0:T(128)} %param.15) | copy-start | bytes 388
  151.4 12.8 %copy-start.2 = (f32[2,128,4096]{2,1,0:T(8,128)S(1)}, f32[2,128,4096]{2,1,0:T(8,128)}, u32[]{:S(2)}) copy-start(f32[2,128,4096]{2,1,0:T(8,128)} %all_to_all.33) | copy-start | bytes 12582916
  151.4 12.8 %copy-start.3 = (f32[2,128,2048]{2,1,0:T(8,128)S(1)}, f32[2,128,2048]{2,1,0:T(8,128)}, u32[]{:S(2)}) copy-start(f32[2,128,2048]{2,1,0:T(8,128)} %mul.58) | copy-start | bytes 6291460
  176.8 214.9 %copy-start.1 = (f32[16,16]{1,0:T(8,128)S(1)}, f32[16,16]{1,0:T(8,128)}, u32[]{:S(2)}) copy-start(f32[16,16]{1,0:T(8,128)} %param.10) | copy-start | bytes 3076
Sparse Core Ops, SparseCore 0:
  10.0 141.4 all-gather.1
  179.8 211.9 reduce-scatter.1
where the time goes:
time: 401 us; the launch traced here: 399 us
  waiting for transfers between devices  292 us (73%)
  local copies, waits for them, and re-layouts  50.5 us (13%)
  matrix products  31.1 us (8%)
  between operations  13.6 us (3%)
  starting transfers between devices  9.08 us (2%)
    reduce_scatter x1, waiting for transfers between devices, shards(): lax.psum_scatter(partial_value, 'aux', scatter_dimension=1, tiled=True)  212 us
    all_to_all x1, waiting for transfers between devices, shards(): lax.all_to_all(timed, 'freq', split_axis=0, concat_axis=2, tiled=True)  28.1 us
    all_to_all x1, waiting for transfers between devices, shards(): lax.all_to_all(screened, 'freq', split_axis=2, concat_axis=0, tiled=True)  27.2 us
    all_gather x1, waiting for transfers between devices, shards(): lax.all_gather(flat_state, 'aux', axis=0, tiled=True)  24.3 us
    dot_general x1, matrix products, product(): jnp.einsum('tpq,qx->tpx', lower, piece, preferred_element_type=jnp.float32)  12.8 us
    all_to_all x2, local copies, waits for them, and re-layouts, shards(): lax.all_to_all(timed, 'freq', split_axis=0, concat_axis=2, tiled=True)  11.9 us
    dot_general x1, matrix products, product(): jnp.einsum('tpq,qx->tpx', upper, piece, preferred_element_type=jnp.float32)  9.56 us
    all_to_all x2, local copies, waits for them, and re-layouts, shards(): lax.all_to_all(screened, 'freq', split_axis=2, concat_axis=0, tiled=True)  8.37 us
  transfers between devices with their start and end apart: 4, of which 4 were waited for; matrix products, arithmetic and copies ran while one was open for 12% of the time, Pallas kernels for 0%

commit v1 on v0

v1 whole, which is shorter than its diff:
```python
import functools

import jax
import jax.numpy as jnp
from jax import lax
from jax.experimental import pallas as pl
from jax.experimental.pallas import tpu as pltpu
from jax.sharding import PartitionSpec as P

BAND = 16


def cosine_table(grid_weights, count):
    steps_t = jnp.arange(count, dtype=jnp.float32)
    return grid_weights[None, :] * jnp.cos(
        jnp.pi * (steps_t[:, None] + 0.5) * steps_t[None, :] / count
    )


def chunk_kernel(has_total, *refs):
    if has_total:
        pieces_ref, mix_ref, state_ref, greens_ref, dense_ref, total_ref = refs[:6]
        out_ref, timed_ref, scaled_ref = refs[6:]
    else:
        pieces_ref, mix_ref, state_ref, greens_ref, dense_ref = refs[:5]
        out_ref, timed_ref, scaled_ref = refs[5:]
    sources, local, rows, width = pieces_ref.shape
    freqs = sources * local
    times = greens_ref.shape[0]
    bands = rows // BAND
    targets = scaled_ref.shape[1] // times
    tall = times * BAND
    for band in range(bands):
        piece = pieces_ref[:, :, band * BAND : (band + 1) * BAND, :].reshape(freqs * BAND, width)
        mixed = jnp.dot(mix_ref[...], piece, preferred_element_type=jnp.float32)
        timed_ref[band * tall : (band + 1) * tall, :] = (mixed[:tall] + mixed[tall:]).astype(jnp.bfloat16)

    pair = 2 * targets

    def states(step, carry):
        columns = pl.ds(pl.multiple_of(step * pair, pair), pair)
        contracted = jnp.dot(timed_ref[...], state_ref[:, columns], preferred_element_type=jnp.float32)
        gains = greens_ref[:, columns]
        for time in range(times):
            gain = gains[time : time + 1, :]
            for band in range(bands):
                first = band * tall + time * BAND
                block = (contracted[first : first + BAND, :] * gain).astype(jnp.bfloat16)
                for state in range(2):
                    start = pl.multiple_of(step * 2 * rows + state * rows + band * BAND, BAND)
                    scaled_ref[pl.ds(start, BAND), time * targets : (time + 1) * targets] = block[
                        :, state * targets : (state + 1) * targets
                    ]
        return carry

    lax.fori_loop(0, state_ref.shape[1] // pair, states, 0)

    owners, inner = out_ref.shape[1], out_ref.shape[3]
    for place in range(times // 2):
        columns = slice(place * pair, (place + 1) * pair)
        value = jnp.dot(dense_ref[...], scaled_ref[:, columns], preferred_element_type=jnp.float32)
        for time in range(2):
            part = value[:, time * targets : (time + 1) * targets].reshape(owners, inner, targets)
            if has_total:
                part = part + total_ref[place, :, time, :, :]
            out_ref[place, :, time, :, :] = part.astype(out_ref.dtype)


def chunk(pieces, mix, state, gains, dense, total, owners, dtype):
    sources, local, rows, width = pieces.shape
    times = gains.shape[0]
    depth = dense.shape[1]
    targets = state.shape[1] * rows // depth
    shape = (times // 2, owners, 2, dense.shape[0] // owners, targets)
    operands = [pieces, mix, state, gains, dense]
    if total is not None:
        operands.append(total)
    return pl.pallas_call(
        functools.partial(chunk_kernel, total is not None),
        out_shape=jax.ShapeDtypeStruct(shape, dtype),
        in_specs=[pl.BlockSpec(memory_space=pltpu.VMEM)] * len(operands),
        out_specs=pl.BlockSpec(memory_space=pltpu.VMEM),
        scratch_shapes=[
            pltpu.VMEM((times * rows, width), jnp.bfloat16),
            pltpu.VMEM((depth, times * targets), jnp.bfloat16),
        ],
        compiler_params=pltpu.CompilerParams(vmem_limit_bytes=32 * 1024 * 1024),
        cost_estimate=pl.CostEstimate(
            flops=2 * times * rows * width * state.shape[1] + 2 * dense.shape[0] * depth * times * targets,
            bytes_accessed=8 * 1024 * 1024,
            transcendentals=0,
        ),
    )(*operands)


def shards(
    screened, grid_weights, greens, three_state, three_orbital, block_ids, block_counts, owners
):
    freq_count = lax.axis_size("freq")
    aux_count = lax.axis_size("aux")
    freq = lax.axis_index("freq")
    core = freq % 2
    local_times, rows, width = screened.shape
    total_times = local_times * freq_count
    states = three_state.shape[1]
    targets = three_state.shape[2]
    piece_width = width // freq_count
    block_count, slot_count = block_ids.shape
    orbitals = three_orbital.shape[2]
    block_width = orbitals // slot_count
    row_block = rows // block_count
    chips = freq_count // 2

    pieces = []
    for block in range(block_count):
        own = screened[:, block * row_block : (block + 1) * row_block, :]
        own = own.reshape(local_times, row_block, freq_count, piece_width).transpose(2, 0, 1, 3)
        pieces.append(lax.all_to_all(own, "freq", split_axis=0, concat_axis=0, tiled=True))

    share = rows // freq_count
    flat_state = three_state.reshape(rows, states * targets)
    own_state = lax.dynamic_slice_in_dim(flat_state, freq * share, share, 0)
    slabs = aux_count // freq_count
    moves = []
    for f in range(freq_count):
        for a in range(aux_count):
            moves.append(((a % freq_count) * aux_count + slabs * f + a // freq_count, f * aux_count + a))
    own_state = lax.ppermute(own_state, ("freq", "aux"), moves)
    state = lax.all_gather(own_state, "aux", axis=0, tiled=True)

    table = cosine_table(grid_weights, total_times)

    def halves(array):
        array = array.reshape(chips, 2, local_times, array.shape[1]).transpose(1, 0, 2, 3)
        array = array.reshape(2, chips * local_times, array.shape[3])
        return jnp.where(core == 0, array[::-1], array)

    table = halves(table)
    upper = table.astype(jnp.bfloat16)
    lower = (table - upper.astype(jnp.float32)).astype(jnp.bfloat16)
    same = jnp.eye(BAND, dtype=jnp.bfloat16)
    mix = jnp.stack([upper, lower], 1)
    mix = mix[:, :, :, None, :, None] * same[None, None, None, :, None, :]
    mix = mix.reshape(2, 2 * chips * local_times * BAND, total_times * BAND)
    gains = jnp.repeat(halves(greens), targets, axis=2)

    device = jnp.arange(aux_count, dtype=jnp.int32)
    owned = jnp.sum(jnp.where(owners[None, :] == device[:, None], device[None, :], 0), axis=1)
    inner = orbitals // aux_count
    wanted = (owned[:, None] * inner + jnp.arange(inner, dtype=jnp.int32)[None, :]).reshape(orbitals)
    slot = jnp.arange(slot_count, dtype=jnp.int32)
    listed = block_ids[:, :, None] * block_width + jnp.arange(block_width, dtype=jnp.int32)
    listed = jnp.where(slot[None, :, None] < block_counts[:, None, None], listed, -1).reshape(block_count, orbitals)
    choose = (wanted[None, :, None] == listed[:, None, :]).astype(jnp.bfloat16)
    values = three_orbital.reshape(block_count, row_block, states, orbitals)
    values = values.transpose(0, 2, 1, 3).reshape(block_count, states * row_block, orbitals)
    dense = jnp.einsum("bns,brs->bnr", choose, values, preferred_element_type=jnp.float32).astype(jnp.bfloat16)

    totals = [None, None]
    for block in range(block_count):
        last = block == block_count - 1
        for half in range(2):
            totals[half] = chunk(
                pieces[block], mix[half], state, gains[half], dense[block], totals[half], aux_count,
                jnp.bfloat16 if last and half == 0 else jnp.float32,
            )
    swap = [(f, f ^ 1) for f in range(freq_count)]
    other = lax.ppermute(totals[0], "freq", swap)
    summed = (totals[1] + other.astype(jnp.float32)).astype(jnp.bfloat16)
    groups = [[2 * chip + c for chip in range(chips)] for c in range(2)]
    spread = lax.all_to_all(
        summed, "freq", split_axis=0, concat_axis=0, axis_index_groups=groups, tiled=True
    )
    summed = jnp.sum(spread.astype(jnp.float32), axis=0).astype(jnp.bfloat16)
    spread = lax.all_to_all(summed, "aux", split_axis=0, concat_axis=0, tiled=True)
    return jnp.sum(spread.astype(jnp.float32), axis=0)


def solution(mesh):
    return jax.shard_map(
        shards,
        mesh=mesh,
        in_specs=(
            P("freq", "aux", None),
            P(),
            P(),
            P("aux", None, None),
            P("aux", None, None),
            P("aux", None),
            P("aux"),
            P(),
        ),
        out_specs=P("freq", "aux", None),
        check_vma=False,
    )
```

time: 401 us -> 183 us (0.46)
  waiting for transfers between devices: 292 us -> 59.6 us
  blocking collectives: 0 us -> 38.4 us
  matrix products: 31.1 us -> 2.63 us
  local copies, waits for them, and re-layouts: 50.5 us -> 29.6 us
  Pallas kernels: 0 us -> 18.1 us
  starting transfers between devices: 9.08 us -> 16.9 us
    reduce_scatter x1 -> x0, waiting for transfers between devices: 212 us -> none  [shards(): lax.psum_scatter(partial_value, 'aux', scatter_dimension=1, tiled=True)]
    all_to_all x2, waiting for transfers between devices: 55.3 us -> 3.02 us  [shards(): lax.all_to_all(own, 'freq', split_axis=0, concat_axis=0, tiled=True)]
    all_to_all x0 -> x2, blocking collectives: none -> 38.4 us  [the longest x1 19.8 us: shards(): lax.all_to_all(summed, 'freq', split_axis=0, concat_axis=0, axis_index_gr...]
    all_gather x1, waiting for transfers between devices: 24.3 us -> 56.6 us  [shards(): state = lax.all_gather(own_state, 'aux', axis=0, tiled=True)]
    dot_general x5 -> x1, matrix products: 31.1 us -> 2.63 us  [shards(): jnp.einsum('bns,brs->bnr', choose, values, preferred_element_type=jnp.flo...]
    all_to_all x4 -> x0, local copies, waits for them, and re-layouts: 20.3 us -> none  [the longest x2 11.9 us: shards(): lax.all_to_all(timed, 'freq', split_axis=0, concat_axis=2, tiled=True)]
    pallas_call x0 -> x4, Pallas kernels: none -> 18.1 us  [chunk(): pl.pallas_call(functools.partial(chunk_kernel, total is not None), out_sh...]
    squeeze x0 -> x3, local copies, waits for them, and re-layouts: none -> 7.14 us  [the longest x2 4.42 us: shards(): mix[half]]
  transfers between devices with their start and end apart: 4 -> 5, of which waited for: 4 -> 2; matrix products, arithmetic and copies ran while one was open for 12% -> 12% of each run, Pallas kernels for 0% -> 7%
where the time goes in v1:
time: 183 us; the launch traced here: 182 us
  waiting for transfers between devices  59.6 us (33%)
  blocking collectives  38.4 us (21%)
  local copies, waits for them, and re-layouts  29.6 us (16%)
  Pallas kernels  18.1 us (10%)
  starting transfers between devices  16.9 us (9%)
  between operations  13.7 us (7%)
  other arithmetic  3.31 us (2%)
  matrix products  2.63 us (1%)
    all_gather x1, waiting for transfers between devices, shards(): state = lax.all_gather(own_state, 'aux', axis=0, tiled=True)  56.6 us
    all_to_all x1, blocking collectives, shards(): lax.all_to_all(summed, 'freq', split_axis=0, concat_axis=0, axis_index_gr...  19.8 us
    all_to_all x1, blocking collectives, shards(): lax.all_to_all(summed, 'aux', split_axis=0, concat_axis=0, tiled=True)  18.6 us
    pallas_call x4, Pallas kernels, chunk(): pl.pallas_call(functools.partial(chunk_kernel, total is not None), out_sh...  18.1 us
    all_to_all x2, starting transfers between devices, shards(): lax.all_to_all(own, 'freq', split_axis=0, concat_axis=0, tiled=True)  13.8 us
    unnamed x31, local copies, waits for them, and re-layouts  11.9 us
    squeeze x2, local copies, waits for them, and re-layouts, shards(): mix[half]  4.42 us
  transfers between devices with their start and end apart: 5, of which 2 were waited for; matrix products, arithmetic and copies ran while one was open for 12% of the time, Pallas kernels for 7%

profile of v1, /device:TPU:32, one launch (start us, length us, event | category | flops | bytes accessed | tf_op | source)
XLA Modules:
  0.0 182.2 jit_solution(12155296390042158527)
XLA Ops:
  7.7 3.0 %collective-permute-start = (bf16[16,2048]{1,0:T(8,128)(2,1)S(1)}, bf16[16,2048]{1,0:T(8,128)(2,1)S(1)}, u32[]{:S(2)}, u32[]{:S(2)}) collective-permute-start(bf16[16,2048]{1,0:T(8,128)(2,1)S(1)} %constant_dynamic-slice_fusion), channel_id=1, source_target_pairs={{0,0},{32,1},{64,2},{96,3},{128,4},{160,5},{192,6},{224,7},{1,8},{... | collective-permute-start | bytes 196616 | tf_op jit(solution)/shard_map/ppermute | solution.py:128
  10.8 2.7 %fusion.12 = (bf16[2,64,4096]{2,1,0:T(8,128)(2,1)S(1)}, bf16[2,64,4096]{2,1,0:T(8,128)(2,1)}) fusion(bf16[2,128,4096]{2,1,0:T(8,128)(2,1)} %param.8), kind=kLoop, calls=%fused_computation.38 | loop fusion | bytes 4194304 | tf_op jit(solution)/shard_map/slice | solution.py:116
  14.6 10.3 %all-to-all-start.1 = ((bf16[8,2,64,512]{3,2,1,0:T(8,128)(2,1)}), bf16[8,2,64,512]{3,2,1,0:T(8,128)(2,1)S(1)}, u32[]{:S(2)}, u32[]{:S(2)}) async-start(bf16[8,2,64,512]{3,2,1,0:T(8,128)(2,1)} %bitcast.43), calls=%async_computation.1 | async-start | bytes 2097152 | tf_op jit(solution)/shard_map/all_to_all | solution.py:118
  27.3 1.7 fusion.11
  29.1 2.2 %squeeze.11.refs_1_ = bf16[256,256]{1,0:T(8,128)(2,1)S(1)} reshape(bf16[1,2,8,16,16,16]{5,4,3,2,1,0:T(8,128)(2,1)} %get-tuple-element.5) | data formatting | bytes 262144 | tf_op jit(solution)/shard_map/squeeze | solution.py:164
  31.3 2.8 %copy.25 = bf16[2,16,64,512]{3,2,1,0:T(8,128)(2,1)S(1)} copy(bf16[2,16,64,512]{3,1,2,0:T(8,128)(2,1)} %bitcast.49) | data formatting | bytes 4194304 | tf_op jit(solution)/shard_map/transpose | solution.py:156
  35.2 2.6 %fusion.2 = bf16[2,512,1024]{2,1,0:T(8,128)(2,1)} fusion(bf16[2,1024,512]{2,1,0:T(8,128)(2,1)S(1)} %bitcast.50, s32[2,512]{1,0:T(2,128)S(1)} %add_select_fusion, s32[512]{0:T(512)S(1)} %add.75), kind=kOutput, calls=%fused_computation.3 | convolution fusion | flops 1075314688 | bytes 4200448 | tf_op jit(solution)/shard_map/bns,brs->bnr/dot_general | solution.py:157
  37.9 3.0 %all-to-all-done.1.refs_0_ = bf16[8,2,64,512]{3,2,1,0:T(8,128)(2,1)S(1)} async-done(((bf16[8,2,64,512]{3,2,1,0:T(8,128)(2,1)}), bf16[8,2,64,512]{3,2,1,0:T(8,128)(2,1)S(1)}, u32[]{:S(2)}, u32[]{:S(2)}) %all-to-all-start.1) | async-done | bytes 1048608 | tf_op jit(solution)/shard_map/all_to_all | solution.py:118
  40.9 3.6 %all-to-all-start = ((bf16[8,2,64,512]{3,2,1,0:T(8,128)(2,1)}), bf16[8,2,64,512]{3,2,1,0:T(8,128)(2,1)S(1)}, u32[]{:S(2)}, u32[]{:S(2)}) async-start(bf16[8,2,64,512]{3,2,1,0:T(8,128)(2,1)} %bitcast.45), calls=%async_computation | async-start | bytes 2097152 | tf_op jit(solution)/shard_map/all_to_all | solution.py:118
  44.5 2.7 %slice_bitcast_fusion = (bf16[512,1024]{1,0:T(8,128)(2,1)}, bf16[512,1024]{1,0:T(8,128)(2,1)S(1)}) fusion(bf16[2,512,1024]{2,1,0:T(8,128)(2,1)} %fusion.2), kind=kLoop, calls=%fused_computation.6 | loop fusion | bytes 4194304 | tf_op jit(solution)/shard_map/squeeze | solution.py:164
  47.3 56.6 %all-gather.2.cloned.1.call-done.refs_2_ = bf16[512,2048]{1,0:T(8,128)(2,1)} async-done(((bf16[16,2048]{1,0:T(8,128)(2,1)}), bf16[512,2048]{1,0:T(8,128)(2,1)}) %all-gather.2.cloned.1.call-update) | async-done | bytes 2097168 | tf_op jit(solution)/shard_map/all_gather | solution.py:129
  103.8 1.6 copy-done
  106.6 4.3 %shard_map.84.refs_5_ = f32[4,32,2,16,128]{4,3,2,1,0:T(8,128)S(1)} custom-call(bf16[8,2,64,512]{3,2,1,0:T(8,128)(2,1)S(1)} %all-to-all-done.1.refs_0_, bf16[256,256]{1,0:T(8,128)(2,1)S(1)} %squeeze.11.refs_1_, bf16[512,2048]{1,0:T(8,128)(2,1)S(1)} %copy-done, f32[8,2048]{1,0:T(8,128)S(1)} %broadcast_bitcast_fusion.refs_3_, bf16[512,1024]{1,0:T(8,128)(2,1)S(1)} %copy-done.4), custom_call_target="tpu_custom_call" | custom-call | flops 2147483648 | bytes 8388608 | tf_op jit(solution)/shard_map/pallas_call | solution.py:78
  110.9 1.3 copy-done.6
  112.3 1.6 copy-done.1
  113.8 1.6 copy-done.7
  115.4 5.3 %shard_map.85 = bf16[4,32,2,16,128]{4,3,2,1,0:T(8,128)(2,1)} custom-call(bf16[8,2,64,512]{3,2,1,0:T(8,128)(2,1)S(1)} %all-to-all-done.refs_0_, bf16[256,256]{1,0:T(8,128)(2,1)S(1)} %squeeze.11.refs_1_, bf16[512,2048]{1,0:T(8,128)(2,1)S(1)} %copy-done.1, f32[8,2048]{1,0:T(8,128)S(1)} %broadcast_bitcast_fusion.refs_3_, ...), custom_call_target="tpu_custom_call" | custom-call | flops 2147483648 | bytes 8388608 | tf_op jit(solution)/shard_map/pallas_call | solution.py:78
  120.8 2.2 %squeeze.8.refs_1_ = bf16[256,256]{1,0:T(8,128)(2,1)S(1)} reshape(bf16[1,2,8,16,16,16]{5,4,3,2,1,0:T(8,128)(2,1)} %get-tuple-element.6) | data formatting | bytes 262144 | tf_op jit(solution)/shard_map/squeeze | solution.py:164
  123.1 1.6 copy-done.2
  125.9 4.3 %shard_map.82.refs_5_ = f32[4,32,2,16,128]{4,3,2,1,0:T(8,128)S(1)} custom-call(bf16[8,2,64,512]{3,2,1,0:T(8,128)(2,1)S(1)} %all-to-all-done.1.refs_0_, bf16[256,256]{1,0:T(8,128)(2,1)S(1)} %squeeze.8.refs_1_, bf16[512,2048]{1,0:T(8,128)(2,1)S(1)} %copy-done.2, f32[8,2048]{1,0:T(8,128)S(1)} %broadcast_bitcast_fusion.1.refs_3_, bf16[512,1024]{1,0:T(8,128)(2,1)S(1)} %copy-done.5), custom_call_target="tpu_custom_call" | custom-call | flops 2147483648 | bytes 8388608 | tf_op jit(solution)/shard_map/pallas_call | solution.py:78
  130.2 4.3 %shard_map.83 = f32[4,32,2,16,128]{4,3,2,1,0:T(8,128)S(1)} custom-call(bf16[8,2,64,512]{3,2,1,0:T(8,128)(2,1)S(1)} %all-to-all-done.refs_0_, bf16[256,256]{1,0:T(8,128)(2,1)S(1)} %squeeze.8.refs_1_, bf16[512,2048]{1,0:T(8,128)(2,1)S(1)} %copy-done.3, f32[8,2048]{1,0:T(8,128)S(1)} %broadcast_bitcast_fusion.1.refs_3_, ...), custom_call_target="tpu_custom_call" | custom-call | flops 2147483648 | bytes 8388608 | tf_op jit(solution)/shard_map/pallas_call | solution.py:78
  134.5 1.5 add_convert_fusion
  136.1 19.8 %all_to_all.20 = bf16[4,32,2,16,128]{4,3,2,1,0:T(8,128)(2,1)S(1)} all-to-all(bf16[4,32,2,16,128]{4,3,2,1,0:T(8,128)(2,1)S(1)} %add_convert_fusion), channel_id=1, replica_groups={{0,64,128,192},{32,96,160,224},{1,65,129,193},{33,97,161,225},{2,66,130..., dimensions={0} | all-to-all | bytes 2097152 | tf_op jit(solution)/shard_map/all_to_all | solution.py:171
  156.1 18.6 %all_to_all.21 = bf16[32,2,16,128]{3,2,1,0:T(8,128)(2,1)S(1)} all-to-all(bf16[32,2,16,128]{3,2,1,0:T(8,128)(2,1)S(1)} %reduce_sum.31), channel_id=1, replica_groups=mesh['freq'=8,'aux'=32] {'aux'}, dimensions={0} | all-to-all | bytes 524288 | tf_op jit(solution)/shard_map/all_to_all | solution.py:175
  (67 shorter events, 9.3 us)
Async XLA Ops:
  7.7 17.4 %collective-permute-start = (bf16[16,2048]{1,0:T(8,128)(2,1)S(1)}, bf16[16,2048]{1,0:T(8,128)(2,1)S(1)}, u32[]{:S(2)}, u32[]{:S(2)}) collective-permute-start(bf16[16,2048]{1,0:T(8,128)(2,1)S(1)} %constant_dynamic-slice_fusion), channel_id=1, source_target_pairs={{0,0},{32,1},{64,2},{96,3},{128,4},{160,5},{192,6},{224,7},{1,8},{... | collective-permute-start | bytes 196616 | tf_op jit(solution)/shard_map/ppermute | solution.py:128
  13.5 11.5 %copy-start.13 = (s32[32]{0:T(128)S(1)}, s32[32]{0:T(128)}, u32[]{:S(2)}) copy-start(s32[32]{0:T(128)} %param.15) | copy-start | bytes 388
  13.5 12.4 %copy-start.10 = (f32[16,16]{1,0:T(8,128)S(1)}, f32[16,16]{1,0:T(8,128)}, u32[]{:S(2)}) copy-start(f32[16,16]{1,0:T(8,128)} %param.10) | copy-start | bytes 3076
  13.5 12.5 %copy-start.11 = (s32[2,8]{1,0:T(2,128)S(1)}, s32[2,8]{1,0:T(2,128)}, u32[]{:S(2)}) copy-start(s32[2,8]{1,0:T(2,128)} %param.13) | copy-start | bytes 196
  13.5 12.5 %copy-start.12 = (f32[16]{0:T(128)S(1)}, f32[16]{0:T(128)}, u32[]{:S(2)}) copy-start(f32[16]{0:T(128)} %param.9) | copy-start | bytes 196
  14.6 12.1 %copy-start.14 = (s32[2]{0:T(128)S(1)}, s32[2]{0:T(128)}, u32[]{:S(2)}) copy-start(s32[2]{0:T(128)} %param.14) | copy-start | bytes 28
  14.6 26.2 %all-to-all-start.1 = ((bf16[8,2,64,512]{3,2,1,0:T(8,128)(2,1)}), bf16[8,2,64,512]{3,2,1,0:T(8,128)(2,1)S(1)}, u32[]{:S(2)}, u32[]{:S(2)}) async-start(bf16[8,2,64,512]{3,2,1,0:T(8,128)(2,1)} %bitcast.43), calls=%async_computation.1 | async-start | bytes 2097152 | tf_op jit(solution)/shard_map/all_to_all | solution.py:118
  24.9 78.9 %all-gather.2.cloned.1.call-start = ((), (), s32[]{:S(2)}) async-start(), calls=%async_computation.4 | async-start | bytes 2162688 | tf_op jit(solution)/shard_map/all_gather | solution.py:129
  25.1 0.6 copy-start.9
  31.3 2.9 %copy-start.8 = (bf16[2,64,4096]{2,1,0:T(8,128)(2,1)S(1)}, bf16[2,64,4096]{2,1,0:T(8,128)(2,1)}, u32[]{:S(2)}) copy-start(bf16[2,64,4096]{2,1,0:T(8,128)(2,1)} %get-tuple-element.10) | copy-start | bytes 3145732
  40.9 71.4 %all-to-all-start = ((bf16[8,2,64,512]{3,2,1,0:T(8,128)(2,1)}), bf16[8,2,64,512]{3,2,1,0:T(8,128)(2,1)S(1)}, u32[]{:S(2)}, u32[]{:S(2)}) async-start(bf16[8,2,64,512]{3,2,1,0:T(8,128)(2,1)} %bitcast.45), calls=%async_computation | async-start | bytes 2097152 | tf_op jit(solution)/shard_map/all_to_all | solution.py:118
  103.8 1.6 copy-start
  105.4 1.2 copy-start.4
  110.9 1.3 copy-start.6
  112.2 1.6 copy-start.1
  113.8 1.6 copy-start.7
  120.7 13.8 %collective-permute-start.1 = (bf16[4,32,2,16,128]{4,3,2,1,0:T(8,128)(2,1)}, bf16[4,32,2,16,128]{4,3,2,1,0:T(8,128)(2,1)}, u32[]{:S(2)}, u32[]{:S(2)}) collective-permute-start(bf16[4,32,2,16,128]{4,3,2,1,0:T(8,128)(2,1)} %shard_map.85), channel_id=1, source_target_pairs={{0,32},{32,0},{64,96},{96,64},{128,160},{160,128},{192,224},{224,1... | collective-permute-start | bytes 3145736 | tf_op jit(solution)/shard_map/ppermute | solution.py:168
  123.1 1.6 copy-start.2
  124.7 1.2 copy-start.5
  125.9 4.3 %copy-start.3 = (bf16[512,2048]{1,0:T(8,128)(2,1)S(1)}, bf16[512,2048]{1,0:T(8,128)(2,1)}, u32[]{:S(2)}) copy-start(bf16[512,2048]{1,0:T(8,128)(2,1)} %all-gather.2.cloned.1.call-done.refs_2_) | copy-start | bytes 6291460
Sparse Core Ops, SparseCore 0:
  28.4 75.4 all-gather.1

commit v2 on v1

v2 whole, which is shorter than its diff:
```python
import functools

import jax
import jax.numpy as jnp
from jax import lax
from jax.experimental import pallas as pl
from jax.experimental.pallas import tpu as pltpu
from jax.sharding import PartitionSpec as P

BAND = 16
DEPTH = 8
SHIFTS = ((0, 4, 3, 5, 2, 6, 1, 7), (0, 4, 1, 7, 2, 6, 3, 5))
WHOLE = pl.BlockSpec(memory_space=pltpu.VMEM)


def params():
    return pltpu.CompilerParams(vmem_limit_bytes=32 * 1024 * 1024)


def pick_kernel(place_ref, screened_ref, out_ref):
    place = place_ref[0]
    row, column = place // DEPTH, place % DEPTH
    odd = column % 2
    slab = out_ref.shape[3] // 4
    for f in range(out_ref.shape[0]):
        far = lax.rem(column + jnp.where(odd == 1, SHIFTS[1][f], SHIFTS[0][f]), DEPTH)
        for i in range(4):
            start = (lax.rem(row + i, 4) * DEPTH + far) * slab
            out_ref[f, :, :, i * slab : (i + 1) * slab] = screened_ref[:, :, pl.ds(pl.multiple_of(start, slab), slab)]


def pick(place, screened, freqs):
    local, rows, width = screened.shape
    tall = rows // 4
    return pl.pallas_call(
        pick_kernel,
        out_shape=jax.ShapeDtypeStruct((freqs, local, rows, width // freqs), screened.dtype),
        grid_spec=pltpu.PrefetchScalarGridSpec(
            num_scalar_prefetch=1,
            grid=(rows // tall,),
            in_specs=[pl.BlockSpec((local, tall, width), lambda i, place: (0, i, 0))],
            out_specs=pl.BlockSpec((freqs, local, tall, width // freqs), lambda i, place: (0, 0, i, 0)),
        ),
        compiler_params=params(),
    )(place, screened)


def mix_kernel(pieces_ref, mix_ref, out_ref):
    sources, local, rows, width = pieces_ref.shape
    freqs = sources * local
    tall = out_ref.shape[1] // (rows // BAND)
    for band in range(rows // BAND):
        piece = pieces_ref[:, :, band * BAND : (band + 1) * BAND, :].reshape(freqs * BAND, width)
        for half in range(2):
            mixed = jnp.dot(mix_ref[half], piece, preferred_element_type=jnp.float32)
            out_ref[half, band * tall : (band + 1) * tall, :] = (mixed[:tall] + mixed[tall:]).astype(jnp.bfloat16)


def transform(pieces, mix):
    sources, local, rows, width = pieces.shape
    times = sources * local // 2
    return pl.pallas_call(
        mix_kernel,
        out_shape=jax.ShapeDtypeStruct((2, times * rows, width), jnp.bfloat16),
        in_specs=[WHOLE] * 2,
        out_specs=WHOLE,
        compiler_params=params(),
    )(pieces, mix)


def contract_kernel(half, part, has_total, *refs):
    timed_ref, gains_ref, dense_ref = refs[:3]
    slabs = refs[3:7]
    refs = refs[7:]
    total_ref = None
    if has_total:
        total_ref, refs = refs[0], refs[1:]
    out_ref, state_ref, scaled_ref = refs
    slab = slabs[0].shape[0]
    for i in range(4):
        state_ref[i * slab : (i + 1) * slab, :] = slabs[i][...]
    times = gains_ref.shape[1]
    bands = timed_ref.shape[1] // (times * BAND)
    targets = scaled_ref.shape[1] // times
    span = state_ref.shape[1]
    blocks = dense_ref.shape[0]
    deep = scaled_ref.shape[0] // blocks
    bands_in = bands // blocks
    row_block = bands_in * BAND
    tall = times * BAND
    pair = 2 * targets

    def states(step, carry):
        columns = pl.ds(pl.multiple_of(step * pair, pair), pair)
        contracted = jnp.dot(timed_ref[half], state_ref[:, columns], preferred_element_type=jnp.float32)
        gains = gains_ref[half, :, pl.ds(pl.multiple_of(part * span + step * pair, pair), pair)]
        for time in range(times):
            gain = gains[time : time + 1, :]
            for band in range(bands):
                first = band * tall + time * BAND
                block = (contracted[first : first + BAND, :] * gain).astype(jnp.bfloat16)
                base = (band // bands_in) * deep + (band % bands_in) * BAND
                for state in range(2):
                    start = pl.multiple_of(base + (step * 2 + state) * row_block, BAND)
                    scaled_ref[pl.ds(start, BAND), time * targets : (time + 1) * targets] = block[
                        :, state * targets : (state + 1) * targets
                    ]
        return carry

    lax.fori_loop(0, span // pair, states, 0)

    owners, inner = out_ref.shape[1], out_ref.shape[3]
    for place in range(times // 2):
        columns = slice(place * pair, (place + 1) * pair)
        value = sum(
            jnp.dot(
                dense_ref[block, :, part * deep : (part + 1) * deep],
                scaled_ref[block * deep : (block + 1) * deep, columns],
                preferred_element_type=jnp.float32,
            )
            for block in range(blocks)
        )
        for time in range(2):
            piece = value[:, time * targets : (time + 1) * targets].reshape(owners, inner, targets)
            if has_total:
                piece = piece + total_ref[place, :, time, :, :]
            out_ref[place, :, time, :, :] = piece.astype(out_ref.dtype)


def contract(half, part, timed, gains, dense, slabs, total, owners, dtype):
    times = gains.shape[1]
    slab, span = slabs[0].shape
    rows = timed.shape[1] // times
    states = dense.shape[0] * dense.shape[2] // rows
    targets = gains.shape[2] // states
    depth = span // targets * rows
    shape = (times // 2, owners, 2, dense.shape[1] // owners, targets)
    operands = [timed, gains, dense, *slabs]
    if total is not None:
        operands.append(total)
    return pl.pallas_call(
        functools.partial(contract_kernel, half, part, total is not None),
        out_shape=jax.ShapeDtypeStruct(shape, dtype),
        in_specs=[WHOLE] * len(operands),
        out_specs=WHOLE,
        scratch_shapes=[
            pltpu.VMEM((4 * slab, span), jnp.bfloat16),
            pltpu.VMEM((depth, times * targets), jnp.bfloat16),
        ],
        compiler_params=params(),
        cost_estimate=pl.CostEstimate(
            flops=2 * timed.shape[1] * 4 * slab * span + 2 * dense.shape[1] * depth * times * targets,
            bytes_accessed=8 * 1024 * 1024,
            transcendentals=0,
        ),
    )(*operands)


def shards(
    screened, grid_weights, greens, three_state, three_orbital, block_ids, block_counts, owners
):
    freq_count = lax.axis_size("freq")
    aux_count = lax.axis_size("aux")
    freq = lax.axis_index("freq")
    chip, core = freq // 2, freq % 2
    local_times, rows, width = screened.shape
    total_times = local_times * freq_count
    states = three_state.shape[1]
    targets = three_state.shape[2]
    block_count, slot_count = block_ids.shape
    orbitals = three_orbital.shape[2]
    block_width = orbitals // slot_count
    row_block = rows // block_count
    chips = freq_count // 2
    height = aux_count // DEPTH

    along = []
    for f in range(freq_count):
        for y in range(height):
            for z in range(DEPTH):
                far = (z + SHIFTS[z % 2][f]) % DEPTH
                along.append((f * aux_count + y * DEPTH + far, f * aux_count + y * DEPTH + z))
    across = [
        [(((y + i) % height) * DEPTH + z, y * DEPTH + z) for y in range(height) for z in range(DEPTH)]
        for i in range(height)
    ]
    flat_state = three_state.reshape(rows, states * targets)
    span = states * targets // 2
    slabs = []
    for part in range(2):
        own = lax.ppermute(flat_state[:, part * span : (part + 1) * span], ("freq", "aux"), along)
        slabs.append([own] + [lax.ppermute(own, "aux", across[i]) for i in range(1, height)])

    place = lax.axis_index("aux").astype(jnp.int32).reshape(1)
    pieces = pick(place, screened, freq_count)
    pieces = lax.all_to_all(pieces, "freq", split_axis=0, concat_axis=0, tiled=True)

    half = jnp.arange(2, dtype=jnp.int32)[:, None, None]
    other = jnp.arange(chips, dtype=jnp.int32)[None, :, None]
    step = jnp.arange(local_times, dtype=jnp.int32)[None, None, :]
    time = ((chip + other) % chips) * 2 * local_times + ((core + 1 + half) % 2) * local_times + step
    time = time.reshape(2, chips * local_times)
    freqs = jnp.arange(total_times, dtype=jnp.int32)
    table = grid_weights * jnp.cos(
        jnp.pi * (time[:, :, None].astype(jnp.float32) + 0.5) * freqs.astype(jnp.float32) / total_times
    )
    upper = table.astype(jnp.bfloat16)
    lower = (table - upper.astype(jnp.float32)).astype(jnp.bfloat16)
    same = jnp.eye(BAND, dtype=jnp.bfloat16)
    mix = jnp.stack([upper, lower], 1)
    mix = mix[:, :, :, None, :, None] * same[None, None, None, :, None, :]
    mix = mix.reshape(2, 2 * chips * local_times * BAND, total_times * BAND)
    gains = jnp.sum(jnp.where(time[:, :, None, None] == freqs[:, None], greens, 0.0), axis=2)
    gains = jnp.repeat(gains, targets, axis=2)

    device = jnp.arange(aux_count, dtype=jnp.int32)
    owned = jnp.sum(jnp.where(owners[None, :] == device[:, None], device[None, :], 0), axis=1)
    inner = orbitals // aux_count
    wanted = (owned[:, None] * inner + jnp.arange(inner, dtype=jnp.int32)[None, :]).reshape(orbitals)
    slot = jnp.arange(slot_count, dtype=jnp.int32)
    listed = block_ids[:, :, None] * block_width + jnp.arange(block_width, dtype=jnp.int32)
    listed = jnp.where(slot[None, :, None] < block_counts[:, None, None], listed, -1).reshape(block_count, orbitals)
    choose = (wanted[None, :, None] == listed[:, None, :]).astype(jnp.bfloat16)
    values = three_orbital.reshape(block_count, row_block, states, orbitals)
    values = values.transpose(0, 2, 1, 3).reshape(block_count, states * row_block, orbitals)
    dense = jnp.einsum("bns,brs->bnr", choose, values, preferred_element_type=jnp.float32).astype(jnp.bfloat16)

    timed = transform(pieces, mix)
    partial = functools.partial(contract, timed=timed, gains=gains, dense=dense, owners=aux_count)
    given = partial(0, 0, slabs=slabs[0], total=None, dtype=jnp.float32)
    kept = partial(1, 0, slabs=slabs[0], total=None, dtype=jnp.float32)
    given = partial(0, 1, slabs=slabs[1], total=given, dtype=jnp.bfloat16)
    kept = partial(1, 1, slabs=slabs[1], total=kept, dtype=jnp.float32)
    taken = lax.ppermute(given, "freq", [(f, f ^ 1) for f in range(freq_count)])

    def chip_shift(by):
        return [(2 * x + c, 2 * ((x + by) % chips) + c) for x in range(chips) for c in range(2)]

    def joined(index):
        return kept[index] + taken[index].astype(jnp.float32)

    cut = aux_count // 2
    far = joined(2).astype(jnp.bfloat16)
    from_left = lax.ppermute(far[:cut], "freq", chip_shift(1))
    from_right = lax.ppermute(far[cut:], "freq", chip_shift(-1))
    right = joined(1).at[:cut].add(from_left.astype(jnp.float32)).astype(jnp.bfloat16)
    left = joined(3).at[cut:].add(from_right.astype(jnp.float32)).astype(jnp.bfloat16)
    from_left = lax.ppermute(right, "freq", chip_shift(1))
    from_right = lax.ppermute(left, "freq", chip_shift(-1))
    summed = joined(0) + from_left.astype(jnp.float32) + from_right.astype(jnp.float32)
    spread = lax.all_to_all(summed.astype(jnp.bfloat16), "aux", split_axis=0, concat_axis=0, tiled=True)
    return jnp.sum(spread.astype(jnp.float32), axis=0)


def solution(mesh):
    return jax.shard_map(
        shards,
        mesh=mesh,
        in_specs=(
            P("freq", "aux", None),
            P(),
            P(),
            P("aux", None, None),
            P("aux", None, None),
            P("aux", None),
            P("aux"),
            P(),
        ),
        out_specs=P("freq", "aux", None),
        check_vma=False,
    )
```

time: 183 us -> 106 us (0.58)
  waiting for transfers between devices: 59.6 us -> 16.2 us
  blocking collectives: 38.4 us -> 17.4 us
  starting transfers between devices: 16.9 us -> 31.4 us
  between operations: 13.7 us -> 0.32 us
  local copies, waits for them, and re-layouts: 29.6 us -> 17 us
    all_gather x1 -> x0, waiting for transfers between devices: 56.6 us -> none  [shards(): state = lax.all_gather(own_state, 'aux', axis=0, tiled=True)]
    all_to_all x2 -> x1, blocking collectives: 38.4 us -> 17.4 us  [shards(): lax.all_to_all(summed.astype(jnp.bfloat16), 'aux', split_axis=0, concat_a...]
    ppermute x2 -> x13, waiting for transfers between devices: 0.01 us -> 16.2 us  [the longest x1 5.27 us: shards(): from_right = lax.ppermute(left, 'freq', chip_shift(-1))]
    ppermute x2 -> x13, starting transfers between devices: 3.03 us -> 18.3 us  [the longest x6 9.35 us: shards(): lax.ppermute(own, 'aux', across[i])]
    mul x0 -> x4, local copies, waits for them, and re-layouts: none -> 9.55 us  [shards(): mix = mix[:, :, :, None, :, None] * same[None, None, None, :, None, :]]
    unnamed x31 -> x23, local copies, waits for them, and re-layouts: 11.9 us -> 3.77 us
    squeeze x3 -> x0, local copies, waits for them, and re-layouts: 7.14 us -> none  [the longest x2 4.42 us: shards(): mix[half]]
    slice x5 -> x2, local copies, waits for them, and re-layouts: 4.61 us -> 0.06 us  [the longest x1 0.04 us: shards(): flat_state[:, part * span:(part + 1) * span]]
  transfers between devices with their start and end apart: 5 -> 14, of which waited for: 2 -> 5; matrix products, arithmetic and copies ran while one was open for 12% -> 17% of each run, Pallas kernels for 7% -> 14%
where the time goes in v2:
time: 106 us
  starting transfers between devices  31.4 us (30%)
  Pallas kernels  18.2 us (17%)
  blocking collectives  17.4 us (16%)
  local copies, waits for them, and re-layouts  17 us (16%)
  waiting for transfers between devices  16.2 us (15%)
  other arithmetic  2.9 us (3%)
  matrix products  2.63 us (2%)
    all_to_all x1, blocking collectives, shards(): lax.all_to_all(summed.astype(jnp.bfloat16), 'aux', split_axis=0, concat_a...  17.4 us
    pallas_call x4, Pallas kernels, contract(): pl.pallas_call(functools.partial(contract_kernel, half, part, total is no...  15.9 us
    all_to_all x1, starting transfers between devices, shards(): lax.all_to_all(pieces, 'freq', split_axis=0, concat_axis=0, tiled=True)  13.1 us
    mul x4, local copies, waits for them, and re-layouts, shards(): mix = mix[:, :, :, None, :, None] * same[None, None, None, :, None, :]  9.55 us
    ppermute x6, starting transfers between devices, shards(): lax.ppermute(own, 'aux', across[i])  9.35 us
    ppermute x1, waiting for transfers between devices, shards(): from_right = lax.ppermute(left, 'freq', chip_shift(-1))  5.27 us
    ppermute x6, waiting for transfers between devices, shards(): lax.ppermute(own, 'aux', across[i])  4.02 us
    ppermute x1, starting transfers between devices, shards(): from_right = lax.ppermute(left, 'freq', chip_shift(-1))  3.77 us
  transfers between devices with their start and end apart: 14, of which 5 were waited for; matrix products, arithmetic and copies ran while one was open for 17% of the time, Pallas kernels for 14%

profile of v2, /device:TPU:32, one launch (start us, length us, event | category | flops | bytes accessed | tf_op | source)
XLA Modules:
  0.0 106.0 jit_solution(8590112973449917548)
XLA Ops:
  0.0 1.3 %copy.15 = bf16[16,8,16,128]{3,1,2,0:T(8,128)(2,1)S(1)} copy(bf16[16,8,16,128]{3,2,1,0:T(8,128)(2,1)} %bitcast.47) | data formatting | bytes 1048576
  1.4 1.4 %collective-permute-start.4 = (bf16[128,1024]{1,0:T(8,128)(2,1)S(1)}, bf16[128,1024]{1,0:T(8,128)(2,1)}, u32[]{:S(2)}, u32[]{:S(2)}) collective-permute-start(bf16[128,1024]{1,0:T(8,128)(2,1)S(1)} %get-tuple-element.34), channel_id=1, source_target_pairs={{0,0},{1,1},{2,2},{3,3},{4,4},{5,5},{6,6},{7,7},{8,8},{9,9},{10,10... | collective-permute-start | bytes 786440 | tf_op jit(solution)/shard_map/ppermute | solution.py:191
  4.4 1.3 %copy-done = bf16[8,2,128,512]{3,2,1,0:T(8,128)(2,1)} copy-done((bf16[8,2,128,512]{3,2,1,0:T(8,128)(2,1)}, bf16[8,2,128,512]{3,2,1,0:T(8,128)(2,1)S(1)}, u32[]{:S(2)}) %copy-start) | copy-done | bytes 2097176
  5.8 13.1 %all-to-all-start = ((bf16[8,2,128,512]{3,2,1,0:T(8,128)(2,1)}), bf16[8,2,128,512]{3,2,1,0:T(8,128)(2,1)S(1)}, u32[]{:S(2)}, u32[]{:S(2)}) async-start(bf16[8,2,128,512]{3,2,1,0:T(8,128)(2,1)} %copy-done), calls=%async_computation | async-start | bytes 4194304 | tf_op jit(solution)/shard_map/all_to_all | solution.py:196
  20.3 2.8 %copy.12 = bf16[2,16,64,512]{3,2,1,0:T(8,128)(2,1)S(1)} copy(bf16[2,16,64,512]{3,1,2,0:T(8,128)(2,1)} %bitcast.44) | data formatting | bytes 4194304 | tf_op jit(solution)/shard_map/transpose | solution.py:225
  23.2 2.6 %fusion.2.refs_2_ = bf16[2,512,1024]{2,1,0:T(8,128)(2,1)} fusion(bf16[2,1024,512]{2,1,0:T(8,128)(2,1)S(1)} %bitcast.45, s32[2,512]{1,0:T(2,128)S(1)} %add_select_fusion, s32[512]{0:T(512)S(1)} %add.212), kind=kOutput, calls=%fused_computation.2 | convolution fusion | flops 1075314688 | bytes 4200448 | tf_op jit(solution)/shard_map/bns,brs->bnr/dot_general | solution.py:226
  25.8 1.6 %collective-permute-start.7 = (bf16[128,1024]{1,0:T(8,128)(2,1)}, bf16[128,1024]{1,0:T(8,128)(2,1)S(1)}, u32[]{:S(2)}, u32[]{:S(2)}) collective-permute-start(bf16[128,1024]{1,0:T(8,128)(2,1)} %collective-permute-done.4.refs_3_), channel_id=1, source_target_pairs={{24,0},{25,1},{26,2},{27,3},{28,4},{29,5},{30,6},{31,7},{0,8},{1,9... | collective-permute-start | bytes 786440 | tf_op jit(solution)/shard_map/ppermute | solution.py:192
  27.5 3.0 %collective-permute-start.6 = (bf16[128,1024]{1,0:T(8,128)(2,1)}, bf16[128,1024]{1,0:T(8,128)(2,1)}, u32[]{:S(2)}, u32[]{:S(2)}) collective-permute-start(bf16[128,1024]{1,0:T(8,128)(2,1)} %collective-permute-done.4.refs_3_), channel_id=1, source_target_pairs={{16,0},{17,1},{18,2},{19,3},{20,4},{21,5},{22,6},{23,7},{24,8},{25... | collective-permute-start | bytes 786440 | tf_op jit(solution)/shard_map/ppermute | solution.py:192
  30.5 1.3 %collective-permute-start.5 = (bf16[128,1024]{1,0:T(8,128)(2,1)}, bf16[128,1024]{1,0:T(8,128)(2,1)}, u32[]{:S(2)}, u32[]{:S(2)}) collective-permute-start(bf16[128,1024]{1,0:T(8,128)(2,1)} %collective-permute-done.4.refs_3_), channel_id=1, source_target_pairs={{8,0},{9,1},{10,2},{11,3},{12,4},{13,5},{14,6},{15,7},{16,8},{17,9... | collective-permute-start | bytes 786440 | tf_op jit(solution)/shard_map/ppermute | solution.py:192
  33.0 2.8 %mul.114 = bf16[256,256]{1,0:T(8,128)(2,1)} reshape(bf16[2,8,16,16,16]{4,3,2,1,0:T(8,128)(2,1)} %mul.113) | data formatting | bytes 262144 | tf_op jit(solution)/shard_map/mul | solution.py:211
  35.9 1.7 %mul.111 = bf16[2,2,8,16,16,16]{5,4,3,2,1,0:T(8,128)(2,1)} broadcast(bf16[2,2,8,16]{3,2,1,0:T(8,128)(2,1)S(1)} %pad_maximum_fusion), dimensions={0,1,2,4} | broadcast | bytes 263168 | tf_op jit(solution)/shard_map/mul | solution.py:211
  37.6 3.9 %mul.112 = bf16[2,256,256]{2,1,0:T(8,128)(2,1)} reshape(bf16[2,2,8,16,16,16]{5,4,3,2,1,0:T(8,128)(2,1)} %mul.111) | data formatting | bytes 524288 | tf_op jit(solution)/shard_map/mul | solution.py:211
  43.6 2.0 %collective-permute-start.1 = (bf16[128,1024]{1,0:T(8,128)(2,1)S(1)}, bf16[128,1024]{1,0:T(8,128)(2,1)S(1)}, u32[]{:S(2)}, u32[]{:S(2)}) collective-permute-start(bf16[128,1024]{1,0:T(8,128)(2,1)S(1)} %collective-permute-done.refs_3_), channel_id=1, source_target_pairs={{8,0},{9,1},{10,2},{11,3},{12,4},{13,5},{14,6},{15,7},{16,8},{17,9... | collective-permute-start | bytes 786440 | tf_op jit(solution)/shard_map/ppermute | solution.py:192
  48.2 4.5 %shard_map.86.refs_7_ = f32[4,32,2,16,128]{4,3,2,1,0:T(8,128)S(1)} custom-call(bf16[2,1024,512]{2,1,0:T(8,128)(2,1)S(1)} %shard_map.83.refs_0_, f32[2,8,2048]{2,1,0:T(8,128)S(1)} %broadcast_bitcast_fusion.refs_1_, bf16[2,512,1024]{2,1,0:T(8,128)(2,1)S(1)} %copy-done.1, bf16[128,1024]{1,0:T(8,128)(2,1)} %collective-permute-done.4.refs_3_, ...), custom_call_target="tpu_custom_call" | custom-call | flops 2147483648 | bytes 8388608 | tf_op jit(solution)/shard_map/pallas_call | solution.py:141
  52.7 3.4 %collective-permute-done.3.refs_6_ = bf16[128,1024]{1,0:T(8,128)(2,1)S(1)} collective-permute-done((bf16[128,1024]{1,0:T(8,128)(2,1)S(1)}, bf16[128,1024]{1,0:T(8,128)(2,1)S(1)}, u32[]{:S(2)}, u32[]{:S(2)}) %collective-permute-start.3) | collective-permute-done | bytes 262176 | tf_op jit(solution)/shard_map/ppermute | solution.py:192
  56.7 3.4 %shard_map.87 = bf16[4,32,2,16,128]{4,3,2,1,0:T(8,128)(2,1)S(1)} custom-call(bf16[2,1024,512]{2,1,0:T(8,128)(2,1)S(1)} %shard_map.83.refs_0_, f32[2,8,2048]{2,1,0:T(8,128)S(1)} %broadcast_bitcast_fusion.refs_1_, bf16[2,512,1024]{2,1,0:T(8,128)(2,1)S(1)} %copy-done.1, bf16[128,1024]{1,0:T(8,128)(2,1)S(1)} %collective-permute-done.refs_3_, ...), custom_call_target="tpu_custom_call" | custom-call | flops 2147483648 | bytes 8388608 | tf_op jit(solution)/shard_map/pallas_call | solution.py:141
  60.3 4.5 %shard_map.84.refs_7_ = f32[4,32,2,16,128]{4,3,2,1,0:T(8,128)S(1)} custom-call(bf16[2,1024,512]{2,1,0:T(8,128)(2,1)S(1)} %shard_map.83.refs_0_, f32[2,8,2048]{2,1,0:T(8,128)S(1)} %broadcast_bitcast_fusion.refs_1_, bf16[2,512,1024]{2,1,0:T(8,128)(2,1)S(1)} %copy-done.1, bf16[128,1024]{1,0:T(8,128)(2,1)} %collective-permute-done.4.refs_3_, ...), custom_call_target="tpu_custom_call" | custom-call | flops 2147483648 | bytes 8388608 | tf_op jit(solution)/shard_map/pallas_call | solution.py:141
  64.8 3.4 %shard_map.85 = f32[4,32,2,16,128]{4,3,2,1,0:T(8,128)S(1)} custom-call(bf16[2,1024,512]{2,1,0:T(8,128)(2,1)S(1)} %shard_map.83.refs_0_, f32[2,8,2048]{2,1,0:T(8,128)S(1)} %broadcast_bitcast_fusion.refs_1_, bf16[2,512,1024]{2,1,0:T(8,128)(2,1)S(1)} %copy-done.1, bf16[128,1024]{1,0:T(8,128)(2,1)S(1)} %collective-permute-done.refs_3_, ...), custom_call_target="tpu_custom_call" | custom-call | flops 2147483648 | bytes 8388608 | tf_op jit(solution)/shard_map/pallas_call | solution.py:141
  68.6 3.0 %collective-permute-start.11 = (bf16[16,2,16,128]{3,2,1,0:T(8,128)(2,1)S(1)}, bf16[16,2,16,128]{3,2,1,0:T(8,128)(2,1)S(1)}, u32[]{:S(2)}, u32[]{:S(2)}) collective-permute-start(bf16[16,2,16,128]{3,2,1,0:T(8,128)(2,1)S(1)} %get-tuple-element.37), channel_id=1, source_target_pairs={{0,192},{32,224},{64,0},{96,32},{128,64},{160,96},{192,128},{224,1... | collective-permute-start | bytes 393224 | tf_op jit(solution)/shard_map/ppermute | solution.py:245
  71.6 3.3 %collective-permute-done.11 = bf16[16,2,16,128]{3,2,1,0:T(8,128)(2,1)S(1)} collective-permute-done((bf16[16,2,16,128]{3,2,1,0:T(8,128)(2,1)S(1)}, bf16[16,2,16,128]{3,2,1,0:T(8,128)(2,1)S(1)}, u32[]{:S(2)}, u32[]{:S(2)}) %collective-permute-start.11) | collective-permute-done | bytes 131104 | tf_op jit(solution)/shard_map/ppermute | solution.py:245
  75.0 3.8 %collective-permute-start.12 = (bf16[32,2,16,128]{3,2,1,0:T(8,128)(2,1)S(1)}, bf16[32,2,16,128]{3,2,1,0:T(8,128)(2,1)S(1)}, u32[]{:S(2)}, u32[]{:S(2)}) collective-permute-start(bf16[32,2,16,128]{3,2,1,0:T(8,128)(2,1)S(1)} %convert_element_type.120), channel_id=1, source_target_pairs={{0,192},{32,224},{64,0},{96,32},{128,64},{160,96},{192,128},{224,1... | collective-permute-start | bytes 786440 | tf_op jit(solution)/shard_map/ppermute | solution.py:249
  79.0 5.3 %collective-permute-done.12 = bf16[32,2,16,128]{3,2,1,0:T(8,128)(2,1)S(1)} collective-permute-done((bf16[32,2,16,128]{3,2,1,0:T(8,128)(2,1)S(1)}, bf16[32,2,16,128]{3,2,1,0:T(8,128)(2,1)S(1)}, u32[]{:S(2)}, u32[]{:S(2)}) %collective-permute-start.12) | collective-permute-done | bytes 262176 | tf_op jit(solution)/shard_map/ppermute | solution.py:249
  84.2 3.6 %collective-permute-done.10 = bf16[32,2,16,128]{3,2,1,0:T(8,128)(2,1)S(1)} collective-permute-done((bf16[32,2,16,128]{3,2,1,0:T(8,128)(2,1)S(1)}, bf16[32,2,16,128]{3,2,1,0:T(8,128)(2,1)S(1)}, u32[]{:S(2)}, u32[]{:S(2)}) %collective-permute-start.10) | collective-permute-done | bytes 262176 | tf_op jit(solution)/shard_map/ppermute | solution.py:248
  88.0 17.4 %all_to_all.10 = bf16[32,2,16,128]{3,2,1,0:T(8,128)(2,1)S(1)} all-to-all(bf16[32,2,16,128]{3,2,1,0:T(8,128)(2,1)S(1)} %fusion.11), channel_id=1, replica_groups=mesh['freq'=8,'aux'=32] {'aux'}, dimensions={0} | all-to-all | bytes 524288 | tf_op jit(solution)/shard_map/all_to_all | solution.py:251
  (79 shorter events, 11.3 us)
Async XLA Ops:
  0.0 3.4 %copy-start.2 = (bf16[2,128,4096]{2,1,0:T(8,128)(2,1)S(1)}, bf16[2,128,4096]{2,1,0:T(8,128)(2,1)}, u32[]{:S(2)}) copy-start(bf16[2,128,4096]{2,1,0:T(8,128)(2,1)} %screened_ref.1) | copy-start | bytes 6291460
  1.4 24.4 %collective-permute-start.4 = (bf16[128,1024]{1,0:T(8,128)(2,1)S(1)}, bf16[128,1024]{1,0:T(8,128)(2,1)}, u32[]{:S(2)}, u32[]{:S(2)}) collective-permute-start(bf16[128,1024]{1,0:T(8,128)(2,1)S(1)} %get-tuple-element.34), channel_id=1, source_target_pairs={{0,0},{1,1},{2,2},{3,3},{4,4},{5,5},{6,6},{7,7},{8,8},{9,9},{10,10... | collective-permute-start | bytes 786440 | tf_op jit(solution)/shard_map/ppermute | solution.py:191
  2.7 38.7 %collective-permute-start = (bf16[128,1024]{1,0:T(8,128)(2,1)S(1)}, bf16[128,1024]{1,0:T(8,128)(2,1)S(1)}, u32[]{:S(2)}, u32[]{:S(2)}) collective-permute-start(bf16[128,1024]{1,0:T(8,128)(2,1)S(1)} %get-tuple-element.35), channel_id=1, source_target_pairs={{0,0},{1,1},{2,2},{3,3},{4,4},{5,5},{6,6},{7,7},{8,8},{9,9},{10,10... | collective-permute-start | bytes 786440 | tf_op jit(solution)/shard_map/ppermute | solution.py:191
  4.4 1.3 %copy-start = (bf16[8,2,128,512]{3,2,1,0:T(8,128)(2,1)}, bf16[8,2,128,512]{3,2,1,0:T(8,128)(2,1)S(1)}, u32[]{:S(2)}) copy-start(bf16[8,2,128,512]{3,2,1,0:T(8,128)(2,1)S(1)} %shard_map.82) | copy-start | bytes 6291460
  5.8 13.1 %copy-start.8 = (s32[2]{0:T(128)S(1)}, s32[2]{0:T(128)}, u32[]{:S(2)}) copy-start(s32[2]{0:T(128)} %param.18) | copy-start | bytes 28
  5.8 13.2 %copy-start.9 = (s32[32]{0:T(128)S(1)}, s32[32]{0:T(128)}, u32[]{:S(2)}) copy-start(s32[32]{0:T(128)} %param.19) | copy-start | bytes 388
  5.8 13.3 %copy-start.6 = (s32[2,8]{1,0:T(2,128)S(1)}, s32[2,8]{1,0:T(2,128)}, u32[]{:S(2)}) copy-start(s32[2,8]{1,0:T(2,128)} %param.17) | copy-start | bytes 196
  5.8 13.8 %copy-start.5 = (f32[16,16]{1,0:T(8,128)S(1)}, f32[16,16]{1,0:T(8,128)}, u32[]{:S(2)}) copy-start(f32[16,16]{1,0:T(8,128)} %param.14) | copy-start | bytes 3076
  5.8 40.8 %all-to-all-start = ((bf16[8,2,128,512]{3,2,1,0:T(8,128)(2,1)}), bf16[8,2,128,512]{3,2,1,0:T(8,128)(2,1)S(1)}, u32[]{:S(2)}, u32[]{:S(2)}) async-start(bf16[8,2,128,512]{3,2,1,0:T(8,128)(2,1)} %copy-done), calls=%async_computation | async-start | bytes 4194304 | tf_op jit(solution)/shard_map/all_to_all | solution.py:196
  23.2 4.2 %copy-start.7 = (f32[16]{0:T(128)S(1)}, f32[16]{0:T(128)}, u32[]{:S(2)}) copy-start(f32[16]{0:T(128)} %param.13) | copy-start | bytes 196
  25.8 17.1 %collective-permute-start.7 = (bf16[128,1024]{1,0:T(8,128)(2,1)}, bf16[128,1024]{1,0:T(8,128)(2,1)S(1)}, u32[]{:S(2)}, u32[]{:S(2)}) collective-permute-start(bf16[128,1024]{1,0:T(8,128)(2,1)} %collective-permute-done.4.refs_3_), channel_id=1, source_target_pairs={{24,0},{25,1},{26,2},{27,3},{28,4},{29,5},{30,6},{31,7},{0,8},{1,9... | collective-permute-start | bytes 786440 | tf_op jit(solution)/shard_map/ppermute | solution.py:192
  27.5 20.4 %collective-permute-start.6 = (bf16[128,1024]{1,0:T(8,128)(2,1)}, bf16[128,1024]{1,0:T(8,128)(2,1)}, u32[]{:S(2)}, u32[]{:S(2)}) collective-permute-start(bf16[128,1024]{1,0:T(8,128)(2,1)} %collective-permute-done.4.refs_3_), channel_id=1, source_target_pairs={{16,0},{17,1},{18,2},{19,3},{20,4},{21,5},{22,6},{23,7},{24,8},{25... | collective-permute-start | bytes 786440 | tf_op jit(solution)/shard_map/ppermute | solution.py:192
  30.5 17.4 %collective-permute-start.5 = (bf16[128,1024]{1,0:T(8,128)(2,1)}, bf16[128,1024]{1,0:T(8,128)(2,1)}, u32[]{:S(2)}, u32[]{:S(2)}) collective-permute-start(bf16[128,1024]{1,0:T(8,128)(2,1)} %collective-permute-done.4.refs_3_), channel_id=1, source_target_pairs={{8,0},{9,1},{10,2},{11,3},{12,4},{13,5},{14,6},{15,7},{16,8},{17,9... | collective-permute-start | bytes 786440 | tf_op jit(solution)/shard_map/ppermute | solution.py:192
  41.4 14.7 %collective-permute-start.3 = (bf16[128,1024]{1,0:T(8,128)(2,1)S(1)}, bf16[128,1024]{1,0:T(8,128)(2,1)S(1)}, u32[]{:S(2)}, u32[]{:S(2)}) collective-permute-start(bf16[128,1024]{1,0:T(8,128)(2,1)S(1)} %collective-permute-done.refs_3_), channel_id=1, source_target_pairs={{24,0},{25,1},{26,2},{27,3},{28,4},{29,5},{30,6},{31,7},{0,8},{1,9... | collective-permute-start | bytes 786440 | tf_op jit(solution)/shard_map/ppermute | solution.py:192
  42.1 14.0 %collective-permute-start.2 = (bf16[128,1024]{1,0:T(8,128)(2,1)S(1)}, bf16[128,1024]{1,0:T(8,128)(2,1)S(1)}, u32[]{:S(2)}, u32[]{:S(2)}) collective-permute-start(bf16[128,1024]{1,0:T(8,128)(2,1)S(1)} %collective-permute-done.refs_3_), channel_id=1, source_target_pairs={{16,0},{17,1},{18,2},{19,3},{20,4},{21,5},{22,6},{23,7},{24,8},{25... | collective-permute-start | bytes 786440 | tf_op jit(solution)/shard_map/ppermute | solution.py:192
  42.9 0.7 copy-start.3
  43.6 13.1 %collective-permute-start.1 = (bf16[128,1024]{1,0:T(8,128)(2,1)S(1)}, bf16[128,1024]{1,0:T(8,128)(2,1)S(1)}, u32[]{:S(2)}, u32[]{:S(2)}) collective-permute-start(bf16[128,1024]{1,0:T(8,128)(2,1)S(1)} %collective-permute-done.refs_3_), channel_id=1, source_target_pairs={{8,0},{9,1},{10,2},{11,3},{12,4},{13,5},{14,6},{15,7},{16,8},{17,9... | collective-permute-start | bytes 786440 | tf_op jit(solution)/shard_map/ppermute | solution.py:192
  46.6 1.6 %copy-start.1 = (bf16[2,512,1024]{2,1,0:T(8,128)(2,1)S(1)}, bf16[2,512,1024]{2,1,0:T(8,128)(2,1)}, u32[]{:S(2)}) copy-start(bf16[2,512,1024]{2,1,0:T(8,128)(2,1)} %fusion.2.refs_2_) | copy-start | bytes 6291460
  46.6 1.6 %copy-start.4 = (bf16[128,1024]{1,0:T(8,128)(2,1)S(1)}, bf16[128,1024]{1,0:T(8,128)(2,1)}, u32[]{:S(2)}) copy-start(bf16[128,1024]{1,0:T(8,128)(2,1)} %copy-done.3) | copy-start | bytes 786436
  60.2 8.1 %collective-permute-start.8 = (bf16[4,32,2,16,128]{4,3,2,1,0:T(8,128)(2,1)S(1)}, bf16[4,32,2,16,128]{4,3,2,1,0:T(8,128)(2,1)S(1)}, u32[]{:S(2)}, u32[]{:S(2)}) collective-permute-start(bf16[4,32,2,16,128]{4,3,2,1,0:T(8,128)(2,1)S(1)} %shard_map.87), channel_id=1, source_target_pairs={{0,32},{32,0},{64,96},{96,64},{128,160},{160,128},{192,224},{224,1... | collective-permute-start | bytes 3145736 | tf_op jit(solution)/shard_map/ppermute | solution.py:234
  68.6 6.4 %collective-permute-start.11 = (bf16[16,2,16,128]{3,2,1,0:T(8,128)(2,1)S(1)}, bf16[16,2,16,128]{3,2,1,0:T(8,128)(2,1)S(1)}, u32[]{:S(2)}, u32[]{:S(2)}) collective-permute-start(bf16[16,2,16,128]{3,2,1,0:T(8,128)(2,1)S(1)} %get-tuple-element.37), channel_id=1, source_target_pairs={{0,192},{32,224},{64,0},{96,32},{128,64},{160,96},{192,128},{224,1... | collective-permute-start | bytes 393224 | tf_op jit(solution)/shard_map/ppermute | solution.py:245
  71.5 7.3 %collective-permute-start.9 = (bf16[16,2,16,128]{3,2,1,0:T(8,128)(2,1)S(1)}, bf16[16,2,16,128]{3,2,1,0:T(8,128)(2,1)S(1)}, u32[]{:S(2)}, u32[]{:S(2)}) collective-permute-start(bf16[16,2,16,128]{3,2,1,0:T(8,128)(2,1)S(1)} %get-tuple-element.36), channel_id=1, source_target_pairs={{0,64},{32,96},{64,128},{96,160},{128,192},{160,224},{192,0},{224,... | collective-permute-start | bytes 393224 | tf_op jit(solution)/shard_map/ppermute | solution.py:244
  75.0 9.2 %collective-permute-start.12 = (bf16[32,2,16,128]{3,2,1,0:T(8,128)(2,1)S(1)}, bf16[32,2,16,128]{3,2,1,0:T(8,128)(2,1)S(1)}, u32[]{:S(2)}, u32[]{:S(2)}) collective-permute-start(bf16[32,2,16,128]{3,2,1,0:T(8,128)(2,1)S(1)} %convert_element_type.120), channel_id=1, source_target_pairs={{0,192},{32,224},{64,0},{96,32},{128,64},{160,96},{192,128},{224,1... | collective-permute-start | bytes 786440 | tf_op jit(solution)/shard_map/ppermute | solution.py:249
  78.9 8.9 %collective-permute-start.10 = (bf16[32,2,16,128]{3,2,1,0:T(8,128)(2,1)S(1)}, bf16[32,2,16,128]{3,2,1,0:T(8,128)(2,1)S(1)}, u32[]{:S(2)}, u32[]{:S(2)}) collective-permute-start(bf16[32,2,16,128]{3,2,1,0:T(8,128)(2,1)S(1)} %convert_element_type.116), channel_id=1, source_target_pairs={{0,64},{32,96},{64,128},{96,160},{128,192},{160,224},{192,0},{224,... | collective-permute-start | bytes 786440 | tf_op jit(solution)/shard_map/ppermute | solution.py:248

commit v3 on v2

v3 whole, which is shorter than its diff:
```python
import functools

import jax
import jax.numpy as jnp
from jax import lax
from jax.experimental import pallas as pl
from jax.experimental.pallas import tpu as pltpu
from jax.sharding import PartitionSpec as P

BAND = 16
DEPTH = 8
SHIFTS = ((0, 4, 3, 5, 2, 6, 1, 7), (0, 4, 1, 7, 2, 6, 3, 5))
WHOLE = pl.BlockSpec(memory_space=pltpu.VMEM)


def params():
    return pltpu.CompilerParams(vmem_limit_bytes=32 * 1024 * 1024)


def pick_kernel(place_ref, screened_ref, out_ref):
    place = place_ref[0]
    row, column = place // DEPTH, place % DEPTH
    odd = column % 2
    slab = out_ref.shape[3] // 4
    for f in range(out_ref.shape[0]):
        far = lax.rem(column + jnp.where(odd == 1, SHIFTS[1][f], SHIFTS[0][f]), DEPTH)
        for i in range(4):
            start = (lax.rem(row + i, 4) * DEPTH + far) * slab
            out_ref[f, :, :, i * slab : (i + 1) * slab] = screened_ref[:, :, pl.ds(pl.multiple_of(start, slab), slab)]


def pick(place, screened, freqs):
    local, rows, width = screened.shape
    tall = rows // 4
    return pl.pallas_call(
        pick_kernel,
        out_shape=jax.ShapeDtypeStruct((freqs, local, rows, width // freqs), screened.dtype),
        grid_spec=pltpu.PrefetchScalarGridSpec(
            num_scalar_prefetch=1,
            grid=(rows // tall,),
            in_specs=[pl.BlockSpec((local, tall, width), lambda i, place: (0, i, 0))],
            out_specs=pl.BlockSpec((freqs, local, tall, width // freqs), lambda i, place: (0, 0, i, 0)),
        ),
        compiler_params=params(),
    )(place, screened)


def mix_kernel(pieces_ref, table_ref, out_ref, mix_ref):
    sources, local, rows, width = pieces_ref.shape
    freqs = sources * local
    times = table_ref.shape[1]
    places = out_ref.shape[1]
    pair = 2 * BAND
    tall = times * BAND
    lane = lax.broadcasted_iota(jnp.int32, (BAND, freqs * BAND), 1) % BAND
    keep = lane == lax.broadcasted_iota(jnp.int32, (BAND, freqs * BAND), 0)
    for half in range(2):
        for time in range(times):
            value = jnp.where(keep, table_ref[half, time : time + 1, :], 0.0)
            upper = value.astype(jnp.bfloat16)
            lower = (value - upper.astype(jnp.float32)).astype(jnp.bfloat16)
            mix_ref[half, time * BAND : (time + 1) * BAND, :] = upper
            mix_ref[half, tall + time * BAND : tall + (time + 1) * BAND, :] = lower
    for band in range(rows // BAND):
        piece = pieces_ref[:, :, band * BAND : (band + 1) * BAND, :].reshape(freqs * BAND, width)
        for half in range(2):
            mixed = jnp.dot(mix_ref[half], piece, preferred_element_type=jnp.float32)
            mixed = (mixed[:tall] + mixed[tall:]).astype(jnp.bfloat16)
            for place in range(places):
                out_ref[half, place, band * pair : (band + 1) * pair, :] = mixed[place * pair : (place + 1) * pair]


def transform(pieces, table):
    sources, local, rows, width = pieces.shape
    freqs = sources * local
    times = table.shape[1]
    return pl.pallas_call(
        mix_kernel,
        out_shape=jax.ShapeDtypeStruct((2, times // 2, 2 * rows, width), jnp.bfloat16),
        in_specs=[WHOLE] * 2,
        out_specs=WHOLE,
        scratch_shapes=[pltpu.VMEM((2, 2 * times * BAND, freqs * BAND), jnp.bfloat16)],
        compiler_params=params(),
    )(pieces, table)


def contract_kernel(jobs, part, has_total, *refs):
    timed_ref, gains_ref, dense_ref = refs[:3]
    slabs = refs[3:7]
    refs = refs[7:]
    totals = [None] * len(jobs)
    if has_total:
        totals, refs = refs[: len(jobs)], refs[len(jobs) :]
    outs, (state_ref, scaled_ref) = refs[: len(jobs)], refs[len(jobs) :]
    slab = slabs[0].shape[0]
    for i in range(4):
        state_ref[i * slab : (i + 1) * slab, :] = slabs[i][...]
    span = state_ref.shape[1]
    blocks = dense_ref.shape[0]
    deep = scaled_ref.shape[0] // blocks
    tall, depth = timed_ref.shape[2:]
    bands = tall // (2 * BAND)
    bands_in = bands // blocks
    row_block = bands_in * BAND
    owners, inner, targets = outs[0].shape[1], outs[0].shape[3], outs[0].shape[4]
    pair = 2 * targets

    for (half, first, count), total_ref, out_ref in zip(jobs, totals, outs):
        timed = timed_ref[half, first : first + count].reshape(count * tall, depth)

        def states(step, carry):
            columns = pl.ds(pl.multiple_of(step * pair, pair), pair)
            contracted = jnp.dot(timed, state_ref[:, columns], preferred_element_type=jnp.float32)
            gains = gains_ref[half, :, pl.ds(pl.multiple_of(part * span + step * pair, pair), pair)]
            for place in range(count):
                for time in range(2):
                    at = 2 * (first + place) + time
                    gain = gains[at : at + 1, :]
                    column = (2 * place + time) * targets
                    for band in range(bands):
                        row = place * tall + (2 * band + time) * BAND
                        block = (contracted[row : row + BAND, :] * gain).astype(jnp.bfloat16)
                        base = (band // bands_in) * deep + (band % bands_in) * BAND
                        for state in range(2):
                            start = pl.multiple_of(base + (step * 2 + state) * row_block, BAND)
                            scaled_ref[pl.ds(start, BAND), column : column + targets] = block[
                                :, state * targets : (state + 1) * targets
                            ]
            return carry

        lax.fori_loop(0, span // pair, states, 0)
        for place in range(count):
            columns = slice(place * pair, (place + 1) * pair)
            value = sum(
                jnp.dot(
                    dense_ref[block, :, part * deep : (part + 1) * deep],
                    scaled_ref[block * deep : (block + 1) * deep, columns],
                    preferred_element_type=jnp.float32,
                )
                for block in range(blocks)
            )
            for time in range(2):
                piece = value[:, time * targets : (time + 1) * targets].reshape(owners, inner, targets)
                if has_total:
                    piece = piece + total_ref[place, :, time, :, :]
                out_ref[place, :, time, :, :] = piece.astype(out_ref.dtype)


def contract(jobs, part, timed, gains, dense, slabs, totals, owners, dtypes):
    slab, span = slabs[0].shape
    rows = timed.shape[2] // 2
    states = dense.shape[0] * dense.shape[2] // rows
    targets = gains.shape[2] // states
    depth = span // targets * rows
    operands = [timed, gains, dense, *slabs, *totals]
    wide = max(count for _, _, count in jobs)
    work = sum(count for _, _, count in jobs)
    return pl.pallas_call(
        functools.partial(contract_kernel, jobs, part, bool(totals)),
        out_shape=[
            jax.ShapeDtypeStruct((count, owners, 2, dense.shape[1] // owners, targets), dtype)
            for (_, _, count), dtype in zip(jobs, dtypes)
        ],
        in_specs=[WHOLE] * len(operands),
        out_specs=[WHOLE] * len(jobs),
        scratch_shapes=[
            pltpu.VMEM((4 * slab, span), jnp.bfloat16),
            pltpu.VMEM((depth, wide * 2 * targets), jnp.bfloat16),
        ],
        compiler_params=params(),
        cost_estimate=pl.CostEstimate(
            flops=4 * work * (rows * 4 * slab * span + dense.shape[1] * depth * targets),
            bytes_accessed=2 * 1024 * 1024 * work,
            transcendentals=0,
        ),
    )(*operands)


def shards(
    screened, grid_weights, greens, three_state, three_orbital, block_ids, block_counts, owners
):
    freq_count = lax.axis_size("freq")
    aux_count = lax.axis_size("aux")
    freq = lax.axis_index("freq")
    chip, core = freq // 2, freq % 2
    local_times, rows, width = screened.shape
    total_times = local_times * freq_count
    states = three_state.shape[1]
    targets = three_state.shape[2]
    block_count, slot_count = block_ids.shape
    orbitals = three_orbital.shape[2]
    block_width = orbitals // slot_count
    row_block = rows // block_count
    chips = freq_count // 2
    height = aux_count // DEPTH

    along = []
    for f in range(freq_count):
        for y in range(height):
            for z in range(DEPTH):
                far = (z + SHIFTS[z % 2][f]) % DEPTH
                along.append((f * aux_count + y * DEPTH + far, f * aux_count + y * DEPTH + z))
    across = [
        [(((y + i) % height) * DEPTH + z, y * DEPTH + z) for y in range(height) for z in range(DEPTH)]
        for i in range(height)
    ]
    flat_state = three_state.reshape(rows, states * targets)
    flat_state, screened = lax.optimization_barrier((flat_state, screened))
    span = states * targets // 2
    slabs = []
    for part in range(2):
        own = lax.ppermute(flat_state[:, part * span : (part + 1) * span], ("freq", "aux"), along)
        slabs.append([own] + [lax.ppermute(own, "aux", across[i]) for i in range(1, height)])

    place = lax.axis_index("aux").astype(jnp.int32).reshape(1)
    pieces = pick(place, screened, freq_count)
    pieces = lax.all_to_all(pieces, "freq", split_axis=0, concat_axis=0, tiled=True)

    half = jnp.arange(2, dtype=jnp.int32)[:, None, None]
    other = jnp.arange(chips, dtype=jnp.int32)[None, :, None]
    step = jnp.arange(local_times, dtype=jnp.int32)[None, None, :]
    time = ((chip + other) % chips) * 2 * local_times + ((core + 1 + half) % 2) * local_times + step
    time = time.reshape(2, chips * local_times)
    freqs = jnp.arange(total_times, dtype=jnp.int32)
    lanes = jnp.arange(total_times * BAND, dtype=jnp.int32) // BAND
    weights = jnp.repeat(grid_weights, BAND)
    table = weights * jnp.cos(
        jnp.pi * (time[:, :, None].astype(jnp.float32) + 0.5) * lanes.astype(jnp.float32) / total_times
    )
    gains = jnp.sum(jnp.where(time[:, :, None, None] == freqs[:, None], greens, 0.0), axis=2)
    gains = jnp.repeat(gains, targets, axis=2)

    device = jnp.arange(aux_count, dtype=jnp.int32)
    owned = jnp.sum(jnp.where(owners[None, :] == device[:, None], device[None, :], 0), axis=1)
    inner = orbitals // aux_count
    wanted = (owned[:, None] * inner + jnp.arange(inner, dtype=jnp.int32)[None, :]).reshape(orbitals)
    slot = jnp.arange(slot_count, dtype=jnp.int32)
    listed = block_ids[:, :, None] * block_width + jnp.arange(block_width, dtype=jnp.int32)
    listed = jnp.where(slot[None, :, None] < block_counts[:, None, None], listed, -1).reshape(block_count, orbitals)
    choose = (wanted[None, :, None] == listed[:, None, :]).astype(jnp.bfloat16)
    _, three_orbital = lax.optimization_barrier((slabs[0][0], three_orbital))
    values = three_orbital.reshape(block_count, row_block, states, orbitals)
    values = values.transpose(0, 2, 1, 3).reshape(block_count, states * row_block, orbitals)
    dense = jnp.einsum("bns,brs->bnr", choose, values, preferred_element_type=jnp.float32).astype(jnp.bfloat16)

    slabs[0][1], pieces = lax.optimization_barrier((slabs[0][1], pieces))
    timed = transform(pieces, table)
    run = functools.partial(contract, timed=timed, gains=gains, dense=dense, owners=aux_count)
    swap = [(f, f ^ 1) for f in range(freq_count)]
    jobs = ((0, 0, chips), (1, 1, chips - 1), (1, 0, 1))
    totals = list(run(jobs, 0, slabs=slabs[0], totals=[], dtypes=(jnp.float32,) * 3))
    (given,) = run(jobs[:1], 1, slabs=slabs[1], totals=totals[:1], dtypes=(jnp.bfloat16,))
    taken = lax.ppermute(given, "freq", swap)
    (kept,) = run(jobs[1:2], 1, slabs=slabs[1], totals=totals[1:2], dtypes=(jnp.float32,))
    sent = [
        (kept[i - 1] + taken[i].astype(jnp.float32)).astype(jnp.bfloat16) for i in range(1, chips)
    ]

    def chip_shift(by):
        return [(2 * x + c, 2 * ((x + by) % chips) + c) for x in range(chips) for c in range(2)]

    totals[2], sent[0] = lax.optimization_barrier((totals[2], sent[0]))
    arrived = [lax.ppermute(sent[i], "freq", chip_shift(i + 1)) for i in range(chips - 1)]
    (kept,) = run(jobs[2:], 1, slabs=slabs[1], totals=totals[2:], dtypes=(jnp.float32,))
    summed = kept[0] + taken[0].astype(jnp.float32)
    for piece in arrived:
        summed = summed + piece.astype(jnp.float32)
    spread = lax.all_to_all(summed.astype(jnp.bfloat16), "aux", split_axis=0, concat_axis=0, tiled=True)
    return jnp.sum(spread.astype(jnp.float32), axis=0)


def solution(mesh):
    return jax.shard_map(
        shards,
        mesh=mesh,
        in_specs=(
            P("freq", "aux", None),
            P(),
            P(),
            P("aux", None, None),
            P("aux", None, None),
            P("aux", None),
            P("aux"),
            P(),
        ),
        out_specs=P("freq", "aux", None),
        check_vma=False,
    )
```

time: 106 us -> 102 us (0.962)
  local copies, waits for them, and re-layouts: 17 us -> 4.92 us
  waiting for transfers between devices: 16.2 us -> 23.4 us
  Pallas kernels: 18.2 us -> 21.1 us
  matrix products: 2.63 us -> 1.3 us
    mul x4 -> x1, local copies, waits for them, and re-layouts: 9.55 us -> 0.08 us  [shards(): weights * jnp.cos(jnp.pi * (time[:, :, None].astype(jnp.float32) + 0.5) *...]
    ppermute x6, waiting for transfers between devices: 4.02 us -> 13.4 us  [shards(): lax.ppermute(own, 'aux', across[i])]
    ppermute x5 -> x4, waiting for transfers between devices: 12.2 us -> 9.92 us  [the longest x3 9.92 us: shards(): lax.ppermute(sent[i], 'freq', chip_shift(i + 1))]
    ppermute x5 -> x4, starting transfers between devices: 6.9 us -> 4.83 us  [the longest x3 4.74 us: shards(): lax.ppermute(sent[i], 'freq', chip_shift(i + 1))]
    unnamed x23, local copies, waits for them, and re-layouts: 3.77 us -> 2.1 us
    pallas_call x5, Pallas kernels: 17.2 us -> 18.8 us  [the longest x4 15.9 us: contract(): pl.pallas_call(functools.partial(contract_kernel, jobs, part, bool(totals...]
    transpose x1, local copies, waits for them, and re-layouts: 2.76 us -> 1.16 us  [shards(): values.transpose(0, 2, 1, 3)]
    pallas_call x1, Pallas kernels: 0.98 us -> 2.32 us  [pick(): pl.pallas_call(pick_kernel, out_shape=jax.ShapeDtypeStruct((freqs, local,...]
  transfers between devices with their start and end apart: 14 -> 13, of which waited for: 5 -> 4; matrix products, arithmetic and copies ran while one was open for 17% -> 5% of each run, Pallas kernels for 14% -> 17%
where the time goes in v3:
time: 102 us
  starting transfers between devices  30.4 us (30%)
  waiting for transfers between devices  23.4 us (23%)
  Pallas kernels  21.1 us (21%)
  blocking collectives  18 us (18%)
  local copies, waits for them, and re-layouts  4.92 us (5%)
  other arithmetic  2.38 us (2%)
  matrix products  1.3 us (1%)
    all_to_all x1, blocking collectives, shards(): lax.all_to_all(summed.astype(jnp.bfloat16), 'aux', split_axis=0, concat_a...  18 us
    pallas_call x4, Pallas kernels, contract(): pl.pallas_call(functools.partial(contract_kernel, jobs, part, bool(totals...  15.9 us
    all_to_all x1, starting transfers between devices, shards(): lax.all_to_all(pieces, 'freq', split_axis=0, concat_axis=0, tiled=True)  13.8 us
    ppermute x6, waiting for transfers between devices, shards(): lax.ppermute(own, 'aux', across[i])  13.4 us
    ppermute x6, starting transfers between devices, shards(): lax.ppermute(own, 'aux', across[i])  10.4 us
    ppermute x3, waiting for transfers between devices, shards(): lax.ppermute(sent[i], 'freq', chip_shift(i + 1))  9.92 us
    ppermute x3, starting transfers between devices, shards(): lax.ppermute(sent[i], 'freq', chip_shift(i + 1))  4.74 us
    pallas_call x1, Pallas kernels, transform(): pl.pallas_call(mix_kernel, out_shape=jax.ShapeDtypeStruct((2, times // 2,...  2.88 us
  transfers between devices with their start and end apart: 13, of which 4 were waited for; matrix products, arithmetic and copies ran while one was open for 5% of the time, Pallas kernels for 17%

profile of v3, /device:TPU:32, one launch (start us, length us, event | category | flops | bytes accessed | tf_op | source)
XLA Modules:
  0.0 101.8 jit_solution(2845396362452243858)
XLA Ops:
  0.0 1.3 %copy.15 = bf16[16,8,16,128]{3,1,2,0:T(8,128)(2,1)S(1)} copy(bf16[16,8,16,128]{3,2,1,0:T(8,128)(2,1)} %bitcast.29) | data formatting | bytes 1048576
  1.4 0.7 collective-permute-start.2
  2.8 2.3 %shard_map.82 = bf16[8,2,128,512]{3,2,1,0:T(8,128)(2,1)} custom-call(s32[1]{0:T(128)} %bitcast.place_ref, bf16[2,128,4096]{2,1,0:T(8,128)(2,1)S(1)} %copy-done), custom_call_target="tpu_custom_call" | custom-call | tf_op jit(solution)/shard_map/pallas_call | solution.py:35
  5.1 13.8 %all-to-all-start = ((bf16[8,2,128,512]{3,2,1,0:T(8,128)(2,1)}), bf16[8,2,128,512]{3,2,1,0:T(8,128)(2,1)}, u32[]{:S(2)}, u32[]{:S(2)}) async-start(bf16[8,2,128,512]{3,2,1,0:T(8,128)(2,1)} %shard_map.82), calls=%async_computation | async-start | bytes 4194304 | tf_op jit(solution)/shard_map/all_to_all | solution.py:217
  21.9 1.2 %copy.12 = bf16[2,16,64,512]{3,2,1,0:T(8,128)(2,1)S(1)} copy(bf16[2,16,64,512]{3,1,2,0:T(8,128)(2,1)S(1)} %bitcast.26) | data formatting | bytes 4194304 | tf_op jit(solution)/shard_map/transpose | solution.py:243
  23.1 1.7 %collective-permute-start.5 = (bf16[128,1024]{1,0:T(8,128)(2,1)S(1)}, bf16[128,1024]{1,0:T(8,128)(2,1)S(1)}, u32[]{:S(2)}, u32[]{:S(2)}) collective-permute-start(bf16[128,1024]{1,0:T(8,128)(2,1)S(1)} %collective-permute-done.2.refs_3_), channel_id=1, source_target_pairs={{24,0},{25,1},{26,2},{27,3},{28,4},{29,5},{30,6},{31,7},{0,8},{1,9... | collective-permute-start | bytes 786440 | tf_op jit(solution)/shard_map/ppermute | solution.py:213
  24.8 2.9 %collective-permute-start.4 = (bf16[128,1024]{1,0:T(8,128)(2,1)S(1)}, bf16[128,1024]{1,0:T(8,128)(2,1)S(1)}, u32[]{:S(2)}, u32[]{:S(2)}) collective-permute-start(bf16[128,1024]{1,0:T(8,128)(2,1)S(1)} %collective-permute-done.2.refs_3_), channel_id=1, source_target_pairs={{16,0},{17,1},{18,2},{19,3},{20,4},{21,5},{22,6},{23,7},{24,8},{25... | collective-permute-start | bytes 786440 | tf_op jit(solution)/shard_map/ppermute | solution.py:213
  27.7 2.8 %collective-permute-start.6 = (bf16[128,1024]{1,0:T(8,128)(2,1)S(1)}, bf16[128,1024]{1,0:T(8,128)(2,1)}, u32[]{:S(2)}, u32[]{:S(2)}) collective-permute-start(bf16[128,1024]{1,0:T(8,128)(2,1)S(1)} %collective-permute-done.refs_3_), channel_id=1, source_target_pairs={{16,0},{17,1},{18,2},{19,3},{20,4},{21,5},{22,6},{23,7},{24,8},{25... | collective-permute-start | bytes 786440 | tf_op jit(solution)/shard_map/ppermute | solution.py:213
  30.9 1.3 %fusion.2.refs_2_ = bf16[2,512,1024]{2,1,0:T(8,128)(2,1)S(1)} fusion(bf16[2,1024,512]{2,1,0:T(8,128)(2,1)S(1)} %bitcast.27, s32[2,512]{1,0:T(2,128)S(1)} %copy-done.5, s32[512]{0:T(512)S(1)} %copy-done.6), kind=kOutput, calls=%fused_computation.2 | convolution fusion | flops 1075314688 | bytes 4200448 | tf_op jit(solution)/shard_map/bns,brs->bnr/dot_general | solution.py:244
  32.2 13.4 %collective-permute-done.1.refs_4_ = bf16[128,1024]{1,0:T(8,128)(2,1)S(1)} collective-permute-done((bf16[128,1024]{1,0:T(8,128)(2,1)S(1)}, bf16[128,1024]{1,0:T(8,128)(2,1)S(1)}, u32[]{:S(2)}, u32[]{:S(2)}) %collective-permute-start.1) | collective-permute-done | bytes 262176 | tf_op jit(solution)/shard_map/ppermute | solution.py:213
  45.7 0.7 copy-done.1
  46.4 2.6 %collective-permute-start.3 = (bf16[128,1024]{1,0:T(8,128)(2,1)S(1)}, bf16[128,1024]{1,0:T(8,128)(2,1)S(1)}, u32[]{:S(2)}, u32[]{:S(2)}) collective-permute-start(bf16[128,1024]{1,0:T(8,128)(2,1)S(1)} %collective-permute-done.2.refs_3_), channel_id=1, source_target_pairs={{8,0},{9,1},{10,2},{11,3},{12,4},{13,5},{14,6},{15,7},{16,8},{17,9... | collective-permute-start | bytes 786440 | tf_op jit(solution)/shard_map/ppermute | solution.py:213
  49.0 2.9 %shard_map.83.refs_0_ = bf16[2,4,256,512]{3,2,1,0:T(8,128)(2,1)S(1)} custom-call(bf16[8,2,128,512]{3,2,1,0:T(8,128)(2,1)} %all-to-all-done.pieces_ref, f32[2,8,256]{2,1,0:T(8,128)S(1)} %cosine_multiply_fusion.table_ref), custom_call_target="tpu_custom_call" | custom-call | tf_op jit(solution)/shard_map/pallas_call | solution.py:77
  52.0 8.4 %shard_map.84 = (f32[4,32,2,16,128]{4,3,2,1,0:T(8,128)S(1)}, f32[3,32,2,16,128]{4,3,2,1,0:T(8,128)S(1)}, f32[1,32,2,16,128]{4,3,2,1,0:T(8,128)S(1)}) custom-call(bf16[2,4,256,512]{3,2,1,0:T(8,128)(2,1)S(1)} %shard_map.83.refs_0_, f32[2,8,2048]{2,1,0:T(8,128)S(1)} %broadcast_bitcast_fusion.refs_1_, bf16[2,512,1024]{2,1,0:T(8,128)(2,1)S(1)} %fusion.2.refs_2_, ...), custom_call_target="tpu_custom_call" | custom-call | flops 4294967296 | bytes 16777216 | tf_op jit(solution)/shard_map/pallas_call | solution.py:158
  60.4 3.3 %shard_map.86 = bf16[4,32,2,16,128]{4,3,2,1,0:T(8,128)(2,1)S(1)} custom-call(bf16[2,4,256,512]{3,2,1,0:T(8,128)(2,1)S(1)} %shard_map.83.refs_0_, f32[2,8,2048]{2,1,0:T(8,128)S(1)} %broadcast_bitcast_fusion.refs_1_, bf16[2,512,1024]{2,1,0:T(8,128)(2,1)S(1)} %fusion.2.refs_2_, bf16[128,1024]{1,0:T(8,128)(2,1)S(1)} %collective-permute-done.2.refs_3_, ...), custom_call_target="tpu_custom_call" | custom-call | flops 2147483648 | bytes 8388608 | tf_op jit(solution)/shard_map/pallas_call | solution.py:158
  63.8 2.7 %shard_map.85 = f32[3,32,2,16,128]{4,3,2,1,0:T(8,128)S(1)} custom-call(bf16[2,4,256,512]{3,2,1,0:T(8,128)(2,1)S(1)} %shard_map.83.refs_0_, f32[2,8,2048]{2,1,0:T(8,128)S(1)} %broadcast_bitcast_fusion.refs_1_, bf16[2,512,1024]{2,1,0:T(8,128)(2,1)S(1)} %fusion.2.refs_2_, bf16[128,1024]{1,0:T(8,128)(2,1)S(1)} %collective-permute-done.2.refs_3_, ...), custom_call_target="tpu_custom_call" | custom-call | flops 1610612736 | bytes 6291456 | tf_op jit(solution)/shard_map/pallas_call | solution.py:158
  66.8 1.2 %collective-permute-start.9 = (bf16[32,2,16,128]{3,2,1,0:T(8,128)(2,1)S(1)}, bf16[32,2,16,128]{3,2,1,0:T(8,128)(2,1)S(1)}, u32[]{:S(2)}, u32[]{:S(2)}) collective-permute-start(bf16[32,2,16,128]{3,2,1,0:T(8,128)(2,1)S(1)} %get-tuple-element.24), channel_id=1, source_target_pairs={{0,64},{32,96},{64,128},{96,160},{128,192},{160,224},{192,0},{224,... | collective-permute-start | bytes 786440 | tf_op jit(solution)/shard_map/ppermute | solution.py:263
  68.0 2.1 %collective-permute-start.11 = (bf16[32,2,16,128]{3,2,1,0:T(8,128)(2,1)S(1)}, bf16[32,2,16,128]{3,2,1,0:T(8,128)(2,1)S(1)}, u32[]{:S(2)}, u32[]{:S(2)}) collective-permute-start(bf16[32,2,16,128]{3,2,1,0:T(8,128)(2,1)S(1)} %get-tuple-element.28), channel_id=1, source_target_pairs={{0,192},{32,224},{64,0},{96,32},{128,64},{160,96},{192,128},{224,1... | collective-permute-start | bytes 786440 | tf_op jit(solution)/shard_map/ppermute | solution.py:263
  70.1 1.4 %collective-permute-start.10 = (bf16[32,2,16,128]{3,2,1,0:T(8,128)(2,1)S(1)}, bf16[32,2,16,128]{3,2,1,0:T(8,128)(2,1)S(1)}, u32[]{:S(2)}, u32[]{:S(2)}) collective-permute-start(bf16[32,2,16,128]{3,2,1,0:T(8,128)(2,1)S(1)} %get-tuple-element.29), channel_id=1, source_target_pairs={{0,128},{32,160},{64,192},{96,224},{128,0},{160,32},{192,64},{224,... | collective-permute-start | bytes 786440 | tf_op jit(solution)/shard_map/ppermute | solution.py:263
  71.5 1.5 %shard_map.87 = f32[1,32,2,16,128]{4,3,2,1,0:T(8,128)S(1)} custom-call(bf16[2,4,256,512]{3,2,1,0:T(8,128)(2,1)S(1)} %shard_map.83.refs_0_, f32[2,8,2048]{2,1,0:T(8,128)S(1)} %broadcast_bitcast_fusion.refs_1_, bf16[2,512,1024]{2,1,0:T(8,128)(2,1)S(1)} %fusion.2.refs_2_, bf16[128,1024]{1,0:T(8,128)(2,1)S(1)} %collective-permute-done.2.refs_3_, ...), custom_call_target="tpu_custom_call" | custom-call | flops 536870912 | bytes 2097152 | tf_op jit(solution)/shard_map/pallas_call | solution.py:158
  73.0 3.7 %collective-permute-done.9 = bf16[32,2,16,128]{3,2,1,0:T(8,128)(2,1)S(1)} collective-permute-done((bf16[32,2,16,128]{3,2,1,0:T(8,128)(2,1)S(1)}, bf16[32,2,16,128]{3,2,1,0:T(8,128)(2,1)S(1)}, u32[]{:S(2)}, u32[]{:S(2)}) %collective-permute-start.9) | collective-permute-done | bytes 262176 | tf_op jit(solution)/shard_map/ppermute | solution.py:263
  76.8 4.9 %collective-permute-done.11 = bf16[32,2,16,128]{3,2,1,0:T(8,128)(2,1)S(1)} collective-permute-done((bf16[32,2,16,128]{3,2,1,0:T(8,128)(2,1)S(1)}, bf16[32,2,16,128]{3,2,1,0:T(8,128)(2,1)S(1)}, u32[]{:S(2)}, u32[]{:S(2)}) %collective-permute-start.11) | collective-permute-done | bytes 262176 | tf_op jit(solution)/shard_map/ppermute | solution.py:263
  81.7 1.3 %collective-permute-done.10 = bf16[32,2,16,128]{3,2,1,0:T(8,128)(2,1)S(1)} collective-permute-done((bf16[32,2,16,128]{3,2,1,0:T(8,128)(2,1)S(1)}, bf16[32,2,16,128]{3,2,1,0:T(8,128)(2,1)S(1)}, u32[]{:S(2)}, u32[]{:S(2)}) %collective-permute-start.10) | collective-permute-done | bytes 262176 | tf_op jit(solution)/shard_map/ppermute | solution.py:263
  83.1 18.0 %all_to_all.10 = bf16[32,2,16,128]{3,2,1,0:T(8,128)(2,1)S(1)} all-to-all(bf16[32,2,16,128]{3,2,1,0:T(8,128)(2,1)S(1)} %fusion.12), channel_id=1, replica_groups=mesh['freq'=8,'aux'=32] {'aux'}, dimensions={0} | all-to-all | bytes 524288 | tf_op jit(solution)/shard_map/all_to_all | solution.py:268
  (67 shorter events, 5.3 us)
Async XLA Ops:
  0.0 2.8 %copy-start = (bf16[2,128,4096]{2,1,0:T(8,128)(2,1)S(1)}, bf16[2,128,4096]{2,1,0:T(8,128)(2,1)}, u32[]{:S(2)}) copy-start(bf16[2,128,4096]{2,1,0:T(8,128)(2,1)} %screened_ref) | copy-start | bytes 6291460
  1.4 21.7 %collective-permute-start.2 = (bf16[128,1024]{1,0:T(8,128)(2,1)S(1)}, bf16[128,1024]{1,0:T(8,128)(2,1)S(1)}, u32[]{:S(2)}, u32[]{:S(2)}) collective-permute-start(bf16[128,1024]{1,0:T(8,128)(2,1)S(1)} %get-tuple-element.30), channel_id=1, source_target_pairs={{0,0},{1,1},{2,2},{3,3},{4,4},{5,5},{6,6},{7,7},{8,8},{9,9},{10,10... | collective-permute-start | bytes 786440 | tf_op jit(solution)/shard_map/ppermute | solution.py:212
  2.1 19.8 %collective-permute-start = (bf16[128,1024]{1,0:T(8,128)(2,1)S(1)}, bf16[128,1024]{1,0:T(8,128)(2,1)S(1)}, u32[]{:S(2)}, u32[]{:S(2)}) collective-permute-start(bf16[128,1024]{1,0:T(8,128)(2,1)S(1)} %get-tuple-element.31), channel_id=1, source_target_pairs={{0,0},{1,1},{2,2},{3,3},{4,4},{5,5},{6,6},{7,7},{8,8},{9,9},{10,10... | collective-permute-start | bytes 786440 | tf_op jit(solution)/shard_map/ppermute | solution.py:212
  5.1 13.8 %copy-start.9 = (s32[2]{0:T(128)S(1)}, s32[2]{0:T(128)}, u32[]{:S(2)}) copy-start(s32[2]{0:T(128)} %param.14) | copy-start | bytes 28
  5.1 13.9 %copy-start.7 = (s32[2,8]{1,0:T(2,128)S(1)}, s32[2,8]{1,0:T(2,128)}, u32[]{:S(2)}) copy-start(s32[2,8]{1,0:T(2,128)} %param.13) | copy-start | bytes 196
  5.1 14.3 %copy-start.4 = (f32[16,16]{1,0:T(8,128)S(1)}, f32[16,16]{1,0:T(8,128)}, u32[]{:S(2)}) copy-start(f32[16,16]{1,0:T(8,128)} %param.10) | copy-start | bytes 3076
  5.1 14.4 %copy-start.10 = (s32[32]{0:T(128)S(1)}, s32[32]{0:T(128)}, u32[]{:S(2)}) copy-start(s32[32]{0:T(128)} %param.15) | copy-start | bytes 388
  5.1 15.8 %copy-start.8 = (f32[16]{0:T(128)S(1)}, f32[16]{0:T(128)}, u32[]{:S(2)}) copy-start(f32[16]{0:T(128)} %param.9) | copy-start | bytes 196
  5.1 16.8 %copy-start.3 = (bf16[128,16,512]{2,1,0:T(8,128)(2,1)S(1)}, bf16[128,16,512]{2,1,0:T(8,128)(2,1)}, u32[]{:S(2)}) copy-start(bf16[128,16,512]{2,1,0:T(8,128)(2,1)} %param.12) | copy-start | bytes 6291460
  5.1 43.9 %all-to-all-start = ((bf16[8,2,128,512]{3,2,1,0:T(8,128)(2,1)}), bf16[8,2,128,512]{3,2,1,0:T(8,128)(2,1)}, u32[]{:S(2)}, u32[]{:S(2)}) async-start(bf16[8,2,128,512]{3,2,1,0:T(8,128)(2,1)} %shard_map.82), calls=%async_computation | async-start | bytes 4194304 | tf_op jit(solution)/shard_map/all_to_all | solution.py:217
  21.9 9.0 %copy-start.5 = (s32[2,512]{1,0:T(2,128)S(1)}, s32[2,512]{1,0:T(2,128)}, u32[]{:S(2)}) copy-start(s32[2,512]{1,0:T(2,128)} %add_select_fusion) | copy-start | bytes 12292
  21.9 9.0 %copy-start.6 = (s32[512]{0:T(512)S(1)}, s32[512]{0:T(512)}, u32[]{:S(2)}) copy-start(s32[512]{0:T(512)} %add.202) | copy-start | bytes 6148
  23.1 37.3 %collective-permute-start.5 = (bf16[128,1024]{1,0:T(8,128)(2,1)S(1)}, bf16[128,1024]{1,0:T(8,128)(2,1)S(1)}, u32[]{:S(2)}, u32[]{:S(2)}) collective-permute-start(bf16[128,1024]{1,0:T(8,128)(2,1)S(1)} %collective-permute-done.2.refs_3_), channel_id=1, source_target_pairs={{24,0},{25,1},{26,2},{27,3},{28,4},{29,5},{30,6},{31,7},{0,8},{1,9... | collective-permute-start | bytes 786440 | tf_op jit(solution)/shard_map/ppermute | solution.py:213
  24.8 35.6 %collective-permute-start.4 = (bf16[128,1024]{1,0:T(8,128)(2,1)S(1)}, bf16[128,1024]{1,0:T(8,128)(2,1)S(1)}, u32[]{:S(2)}, u32[]{:S(2)}) collective-permute-start(bf16[128,1024]{1,0:T(8,128)(2,1)S(1)} %collective-permute-done.2.refs_3_), channel_id=1, source_target_pairs={{16,0},{17,1},{18,2},{19,3},{20,4},{21,5},{22,6},{23,7},{24,8},{25... | collective-permute-start | bytes 786440 | tf_op jit(solution)/shard_map/ppermute | solution.py:213
  27.7 24.3 %collective-permute-start.7 = (bf16[128,1024]{1,0:T(8,128)(2,1)S(1)}, bf16[128,1024]{1,0:T(8,128)(2,1)}, u32[]{:S(2)}, u32[]{:S(2)}) collective-permute-start(bf16[128,1024]{1,0:T(8,128)(2,1)S(1)} %collective-permute-done.refs_3_), channel_id=1, source_target_pairs={{24,0},{25,1},{26,2},{27,3},{28,4},{29,5},{30,6},{31,7},{0,8},{1,9... | collective-permute-start | bytes 786440 | tf_op jit(solution)/shard_map/ppermute | solution.py:213
  27.7 24.3 %collective-permute-start.6 = (bf16[128,1024]{1,0:T(8,128)(2,1)S(1)}, bf16[128,1024]{1,0:T(8,128)(2,1)}, u32[]{:S(2)}, u32[]{:S(2)}) collective-permute-start(bf16[128,1024]{1,0:T(8,128)(2,1)S(1)} %collective-permute-done.refs_3_), channel_id=1, source_target_pairs={{16,0},{17,1},{18,2},{19,3},{20,4},{21,5},{22,6},{23,7},{24,8},{25... | collective-permute-start | bytes 786440 | tf_op jit(solution)/shard_map/ppermute | solution.py:213
  30.5 15.2 %collective-permute-start.1 = (bf16[128,1024]{1,0:T(8,128)(2,1)S(1)}, bf16[128,1024]{1,0:T(8,128)(2,1)S(1)}, u32[]{:S(2)}, u32[]{:S(2)}) collective-permute-start(bf16[128,1024]{1,0:T(8,128)(2,1)S(1)} %collective-permute-done.refs_3_), channel_id=1, source_target_pairs={{8,0},{9,1},{10,2},{11,3},{12,4},{13,5},{14,6},{15,7},{16,8},{17,9... | collective-permute-start | bytes 786440 | tf_op jit(solution)/shard_map/ppermute | solution.py:213
  45.7 0.7 copy-start.1
  46.4 14.0 %collective-permute-start.3 = (bf16[128,1024]{1,0:T(8,128)(2,1)S(1)}, bf16[128,1024]{1,0:T(8,128)(2,1)S(1)}, u32[]{:S(2)}, u32[]{:S(2)}) collective-permute-start(bf16[128,1024]{1,0:T(8,128)(2,1)S(1)} %collective-permute-done.2.refs_3_), channel_id=1, source_target_pairs={{8,0},{9,1},{10,2},{11,3},{12,4},{13,5},{14,6},{15,7},{16,8},{17,9... | collective-permute-start | bytes 786440 | tf_op jit(solution)/shard_map/ppermute | solution.py:213
  49.0 2.9 %copy-start.2 = (bf16[128,1024]{1,0:T(8,128)(2,1)S(1)}, bf16[128,1024]{1,0:T(8,128)(2,1)}, u32[]{:S(2)}) copy-start(bf16[128,1024]{1,0:T(8,128)(2,1)} %copy-done.1) | copy-start | bytes 786436
  63.7 2.8 %collective-permute-start.8 = (bf16[4,32,2,16,128]{4,3,2,1,0:T(8,128)(2,1)S(1)}, bf16[4,32,2,16,128]{4,3,2,1,0:T(8,128)(2,1)S(1)}, u32[]{:S(2)}, u32[]{:S(2)}) collective-permute-start(bf16[4,32,2,16,128]{4,3,2,1,0:T(8,128)(2,1)S(1)} %shard_map.86), channel_id=1, source_target_pairs={{0,32},{32,0},{64,96},{96,64},{128,160},{160,128},{192,224},{224,1... | collective-permute-start | bytes 3145736 | tf_op jit(solution)/shard_map/ppermute | solution.py:253
  66.8 10.0 %collective-permute-start.9 = (bf16[32,2,16,128]{3,2,1,0:T(8,128)(2,1)S(1)}, bf16[32,2,16,128]{3,2,1,0:T(8,128)(2,1)S(1)}, u32[]{:S(2)}, u32[]{:S(2)}) collective-permute-start(bf16[32,2,16,128]{3,2,1,0:T(8,128)(2,1)S(1)} %get-tuple-element.24), channel_id=1, source_target_pairs={{0,64},{32,96},{64,128},{96,160},{128,192},{160,224},{192,0},{224,... | collective-permute-start | bytes 786440 | tf_op jit(solution)/shard_map/ppermute | solution.py:263
  68.0 13.7 %collective-permute-start.11 = (bf16[32,2,16,128]{3,2,1,0:T(8,128)(2,1)S(1)}, bf16[32,2,16,128]{3,2,1,0:T(8,128)(2,1)S(1)}, u32[]{:S(2)}, u32[]{:S(2)}) collective-permute-start(bf16[32,2,16,128]{3,2,1,0:T(8,128)(2,1)S(1)} %get-tuple-element.28), channel_id=1, source_target_pairs={{0,192},{32,224},{64,0},{96,32},{128,64},{160,96},{192,128},{224,1... | collective-permute-start | bytes 786440 | tf_op jit(solution)/shard_map/ppermute | solution.py:263
  70.1 12.9 %collective-permute-start.10 = (bf16[32,2,16,128]{3,2,1,0:T(8,128)(2,1)S(1)}, bf16[32,2,16,128]{3,2,1,0:T(8,128)(2,1)S(1)}, u32[]{:S(2)}, u32[]{:S(2)}) collective-permute-start(bf16[32,2,16,128]{3,2,1,0:T(8,128)(2,1)S(1)} %get-tuple-element.29), channel_id=1, source_target_pairs={{0,128},{32,160},{64,192},{96,224},{128,0},{160,32},{192,64},{224,... | collective-permute-start | bytes 786440 | tf_op jit(solution)/shard_map/ppermute | solution.py:263

commit v4 on v3

--- a/solution.py
+++ b/solution.py
@@ -45,22 +45,37 @@
     )(place, screened)
 
 
-def mix_kernel(pieces_ref, table_ref, out_ref, mix_ref):
-    sources, local, rows, width = pieces_ref.shape
-    freqs = sources * local
-    times = table_ref.shape[1]
-    places = out_ref.shape[1]
-    pair = 2 * BAND
+def spread_kernel(table_ref, out_ref):
+    times, wide = table_ref.shape[1:]
+    lane = lax.broadcasted_iota(jnp.int32, (BAND, wide), 1) % BAND
+    keep = lane == lax.broadcasted_iota(jnp.int32, (BAND, wide), 0)
     tall = times * BAND
-    lane = lax.broadcasted_iota(jnp.int32, (BAND, freqs * BAND), 1) % BAND
-    keep = lane == lax.broadcasted_iota(jnp.int32, (BAND, freqs * BAND), 0)
     for half in range(2):
         for time in range(times):
             value = jnp.where(keep, table_ref[half, time : time + 1, :], 0.0)
             upper = value.astype(jnp.bfloat16)
             lower = (value - upper.astype(jnp.float32)).astype(jnp.bfloat16)
-            mix_ref[half, time * BAND : (time + 1) * BAND, :] = upper
-            mix_ref[half, tall + time * BAND : tall + (time + 1) * BAND, :] = lower
+            out_ref[half, time * BAND : (time + 1) * BAND, :] = upper
+            out_ref[half, tall + time * BAND : tall + (time + 1) * BAND, :] = lower
+
+
+def spread_table(table):
+    _, times, wide = table.shape
+    return pl.pallas_call(
+        spread_kernel,
+        out_shape=jax.ShapeDtypeStruct((2, 2 * times * BAND, wide), jnp.bfloat16),
+        in_specs=[WHOLE],
+        out_specs=WHOLE,
+        compiler_params=params(),
+    )(table)
+
+
+def mix_kernel(pieces_ref, mix_ref, out_ref):
+    sources, local, rows, width = pieces_ref.shape
+    freqs = sources * local
+    places = out_ref.shape[1]
+    pair = 2 * BAND
+    tall = places * pair
     for band in range(rows // BAND):
         piece = pieces_ref[:, :, band * BAND : (band + 1) * BAND, :].reshape(freqs * BAND, width)
         for half in range(2):
@@ -70,18 +85,16 @@
                 out_ref[half, place, band * pair : (band + 1) * pair, :] = mixed[place * pair : (place + 1) * pair]
 
 
-def transform(pieces, table):
+def transform(pieces, mix):
     sources, local, rows, width = pieces.shape
-    freqs = sources * local
-    times = table.shape[1]
+    times = mix.shape[1] // (2 * BAND)
     return pl.pallas_call(
         mix_kernel,
         out_shape=jax.ShapeDtypeStruct((2, times // 2, 2 * rows, width), jnp.bfloat16),
         in_specs=[WHOLE] * 2,
         out_specs=WHOLE,
-        scratch_shapes=[pltpu.VMEM((2, 2 * times * BAND, freqs * BAND), jnp.bfloat16)],
         compiler_params=params(),
-    )(pieces, table)
+    )(pieces, mix)
 
 
 def contract_kernel(jobs, part, has_total, *refs):
@@ -207,10 +220,15 @@
     flat_state = three_state.reshape(rows, states * targets)
     flat_state, screened = lax.optimization_barrier((flat_state, screened))
     span = states * targets // 2
-    slabs = []
-    for part in range(2):
-        own = lax.ppermute(flat_state[:, part * span : (part + 1) * span], ("freq", "aux"), along)
-        slabs.append([own] + [lax.ppermute(own, "aux", across[i]) for i in range(1, height)])
+    parts = [flat_state[:, part * span : (part + 1) * span] for part in range(2)]
+    own = lax.ppermute(parts[0], ("freq", "aux"), along)
+    slabs = [[own] + [lax.ppermute(own, "aux", across[i]) for i in range(1, height)]]
+    parts[1], slabs[0][0] = lax.optimization_barrier((parts[1], slabs[0][0]))
+    own = lax.ppermute(parts[1], ("freq", "aux"), along)
+    slabs.append([own])
+    for i in range(1, height):
+        ready, slabs[0][i] = lax.optimization_barrier((own, slabs[0][i]))
+        slabs[1].append(lax.ppermute(ready, "aux", across[i]))
 
     place = lax.axis_index("aux").astype(jnp.int32).reshape(1)
     pieces = pick(place, screened, freq_count)
@@ -244,7 +262,7 @@
     dense = jnp.einsum("bns,brs->bnr", choose, values, preferred_element_type=jnp.float32).astype(jnp.bfloat16)
 
     slabs[0][1], pieces = lax.optimization_barrier((slabs[0][1], pieces))
-    timed = transform(pieces, table)
+    timed = transform(pieces, spread_table(table))
     run = functools.partial(contract, timed=timed, gains=gains, dense=dense, owners=aux_count)
     swap = [(f, f ^ 1) for f in range(freq_count)]
     jobs = ((0, 0, chips), (1, 1, chips - 1), (1, 0, 1))

time: 102 us -> 98.5 us (0.966)
  waiting for transfers between devices: 23.4 us -> 19 us
  blocking collectives: 18 us -> 20.3 us
  starting transfers between devices: 30.4 us -> 28.8 us
  local copies, waits for them, and re-layouts: 4.92 us -> 6.48 us
    ppermute x6 -> x3, waiting for transfers between devices: 13.4 us -> 6.01 us  [shards(): lax.ppermute(own, 'aux', across[i])]
    ppermute x2 -> x5, starting transfers between devices: 1.35 us -> 7.31 us  [the longest x3 5.04 us: shards(): slabs[1].append(lax.ppermute(ready, 'aux', across[i]))]
    ppermute x6 -> x3, starting transfers between devices: 10.4 us -> 5.9 us  [shards(): lax.ppermute(own, 'aux', across[i])]
    all_to_all x1, starting transfers between devices: 13.8 us -> 11.1 us  [shards(): lax.all_to_all(pieces, 'freq', split_axis=0, concat_axis=0, tiled=True)]
    all_to_all x1, blocking collectives: 18 us -> 20.3 us  [shards(): lax.all_to_all(summed.astype(jnp.bfloat16), 'aux', split_axis=0, concat_a...]
    all_to_all x1, waiting for transfers between devices: 0.01 us -> 2.18 us  [shards(): lax.all_to_all(pieces, 'freq', split_axis=0, concat_axis=0, tiled=True)]
    unnamed x23 -> x31, local copies, waits for them, and re-layouts: 2.1 us -> 3.52 us
  transfers between devices with their start and end apart: 13 -> 13, of which waited for: 4 -> 6; matrix products, arithmetic and copies ran while one was open for 5% -> 4% of each run, Pallas kernels for 17% -> 17%
where the time goes in v4:
time: 98.5 us; the launch traced here: 98.2 us
  starting transfers between devices  28.8 us (29%)
  blocking collectives  20.3 us (21%)
  Pallas kernels  20.2 us (21%)
  waiting for transfers between devices  19 us (19%)
  local copies, waits for them, and re-layouts  6.48 us (7%)
  other arithmetic  1.79 us (2%)
  matrix products  1.3 us (1%)
    all_to_all x1, blocking collectives, shards(): lax.all_to_all(summed.astype(jnp.bfloat16), 'aux', split_axis=0, concat_a...  20.3 us
    pallas_call x4, Pallas kernels, contract(): pl.pallas_call(functools.partial(contract_kernel, jobs, part, bool(totals...  14.9 us
    all_to_all x1, starting transfers between devices, shards(): lax.all_to_all(pieces, 'freq', split_axis=0, concat_axis=0, tiled=True)  11.1 us
    ppermute x3, waiting for transfers between devices, shards(): lax.ppermute(sent[i], 'freq', chip_shift(i + 1))  10.8 us
    ppermute x3, waiting for transfers between devices, shards(): lax.ppermute(own, 'aux', across[i])  6.01 us
    ppermute x3, starting transfers between devices, shards(): lax.ppermute(own, 'aux', across[i])  5.9 us
    ppermute x3, starting transfers between devices, shards(): slabs[1].append(lax.ppermute(ready, 'aux', across[i]))  5.04 us
    ppermute x3, starting transfers between devices, shards(): lax.ppermute(sent[i], 'freq', chip_shift(i + 1))  4.4 us
  transfers between devices with their start and end apart: 13, of which 6 were waited for; matrix products, arithmetic and copies ran while one was open for 4% of the time, Pallas kernels for 17%

profile of v4, /device:TPU:32, one launch (start us, length us, event | category | flops | bytes accessed | tf_op | source)
XLA Modules:
  0.0 98.2 jit_solution(1369482050505799221)
XLA Ops:
  0.0 1.3 %copy.15 = bf16[16,8,16,128]{3,1,2,0:T(8,128)(2,1)S(1)} copy(bf16[16,8,16,128]{3,2,1,0:T(8,128)(2,1)} %bitcast.29) | data formatting | bytes 1048576
  2.8 2.3 %shard_map.82 = bf16[8,2,128,512]{3,2,1,0:T(8,128)(2,1)} custom-call(s32[1]{0:T(128)} %bitcast.place_ref, bf16[2,128,4096]{2,1,0:T(8,128)(2,1)S(1)} %copy-done), custom_call_target="tpu_custom_call" | custom-call | tf_op jit(solution)/shard_map/pallas_call | solution.py:35
  5.2 11.1 %all-to-all-start = ((bf16[8,2,128,512]{3,2,1,0:T(8,128)(2,1)}), bf16[8,2,128,512]{3,2,1,0:T(8,128)(2,1)}, u32[]{:S(2)}, u32[]{:S(2)}) async-start(bf16[8,2,128,512]{3,2,1,0:T(8,128)(2,1)} %shard_map.82), calls=%async_computation | async-start | bytes 4194304 | tf_op jit(solution)/shard_map/all_to_all | solution.py:235
  18.2 1.6 %collective-permute-start.1 = (bf16[128,1024]{1,0:T(8,128)(2,1)}, bf16[128,1024]{1,0:T(8,128)(2,1)S(1)}, u32[]{:S(2)}, u32[]{:S(2)}) collective-permute-start(bf16[128,1024]{1,0:T(8,128)(2,1)} %get-tuple-element.24), channel_id=1, source_target_pairs={{0,0},{1,1},{2,2},{3,3},{4,4},{5,5},{6,6},{7,7},{8,8},{9,9},{10,10... | collective-permute-start | bytes 786440 | tf_op jit(solution)/shard_map/ppermute | solution.py:227
  19.8 1.2 %copy.12 = bf16[2,16,64,512]{3,2,1,0:T(8,128)(2,1)S(1)} copy(bf16[2,16,64,512]{3,1,2,0:T(8,128)(2,1)S(1)} %bitcast.26) | data formatting | bytes 4194304 | tf_op jit(solution)/shard_map/transpose | solution.py:261
  20.9 1.7 %collective-permute-start.6 = (bf16[128,1024]{1,0:T(8,128)(2,1)S(1)}, bf16[128,1024]{1,0:T(8,128)(2,1)S(1)}, u32[]{:S(2)}, u32[]{:S(2)}) collective-permute-start(bf16[128,1024]{1,0:T(8,128)(2,1)S(1)} %collective-permute-done.refs_3_), channel_id=1, source_target_pairs={{24,0},{25,1},{26,2},{27,3},{28,4},{29,5},{30,6},{31,7},{0,8},{1,9... | collective-permute-start | bytes 786440 | tf_op jit(solution)/shard_map/ppermute | solution.py:225
  22.6 2.9 %collective-permute-start.4 = (bf16[128,1024]{1,0:T(8,128)(2,1)S(1)}, bf16[128,1024]{1,0:T(8,128)(2,1)S(1)}, u32[]{:S(2)}, u32[]{:S(2)}) collective-permute-start(bf16[128,1024]{1,0:T(8,128)(2,1)S(1)} %collective-permute-done.refs_3_), channel_id=1, source_target_pairs={{16,0},{17,1},{18,2},{19,3},{20,4},{21,5},{22,6},{23,7},{24,8},{25... | collective-permute-start | bytes 786440 | tf_op jit(solution)/shard_map/ppermute | solution.py:225
  25.5 1.3 %collective-permute-start.2 = (bf16[128,1024]{1,0:T(8,128)(2,1)S(1)}, bf16[128,1024]{1,0:T(8,128)(2,1)S(1)}, u32[]{:S(2)}, u32[]{:S(2)}) collective-permute-start(bf16[128,1024]{1,0:T(8,128)(2,1)S(1)} %collective-permute-done.refs_3_), channel_id=1, source_target_pairs={{8,0},{9,1},{10,2},{11,3},{12,4},{13,5},{14,6},{15,7},{16,8},{17,9... | collective-permute-start | bytes 786440 | tf_op jit(solution)/shard_map/ppermute | solution.py:225
  26.8 1.3 %fusion.2.refs_2_ = bf16[2,512,1024]{2,1,0:T(8,128)(2,1)S(1)} fusion(bf16[2,1024,512]{2,1,0:T(8,128)(2,1)S(1)} %bitcast.27, s32[2,512]{1,0:T(2,128)S(1)} %add_select_fusion, s32[512]{0:T(512)S(1)} %add.202), kind=kOutput, calls=%fused_computation.2 | convolution fusion | flops 1075314688 | bytes 4200448 | tf_op jit(solution)/shard_map/bns,brs->bnr/dot_general | solution.py:262
  29.7 5.6 %collective-permute-done.4.refs_5_ = bf16[128,1024]{1,0:T(8,128)(2,1)S(1)} collective-permute-done((bf16[128,1024]{1,0:T(8,128)(2,1)S(1)}, bf16[128,1024]{1,0:T(8,128)(2,1)S(1)}, u32[]{:S(2)}, u32[]{:S(2)}) %collective-permute-start.4) | collective-permute-done | bytes 262176 | tf_op jit(solution)/shard_map/ppermute | solution.py:225
  37.6 3.8 %collective-permute-start.3 = (bf16[128,1024]{1,0:T(8,128)(2,1)S(1)}, bf16[128,1024]{1,0:T(8,128)(2,1)S(1)}, u32[]{:S(2)}, u32[]{:S(2)}) collective-permute-start(bf16[128,1024]{1,0:T(8,128)(2,1)S(1)} %collective-permute-done.1.refs_3_), channel_id=1, source_target_pairs={{8,0},{9,1},{10,2},{11,3},{12,4},{13,5},{14,6},{15,7},{16,8},{17,9... | collective-permute-start | bytes 786440 | tf_op jit(solution)/shard_map/ppermute | solution.py:231
  41.4 2.2 %all-to-all-done.pieces_ref = bf16[8,2,128,512]{3,2,1,0:T(8,128)(2,1)} async-done(((bf16[8,2,128,512]{3,2,1,0:T(8,128)(2,1)}), bf16[8,2,128,512]{3,2,1,0:T(8,128)(2,1)}, u32[]{:S(2)}, u32[]{:S(2)}) %all-to-all-start) | async-done | bytes 2097184 | tf_op jit(solution)/shard_map/all_to_all | solution.py:235
  43.6 2.9 %shard_map.84.refs_0_ = bf16[2,4,256,512]{3,2,1,0:T(8,128)(2,1)S(1)} custom-call(bf16[8,2,128,512]{3,2,1,0:T(8,128)(2,1)} %all-to-all-done.pieces_ref, bf16[2,256,256]{2,1,0:T(8,128)(2,1)S(1)} %shard_map.83.mix_ref), custom_call_target="tpu_custom_call" | custom-call | tf_op jit(solution)/shard_map/pallas_call | solution.py:91
  46.5 7.4 %shard_map.85 = (f32[4,32,2,16,128]{4,3,2,1,0:T(8,128)S(1)}, f32[3,32,2,16,128]{4,3,2,1,0:T(8,128)S(1)}, f32[1,32,2,16,128]{4,3,2,1,0:T(8,128)S(1)}) custom-call(bf16[2,4,256,512]{3,2,1,0:T(8,128)(2,1)S(1)} %shard_map.84.refs_0_, f32[2,8,2048]{2,1,0:T(8,128)S(1)} %broadcast_bitcast_fusion.refs_1_, bf16[2,512,1024]{2,1,0:T(8,128)(2,1)S(1)} %fusion.2.refs_2_, ...), custom_call_target="tpu_custom_call" | custom-call | flops 4294967296 | bytes 16777216 | tf_op jit(solution)/shard_map/pallas_call | solution.py:171
  54.0 3.3 %shard_map.87 = bf16[4,32,2,16,128]{4,3,2,1,0:T(8,128)(2,1)S(1)} custom-call(bf16[2,4,256,512]{3,2,1,0:T(8,128)(2,1)S(1)} %shard_map.84.refs_0_, f32[2,8,2048]{2,1,0:T(8,128)S(1)} %broadcast_bitcast_fusion.refs_1_, bf16[2,512,1024]{2,1,0:T(8,128)(2,1)S(1)} %fusion.2.refs_2_, bf16[128,1024]{1,0:T(8,128)(2,1)S(1)} %collective-permute-done.1.refs_3_, ...), custom_call_target="tpu_custom_call" | custom-call | flops 2147483648 | bytes 8388608 | tf_op jit(solution)/shard_map/pallas_call | solution.py:171
  57.4 2.6 %shard_map.86 = f32[3,32,2,16,128]{4,3,2,1,0:T(8,128)S(1)} custom-call(bf16[2,4,256,512]{3,2,1,0:T(8,128)(2,1)S(1)} %shard_map.84.refs_0_, f32[2,8,2048]{2,1,0:T(8,128)S(1)} %broadcast_bitcast_fusion.refs_1_, bf16[2,512,1024]{2,1,0:T(8,128)(2,1)S(1)} %fusion.2.refs_2_, bf16[128,1024]{1,0:T(8,128)(2,1)S(1)} %collective-permute-done.1.refs_3_, ...), custom_call_target="tpu_custom_call" | custom-call | flops 1610612736 | bytes 6291456 | tf_op jit(solution)/shard_map/pallas_call | solution.py:171
  60.3 2.1 %collective-permute-start.9 = (bf16[32,2,16,128]{3,2,1,0:T(8,128)(2,1)S(1)}, bf16[32,2,16,128]{3,2,1,0:T(8,128)(2,1)S(1)}, u32[]{:S(2)}, u32[]{:S(2)}) collective-permute-start(bf16[32,2,16,128]{3,2,1,0:T(8,128)(2,1)S(1)} %get-tuple-element.40), channel_id=1, source_target_pairs={{0,64},{32,96},{64,128},{96,160},{128,192},{160,224},{192,0},{224,... | collective-permute-start | bytes 786440 | tf_op jit(solution)/shard_map/ppermute | solution.py:281
  62.4 1.2 %collective-permute-start.11 = (bf16[32,2,16,128]{3,2,1,0:T(8,128)(2,1)S(1)}, bf16[32,2,16,128]{3,2,1,0:T(8,128)(2,1)S(1)}, u32[]{:S(2)}, u32[]{:S(2)}) collective-permute-start(bf16[32,2,16,128]{3,2,1,0:T(8,128)(2,1)S(1)} %get-tuple-element.44), channel_id=1, source_target_pairs={{0,192},{32,224},{64,0},{96,32},{128,64},{160,96},{192,128},{224,1... | collective-permute-start | bytes 786440 | tf_op jit(solution)/shard_map/ppermute | solution.py:281
  63.6 1.1 %collective-permute-start.10 = (bf16[32,2,16,128]{3,2,1,0:T(8,128)(2,1)S(1)}, bf16[32,2,16,128]{3,2,1,0:T(8,128)(2,1)S(1)}, u32[]{:S(2)}, u32[]{:S(2)}) collective-permute-start(bf16[32,2,16,128]{3,2,1,0:T(8,128)(2,1)S(1)} %get-tuple-element.45), channel_id=1, source_target_pairs={{0,128},{32,160},{64,192},{96,224},{128,0},{160,32},{192,64},{224,... | collective-permute-start | bytes 786440 | tf_op jit(solution)/shard_map/ppermute | solution.py:281
  64.7 1.5 %shard_map.88 = f32[1,32,2,16,128]{4,3,2,1,0:T(8,128)S(1)} custom-call(bf16[2,4,256,512]{3,2,1,0:T(8,128)(2,1)S(1)} %shard_map.84.refs_0_, f32[2,8,2048]{2,1,0:T(8,128)S(1)} %broadcast_bitcast_fusion.refs_1_, bf16[2,512,1024]{2,1,0:T(8,128)(2,1)S(1)} %fusion.2.refs_2_, bf16[128,1024]{1,0:T(8,128)(2,1)S(1)} %collective-permute-done.1.refs_3_, ...), custom_call_target="tpu_custom_call" | custom-call | flops 536870912 | bytes 2097152 | tf_op jit(solution)/shard_map/pallas_call | solution.py:171
  66.3 4.1 %collective-permute-done.9 = bf16[32,2,16,128]{3,2,1,0:T(8,128)(2,1)S(1)} collective-permute-done((bf16[32,2,16,128]{3,2,1,0:T(8,128)(2,1)S(1)}, bf16[32,2,16,128]{3,2,1,0:T(8,128)(2,1)S(1)}, u32[]{:S(2)}, u32[]{:S(2)}) %collective-permute-start.9) | collective-permute-done | bytes 262176 | tf_op jit(solution)/shard_map/ppermute | solution.py:281
  70.3 1.2 %collective-permute-done.11 = bf16[32,2,16,128]{3,2,1,0:T(8,128)(2,1)S(1)} collective-permute-done((bf16[32,2,16,128]{3,2,1,0:T(8,128)(2,1)S(1)}, bf16[32,2,16,128]{3,2,1,0:T(8,128)(2,1)S(1)}, u32[]{:S(2)}, u32[]{:S(2)}) %collective-permute-start.11) | collective-permute-done | bytes 262176 | tf_op jit(solution)/shard_map/ppermute | solution.py:281
  71.5 5.5 %collective-permute-done.10 = bf16[32,2,16,128]{3,2,1,0:T(8,128)(2,1)S(1)} collective-permute-done((bf16[32,2,16,128]{3,2,1,0:T(8,128)(2,1)S(1)}, bf16[32,2,16,128]{3,2,1,0:T(8,128)(2,1)S(1)}, u32[]{:S(2)}, u32[]{:S(2)}) %collective-permute-start.10) | collective-permute-done | bytes 262176 | tf_op jit(solution)/shard_map/ppermute | solution.py:281
  77.2 20.3 %all_to_all.10 = bf16[32,2,16,128]{3,2,1,0:T(8,128)(2,1)S(1)} all-to-all(bf16[32,2,16,128]{3,2,1,0:T(8,128)(2,1)S(1)} %fusion.12), channel_id=1, replica_groups=mesh['freq'=8,'aux'=32] {'aux'}, dimensions={0} | all-to-all | bytes 524288 | tf_op jit(solution)/shard_map/all_to_all | solution.py:286
  (76 shorter events, 8.3 us)
Async XLA Ops:
  2.1 16.0 %collective-permute-start = (bf16[128,1024]{1,0:T(8,128)(2,1)S(1)}, bf16[128,1024]{1,0:T(8,128)(2,1)S(1)}, u32[]{:S(2)}, u32[]{:S(2)}) collective-permute-start(bf16[128,1024]{1,0:T(8,128)(2,1)S(1)} %get-tuple-element.46), channel_id=1, source_target_pairs={{0,0},{1,1},{2,2},{3,3},{4,4},{5,5},{6,6},{7,7},{8,8},{9,9},{10,10... | collective-permute-start | bytes 786440 | tf_op jit(solution)/shard_map/ppermute | solution.py:224
  5.1 11.1 %copy-start.13 = (s32[32]{0:T(128)S(1)}, s32[32]{0:T(128)}, u32[]{:S(2)}) copy-start(s32[32]{0:T(128)} %param.15) | copy-start | bytes 388
  5.1 11.3 %copy-start.11 = (s32[2,8]{1,0:T(2,128)S(1)}, s32[2,8]{1,0:T(2,128)}, u32[]{:S(2)}) copy-start(s32[2,8]{1,0:T(2,128)} %param.13) | copy-start | bytes 196
  5.1 11.7 %copy-start.10 = (f32[16,16]{1,0:T(8,128)S(1)}, f32[16,16]{1,0:T(8,128)}, u32[]{:S(2)}) copy-start(f32[16,16]{1,0:T(8,128)} %param.10) | copy-start | bytes 3076
  5.1 11.9 %copy-start.12 = (f32[16]{0:T(128)S(1)}, f32[16]{0:T(128)}, u32[]{:S(2)}) copy-start(f32[16]{0:T(128)} %param.9) | copy-start | bytes 196
  5.1 12.4 %copy-start.14 = (s32[2]{0:T(128)S(1)}, s32[2]{0:T(128)}, u32[]{:S(2)}) copy-start(s32[2]{0:T(128)} %param.14) | copy-start | bytes 28
  5.1 14.6 %copy-start.9 = (bf16[128,16,512]{2,1,0:T(8,128)(2,1)S(1)}, bf16[128,16,512]{2,1,0:T(8,128)(2,1)}, u32[]{:S(2)}) copy-start(bf16[128,16,512]{2,1,0:T(8,128)(2,1)} %param.12) | copy-start | bytes 6291460
  5.2 38.4 %all-to-all-start = ((bf16[8,2,128,512]{3,2,1,0:T(8,128)(2,1)}), bf16[8,2,128,512]{3,2,1,0:T(8,128)(2,1)}, u32[]{:S(2)}, u32[]{:S(2)}) async-start(bf16[8,2,128,512]{3,2,1,0:T(8,128)(2,1)} %shard_map.82), calls=%async_computation | async-start | bytes 4194304 | tf_op jit(solution)/shard_map/all_to_all | solution.py:235
  18.2 7.3 %copy-start.1 = (bf16[128,1024]{1,0:T(8,128)(2,1)}, bf16[128,1024]{1,0:T(8,128)(2,1)S(1)}, u32[]{:S(2)}) copy-start(bf16[128,1024]{1,0:T(8,128)(2,1)S(1)} %collective-permute-done.refs_3_) | copy-start | bytes 786436
  18.2 10.0 %collective-permute-start.1 = (bf16[128,1024]{1,0:T(8,128)(2,1)}, bf16[128,1024]{1,0:T(8,128)(2,1)S(1)}, u32[]{:S(2)}, u32[]{:S(2)}) collective-permute-start(bf16[128,1024]{1,0:T(8,128)(2,1)} %get-tuple-element.24), channel_id=1, source_target_pairs={{0,0},{1,1},{2,2},{3,3},{4,4},{5,5},{6,6},{7,7},{8,8},{9,9},{10,10... | collective-permute-start | bytes 786440 | tf_op jit(solution)/shard_map/ppermute | solution.py:227
  20.9 7.7 %collective-permute-start.6 = (bf16[128,1024]{1,0:T(8,128)(2,1)S(1)}, bf16[128,1024]{1,0:T(8,128)(2,1)S(1)}, u32[]{:S(2)}, u32[]{:S(2)}) collective-permute-start(bf16[128,1024]{1,0:T(8,128)(2,1)S(1)} %collective-permute-done.refs_3_), channel_id=1, source_target_pairs={{24,0},{25,1},{26,2},{27,3},{28,4},{29,5},{30,6},{31,7},{0,8},{1,9... | collective-permute-start | bytes 786440 | tf_op jit(solution)/shard_map/ppermute | solution.py:225
  22.6 12.7 %collective-permute-start.4 = (bf16[128,1024]{1,0:T(8,128)(2,1)S(1)}, bf16[128,1024]{1,0:T(8,128)(2,1)S(1)}, u32[]{:S(2)}, u32[]{:S(2)}) collective-permute-start(bf16[128,1024]{1,0:T(8,128)(2,1)S(1)} %collective-permute-done.refs_3_), channel_id=1, source_target_pairs={{16,0},{17,1},{18,2},{19,3},{20,4},{21,5},{22,6},{23,7},{24,8},{25... | collective-permute-start | bytes 786440 | tf_op jit(solution)/shard_map/ppermute | solution.py:225
  25.5 11.3 %collective-permute-start.2 = (bf16[128,1024]{1,0:T(8,128)(2,1)S(1)}, bf16[128,1024]{1,0:T(8,128)(2,1)S(1)}, u32[]{:S(2)}, u32[]{:S(2)}) collective-permute-start(bf16[128,1024]{1,0:T(8,128)(2,1)S(1)} %collective-permute-done.refs_3_), channel_id=1, source_target_pairs={{8,0},{9,1},{10,2},{11,3},{12,4},{13,5},{14,6},{15,7},{16,8},{17,9... | collective-permute-start | bytes 786440 | tf_op jit(solution)/shard_map/ppermute | solution.py:225
  29.3 24.6 %collective-permute-start.7 = (bf16[128,1024]{1,0:T(8,128)(2,1)S(1)}, bf16[128,1024]{1,0:T(8,128)(2,1)S(1)}, u32[]{:S(2)}, u32[]{:S(2)}) collective-permute-start(bf16[128,1024]{1,0:T(8,128)(2,1)S(1)} %collective-permute-done.1.refs_3_), channel_id=1, source_target_pairs={{24,0},{25,1},{26,2},{27,3},{28,4},{29,5},{30,6},{31,7},{0,8},{1,9... | collective-permute-start | bytes 786440 | tf_op jit(solution)/shard_map/ppermute | solution.py:231
  36.0 18.0 %collective-permute-start.5 = (bf16[128,1024]{1,0:T(8,128)(2,1)S(1)}, bf16[128,1024]{1,0:T(8,128)(2,1)S(1)}, u32[]{:S(2)}, u32[]{:S(2)}) collective-permute-start(bf16[128,1024]{1,0:T(8,128)(2,1)S(1)} %collective-permute-done.1.refs_3_), channel_id=1, source_target_pairs={{16,0},{17,1},{18,2},{19,3},{20,4},{21,5},{22,6},{23,7},{24,8},{25... | collective-permute-start | bytes 786440 | tf_op jit(solution)/shard_map/ppermute | solution.py:231
  37.6 16.4 %collective-permute-start.3 = (bf16[128,1024]{1,0:T(8,128)(2,1)S(1)}, bf16[128,1024]{1,0:T(8,128)(2,1)S(1)}, u32[]{:S(2)}, u32[]{:S(2)}) collective-permute-start(bf16[128,1024]{1,0:T(8,128)(2,1)S(1)} %collective-permute-done.1.refs_3_), channel_id=1, source_target_pairs={{8,0},{9,1},{10,2},{11,3},{12,4},{13,5},{14,6},{15,7},{16,8},{17,9... | collective-permute-start | bytes 786440 | tf_op jit(solution)/shard_map/ppermute | solution.py:231
  43.5 2.9 %copy-start.2 = (bf16[128,1024]{1,0:T(8,128)(2,1)S(1)}, bf16[128,1024]{1,0:T(8,128)(2,1)}, u32[]{:S(2)}) copy-start(bf16[128,1024]{1,0:T(8,128)(2,1)} %copy-done.1) | copy-start | bytes 786436
  43.5 3.0 %copy-start.4 = (bf16[128,1024]{1,0:T(8,128)(2,1)S(1)}, bf16[128,1024]{1,0:T(8,128)(2,1)}, u32[]{:S(2)}) copy-start(bf16[128,1024]{1,0:T(8,128)(2,1)} %copy-done.3) | copy-start | bytes 786436
  43.5 3.0 %copy-start.6 = (bf16[128,1024]{1,0:T(8,128)(2,1)S(1)}, bf16[128,1024]{1,0:T(8,128)(2,1)}, u32[]{:S(2)}) copy-start(bf16[128,1024]{1,0:T(8,128)(2,1)} %copy-done.5) | copy-start | bytes 786436
  43.5 3.0 %copy-start.8 = (bf16[128,1024]{1,0:T(8,128)(2,1)S(1)}, bf16[128,1024]{1,0:T(8,128)(2,1)}, u32[]{:S(2)}) copy-start(bf16[128,1024]{1,0:T(8,128)(2,1)} %copy-done.7) | copy-start | bytes 786436
  57.3 2.8 %collective-permute-start.8 = (bf16[4,32,2,16,128]{4,3,2,1,0:T(8,128)(2,1)S(1)}, bf16[4,32,2,16,128]{4,3,2,1,0:T(8,128)(2,1)S(1)}, u32[]{:S(2)}, u32[]{:S(2)}) collective-permute-start(bf16[4,32,2,16,128]{4,3,2,1,0:T(8,128)(2,1)S(1)} %shard_map.87), channel_id=1, source_target_pairs={{0,32},{32,0},{64,96},{96,64},{128,160},{160,128},{192,224},{224,1... | collective-permute-start | bytes 3145736 | tf_op jit(solution)/shard_map/ppermute | solution.py:271
  60.3 10.0 %collective-permute-start.9 = (bf16[32,2,16,128]{3,2,1,0:T(8,128)(2,1)S(1)}, bf16[32,2,16,128]{3,2,1,0:T(8,128)(2,1)S(1)}, u32[]{:S(2)}, u32[]{:S(2)}) collective-permute-start(bf16[32,2,16,128]{3,2,1,0:T(8,128)(2,1)S(1)} %get-tuple-element.40), channel_id=1, source_target_pairs={{0,64},{32,96},{64,128},{96,160},{128,192},{160,224},{192,0},{224,... | collective-permute-start | bytes 786440 | tf_op jit(solution)/shard_map/ppermute | solution.py:281
  62.4 9.1 %collective-permute-start.11 = (bf16[32,2,16,128]{3,2,1,0:T(8,128)(2,1)S(1)}, bf16[32,2,16,128]{3,2,1,0:T(8,128)(2,1)S(1)}, u32[]{:S(2)}, u32[]{:S(2)}) collective-permute-start(bf16[32,2,16,128]{3,2,1,0:T(8,128)(2,1)S(1)} %get-tuple-element.44), channel_id=1, source_target_pairs={{0,192},{32,224},{64,0},{96,32},{128,64},{160,96},{192,128},{224,1... | collective-permute-start | bytes 786440 | tf_op jit(solution)/shard_map/ppermute | solution.py:281
  63.6 13.4 %collective-permute-start.10 = (bf16[32,2,16,128]{3,2,1,0:T(8,128)(2,1)S(1)}, bf16[32,2,16,128]{3,2,1,0:T(8,128)(2,1)S(1)}, u32[]{:S(2)}, u32[]{:S(2)}) collective-permute-start(bf16[32,2,16,128]{3,2,1,0:T(8,128)(2,1)S(1)} %get-tuple-element.45), channel_id=1, source_target_pairs={{0,128},{32,160},{64,192},{96,224},{128,0},{160,32},{192,64},{224,... | collective-permute-start | bytes 786440 | tf_op jit(solution)/shard_map/ppermute | solution.py:281
  (4 other events, 4.9 us)

commit v5 on v4

--- a/solution.py
+++ b/solution.py
@@ -13,8 +13,8 @@
 WHOLE = pl.BlockSpec(memory_space=pltpu.VMEM)
 
 
-def params():
-    return pltpu.CompilerParams(vmem_limit_bytes=32 * 1024 * 1024)
+def params(mebibytes=32):
+    return pltpu.CompilerParams(vmem_limit_bytes=mebibytes * 1024 * 1024)
 
 
 def pick_kernel(place_ref, screened_ref, out_ref):
@@ -41,7 +41,7 @@
             in_specs=[pl.BlockSpec((local, tall, width), lambda i, place: (0, i, 0))],
             out_specs=pl.BlockSpec((freqs, local, tall, width // freqs), lambda i, place: (0, 0, i, 0)),
         ),
-        compiler_params=params(),
+        compiler_params=params(60),
     )(place, screened)
 
 
@@ -76,11 +76,14 @@
     places = out_ref.shape[1]
     pair = 2 * BAND
     tall = places * pair
+    mix = mix_ref[...].reshape(4 * tall, freqs * BAND)
     for band in range(rows // BAND):
         piece = pieces_ref[:, :, band * BAND : (band + 1) * BAND, :].reshape(freqs * BAND, width)
+        both = jnp.dot(mix, piece, preferred_element_type=jnp.float32)
         for half in range(2):
-            mixed = jnp.dot(mix_ref[half], piece, preferred_element_type=jnp.float32)
-            mixed = (mixed[:tall] + mixed[tall:]).astype(jnp.bfloat16)
+            upper = both[2 * half * tall : (2 * half + 1) * tall]
+            lower = both[(2 * half + 1) * tall : (2 * half + 2) * tall]
+            mixed = (upper + lower).astype(jnp.bfloat16)
             for place in range(places):
                 out_ref[half, place, band * pair : (band + 1) * pair, :] = mixed[place * pair : (place + 1) * pair]
 
@@ -217,22 +220,27 @@
         [(((y + i) % height) * DEPTH + z, y * DEPTH + z) for y in range(height) for z in range(DEPTH)]
         for i in range(height)
     ]
-    flat_state = three_state.reshape(rows, states * targets)
-    flat_state, screened = lax.optimization_barrier((flat_state, screened))
-    span = states * targets // 2
-    parts = [flat_state[:, part * span : (part + 1) * span] for part in range(2)]
-    own = lax.ppermute(parts[0], ("freq", "aux"), along)
-    slabs = [[own] + [lax.ppermute(own, "aux", across[i]) for i in range(1, height)]]
-    parts[1], slabs[0][0] = lax.optimization_barrier((parts[1], slabs[0][0]))
-    own = lax.ppermute(parts[1], ("freq", "aux"), along)
-    slabs.append([own])
-    for i in range(1, height):
-        ready, slabs[0][i] = lax.optimization_barrier((own, slabs[0][i]))
-        slabs[1].append(lax.ppermute(ready, "aux", across[i]))
-
     place = lax.axis_index("aux").astype(jnp.int32).reshape(1)
     pieces = pick(place, screened, freq_count)
+    pieces, three_state = lax.optimization_barrier((pieces, three_state))
     pieces = lax.all_to_all(pieces, "freq", split_axis=0, concat_axis=0, tiled=True)
+
+    def after(value, done):
+        return lax.optimization_barrier((value, done))
+
+    flat_state = three_state.reshape(rows, states * targets)
+    span = states * targets // 2
+    first, second = (flat_state[:, part * span : (part + 1) * span] for part in range(2))
+    own = lax.ppermute(first, ("freq", "aux"), along)
+    far = lax.ppermute(second, "aux", across[2])
+    slabs = [[own] + [lax.ppermute(own, "aux", across[i]) for i in range(1, height)]]
+    second, slabs[0][0] = after(second, slabs[0][0])
+    own = lax.ppermute(second, ("freq", "aux"), along)
+    far = lax.ppermute(far, ("freq", "aux"), along)
+    slabs.append([own, own, far, own])
+    for i in (1, 3):
+        ready, slabs[0][i] = after(own, slabs[0][i])
+        slabs[1][i] = lax.ppermute(ready, "aux", across[i])
 
     half = jnp.arange(2, dtype=jnp.int32)[:, None, None]
     other = jnp.arange(chips, dtype=jnp.int32)[None, :, None]

time: 98.5 us -> 104 us (1.056)
  starting transfers between devices: 28.8 us -> 36.8 us
  waiting for transfers between devices: 19 us -> 16 us
  Pallas kernels: 20.2 us -> 22.9 us
  local copies, waits for them, and re-layouts: 6.48 us -> 4.52 us
    ppermute x1, starting transfers between devices: 0.09 us -> 13 us  [shards(): taken = lax.ppermute(given, 'freq', swap)]
    all_to_all x1, starting transfers between devices: 11.1 us -> 4.47 us  [shards(): lax.all_to_all(pieces, 'freq', split_axis=0, concat_axis=0, tiled=True)]
    ppermute x5 -> x6, starting transfers between devices: 7.31 us -> 11 us  [the longest x2 3.24 us: shards(): slabs[1][i] = lax.ppermute(ready, 'aux', across[i])]
    ppermute x3, starting transfers between devices: 5.9 us -> 3.66 us  [shards(): lax.ppermute(own, 'aux', across[i])]
    unnamed x31 -> x23, local copies, waits for them, and re-layouts: 3.52 us -> 1.59 us
    all_to_all x1, waiting for transfers between devices: 2.18 us -> 0.48 us  [shards(): lax.all_to_all(pieces, 'freq', split_axis=0, concat_axis=0, tiled=True)]
    pallas_call x1, Pallas kernels: 2.34 us -> 4.04 us  [pick(): pl.pallas_call(pick_kernel, out_shape=jax.ShapeDtypeStruct((freqs, local,...]
  transfers between devices with their start and end apart: 13 -> 14, of which waited for: 6 -> 5; matrix products, arithmetic and copies ran while one was open for 4% -> 5% of each run, Pallas kernels for 17% -> 15%
where the time goes in v5:
time: 104 us
  starting transfers between devices  36.8 us (35%)
  Pallas kernels  22.9 us (22%)
  blocking collectives  19.9 us (19%)
  waiting for transfers between devices  16 us (15%)
  local copies, waits for them, and re-layouts  4.52 us (4%)
  other arithmetic  1.78 us (2%)
  matrix products  1.3 us (1%)
    all_to_all x1, blocking collectives, shards(): lax.all_to_all(summed.astype(jnp.bfloat16), 'aux', split_axis=0, concat_a...  19.9 us
    pallas_call x4, Pallas kernels, contract(): pl.pallas_call(functools.partial(contract_kernel, jobs, part, bool(totals...  15.9 us
    ppermute x1, starting transfers between devices, shards(): taken = lax.ppermute(given, 'freq', swap)  13 us
    ppermute x3, waiting for transfers between devices, shards(): lax.ppermute(sent[i], 'freq', chip_shift(i + 1))  10.1 us
    ppermute x3, waiting for transfers between devices, shards(): lax.ppermute(own, 'aux', across[i])  5.36 us
    ppermute x3, starting transfers between devices, shards(): lax.ppermute(sent[i], 'freq', chip_shift(i + 1))  4.63 us
    all_to_all x1, starting transfers between devices, shards(): lax.all_to_all(pieces, 'freq', split_axis=0, concat_axis=0, tiled=True)  4.47 us
    pallas_call x1, Pallas kernels, pick(): pl.pallas_call(pick_kernel, out_shape=jax.ShapeDtypeStruct((freqs, local,...  4.04 us
  transfers between devices with their start and end apart: 14, of which 5 were waited for; matrix products, arithmetic and copies ran while one was open for 5% of the time, Pallas kernels for 15%

profile of v5, /device:TPU:32, one launch (start us, length us, event | category | flops | bytes accessed | tf_op | source)
XLA Modules:
  0.0 103.5 jit_solution(6234781566619999028)
XLA Ops:
  0.0 4.0 %shard_map.82 = bf16[8,2,128,512]{3,2,1,0:T(8,128)(2,1)} custom-call(s32[1]{0:T(128)} %bitcast.place_ref, bf16[2,128,4096]{2,1,0:T(8,128)(2,1)} %screened_ref.1), custom_call_target="tpu_custom_call" | custom-call | tf_op jit(solution)/shard_map/pallas_call | solution.py:35
  4.0 4.5 %all-to-all-start = ((bf16[8,2,128,512]{3,2,1,0:T(8,128)(2,1)}), bf16[8,2,128,512]{3,2,1,0:T(8,128)(2,1)}, u32[]{:S(2)}, u32[]{:S(2)}) async-start(bf16[8,2,128,512]{3,2,1,0:T(8,128)(2,1)} %shard_map.82), calls=%async_computation | async-start | bytes 4194304 | tf_op jit(solution)/shard_map/all_to_all | solution.py:226
  9.5 1.4 %collective-permute-start = (bf16[128,1024]{1,0:T(8,128)(2,1)S(1)}, bf16[128,1024]{1,0:T(8,128)(2,1)}, u32[]{:S(2)}, u32[]{:S(2)}) collective-permute-start(bf16[128,1024]{1,0:T(8,128)(2,1)S(1)} %get-tuple-element.42), channel_id=1, source_target_pairs={{0,0},{1,1},{2,2},{3,3},{4,4},{5,5},{6,6},{7,7},{8,8},{9,9},{10,10... | collective-permute-start | bytes 786440 | tf_op jit(solution)/shard_map/ppermute | solution.py:234
  10.8 3.2 %collective-permute-start.4 = (bf16[128,1024]{1,0:T(8,128)(2,1)}, bf16[128,1024]{1,0:T(8,128)(2,1)}, u32[]{:S(2)}, u32[]{:S(2)}) collective-permute-start(bf16[128,1024]{1,0:T(8,128)(2,1)} %get-tuple-element.22), channel_id=1, source_target_pairs={{16,0},{17,1},{18,2},{19,3},{20,4},{21,5},{22,6},{23,7},{24,8},{25... | collective-permute-start | bytes 786440 | tf_op jit(solution)/shard_map/ppermute | solution.py:235
  15.9 1.6 %collective-permute-start.1 = (bf16[128,1024]{1,0:T(8,128)(2,1)}, bf16[128,1024]{1,0:T(8,128)(2,1)S(1)}, u32[]{:S(2)}, u32[]{:S(2)}) collective-permute-start(bf16[128,1024]{1,0:T(8,128)(2,1)} %get-tuple-element.22), channel_id=1, source_target_pairs={{0,0},{1,1},{2,2},{3,3},{4,4},{5,5},{6,6},{7,7},{8,8},{9,9},{10,10... | collective-permute-start | bytes 786440 | tf_op jit(solution)/shard_map/ppermute | solution.py:238
  17.6 1.2 %copy.12 = bf16[2,16,64,512]{3,2,1,0:T(8,128)(2,1)S(1)} copy(bf16[2,16,64,512]{3,1,2,0:T(8,128)(2,1)S(1)} %bitcast.26) | data formatting | bytes 4194304 | tf_op jit(solution)/shard_map/transpose | solution.py:269
  19.1 1.6 %collective-permute-start.6 = (bf16[128,1024]{1,0:T(8,128)(2,1)}, bf16[128,1024]{1,0:T(8,128)(2,1)S(1)}, u32[]{:S(2)}, u32[]{:S(2)}) collective-permute-start(bf16[128,1024]{1,0:T(8,128)(2,1)} %collective-permute-done.refs_3_), channel_id=1, source_target_pairs={{24,0},{25,1},{26,2},{27,3},{28,4},{29,5},{30,6},{31,7},{0,8},{1,9... | collective-permute-start | bytes 786440 | tf_op jit(solution)/shard_map/ppermute | solution.py:236
  20.7 1.7 %collective-permute-start.2 = (bf16[128,1024]{1,0:T(8,128)(2,1)}, bf16[128,1024]{1,0:T(8,128)(2,1)S(1)}, u32[]{:S(2)}, u32[]{:S(2)}) collective-permute-start(bf16[128,1024]{1,0:T(8,128)(2,1)} %collective-permute-done.refs_3_), channel_id=1, source_target_pairs={{8,0},{9,1},{10,2},{11,3},{12,4},{13,5},{14,6},{15,7},{16,8},{17,9... | collective-permute-start | bytes 786440 | tf_op jit(solution)/shard_map/ppermute | solution.py:236
  22.4 1.6 %collective-permute-start.5 = (bf16[128,1024]{1,0:T(8,128)(2,1)}, bf16[128,1024]{1,0:T(8,128)(2,1)S(1)}, u32[]{:S(2)}, u32[]{:S(2)}) collective-permute-start(bf16[128,1024]{1,0:T(8,128)(2,1)} %collective-permute-done.4), channel_id=1, source_target_pairs={{0,0},{1,1},{2,2},{3,3},{4,4},{5,5},{6,6},{7,7},{8,8},{9,9},{10,10... | collective-permute-start | bytes 786440 | tf_op jit(solution)/shard_map/ppermute | solution.py:239
  24.0 1.3 %fusion.2.refs_2_ = bf16[2,512,1024]{2,1,0:T(8,128)(2,1)S(1)} fusion(bf16[2,1024,512]{2,1,0:T(8,128)(2,1)S(1)} %bitcast.27, s32[2,512]{1,0:T(2,128)S(1)} %add_select_fusion, s32[512]{0:T(512)S(1)} %add.202), kind=kOutput, calls=%fused_computation.2 | convolution fusion | flops 1075314688 | bytes 4200448 | tf_op jit(solution)/shard_map/bns,brs->bnr/dot_general | solution.py:270
  25.3 5.4 %collective-permute-done.6.refs_6_ = bf16[128,1024]{1,0:T(8,128)(2,1)S(1)} collective-permute-done((bf16[128,1024]{1,0:T(8,128)(2,1)}, bf16[128,1024]{1,0:T(8,128)(2,1)S(1)}, u32[]{:S(2)}, u32[]{:S(2)}) %collective-permute-start.6) | collective-permute-done | bytes 262176 | tf_op jit(solution)/shard_map/ppermute | solution.py:236
  32.8 2.5 %collective-permute-start.3 = (bf16[128,1024]{1,0:T(8,128)(2,1)S(1)}, bf16[128,1024]{1,0:T(8,128)(2,1)S(1)}, u32[]{:S(2)}, u32[]{:S(2)}) collective-permute-start(bf16[128,1024]{1,0:T(8,128)(2,1)S(1)} %collective-permute-done.1.refs_3_), channel_id=1, source_target_pairs={{8,0},{9,1},{10,2},{11,3},{12,4},{13,5},{14,6},{15,7},{16,8},{17,9... | collective-permute-start | bytes 786440 | tf_op jit(solution)/shard_map/ppermute | solution.py:243
  35.8 2.9 %shard_map.84.refs_0_ = bf16[2,4,256,512]{3,2,1,0:T(8,128)(2,1)S(1)} custom-call(bf16[8,2,128,512]{3,2,1,0:T(8,128)(2,1)} %all-to-all-done.pieces_ref, bf16[2,256,256]{2,1,0:T(8,128)(2,1)S(1)} %shard_map.83.mix_ref), custom_call_target="tpu_custom_call" | custom-call | tf_op jit(solution)/shard_map/pallas_call | solution.py:94
  38.7 8.4 %shard_map.85 = (f32[4,32,2,16,128]{4,3,2,1,0:T(8,128)S(1)}, f32[3,32,2,16,128]{4,3,2,1,0:T(8,128)S(1)}, f32[1,32,2,16,128]{4,3,2,1,0:T(8,128)S(1)}) custom-call(bf16[2,4,256,512]{3,2,1,0:T(8,128)(2,1)S(1)} %shard_map.84.refs_0_, f32[2,8,2048]{2,1,0:T(8,128)S(1)} %broadcast_bitcast_fusion.refs_1_, bf16[2,512,1024]{2,1,0:T(8,128)(2,1)S(1)} %fusion.2.refs_2_, ...), custom_call_target="tpu_custom_call" | custom-call | flops 4294967296 | bytes 16777216 | tf_op jit(solution)/shard_map/pallas_call | solution.py:174
  47.2 3.3 %shard_map.87 = bf16[4,32,2,16,128]{4,3,2,1,0:T(8,128)(2,1)S(1)} custom-call(bf16[2,4,256,512]{3,2,1,0:T(8,128)(2,1)S(1)} %shard_map.84.refs_0_, f32[2,8,2048]{2,1,0:T(8,128)S(1)} %broadcast_bitcast_fusion.refs_1_, bf16[2,512,1024]{2,1,0:T(8,128)(2,1)S(1)} %fusion.2.refs_2_, bf16[128,1024]{1,0:T(8,128)(2,1)S(1)} %collective-permute-done.1.refs_3_, ...), custom_call_target="tpu_custom_call" | custom-call | flops 2147483648 | bytes 8388608 | tf_op jit(solution)/shard_map/pallas_call | solution.py:174
  50.5 13.0 %collective-permute-start.9 = (bf16[4,32,2,16,128]{4,3,2,1,0:T(8,128)(2,1)S(1)}, bf16[4,32,2,16,128]{4,3,2,1,0:T(8,128)(2,1)S(1)}, u32[]{:S(2)}, u32[]{:S(2)}) collective-permute-start(bf16[4,32,2,16,128]{4,3,2,1,0:T(8,128)(2,1)S(1)} %shard_map.87), channel_id=1, source_target_pairs={{0,32},{32,0},{64,96},{96,64},{128,160},{160,128},{192,224},{224,1... | collective-permute-start | bytes 3145736 | tf_op jit(solution)/shard_map/ppermute | solution.py:279
  63.6 2.6 %shard_map.86 = f32[3,32,2,16,128]{4,3,2,1,0:T(8,128)S(1)} custom-call(bf16[2,4,256,512]{3,2,1,0:T(8,128)(2,1)S(1)} %shard_map.84.refs_0_, f32[2,8,2048]{2,1,0:T(8,128)S(1)} %broadcast_bitcast_fusion.refs_1_, bf16[2,512,1024]{2,1,0:T(8,128)(2,1)S(1)} %fusion.2.refs_2_, bf16[128,1024]{1,0:T(8,128)(2,1)S(1)} %collective-permute-done.1.refs_3_, ...), custom_call_target="tpu_custom_call" | custom-call | flops 1610612736 | bytes 6291456 | tf_op jit(solution)/shard_map/pallas_call | solution.py:174
  66.5 2.5 %collective-permute-start.10 = (bf16[32,2,16,128]{3,2,1,0:T(8,128)(2,1)S(1)}, bf16[32,2,16,128]{3,2,1,0:T(8,128)(2,1)S(1)}, u32[]{:S(2)}, u32[]{:S(2)}) collective-permute-start(bf16[32,2,16,128]{3,2,1,0:T(8,128)(2,1)S(1)} %get-tuple-element.36), channel_id=1, source_target_pairs={{0,64},{32,96},{64,128},{96,160},{128,192},{160,224},{192,0},{224,... | collective-permute-start | bytes 786440 | tf_op jit(solution)/shard_map/ppermute | solution.py:289
  69.8 1.3 %collective-permute-start.11 = (bf16[32,2,16,128]{3,2,1,0:T(8,128)(2,1)S(1)}, bf16[32,2,16,128]{3,2,1,0:T(8,128)(2,1)S(1)}, u32[]{:S(2)}, u32[]{:S(2)}) collective-permute-start(bf16[32,2,16,128]{3,2,1,0:T(8,128)(2,1)S(1)} %get-tuple-element.41), channel_id=1, source_target_pairs={{0,128},{32,160},{64,192},{96,224},{128,0},{160,32},{192,64},{224,... | collective-permute-start | bytes 786440 | tf_op jit(solution)/shard_map/ppermute | solution.py:289
  71.1 1.5 %shard_map.88 = f32[1,32,2,16,128]{4,3,2,1,0:T(8,128)S(1)} custom-call(bf16[2,4,256,512]{3,2,1,0:T(8,128)(2,1)S(1)} %shard_map.84.refs_0_, f32[2,8,2048]{2,1,0:T(8,128)S(1)} %broadcast_bitcast_fusion.refs_1_, bf16[2,512,1024]{2,1,0:T(8,128)(2,1)S(1)} %fusion.2.refs_2_, bf16[128,1024]{1,0:T(8,128)(2,1)S(1)} %collective-permute-done.1.refs_3_, ...), custom_call_target="tpu_custom_call" | custom-call | flops 536870912 | bytes 2097152 | tf_op jit(solution)/shard_map/pallas_call | solution.py:174
  72.6 3.4 %collective-permute-done.10 = bf16[32,2,16,128]{3,2,1,0:T(8,128)(2,1)S(1)} collective-permute-done((bf16[32,2,16,128]{3,2,1,0:T(8,128)(2,1)S(1)}, bf16[32,2,16,128]{3,2,1,0:T(8,128)(2,1)S(1)}, u32[]{:S(2)}, u32[]{:S(2)}) %collective-permute-start.10) | collective-permute-done | bytes 262176 | tf_op jit(solution)/shard_map/ppermute | solution.py:289
  76.0 2.1 %collective-permute-done.12 = bf16[32,2,16,128]{3,2,1,0:T(8,128)(2,1)S(1)} collective-permute-done((bf16[32,2,16,128]{3,2,1,0:T(8,128)(2,1)S(1)}, bf16[32,2,16,128]{3,2,1,0:T(8,128)(2,1)S(1)}, u32[]{:S(2)}, u32[]{:S(2)}) %collective-permute-start.12) | collective-permute-done | bytes 262176 | tf_op jit(solution)/shard_map/ppermute | solution.py:289
  78.1 4.7 %collective-permute-done.11 = bf16[32,2,16,128]{3,2,1,0:T(8,128)(2,1)S(1)} collective-permute-done((bf16[32,2,16,128]{3,2,1,0:T(8,128)(2,1)S(1)}, bf16[32,2,16,128]{3,2,1,0:T(8,128)(2,1)S(1)}, u32[]{:S(2)}, u32[]{:S(2)}) %collective-permute-start.11) | collective-permute-done | bytes 262176 | tf_op jit(solution)/shard_map/ppermute | solution.py:289
  82.9 19.9 %all_to_all.10 = bf16[32,2,16,128]{3,2,1,0:T(8,128)(2,1)S(1)} all-to-all(bf16[32,2,16,128]{3,2,1,0:T(8,128)(2,1)S(1)} %fusion.12), channel_id=1, replica_groups=mesh['freq'=8,'aux'=32] {'aux'}, dimensions={0} | all-to-all | bytes 524288 | tf_op jit(solution)/shard_map/all_to_all | solution.py:294
  (70 shorter events, 7.7 us)
Async XLA Ops:
  4.0 4.6 %copy-start.5 = (bf16[128,16,128]{2,1,0:T(8,128)(2,1)S(1)}, bf16[128,16,128]{2,1,0:T(8,128)(2,1)}, u32[]{:S(2)}) copy-start(bf16[128,16,128]{2,1,0:T(8,128)(2,1)} %param.11) | copy-start | bytes 1572868
  4.0 31.7 %all-to-all-start = ((bf16[8,2,128,512]{3,2,1,0:T(8,128)(2,1)}), bf16[8,2,128,512]{3,2,1,0:T(8,128)(2,1)}, u32[]{:S(2)}, u32[]{:S(2)}) async-start(bf16[8,2,128,512]{3,2,1,0:T(8,128)(2,1)} %shard_map.82), calls=%async_computation | async-start | bytes 4194304 | tf_op jit(solution)/shard_map/all_to_all | solution.py:226
  8.5 5.5 %copy-start.9 = (s32[32]{0:T(128)S(1)}, s32[32]{0:T(128)}, u32[]{:S(2)}) copy-start(s32[32]{0:T(128)} %param.15) | copy-start | bytes 388
  8.5 5.7 %copy-start.7 = (s32[2,8]{1,0:T(2,128)S(1)}, s32[2,8]{1,0:T(2,128)}, u32[]{:S(2)}) copy-start(s32[2,8]{1,0:T(2,128)} %param.13) | copy-start | bytes 196
  8.5 6.1 %copy-start.6 = (f32[16,16]{1,0:T(8,128)S(1)}, f32[16,16]{1,0:T(8,128)}, u32[]{:S(2)}) copy-start(f32[16,16]{1,0:T(8,128)} %param.10) | copy-start | bytes 3076
  8.6 6.3 %copy-start.8 = (f32[16]{0:T(128)S(1)}, f32[16]{0:T(128)}, u32[]{:S(2)}) copy-start(f32[16]{0:T(128)} %param.9) | copy-start | bytes 196
  8.6 6.7 %copy-start.10 = (s32[2]{0:T(128)S(1)}, s32[2]{0:T(128)}, u32[]{:S(2)}) copy-start(s32[2]{0:T(128)} %param.14) | copy-start | bytes 28
  8.6 9.0 %copy-start.4 = (bf16[128,16,512]{2,1,0:T(8,128)(2,1)S(1)}, bf16[128,16,512]{2,1,0:T(8,128)(2,1)}, u32[]{:S(2)}) copy-start(bf16[128,16,512]{2,1,0:T(8,128)(2,1)} %param.12) | copy-start | bytes 6291460
  9.5 6.5 %collective-permute-start = (bf16[128,1024]{1,0:T(8,128)(2,1)S(1)}, bf16[128,1024]{1,0:T(8,128)(2,1)}, u32[]{:S(2)}, u32[]{:S(2)}) collective-permute-start(bf16[128,1024]{1,0:T(8,128)(2,1)S(1)} %get-tuple-element.42), channel_id=1, source_target_pairs={{0,0},{1,1},{2,2},{3,3},{4,4},{5,5},{6,6},{7,7},{8,8},{9,9},{10,10... | collective-permute-start | bytes 786440 | tf_op jit(solution)/shard_map/ppermute | solution.py:234
  10.8 11.5 %collective-permute-start.4 = (bf16[128,1024]{1,0:T(8,128)(2,1)}, bf16[128,1024]{1,0:T(8,128)(2,1)}, u32[]{:S(2)}, u32[]{:S(2)}) collective-permute-start(bf16[128,1024]{1,0:T(8,128)(2,1)} %get-tuple-element.22), channel_id=1, source_target_pairs={{16,0},{17,1},{18,2},{19,3},{20,4},{21,5},{22,6},{23,7},{24,8},{25... | collective-permute-start | bytes 786440 | tf_op jit(solution)/shard_map/ppermute | solution.py:235
  15.9 9.3 %collective-permute-start.1 = (bf16[128,1024]{1,0:T(8,128)(2,1)}, bf16[128,1024]{1,0:T(8,128)(2,1)S(1)}, u32[]{:S(2)}, u32[]{:S(2)}) collective-permute-start(bf16[128,1024]{1,0:T(8,128)(2,1)} %get-tuple-element.22), channel_id=1, source_target_pairs={{0,0},{1,1},{2,2},{3,3},{4,4},{5,5},{6,6},{7,7},{8,8},{9,9},{10,10... | collective-permute-start | bytes 786440 | tf_op jit(solution)/shard_map/ppermute | solution.py:238
  18.7 20.0 %collective-permute-start.8 = (bf16[128,1024]{1,0:T(8,128)(2,1)}, bf16[128,1024]{1,0:T(8,128)(2,1)}, u32[]{:S(2)}, u32[]{:S(2)}) collective-permute-start(bf16[128,1024]{1,0:T(8,128)(2,1)} %collective-permute-done.refs_3_), channel_id=1, source_target_pairs={{16,0},{17,1},{18,2},{19,3},{20,4},{21,5},{22,6},{23,7},{24,8},{25... | collective-permute-start | bytes 786440 | tf_op jit(solution)/shard_map/ppermute | solution.py:236
  19.1 11.5 %collective-permute-start.6 = (bf16[128,1024]{1,0:T(8,128)(2,1)}, bf16[128,1024]{1,0:T(8,128)(2,1)S(1)}, u32[]{:S(2)}, u32[]{:S(2)}) collective-permute-start(bf16[128,1024]{1,0:T(8,128)(2,1)} %collective-permute-done.refs_3_), channel_id=1, source_target_pairs={{24,0},{25,1},{26,2},{27,3},{28,4},{29,5},{30,6},{31,7},{0,8},{1,9... | collective-permute-start | bytes 786440 | tf_op jit(solution)/shard_map/ppermute | solution.py:236
  20.7 11.4 %collective-permute-start.2 = (bf16[128,1024]{1,0:T(8,128)(2,1)}, bf16[128,1024]{1,0:T(8,128)(2,1)S(1)}, u32[]{:S(2)}, u32[]{:S(2)}) collective-permute-start(bf16[128,1024]{1,0:T(8,128)(2,1)} %collective-permute-done.refs_3_), channel_id=1, source_target_pairs={{8,0},{9,1},{10,2},{11,3},{12,4},{13,5},{14,6},{15,7},{16,8},{17,9... | collective-permute-start | bytes 786440 | tf_op jit(solution)/shard_map/ppermute | solution.py:236
  22.4 24.8 %collective-permute-start.5 = (bf16[128,1024]{1,0:T(8,128)(2,1)}, bf16[128,1024]{1,0:T(8,128)(2,1)S(1)}, u32[]{:S(2)}, u32[]{:S(2)}) collective-permute-start(bf16[128,1024]{1,0:T(8,128)(2,1)} %collective-permute-done.4), channel_id=1, source_target_pairs={{0,0},{1,1},{2,2},{3,3},{4,4},{5,5},{6,6},{7,7},{8,8},{9,9},{10,10... | collective-permute-start | bytes 786440 | tf_op jit(solution)/shard_map/ppermute | solution.py:239
  30.7 0.7 copy-start
  31.4 15.8 %collective-permute-start.7 = (bf16[128,1024]{1,0:T(8,128)(2,1)S(1)}, bf16[128,1024]{1,0:T(8,128)(2,1)S(1)}, u32[]{:S(2)}, u32[]{:S(2)}) collective-permute-start(bf16[128,1024]{1,0:T(8,128)(2,1)S(1)} %collective-permute-done.1.refs_3_), channel_id=1, source_target_pairs={{24,0},{25,1},{26,2},{27,3},{28,4},{29,5},{30,6},{31,7},{0,8},{1,9... | collective-permute-start | bytes 786440 | tf_op jit(solution)/shard_map/ppermute | solution.py:243
  32.8 14.4 %collective-permute-start.3 = (bf16[128,1024]{1,0:T(8,128)(2,1)S(1)}, bf16[128,1024]{1,0:T(8,128)(2,1)S(1)}, u32[]{:S(2)}, u32[]{:S(2)}) collective-permute-start(bf16[128,1024]{1,0:T(8,128)(2,1)S(1)} %collective-permute-done.1.refs_3_), channel_id=1, source_target_pairs={{8,0},{9,1},{10,2},{11,3},{12,4},{13,5},{14,6},{15,7},{16,8},{17,9... | collective-permute-start | bytes 786440 | tf_op jit(solution)/shard_map/ppermute | solution.py:243
  35.8 2.9 %copy-start.1 = (bf16[128,1024]{1,0:T(8,128)(2,1)S(1)}, bf16[128,1024]{1,0:T(8,128)(2,1)}, u32[]{:S(2)}) copy-start(bf16[128,1024]{1,0:T(8,128)(2,1)} %copy-done) | copy-start | bytes 786436
  35.8 2.9 %copy-start.3 = (bf16[128,1024]{1,0:T(8,128)(2,1)S(1)}, bf16[128,1024]{1,0:T(8,128)(2,1)}, u32[]{:S(2)}) copy-start(bf16[128,1024]{1,0:T(8,128)(2,1)} %copy-done.2) | copy-start | bytes 786436
  50.5 15.7 %collective-permute-start.9 = (bf16[4,32,2,16,128]{4,3,2,1,0:T(8,128)(2,1)S(1)}, bf16[4,32,2,16,128]{4,3,2,1,0:T(8,128)(2,1)S(1)}, u32[]{:S(2)}, u32[]{:S(2)}) collective-permute-start(bf16[4,32,2,16,128]{4,3,2,1,0:T(8,128)(2,1)S(1)} %shard_map.87), channel_id=1, source_target_pairs={{0,32},{32,0},{64,96},{96,64},{128,160},{160,128},{192,224},{224,1... | collective-permute-start | bytes 3145736 | tf_op jit(solution)/shard_map/ppermute | solution.py:279
  66.5 9.5 %collective-permute-start.10 = (bf16[32,2,16,128]{3,2,1,0:T(8,128)(2,1)S(1)}, bf16[32,2,16,128]{3,2,1,0:T(8,128)(2,1)S(1)}, u32[]{:S(2)}, u32[]{:S(2)}) collective-permute-start(bf16[32,2,16,128]{3,2,1,0:T(8,128)(2,1)S(1)} %get-tuple-element.36), channel_id=1, source_target_pairs={{0,64},{32,96},{64,128},{96,160},{128,192},{160,224},{192,0},{224,... | collective-permute-start | bytes 786440 | tf_op jit(solution)/shard_map/ppermute | solution.py:289
  68.9 9.1 %collective-permute-start.12 = (bf16[32,2,16,128]{3,2,1,0:T(8,128)(2,1)S(1)}, bf16[32,2,16,128]{3,2,1,0:T(8,128)(2,1)S(1)}, u32[]{:S(2)}, u32[]{:S(2)}) collective-permute-start(bf16[32,2,16,128]{3,2,1,0:T(8,128)(2,1)S(1)} %get-tuple-element.40), channel_id=1, source_target_pairs={{0,192},{32,224},{64,0},{96,32},{128,64},{160,96},{192,128},{224,1... | collective-permute-start | bytes 786440 | tf_op jit(solution)/shard_map/ppermute | solution.py:289
  69.8 13.0 %collective-permute-start.11 = (bf16[32,2,16,128]{3,2,1,0:T(8,128)(2,1)S(1)}, bf16[32,2,16,128]{3,2,1,0:T(8,128)(2,1)S(1)}, u32[]{:S(2)}, u32[]{:S(2)}) collective-permute-start(bf16[32,2,16,128]{3,2,1,0:T(8,128)(2,1)S(1)} %get-tuple-element.41), channel_id=1, source_target_pairs={{0,128},{32,160},{64,192},{96,224},{128,0},{160,32},{192,64},{224,... | collective-permute-start | bytes 786440 | tf_op jit(solution)/shard_map/ppermute | solution.py:289
  (1 other events, 0.7 us)

commit v6 on v5

--- a/solution.py
+++ b/solution.py
@@ -13,35 +13,37 @@
 WHOLE = pl.BlockSpec(memory_space=pltpu.VMEM)
 
 
-def params(mebibytes=32):
+def params(mebibytes=24):
     return pltpu.CompilerParams(vmem_limit_bytes=mebibytes * 1024 * 1024)
 
 
-def pick_kernel(place_ref, screened_ref, out_ref):
+def pick_kernel(place_ref, screened_ref, out_ref, piece_ref, sems):
     place = place_ref[0]
     row, column = place // DEPTH, place % DEPTH
     odd = column % 2
     slab = out_ref.shape[3] // 4
+    copies = []
     for f in range(out_ref.shape[0]):
         far = lax.rem(column + jnp.where(odd == 1, SHIFTS[1][f], SHIFTS[0][f]), DEPTH)
         for i in range(4):
             start = (lax.rem(row + i, 4) * DEPTH + far) * slab
-            out_ref[f, :, :, i * slab : (i + 1) * slab] = screened_ref[:, :, pl.ds(pl.multiple_of(start, slab), slab)]
+            piece_ref[f, :, :, i * slab : (i + 1) * slab] = screened_ref[:, :, pl.ds(pl.multiple_of(start, slab), slab)]
+        copies.append(pltpu.make_async_copy(piece_ref.at[f], out_ref.at[f], sems.at[f]))
+        copies[-1].start()
+    for copy in copies:
+        copy.wait()
 
 
 def pick(place, screened, freqs):
     local, rows, width = screened.shape
-    tall = rows // 4
+    shape = (freqs, local, rows, width // freqs)
     return pl.pallas_call(
         pick_kernel,
-        out_shape=jax.ShapeDtypeStruct((freqs, local, rows, width // freqs), screened.dtype),
-        grid_spec=pltpu.PrefetchScalarGridSpec(
-            num_scalar_prefetch=1,
-            grid=(rows // tall,),
-            in_specs=[pl.BlockSpec((local, tall, width), lambda i, place: (0, i, 0))],
-            out_specs=pl.BlockSpec((freqs, local, tall, width // freqs), lambda i, place: (0, 0, i, 0)),
-        ),
-        compiler_params=params(60),
+        out_shape=jax.ShapeDtypeStruct(shape, screened.dtype),
+        in_specs=[pl.BlockSpec(memory_space=pltpu.SMEM), WHOLE],
+        out_specs=pl.BlockSpec(memory_space=pl.ANY),
+        scratch_shapes=[pltpu.VMEM(shape, screened.dtype), pltpu.SemaphoreType.DMA((freqs,))],
+        compiler_params=params(16),
     )(place, screened)
 
 
@@ -220,27 +222,37 @@
         [(((y + i) % height) * DEPTH + z, y * DEPTH + z) for y in range(height) for z in range(DEPTH)]
         for i in range(height)
     ]
-    place = lax.axis_index("aux").astype(jnp.int32).reshape(1)
-    pieces = pick(place, screened, freq_count)
-    pieces, three_state = lax.optimization_barrier((pieces, three_state))
-    pieces = lax.all_to_all(pieces, "freq", split_axis=0, concat_axis=0, tiled=True)
-
-    def after(value, done):
-        return lax.optimization_barrier((value, done))
-
     flat_state = three_state.reshape(rows, states * targets)
+    flat_state, screened = lax.optimization_barrier((flat_state, screened))
     span = states * targets // 2
     first, second = (flat_state[:, part * span : (part + 1) * span] for part in range(2))
     own = lax.ppermute(first, ("freq", "aux"), along)
     far = lax.ppermute(second, "aux", across[2])
+    own, far = lax.optimization_barrier((own, far))
     slabs = [[own] + [lax.ppermute(own, "aux", across[i]) for i in range(1, height)]]
-    second, slabs[0][0] = after(second, slabs[0][0])
+    second, far, slabs[0][1] = lax.optimization_barrier((second, far, slabs[0][1]))
     own = lax.ppermute(second, ("freq", "aux"), along)
     far = lax.ppermute(far, ("freq", "aux"), along)
-    slabs.append([own, own, far, own])
+    slabs.append([own, None, far, None])
     for i in (1, 3):
-        ready, slabs[0][i] = after(own, slabs[0][i])
+        ready, slabs[0][i] = lax.optimization_barrier((own, slabs[0][i]))
         slabs[1][i] = lax.ppermute(ready, "aux", across[i])
+
+    device = jnp.arange(aux_count, dtype=jnp.int32)
+    owned = jnp.sum(jnp.where(owners[None, :] == device[:, None], device[None, :], 0), axis=1)
+    inner = orbitals // aux_count
+    wanted = (owned[:, None] * inner + jnp.arange(inner, dtype=jnp.int32)[None, :]).reshape(orbitals)
+    slot = jnp.arange(slot_count, dtype=jnp.int32)
+    listed = block_ids[:, :, None] * block_width + jnp.arange(block_width, dtype=jnp.int32)
+    listed = jnp.where(slot[None, :, None] < block_counts[:, None, None], listed, -1).reshape(block_count, orbitals)
+    choose = (wanted[None, :, None] == listed[:, None, :]).astype(jnp.bfloat16)
+    _, three_orbital = lax.optimization_barrier((slabs[0][1], three_orbital))
+    values = three_orbital.reshape(block_count, row_block, states, orbitals)
+    values = values.transpose(0, 2, 1, 3).reshape(block_count, states * row_block, orbitals)
+    dense = jnp.einsum("bns,brs->bnr", choose, values, preferred_element_type=jnp.float32).astype(jnp.bfloat16)
+    place = lax.axis_index("aux").astype(jnp.int32).reshape(1)
+    pieces = pick(place, screened, freq_count)
+    pieces = lax.all_to_all(pieces, "freq", split_axis=0, concat_axis=0, tiled=True)
 
     half = jnp.arange(2, dtype=jnp.int32)[:, None, None]
     other = jnp.arange(chips, dtype=jnp.int32)[None, :, None]
@@ -255,19 +267,6 @@
     )
     gains = jnp.sum(jnp.where(time[:, :, None, None] == freqs[:, None], greens, 0.0), axis=2)
     gains = jnp.repeat(gains, targets, axis=2)
-
-    device = jnp.arange(aux_count, dtype=jnp.int32)
-    owned = jnp.sum(jnp.where(owners[None, :] == device[:, None], device[None, :], 0), axis=1)
-    inner = orbitals // aux_count
-    wanted = (owned[:, None] * inner + jnp.arange(inner, dtype=jnp.int32)[None, :]).reshape(orbitals)
-    slot = jnp.arange(slot_count, dtype=jnp.int32)
-    listed = block_ids[:, :, None] * block_width + jnp.arange(block_width, dtype=jnp.int32)
-    listed = jnp.where(slot[None, :, None] < block_counts[:, None, None], listed, -1).reshape(block_count, orbitals)
-    choose = (wanted[None, :, None] == listed[:, None, :]).astype(jnp.bfloat16)
-    _, three_orbital = lax.optimization_barrier((slabs[0][0], three_orbital))
-    values = three_orbital.reshape(block_count, row_block, states, orbitals)
-    values = values.transpose(0, 2, 1, 3).reshape(block_count, states * row_block, orbitals)
-    dense = jnp.einsum("bns,brs->bnr", choose, values, preferred_element_type=jnp.float32).astype(jnp.bfloat16)
 
     slabs[0][1], pieces = lax.optimization_barrier((slabs[0][1], pieces))
     timed = transform(pieces, spread_table(table))

time: 104 us -> 103 us (level)
  waiting for transfers between devices: 16 us -> 24.2 us
  starting transfers between devices: 36.8 us -> 30.1 us
  Pallas kernels: 22.9 us -> 20.3 us
    ppermute x1, starting transfers between devices: 13 us -> 1.1 us  [shards(): taken = lax.ppermute(given, 'freq', swap)]
    all_to_all x1, waiting for transfers between devices: 0.48 us -> 6.88 us  [shards(): lax.all_to_all(pieces, 'freq', split_axis=0, concat_axis=0, tiled=True)]
    all_to_all x1, starting transfers between devices: 4.47 us -> 10.5 us  [shards(): lax.all_to_all(pieces, 'freq', split_axis=0, concat_axis=0, tiled=True)]
    pallas_call x1, Pallas kernels: 4.04 us -> 1.45 us  [pick(): pl.pallas_call(pick_kernel, out_shape=jax.ShapeDtypeStruct(shape, screene...]
    ppermute x3, waiting for transfers between devices: 5.36 us -> 6.52 us  [shards(): lax.ppermute(own, 'aux', across[i])]
  transfers between devices with their start and end apart: 14 -> 14, of which waited for: 5 -> 5; matrix products, arithmetic and copies ran while one was open for 5% -> 4% of each run, Pallas kernels for 15% -> 17%
where the time goes in v6:
time: 103 us; the launch traced here: 102 us
  starting transfers between devices  30.1 us (29%)
  waiting for transfers between devices  24.2 us (23%)
  Pallas kernels  20.3 us (20%)
  blocking collectives  19.2 us (19%)
  local copies, waits for them, and re-layouts  5.03 us (5%)
  other arithmetic  1.78 us (2%)
  matrix products  1.3 us (1%)
    all_to_all x1, blocking collectives, shards(): lax.all_to_all(summed.astype(jnp.bfloat16), 'aux', split_axis=0, concat_a...  19.2 us
    pallas_call x4, Pallas kernels, contract(): pl.pallas_call(functools.partial(contract_kernel, jobs, part, bool(totals...  15.9 us
    ppermute x3, waiting for transfers between devices, shards(): lax.ppermute(sent[i], 'freq', chip_shift(i + 1))  10.8 us
    all_to_all x1, starting transfers between devices, shards(): lax.all_to_all(pieces, 'freq', split_axis=0, concat_axis=0, tiled=True)  10.5 us
    all_to_all x1, waiting for transfers between devices, shards(): lax.all_to_all(pieces, 'freq', split_axis=0, concat_axis=0, tiled=True)  6.88 us
    ppermute x3, waiting for transfers between devices, shards(): lax.ppermute(own, 'aux', across[i])  6.52 us
    ppermute x3, starting transfers between devices, shards(): lax.ppermute(sent[i], 'freq', chip_shift(i + 1))  5.11 us
    ppermute x1, starting transfers between devices, shards(): far = lax.ppermute(second, 'aux', across[2])  3.19 us
  transfers between devices with their start and end apart: 14, of which 5 were waited for; matrix products, arithmetic and copies ran while one was open for 4% of the time, Pallas kernels for 17%

profile of v6, /device:TPU:32, one launch (start us, length us, event | category | flops | bytes accessed | tf_op | source)
XLA Modules:
  0.0 102.2 jit_solution(13695771009311121551)
XLA Ops:
  0.0 1.3 %copy.15 = bf16[16,8,16,128]{3,1,2,0:T(8,128)(2,1)S(1)} copy(bf16[16,8,16,128]{3,2,1,0:T(8,128)(2,1)} %bitcast.29) | data formatting | bytes 1048576
  2.1 1.4 %collective-permute-start = (bf16[128,1024]{1,0:T(8,128)(2,1)S(1)}, bf16[128,1024]{1,0:T(8,128)(2,1)}, u32[]{:S(2)}, u32[]{:S(2)}) collective-permute-start(bf16[128,1024]{1,0:T(8,128)(2,1)S(1)} %get-tuple-element.48), channel_id=1, source_target_pairs={{0,0},{1,1},{2,2},{3,3},{4,4},{5,5},{6,6},{7,7},{8,8},{9,9},{10,10... | collective-permute-start | bytes 786440 | tf_op jit(solution)/shard_map/ppermute | solution.py:229
  3.4 3.2 %collective-permute-start.1 = (bf16[128,1024]{1,0:T(8,128)(2,1)}, bf16[128,1024]{1,0:T(8,128)(2,1)}, u32[]{:S(2)}, u32[]{:S(2)}) collective-permute-start(bf16[128,1024]{1,0:T(8,128)(2,1)} %get-tuple-element.27), channel_id=1, source_target_pairs={{16,0},{17,1},{18,2},{19,3},{20,4},{21,5},{22,6},{23,7},{24,8},{25... | collective-permute-start | bytes 786440 | tf_op jit(solution)/shard_map/ppermute | solution.py:230
  6.6 1.4 %shard_map.82 = bf16[8,2,128,512]{3,2,1,0:T(8,128)(2,1)} custom-call(s32[1]{0:T(128)} %bitcast.place_ref, bf16[2,128,4096]{2,1,0:T(8,128)(2,1)S(1)} %copy-done), custom_call_target="tpu_custom_call" | custom-call | tf_op jit(solution)/shard_map/pallas_call | solution.py:40
  8.2 10.5 %all-to-all-start = ((bf16[8,2,128,512]{3,2,1,0:T(8,128)(2,1)}), bf16[8,2,128,512]{3,2,1,0:T(8,128)(2,1)}, u32[]{:S(2)}, u32[]{:S(2)}) async-start(bf16[8,2,128,512]{3,2,1,0:T(8,128)(2,1)} %shard_map.82), calls=%async_computation | async-start | bytes 4194304 | tf_op jit(solution)/shard_map/all_to_all | solution.py:255
  19.6 1.1 %collective-permute-start.2 = (bf16[128,1024]{1,0:T(8,128)(2,1)}, bf16[128,1024]{1,0:T(8,128)(2,1)S(1)}, u32[]{:S(2)}, u32[]{:S(2)}) collective-permute-start(bf16[128,1024]{1,0:T(8,128)(2,1)} %collective-permute-done.refs_3_), channel_id=1, source_target_pairs={{8,0},{9,1},{10,2},{11,3},{12,4},{13,5},{14,6},{15,7},{16,8},{17,9... | collective-permute-start | bytes 786440 | tf_op jit(solution)/shard_map/ppermute | solution.py:232
  22.1 6.5 %collective-permute-done.2.refs_4_ = bf16[128,1024]{1,0:T(8,128)(2,1)S(1)} collective-permute-done((bf16[128,1024]{1,0:T(8,128)(2,1)}, bf16[128,1024]{1,0:T(8,128)(2,1)S(1)}, u32[]{:S(2)}, u32[]{:S(2)}) %collective-permute-start.2) | collective-permute-done | bytes 262176 | tf_op jit(solution)/shard_map/ppermute | solution.py:232
  28.6 1.6 %collective-permute-start.3 = (bf16[128,1024]{1,0:T(8,128)(2,1)}, bf16[128,1024]{1,0:T(8,128)(2,1)S(1)}, u32[]{:S(2)}, u32[]{:S(2)}) collective-permute-start(bf16[128,1024]{1,0:T(8,128)(2,1)} %get-tuple-element.27), channel_id=1, source_target_pairs={{0,0},{1,1},{2,2},{3,3},{4,4},{5,5},{6,6},{7,7},{8,8},{9,9},{10,10... | collective-permute-start | bytes 786440 | tf_op jit(solution)/shard_map/ppermute | solution.py:234
  31.7 1.6 %collective-permute-start.5 = (bf16[128,1024]{1,0:T(8,128)(2,1)}, bf16[128,1024]{1,0:T(8,128)(2,1)S(1)}, u32[]{:S(2)}, u32[]{:S(2)}) collective-permute-start(bf16[128,1024]{1,0:T(8,128)(2,1)} %collective-permute-done.1), channel_id=1, source_target_pairs={{0,0},{1,1},{2,2},{3,3},{4,4},{5,5},{6,6},{7,7},{8,8},{9,9},{10,10... | collective-permute-start | bytes 786440 | tf_op jit(solution)/shard_map/ppermute | solution.py:235
  34.0 2.6 %collective-permute-start.4 = (bf16[128,1024]{1,0:T(8,128)(2,1)S(1)}, bf16[128,1024]{1,0:T(8,128)(2,1)S(1)}, u32[]{:S(2)}, u32[]{:S(2)}) collective-permute-start(bf16[128,1024]{1,0:T(8,128)(2,1)S(1)} %collective-permute-done.3.refs_3_), channel_id=1, source_target_pairs={{8,0},{9,1},{10,2},{11,3},{12,4},{13,5},{14,6},{15,7},{16,8},{17,9... | collective-permute-start | bytes 786440 | tf_op jit(solution)/shard_map/ppermute | solution.py:239
  36.6 1.2 %copy.12 = bf16[2,16,64,512]{3,2,1,0:T(8,128)(2,1)S(1)} copy(bf16[2,16,64,512]{3,1,2,0:T(8,128)(2,1)S(1)} %bitcast.26) | data formatting | bytes 4194304 | tf_op jit(solution)/shard_map/transpose | solution.py:251
  37.8 1.3 %fusion.2.refs_2_ = bf16[2,512,1024]{2,1,0:T(8,128)(2,1)S(1)} fusion(bf16[2,1024,512]{2,1,0:T(8,128)(2,1)S(1)} %bitcast.27, s32[2,512]{1,0:T(2,128)S(1)} %add_select_fusion, s32[512]{0:T(512)S(1)} %add.202), kind=kOutput, calls=%fused_computation.2 | convolution fusion | flops 1075314688 | bytes 4200448 | tf_op jit(solution)/shard_map/bns,brs->bnr/dot_general | solution.py:252
  39.1 6.9 %all-to-all-done.pieces_ref = bf16[8,2,128,512]{3,2,1,0:T(8,128)(2,1)} async-done(((bf16[8,2,128,512]{3,2,1,0:T(8,128)(2,1)}), bf16[8,2,128,512]{3,2,1,0:T(8,128)(2,1)}, u32[]{:S(2)}, u32[]{:S(2)}) %all-to-all-start) | async-done | bytes 2097184 | tf_op jit(solution)/shard_map/all_to_all | solution.py:255
  46.0 2.9 %shard_map.84.refs_0_ = bf16[2,4,256,512]{3,2,1,0:T(8,128)(2,1)S(1)} custom-call(bf16[8,2,128,512]{3,2,1,0:T(8,128)(2,1)} %all-to-all-done.pieces_ref, bf16[2,256,256]{2,1,0:T(8,128)(2,1)S(1)} %shard_map.83.mix_ref), custom_call_target="tpu_custom_call" | custom-call | tf_op jit(solution)/shard_map/pallas_call | solution.py:96
  48.9 8.4 %shard_map.85 = (f32[4,32,2,16,128]{4,3,2,1,0:T(8,128)S(1)}, f32[3,32,2,16,128]{4,3,2,1,0:T(8,128)S(1)}, f32[1,32,2,16,128]{4,3,2,1,0:T(8,128)S(1)}) custom-call(bf16[2,4,256,512]{3,2,1,0:T(8,128)(2,1)S(1)} %shard_map.84.refs_0_, f32[2,8,2048]{2,1,0:T(8,128)S(1)} %broadcast_bitcast_fusion.refs_1_, bf16[2,512,1024]{2,1,0:T(8,128)(2,1)S(1)} %fusion.2.refs_2_, ...), custom_call_target="tpu_custom_call" | custom-call | flops 4294967296 | bytes 16777216 | tf_op jit(solution)/shard_map/pallas_call | solution.py:176
  57.4 3.3 %shard_map.87 = bf16[4,32,2,16,128]{4,3,2,1,0:T(8,128)(2,1)S(1)} custom-call(bf16[2,4,256,512]{3,2,1,0:T(8,128)(2,1)S(1)} %shard_map.84.refs_0_, f32[2,8,2048]{2,1,0:T(8,128)S(1)} %broadcast_bitcast_fusion.refs_1_, bf16[2,512,1024]{2,1,0:T(8,128)(2,1)S(1)} %fusion.2.refs_2_, bf16[128,1024]{1,0:T(8,128)(2,1)S(1)} %collective-permute-done.3.refs_3_, ...), custom_call_target="tpu_custom_call" | custom-call | flops 2147483648 | bytes 8388608 | tf_op jit(solution)/shard_map/pallas_call | solution.py:176
  61.8 2.6 %shard_map.86 = f32[3,32,2,16,128]{4,3,2,1,0:T(8,128)S(1)} custom-call(bf16[2,4,256,512]{3,2,1,0:T(8,128)(2,1)S(1)} %shard_map.84.refs_0_, f32[2,8,2048]{2,1,0:T(8,128)S(1)} %broadcast_bitcast_fusion.refs_1_, bf16[2,512,1024]{2,1,0:T(8,128)(2,1)S(1)} %fusion.2.refs_2_, bf16[128,1024]{1,0:T(8,128)(2,1)S(1)} %collective-permute-done.3.refs_3_, ...), custom_call_target="tpu_custom_call" | custom-call | flops 1610612736 | bytes 6291456 | tf_op jit(solution)/shard_map/pallas_call | solution.py:176
  64.8 3.7 %collective-permute-start.12 = (bf16[32,2,16,128]{3,2,1,0:T(8,128)(2,1)S(1)}, bf16[32,2,16,128]{3,2,1,0:T(8,128)(2,1)S(1)}, u32[]{:S(2)}, u32[]{:S(2)}) collective-permute-start(bf16[32,2,16,128]{3,2,1,0:T(8,128)(2,1)S(1)} %get-tuple-element.46), channel_id=1, source_target_pairs={{0,192},{32,224},{64,0},{96,32},{128,64},{160,96},{192,128},{224,1... | collective-permute-start | bytes 786440 | tf_op jit(solution)/shard_map/ppermute | solution.py:288
  68.5 1.4 %collective-permute-start.11 = (bf16[32,2,16,128]{3,2,1,0:T(8,128)(2,1)S(1)}, bf16[32,2,16,128]{3,2,1,0:T(8,128)(2,1)S(1)}, u32[]{:S(2)}, u32[]{:S(2)}) collective-permute-start(bf16[32,2,16,128]{3,2,1,0:T(8,128)(2,1)S(1)} %get-tuple-element.47), channel_id=1, source_target_pairs={{0,128},{32,160},{64,192},{96,224},{128,0},{160,32},{192,64},{224,... | collective-permute-start | bytes 786440 | tf_op jit(solution)/shard_map/ppermute | solution.py:288
  69.8 1.5 %shard_map.88 = f32[1,32,2,16,128]{4,3,2,1,0:T(8,128)S(1)} custom-call(bf16[2,4,256,512]{3,2,1,0:T(8,128)(2,1)S(1)} %shard_map.84.refs_0_, f32[2,8,2048]{2,1,0:T(8,128)S(1)} %broadcast_bitcast_fusion.refs_1_, bf16[2,512,1024]{2,1,0:T(8,128)(2,1)S(1)} %fusion.2.refs_2_, bf16[128,1024]{1,0:T(8,128)(2,1)S(1)} %collective-permute-done.3.refs_3_, ...), custom_call_target="tpu_custom_call" | custom-call | flops 536870912 | bytes 2097152 | tf_op jit(solution)/shard_map/pallas_call | solution.py:176
  71.4 4.0 %collective-permute-done.10 = bf16[32,2,16,128]{3,2,1,0:T(8,128)(2,1)S(1)} collective-permute-done((bf16[32,2,16,128]{3,2,1,0:T(8,128)(2,1)S(1)}, bf16[32,2,16,128]{3,2,1,0:T(8,128)(2,1)S(1)}, u32[]{:S(2)}, u32[]{:S(2)}) %collective-permute-start.10) | collective-permute-done | bytes 262176 | tf_op jit(solution)/shard_map/ppermute | solution.py:288
  75.3 5.0 %collective-permute-done.12 = bf16[32,2,16,128]{3,2,1,0:T(8,128)(2,1)S(1)} collective-permute-done((bf16[32,2,16,128]{3,2,1,0:T(8,128)(2,1)S(1)}, bf16[32,2,16,128]{3,2,1,0:T(8,128)(2,1)S(1)}, u32[]{:S(2)}, u32[]{:S(2)}) %collective-permute-start.12) | collective-permute-done | bytes 262176 | tf_op jit(solution)/shard_map/ppermute | solution.py:288
  80.3 1.8 %collective-permute-done.11 = bf16[32,2,16,128]{3,2,1,0:T(8,128)(2,1)S(1)} collective-permute-done((bf16[32,2,16,128]{3,2,1,0:T(8,128)(2,1)S(1)}, bf16[32,2,16,128]{3,2,1,0:T(8,128)(2,1)S(1)}, u32[]{:S(2)}, u32[]{:S(2)}) %collective-permute-start.11) | collective-permute-done | bytes 262176 | tf_op jit(solution)/shard_map/ppermute | solution.py:288
  82.3 19.2 %all_to_all.10 = bf16[32,2,16,128]{3,2,1,0:T(8,128)(2,1)S(1)} all-to-all(bf16[32,2,16,128]{3,2,1,0:T(8,128)(2,1)S(1)} %fusion.12), channel_id=1, replica_groups=mesh['freq'=8,'aux'=32] {'aux'}, dimensions={0} | all-to-all | bytes 524288 | tf_op jit(solution)/shard_map/all_to_all | solution.py:293
  (70 shorter events, 7.5 us)
Async XLA Ops:
  0.0 6.6 %copy-start = (bf16[2,128,4096]{2,1,0:T(8,128)(2,1)S(1)}, bf16[2,128,4096]{2,1,0:T(8,128)(2,1)}, u32[]{:S(2)}) copy-start(bf16[2,128,4096]{2,1,0:T(8,128)(2,1)} %screened_ref) | copy-start | bytes 6291460
  2.1 17.5 %collective-permute-start = (bf16[128,1024]{1,0:T(8,128)(2,1)S(1)}, bf16[128,1024]{1,0:T(8,128)(2,1)}, u32[]{:S(2)}, u32[]{:S(2)}) collective-permute-start(bf16[128,1024]{1,0:T(8,128)(2,1)S(1)} %get-tuple-element.48), channel_id=1, source_target_pairs={{0,0},{1,1},{2,2},{3,3},{4,4},{5,5},{6,6},{7,7},{8,8},{9,9},{10,10... | collective-permute-start | bytes 786440 | tf_op jit(solution)/shard_map/ppermute | solution.py:229
  3.4 16.2 %collective-permute-start.1 = (bf16[128,1024]{1,0:T(8,128)(2,1)}, bf16[128,1024]{1,0:T(8,128)(2,1)}, u32[]{:S(2)}, u32[]{:S(2)}) collective-permute-start(bf16[128,1024]{1,0:T(8,128)(2,1)} %get-tuple-element.27), channel_id=1, source_target_pairs={{16,0},{17,1},{18,2},{19,3},{20,4},{21,5},{22,6},{23,7},{24,8},{25... | collective-permute-start | bytes 786440 | tf_op jit(solution)/shard_map/ppermute | solution.py:230
  8.1 11.0 %copy-start.6 = (f32[16,16]{1,0:T(8,128)S(1)}, f32[16,16]{1,0:T(8,128)}, u32[]{:S(2)}) copy-start(f32[16,16]{1,0:T(8,128)} %param.10) | copy-start | bytes 3076
  8.1 11.3 %copy-start.9 = (s32[32]{0:T(128)S(1)}, s32[32]{0:T(128)}, u32[]{:S(2)}) copy-start(s32[32]{0:T(128)} %param.15) | copy-start | bytes 388
  8.1 11.4 %copy-start.7 = (s32[2,8]{1,0:T(2,128)S(1)}, s32[2,8]{1,0:T(2,128)}, u32[]{:S(2)}) copy-start(s32[2,8]{1,0:T(2,128)} %param.13) | copy-start | bytes 196
  8.1 12.6 %copy-start.8 = (f32[16]{0:T(128)S(1)}, f32[16]{0:T(128)}, u32[]{:S(2)}) copy-start(f32[16]{0:T(128)} %param.9) | copy-start | bytes 196
  8.1 22.1 %copy-start.10 = (s32[2]{0:T(128)S(1)}, s32[2]{0:T(128)}, u32[]{:S(2)}) copy-start(s32[2]{0:T(128)} %param.14) | copy-start | bytes 28
  8.2 28.4 %copy-start.5 = (bf16[128,16,512]{2,1,0:T(8,128)(2,1)S(1)}, bf16[128,16,512]{2,1,0:T(8,128)(2,1)}, u32[]{:S(2)}) copy-start(bf16[128,16,512]{2,1,0:T(8,128)(2,1)} %param.12) | copy-start | bytes 6291460
  8.2 37.8 %all-to-all-start = ((bf16[8,2,128,512]{3,2,1,0:T(8,128)(2,1)}), bf16[8,2,128,512]{3,2,1,0:T(8,128)(2,1)}, u32[]{:S(2)}, u32[]{:S(2)}) async-start(bf16[8,2,128,512]{3,2,1,0:T(8,128)(2,1)} %shard_map.82), calls=%async_computation | async-start | bytes 4194304 | tf_op jit(solution)/shard_map/all_to_all | solution.py:255
  19.6 9.0 %collective-permute-start.2 = (bf16[128,1024]{1,0:T(8,128)(2,1)}, bf16[128,1024]{1,0:T(8,128)(2,1)S(1)}, u32[]{:S(2)}, u32[]{:S(2)}) collective-permute-start(bf16[128,1024]{1,0:T(8,128)(2,1)} %collective-permute-done.refs_3_), channel_id=1, source_target_pairs={{8,0},{9,1},{10,2},{11,3},{12,4},{13,5},{14,6},{15,7},{16,8},{17,9... | collective-permute-start | bytes 786440 | tf_op jit(solution)/shard_map/ppermute | solution.py:232
  21.1 12.3 %collective-permute-start.6 = (bf16[128,1024]{1,0:T(8,128)(2,1)}, bf16[128,1024]{1,0:T(8,128)(2,1)S(1)}, u32[]{:S(2)}, u32[]{:S(2)}) collective-permute-start(bf16[128,1024]{1,0:T(8,128)(2,1)} %collective-permute-done.refs_3_), channel_id=1, source_target_pairs={{24,0},{25,1},{26,2},{27,3},{28,4},{29,5},{30,6},{31,7},{0,8},{1,9... | collective-permute-start | bytes 786440 | tf_op jit(solution)/shard_map/ppermute | solution.py:232
  28.6 2.2 %copy-start.1 = (bf16[128,1024]{1,0:T(8,128)(2,1)}, bf16[128,1024]{1,0:T(8,128)(2,1)S(1)}, u32[]{:S(2)}) copy-start(bf16[128,1024]{1,0:T(8,128)(2,1)S(1)} %collective-permute-done.2.refs_4_) | copy-start | bytes 786436
  28.6 5.4 %collective-permute-start.3 = (bf16[128,1024]{1,0:T(8,128)(2,1)}, bf16[128,1024]{1,0:T(8,128)(2,1)S(1)}, u32[]{:S(2)}, u32[]{:S(2)}) collective-permute-start(bf16[128,1024]{1,0:T(8,128)(2,1)} %get-tuple-element.27), channel_id=1, source_target_pairs={{0,0},{1,1},{2,2},{3,3},{4,4},{5,5},{6,6},{7,7},{8,8},{9,9},{10,10... | collective-permute-start | bytes 786440 | tf_op jit(solution)/shard_map/ppermute | solution.py:234
  30.8 18.0 %collective-permute-start.8 = (bf16[128,1024]{1,0:T(8,128)(2,1)}, bf16[128,1024]{1,0:T(8,128)(2,1)}, u32[]{:S(2)}, u32[]{:S(2)}) collective-permute-start(bf16[128,1024]{1,0:T(8,128)(2,1)} %collective-permute-done.refs_3_), channel_id=1, source_target_pairs={{16,0},{17,1},{18,2},{19,3},{20,4},{21,5},{22,6},{23,7},{24,8},{25... | collective-permute-start | bytes 786440 | tf_op jit(solution)/shard_map/ppermute | solution.py:232
  31.7 25.6 %collective-permute-start.5 = (bf16[128,1024]{1,0:T(8,128)(2,1)}, bf16[128,1024]{1,0:T(8,128)(2,1)S(1)}, u32[]{:S(2)}, u32[]{:S(2)}) collective-permute-start(bf16[128,1024]{1,0:T(8,128)(2,1)} %collective-permute-done.1), channel_id=1, source_target_pairs={{0,0},{1,1},{2,2},{3,3},{4,4},{5,5},{6,6},{7,7},{8,8},{9,9},{10,10... | collective-permute-start | bytes 786440 | tf_op jit(solution)/shard_map/ppermute | solution.py:235
  34.0 23.3 %collective-permute-start.4 = (bf16[128,1024]{1,0:T(8,128)(2,1)S(1)}, bf16[128,1024]{1,0:T(8,128)(2,1)S(1)}, u32[]{:S(2)}, u32[]{:S(2)}) collective-permute-start(bf16[128,1024]{1,0:T(8,128)(2,1)S(1)} %collective-permute-done.3.refs_3_), channel_id=1, source_target_pairs={{8,0},{9,1},{10,2},{11,3},{12,4},{13,5},{14,6},{15,7},{16,8},{17,9... | collective-permute-start | bytes 786440 | tf_op jit(solution)/shard_map/ppermute | solution.py:239
  36.6 20.8 %collective-permute-start.7 = (bf16[128,1024]{1,0:T(8,128)(2,1)S(1)}, bf16[128,1024]{1,0:T(8,128)(2,1)S(1)}, u32[]{:S(2)}, u32[]{:S(2)}) collective-permute-start(bf16[128,1024]{1,0:T(8,128)(2,1)S(1)} %collective-permute-done.3.refs_3_), channel_id=1, source_target_pairs={{24,0},{25,1},{26,2},{27,3},{28,4},{29,5},{30,6},{31,7},{0,8},{1,9... | collective-permute-start | bytes 786440 | tf_op jit(solution)/shard_map/ppermute | solution.py:239
  46.0 2.9 %copy-start.2 = (bf16[128,1024]{1,0:T(8,128)(2,1)S(1)}, bf16[128,1024]{1,0:T(8,128)(2,1)}, u32[]{:S(2)}) copy-start(bf16[128,1024]{1,0:T(8,128)(2,1)} %copy-done.1) | copy-start | bytes 786436
  46.0 2.9 %copy-start.4 = (bf16[128,1024]{1,0:T(8,128)(2,1)S(1)}, bf16[128,1024]{1,0:T(8,128)(2,1)}, u32[]{:S(2)}) copy-start(bf16[128,1024]{1,0:T(8,128)(2,1)} %copy-done.3) | copy-start | bytes 786436
  60.7 3.8 %collective-permute-start.9 = (bf16[4,32,2,16,128]{4,3,2,1,0:T(8,128)(2,1)S(1)}, bf16[4,32,2,16,128]{4,3,2,1,0:T(8,128)(2,1)S(1)}, u32[]{:S(2)}, u32[]{:S(2)}) collective-permute-start(bf16[4,32,2,16,128]{4,3,2,1,0:T(8,128)(2,1)S(1)} %shard_map.87), channel_id=1, source_target_pairs={{0,32},{32,0},{64,96},{96,64},{128,160},{160,128},{192,224},{224,1... | collective-permute-start | bytes 3145736 | tf_op jit(solution)/shard_map/ppermute | solution.py:278
  64.7 10.6 %collective-permute-start.10 = (bf16[32,2,16,128]{3,2,1,0:T(8,128)(2,1)S(1)}, bf16[32,2,16,128]{3,2,1,0:T(8,128)(2,1)S(1)}, u32[]{:S(2)}, u32[]{:S(2)}) collective-permute-start(bf16[32,2,16,128]{3,2,1,0:T(8,128)(2,1)S(1)} %get-tuple-element.42), channel_id=1, source_target_pairs={{0,64},{32,96},{64,128},{96,160},{128,192},{160,224},{192,0},{224,... | collective-permute-start | bytes 786440 | tf_op jit(solution)/shard_map/ppermute | solution.py:288
  64.8 15.5 %collective-permute-start.12 = (bf16[32,2,16,128]{3,2,1,0:T(8,128)(2,1)S(1)}, bf16[32,2,16,128]{3,2,1,0:T(8,128)(2,1)S(1)}, u32[]{:S(2)}, u32[]{:S(2)}) collective-permute-start(bf16[32,2,16,128]{3,2,1,0:T(8,128)(2,1)S(1)} %get-tuple-element.46), channel_id=1, source_target_pairs={{0,192},{32,224},{64,0},{96,32},{128,64},{160,96},{192,128},{224,1... | collective-permute-start | bytes 786440 | tf_op jit(solution)/shard_map/ppermute | solution.py:288
  68.5 13.7 %collective-permute-start.11 = (bf16[32,2,16,128]{3,2,1,0:T(8,128)(2,1)S(1)}, bf16[32,2,16,128]{3,2,1,0:T(8,128)(2,1)S(1)}, u32[]{:S(2)}, u32[]{:S(2)}) collective-permute-start(bf16[32,2,16,128]{3,2,1,0:T(8,128)(2,1)S(1)} %get-tuple-element.47), channel_id=1, source_target_pairs={{0,128},{32,160},{64,192},{96,224},{128,0},{160,32},{192,64},{224,... | collective-permute-start | bytes 786440 | tf_op jit(solution)/shard_map/ppermute | solution.py:288
  (1 other events, 0.7 us)

commit v7 on v6

--- a/solution.py
+++ b/solution.py
@@ -72,47 +72,27 @@
     )(table)
 
 
-def mix_kernel(pieces_ref, mix_ref, out_ref):
+def mix_bands(pieces_ref, pieces_at, mix_ref, timed_ref):
     sources, local, rows, width = pieces_ref.shape
-    freqs = sources * local
-    places = out_ref.shape[1]
+    places = timed_ref.shape[1]
     pair = 2 * BAND
     tall = places * pair
-    mix = mix_ref[...].reshape(4 * tall, freqs * BAND)
-    for band in range(rows // BAND):
-        piece = pieces_ref[:, :, band * BAND : (band + 1) * BAND, :].reshape(freqs * BAND, width)
+    bands = rows // BAND
+    mix = mix_ref[...].reshape(4 * tall, sources * local * BAND)
+    for band in range(bands):
+        if band % 2 == 0:
+            pieces_at[band // 2].wait()
+        piece = pieces_ref[:, :, band * BAND : (band + 1) * BAND, :].reshape(sources * local * BAND, width)
         both = jnp.dot(mix, piece, preferred_element_type=jnp.float32)
         for half in range(2):
             upper = both[2 * half * tall : (2 * half + 1) * tall]
             lower = both[(2 * half + 1) * tall : (2 * half + 2) * tall]
             mixed = (upper + lower).astype(jnp.bfloat16)
             for place in range(places):
-                out_ref[half, place, band * pair : (band + 1) * pair, :] = mixed[place * pair : (place + 1) * pair]
-
-
-def transform(pieces, mix):
-    sources, local, rows, width = pieces.shape
-    times = mix.shape[1] // (2 * BAND)
-    return pl.pallas_call(
-        mix_kernel,
-        out_shape=jax.ShapeDtypeStruct((2, times // 2, 2 * rows, width), jnp.bfloat16),
-        in_specs=[WHOLE] * 2,
-        out_specs=WHOLE,
-        compiler_params=params(),
-    )(pieces, mix)
-
-
-def contract_kernel(jobs, part, has_total, *refs):
-    timed_ref, gains_ref, dense_ref = refs[:3]
-    slabs = refs[3:7]
-    refs = refs[7:]
-    totals = [None] * len(jobs)
-    if has_total:
-        totals, refs = refs[: len(jobs)], refs[len(jobs) :]
-    outs, (state_ref, scaled_ref) = refs[: len(jobs)], refs[len(jobs) :]
-    slab = slabs[0].shape[0]
-    for i in range(4):
-        state_ref[i * slab : (i + 1) * slab, :] = slabs[i][...]
+                timed_ref[half, place, band * pair : (band + 1) * pair, :] = mixed[place * pair : (place + 1) * pair]
+
+
+def run_jobs(jobs, part, timed_ref, gains_ref, dense_ref, dense_at, state_ref, scaled_ref, totals, outs):
     span = state_ref.shape[1]
     blocks = dense_ref.shape[0]
     deep = scaled_ref.shape[0] // blocks
@@ -123,7 +103,7 @@
     owners, inner, targets = outs[0].shape[1], outs[0].shape[3], outs[0].shape[4]
     pair = 2 * targets
 
-    for (half, first, count), total_ref, out_ref in zip(jobs, totals, outs):
+    for number, ((half, first, count), total_ref, out_ref) in enumerate(zip(jobs, totals, outs)):
         timed = timed_ref[half, first : first + count].reshape(count * tall, depth)
 
         def states(step, carry):
@@ -147,11 +127,13 @@
             return carry
 
         lax.fori_loop(0, span // pair, states, 0)
+        if number == 0:
+            dense_at.wait()
         for place in range(count):
             columns = slice(place * pair, (place + 1) * pair)
             value = sum(
                 jnp.dot(
-                    dense_ref[block, :, part * deep : (part + 1) * deep],
+                    dense_ref[block],
                     scaled_ref[block * deep : (block + 1) * deep, columns],
                     preferred_element_type=jnp.float32,
                 )
@@ -159,38 +141,132 @@
             )
             for time in range(2):
                 piece = value[:, time * targets : (time + 1) * targets].reshape(owners, inner, targets)
-                if has_total:
+                if total_ref is not None:
                     piece = piece + total_ref[place, :, time, :, :]
                 out_ref[place, :, time, :, :] = piece.astype(out_ref.dtype)
 
 
-def contract(jobs, part, timed, gains, dense, slabs, totals, owners, dtypes):
+def first_kernel(jobs, *refs):
+    pieces_in, mix_ref, gains_ref, dense_in = refs[:4]
+    slabs, refs = refs[4:8], refs[8:]
+    timed_ref, outs = refs[0], refs[1 : 1 + len(jobs)]
+    pieces_ref, state_ref, scaled_ref, dense_ref, pieces_sem, slab_sem, dense_sem = refs[1 + len(jobs) :]
+    deep = dense_ref.shape[2]
+    pieces_at = []
+    for i in range(pieces_sem.shape[0]):
+        rows = pl.ds(i * 2 * BAND, 2 * BAND)
+        pieces_at.append(pltpu.make_async_copy(pieces_in.at[:, :, rows], pieces_ref.at[:, :, rows], pieces_sem.at[i]))
+        pieces_at[-1].start()
+    slabs_at = slab_copies(slabs, state_ref, slab_sem)
+    dense_at = pltpu.make_async_copy(dense_in.at[:, :, pl.ds(0, deep)], dense_ref, dense_sem.at[0])
+    dense_at.start()
+    mix_bands(pieces_ref, pieces_at, mix_ref, timed_ref)
+    for copy in slabs_at:
+        copy.wait()
+    run_jobs(
+        jobs, 0, timed_ref, gains_ref, dense_ref, dense_at, state_ref, scaled_ref, (None,) * len(jobs), outs
+    )
+
+
+def slab_copies(slabs, state_ref, slab_sem):
+    slab = slabs[0].shape[0]
+    copies = []
+    for i in range(4):
+        copies.append(pltpu.make_async_copy(slabs[i], state_ref.at[pl.ds(i * slab, slab)], slab_sem.at[i]))
+        copies[-1].start()
+    return copies
+
+
+def last_kernel(job, gather, *refs):
+    timed_ref, gains_ref, dense_in, total_ref = refs[:4]
+    if gather:
+        slabs, (out_ref, state_ref, scaled_ref, dense_ref, dense_sem, slab_sem) = refs[4:8], refs[8:]
+        slabs_at = slab_copies(slabs, state_ref, slab_sem)
+    else:
+        state_ref, out_ref, scaled_ref, dense_ref, dense_sem = refs[4:]
+    deep = dense_ref.shape[2]
+    dense_at = pltpu.make_async_copy(dense_in.at[:, :, pl.ds(deep, deep)], dense_ref, dense_sem.at[0])
+    dense_at.start()
+    if gather:
+        for copy in slabs_at:
+            copy.wait()
+    run_jobs(
+        (job,), 1, timed_ref, gains_ref, dense_ref, dense_at, state_ref, scaled_ref, (total_ref,), (out_ref,)
+    )
+
+
+AWAY = pl.BlockSpec(memory_space=pl.ANY)
+
+
+def sums_shape(count, dense, owners, targets, dtype):
+    return jax.ShapeDtypeStruct((count, owners, 2, dense.shape[1] // owners, targets), dtype)
+
+
+def cost(work, rows, depth, span, dense, targets):
+    deep = span // targets * rows
+    return pl.CostEstimate(
+        flops=4 * work * (rows * depth * span + dense.shape[1] * deep * targets),
+        bytes_accessed=2 * 1024 * 1024 * work,
+        transcendentals=0,
+    )
+
+
+def first_part(jobs, pieces, mix, gains, dense, slabs, owners):
+    sources, local, rows, width = pieces.shape
     slab, span = slabs[0].shape
-    rows = timed.shape[2] // 2
-    states = dense.shape[0] * dense.shape[2] // rows
-    targets = gains.shape[2] // states
+    blocks = dense.shape[0]
+    targets = gains.shape[2] // (blocks * dense.shape[2] // rows)
+    times = gains.shape[1]
     depth = span // targets * rows
-    operands = [timed, gains, dense, *slabs, *totals]
     wide = max(count for _, _, count in jobs)
-    work = sum(count for _, _, count in jobs)
     return pl.pallas_call(
-        functools.partial(contract_kernel, jobs, part, bool(totals)),
-        out_shape=[
-            jax.ShapeDtypeStruct((count, owners, 2, dense.shape[1] // owners, targets), dtype)
-            for (_, _, count), dtype in zip(jobs, dtypes)
-        ],
-        in_specs=[WHOLE] * len(operands),
-        out_specs=[WHOLE] * len(jobs),
+        functools.partial(first_kernel, jobs),
+        out_shape=[jax.ShapeDtypeStruct((2, times // 2, 2 * rows, width), jnp.bfloat16)]
+        + [sums_shape(count, dense, owners, targets, jnp.float32) for _, _, count in jobs],
+        in_specs=[AWAY, WHOLE, WHOLE, AWAY] + [AWAY] * 4,
+        out_specs=[WHOLE] * (1 + len(jobs)),
         scratch_shapes=[
+            pltpu.VMEM(pieces.shape, jnp.bfloat16),
             pltpu.VMEM((4 * slab, span), jnp.bfloat16),
             pltpu.VMEM((depth, wide * 2 * targets), jnp.bfloat16),
+            pltpu.VMEM((blocks, dense.shape[1], depth // blocks), jnp.bfloat16),
+            pltpu.SemaphoreType.DMA((rows // (2 * BAND),)),
+            pltpu.SemaphoreType.DMA((4,)),
+            pltpu.SemaphoreType.DMA((1,)),
         ],
         compiler_params=params(),
-        cost_estimate=pl.CostEstimate(
-            flops=4 * work * (rows * 4 * slab * span + dense.shape[1] * depth * targets),
-            bytes_accessed=2 * 1024 * 1024 * work,
-            transcendentals=0,
-        ),
+        cost_estimate=cost(sum(count for _, _, count in jobs), rows, 4 * slab, span, dense, targets),
+    )(pieces, mix, gains, dense, *slabs)
+
+
+def last_part(job, timed, gains, dense, state, total, dtype, owners):
+    gather = isinstance(state, list)
+    slabs = state if gather else []
+    span = slabs[0].shape[1] if gather else state.shape[1]
+    depth_in = timed.shape[3]
+    rows = timed.shape[2] // 2
+    blocks = dense.shape[0]
+    targets = gains.shape[2] // (blocks * dense.shape[2] // rows)
+    depth = span // targets * rows
+    count = job[2]
+    out_shape = [sums_shape(count, dense, owners, targets, dtype)]
+    scratch = [
+        pltpu.VMEM((depth, count * 2 * targets), jnp.bfloat16),
+        pltpu.VMEM((blocks, dense.shape[1], depth // blocks), jnp.bfloat16),
+        pltpu.SemaphoreType.DMA((1,)),
+    ]
+    if gather:
+        out_shape.append(jax.ShapeDtypeStruct((depth_in, span), jnp.bfloat16))
+        scratch.append(pltpu.SemaphoreType.DMA((4,)))
+    operands = [timed, gains, dense, total] + (slabs if gather else [state])
+    return pl.pallas_call(
+        functools.partial(last_kernel, job, gather),
+        out_shape=out_shape,
+        in_specs=[WHOLE, WHOLE, AWAY, WHOLE] + ([AWAY] * 4 if gather else [WHOLE]),
+        out_specs=[WHOLE] * len(out_shape),
+        scratch_shapes=scratch,
+        compiler_params=params(),
+        cost_estimate=cost(count, rows, depth_in, span, dense, targets),
     )(*operands)
 
 
@@ -268,15 +344,13 @@
     gains = jnp.sum(jnp.where(time[:, :, None, None] == freqs[:, None], greens, 0.0), axis=2)
     gains = jnp.repeat(gains, targets, axis=2)
 
-    slabs[0][1], pieces = lax.optimization_barrier((slabs[0][1], pieces))
-    timed = transform(pieces, spread_table(table))
-    run = functools.partial(contract, timed=timed, gains=gains, dense=dense, owners=aux_count)
     swap = [(f, f ^ 1) for f in range(freq_count)]
     jobs = ((0, 0, chips), (1, 1, chips - 1), (1, 0, 1))
-    totals = list(run(jobs, 0, slabs=slabs[0], totals=[], dtypes=(jnp.float32,) * 3))
-    (given,) = run(jobs[:1], 1, slabs=slabs[1], totals=totals[:1], dtypes=(jnp.bfloat16,))
+    timed, *totals = first_part(jobs, pieces, spread_table(table), gains, dense, slabs[0], aux_count)
+    run = functools.partial(last_part, timed=timed, gains=gains, dense=dense, owners=aux_count)
+    given, state = run(jobs[0], state=slabs[1], total=totals[0], dtype=jnp.bfloat16)
     taken = lax.ppermute(given, "freq", swap)
-    (kept,) = run(jobs[1:2], 1, slabs=slabs[1], totals=totals[1:2], dtypes=(jnp.float32,))
+    (kept,) = run(jobs[1], state=state, total=totals[1], dtype=jnp.float32)
     sent = [
         (kept[i - 1] + taken[i].astype(jnp.float32)).astype(jnp.bfloat16) for i in range(1, chips)
     ]
@@ -286,7 +360,7 @@
 
     totals[2], sent[0] = lax.optimization_barrier((totals[2], sent[0]))
     arrived = [lax.ppermute(sent[i], "freq", chip_shift(i + 1)) for i in range(chips - 1)]
-    (kept,) = run(jobs[2:], 1, slabs=slabs[1], totals=totals[2:], dtypes=(jnp.float32,))
+    (kept,) = run(jobs[2], state=state, total=totals[2], dtype=jnp.float32)
     summed = kept[0] + taken[0].astype(jnp.float32)
     for piece in arrived:
         summed = summed + piece.astype(jnp.float32)

time: 103 us -> 109 us (1.058)
  local copies, waits for them, and re-layouts: 5.03 us -> 13.4 us
  waiting for transfers between devices: 24.2 us -> 17 us
  starting transfers between devices: 30.1 us -> 32.6 us
  other arithmetic: 1.78 us -> 3.58 us
    all_to_all x1, waiting for transfers between devices: 6.88 us -> 0.01 us  [shards(): lax.all_to_all(pieces, 'freq', split_axis=0, concat_axis=0, tiled=True)]
    add x4, local copies, waits for them, and re-layouts: 0.23 us -> 4.59 us  [shards(): block_ids[:, :, None] * block_width]
    broadcast_in_dim x2, local copies, waits for them, and re-layouts: 0.16 us -> 2.66 us  [shards(): jnp.where(slot[None, :, None] < block_counts[:, None, None], listed, -1)]
    ppermute x1, starting transfers between devices: 1.1 us -> 3.34 us  [shards(): taken = lax.ppermute(given, 'freq', swap)]
    ppermute x1, starting transfers between devices: 1.6 us -> 3.59 us  [shards(): far = lax.ppermute(far, ('freq', 'aux'), along)]
    ppermute x3, starting transfers between devices: 5.11 us -> 3.47 us  [shards(): lax.ppermute(sent[i], 'freq', chip_shift(i + 1))]
    pallas_call x5 -> x4, Pallas kernels: 18.8 us -> 19 us  [the longest x1 10.2 us: first_part(): pl.pallas_call(functools.partial(first_kernel, jobs), out_shape=[jax.Shap...]
  transfers between devices with their start and end apart: 14 -> 14, of which waited for: 5 -> 4; matrix products, arithmetic and copies ran while one was open for 4% -> 12% of each run, Pallas kernels for 17% -> 15%
where the time goes in v7:
time: 109 us
  starting transfers between devices  32.6 us (30%)
  Pallas kernels  20.5 us (19%)
  blocking collectives  20.1 us (18%)
  waiting for transfers between devices  17 us (16%)
  local copies, waits for them, and re-layouts  13.4 us (12%)
  other arithmetic  3.58 us (3%)
  matrix products  1.3 us (1%)
    all_to_all x1, blocking collectives, shards(): lax.all_to_all(summed.astype(jnp.bfloat16), 'aux', split_axis=0, concat_a...  20.1 us
    all_to_all x1, starting transfers between devices, shards(): lax.all_to_all(pieces, 'freq', split_axis=0, concat_axis=0, tiled=True)  11.1 us
    ppermute x3, waiting for transfers between devices, shards(): lax.ppermute(sent[i], 'freq', chip_shift(i + 1))  10.7 us
    pallas_call x1, Pallas kernels, first_part(): pl.pallas_call(functools.partial(first_kernel, jobs), out_shape=[jax.Shap...  10.2 us
    pallas_call x3, Pallas kernels, last_part(): pl.pallas_call(functools.partial(last_kernel, job, gather), out_shape=out...  8.76 us
    ppermute x3, waiting for transfers between devices, shards(): lax.ppermute(own, 'aux', across[i])  6.31 us
    add x4, local copies, waits for them, and re-layouts, shards(): block_ids[:, :, None] * block_width  4.59 us
    ppermute x1, starting transfers between devices, shards(): far = lax.ppermute(far, ('freq', 'aux'), along)  3.59 us
  transfers between devices with their start and end apart: 14, of which 4 were waited for; matrix products, arithmetic and copies ran while one was open for 12% of the time, Pallas kernels for 15%

profile of v7, /device:TPU:32, one launch (start us, length us, event | category | flops | bytes accessed | tf_op | source)
XLA Modules:
  0.0 108.8 jit_solution(6790149313187446114)
XLA Ops:
  0.0 1.3 %copy.15 = bf16[16,8,16,128]{3,1,2,0:T(8,128)(2,1)S(1)} copy(bf16[16,8,16,128]{3,2,1,0:T(8,128)(2,1)} %bitcast.29) | data formatting | bytes 1048576
  2.1 3.2 %collective-permute-start.1 = (bf16[128,1024]{1,0:T(8,128)(2,1)}, bf16[128,1024]{1,0:T(8,128)(2,1)S(1)}, u32[]{:S(2)}, u32[]{:S(2)}) collective-permute-start(bf16[128,1024]{1,0:T(8,128)(2,1)} %get-tuple-element.29), channel_id=1, source_target_pairs={{16,0},{17,1},{18,2},{19,3},{20,4},{21,5},{22,6},{23,7},{24,8},{25... | collective-permute-start | bytes 786440 | tf_op jit(solution)/shard_map/ppermute | solution.py:306
  6.0 1.5 %shard_map.82 = bf16[8,2,128,512]{3,2,1,0:T(8,128)(2,1)} custom-call(s32[1]{0:T(128)} %bitcast.place_ref, bf16[2,128,4096]{2,1,0:T(8,128)(2,1)S(1)} %copy-done), custom_call_target="tpu_custom_call" | custom-call | tf_op jit(solution)/shard_map/pallas_call | solution.py:40
  7.5 11.1 %all-to-all-start = ((bf16[8,2,128,512]{3,2,1,0:T(8,128)(2,1)}), bf16[8,2,128,512]{3,2,1,0:T(8,128)(2,1)}, u32[]{:S(2)}, u32[]{:S(2)}) async-start(bf16[8,2,128,512]{3,2,1,0:T(8,128)(2,1)} %shard_map.82), calls=%async_computation | async-start | bytes 4194304 | tf_op jit(solution)/shard_map/all_to_all | solution.py:331
  22.6 6.3 %collective-permute-done.2.refs_5_ = bf16[128,1024]{1,0:T(8,128)(2,1)S(1)} collective-permute-done((bf16[128,1024]{1,0:T(8,128)(2,1)S(1)}, bf16[128,1024]{1,0:T(8,128)(2,1)S(1)}, u32[]{:S(2)}, u32[]{:S(2)}) %collective-permute-start.2) | collective-permute-done | bytes 262176 | tf_op jit(solution)/shard_map/ppermute | solution.py:308
  28.9 1.6 %collective-permute-start.3 = (bf16[128,1024]{1,0:T(8,128)(2,1)}, bf16[128,1024]{1,0:T(8,128)(2,1)S(1)}, u32[]{:S(2)}, u32[]{:S(2)}) collective-permute-start(bf16[128,1024]{1,0:T(8,128)(2,1)} %get-tuple-element.29), channel_id=1, source_target_pairs={{0,0},{1,1},{2,2},{3,3},{4,4},{5,5},{6,6},{7,7},{8,8},{9,9},{10,10... | collective-permute-start | bytes 786440 | tf_op jit(solution)/shard_map/ppermute | solution.py:310
  31.2 1.3 %add.203 = s32[2,8,64]{2,1,0:T(8,128)} broadcast(s32[2,8]{1,0:T(2,128)} %broadcast_multiply_fusion), dimensions={0,1} | broadcast | bytes 4160 | tf_op jit(solution)/shard_map/add | solution.py:322
  32.5 1.4 %add.204 = s32[2,512]{1,0:T(2,128)} reshape(s32[2,8,64]{2,1,0:T(8,128)} %add.203) | data formatting | bytes 8192 | tf_op jit(solution)/shard_map/add | solution.py:322
  34.5 1.3 %add.206 = s32[512]{0:T(512)} reshape(s32[8,64]{1,0:T(8,128)} %add.205) | data formatting | bytes 4096 | tf_op jit(solution)/shard_map/add | solution.py:322
  35.8 1.3 %broadcast_in_dim.68 = pred[2,8,64]{2,1,0:T(8,128)(4,1)} broadcast(pred[2,8]{1,0:T(4,128)(4,1)} %iota_compare_fusion.2), dimensions={0,1} | broadcast | bytes 1040 | tf_op jit(solution)/shard_map/jit(_where)/broadcast_in_dim | solution.py:323
  37.1 1.3 %broadcast_in_dim.69 = pred[2,512]{1,0:T(4,128)(4,1)} reshape(pred[2,8,64]{2,1,0:T(8,128)(4,1)} %broadcast_in_dim.68) | data formatting | bytes 2048 | tf_op jit(solution)/shard_map/jit(_where)/broadcast_in_dim | solution.py:323
  40.6 3.6 %collective-permute-start.7 = (bf16[128,1024]{1,0:T(8,128)(2,1)}, bf16[128,1024]{1,0:T(8,128)(2,1)}, u32[]{:S(2)}, u32[]{:S(2)}) collective-permute-start(bf16[128,1024]{1,0:T(8,128)(2,1)} %copy-done.8), channel_id=1, source_target_pairs={{0,0},{1,1},{2,2},{3,3},{4,4},{5,5},{6,6},{7,7},{8,8},{9,9},{10,10... | collective-permute-start | bytes 786440 | tf_op jit(solution)/shard_map/ppermute | solution.py:311
  44.2 1.2 %copy.12 = bf16[2,16,64,512]{3,2,1,0:T(8,128)(2,1)S(1)} copy(bf16[2,16,64,512]{3,1,2,0:T(8,128)(2,1)S(1)} %bitcast.26) | data formatting | bytes 4194304 | tf_op jit(solution)/shard_map/transpose | solution.py:327
  45.4 2.6 %collective-permute-start.6 = (bf16[128,1024]{1,0:T(8,128)(2,1)S(1)}, bf16[128,1024]{1,0:T(8,128)(2,1)}, u32[]{:S(2)}, u32[]{:S(2)}) collective-permute-start(bf16[128,1024]{1,0:T(8,128)(2,1)S(1)} %collective-permute-done.3.refs_4_), channel_id=1, source_target_pairs={{8,0},{9,1},{10,2},{11,3},{12,4},{13,5},{14,6},{15,7},{16,8},{17,9... | collective-permute-start | bytes 786440 | tf_op jit(solution)/shard_map/ppermute | solution.py:315
  48.1 1.3 %fusion.2.refs_3_.refs_2_ = bf16[2,512,1024]{2,1,0:T(8,128)(2,1)S(1)} fusion(bf16[2,1024,512]{2,1,0:T(8,128)(2,1)S(1)} %bitcast.27, s32[2,512]{1,0:T(2,128)S(1)} %add_select_fusion, s32[512]{0:T(512)S(1)} %copy-done.5), kind=kOutput, calls=%fused_computation.2 | convolution fusion | flops 1075314688 | bytes 4200448 | tf_op jit(solution)/shard_map/bns,brs->bnr/dot_general | solution.py:328
  51.1 10.2 %shard_map.84 = (bf16[2,4,256,512]{3,2,1,0:T(8,128)(2,1)S(1)}, f32[4,32,2,16,128]{4,3,2,1,0:T(8,128)S(1)}, f32[3,32,2,16,128]{4,3,2,1,0:T(8,128)S(1)}, f32[1,32,2,16,128]{4,3,2,1,0:T(8,128)S(1)}) custom-call(bf16[8,2,128,512]{3,2,1,0:T(8,128)(2,1)} %all-to-all-done.refs_0_, bf16[2,256,256]{2,1,0:T(8,128)(2,1)S(1)} %shard_map.83.refs_1_, ...), custom_call_target="tpu_custom_call" | custom-call | flops 4294967296 | bytes 16777216 | tf_op jit(solution)/shard_map/pallas_call | solution.py:222
  61.3 4.4 %shard_map.85 = (bf16[4,32,2,16,128]{4,3,2,1,0:T(8,128)(2,1)S(1)}, bf16[512,1024]{1,0:T(8,128)(2,1)S(1)}) custom-call(bf16[2,4,256,512]{3,2,1,0:T(8,128)(2,1)S(1)} %get-tuple-element.34.refs_0_, f32[2,8,2048]{2,1,0:T(8,128)S(1)} %broadcast_bitcast_fusion.refs_2_.refs_1_, bf16[2,512,1024]{2,1,0:T(8,128)(2,1)S(1)} %fusion.2.refs_3_.refs_2_, ...), custom_call_target="tpu_custom_call" | custom-call | flops 2147483648 | bytes 8388608 | tf_op jit(solution)/shard_map/pallas_call | solution.py:262
  65.8 3.3 %collective-permute-start.9 = (bf16[4,32,2,16,128]{4,3,2,1,0:T(8,128)(2,1)S(1)}, bf16[4,32,2,16,128]{4,3,2,1,0:T(8,128)(2,1)S(1)}, u32[]{:S(2)}, u32[]{:S(2)}) collective-permute-start(bf16[4,32,2,16,128]{4,3,2,1,0:T(8,128)(2,1)S(1)} %get-tuple-element.42), channel_id=1, source_target_pairs={{0,32},{32,0},{64,96},{96,64},{128,160},{160,128},{192,224},{224,1... | collective-permute-start | bytes 3145736 | tf_op jit(solution)/shard_map/ppermute | solution.py:352
  69.1 2.7 %shard_map.86 = f32[3,32,2,16,128]{4,3,2,1,0:T(8,128)S(1)} custom-call(bf16[2,4,256,512]{3,2,1,0:T(8,128)(2,1)S(1)} %get-tuple-element.34.refs_0_, f32[2,8,2048]{2,1,0:T(8,128)S(1)} %broadcast_bitcast_fusion.refs_2_.refs_1_, bf16[2,512,1024]{2,1,0:T(8,128)(2,1)S(1)} %fusion.2.refs_3_.refs_2_, f32[3,32,2,16,128]{4,3,2,1,0:T(8,128)S(1)} %get-tuple-element.36.refs_3_, ...), custom_call_target="tpu_custom_call" | custom-call | flops 1610612736 | bytes 6291456 | tf_op jit(solution)/shard_map/pallas_call | solution.py:262
  72.6 2.9 %collective-permute-start.11 = (bf16[32,2,16,128]{3,2,1,0:T(8,128)(2,1)S(1)}, bf16[32,2,16,128]{3,2,1,0:T(8,128)(2,1)S(1)}, u32[]{:S(2)}, u32[]{:S(2)}) collective-permute-start(bf16[32,2,16,128]{3,2,1,0:T(8,128)(2,1)S(1)} %get-tuple-element.49), channel_id=1, source_target_pairs={{0,128},{32,160},{64,192},{96,224},{128,0},{160,32},{192,64},{224,... | collective-permute-start | bytes 786440 | tf_op jit(solution)/shard_map/ppermute | solution.py:362
  75.6 1.6 %shard_map.87 = f32[1,32,2,16,128]{4,3,2,1,0:T(8,128)S(1)} custom-call(bf16[2,4,256,512]{3,2,1,0:T(8,128)(2,1)S(1)} %get-tuple-element.34.refs_0_, f32[2,8,2048]{2,1,0:T(8,128)S(1)} %broadcast_bitcast_fusion.refs_2_.refs_1_, bf16[2,512,1024]{2,1,0:T(8,128)(2,1)S(1)} %fusion.2.refs_3_.refs_2_, f32[1,32,2,16,128]{4,3,2,1,0:T(8,128)S(1)} %get-tuple-element.43.refs_3_, ...), custom_call_target="tpu_custom_call" | custom-call | flops 536870912 | bytes 2097152 | tf_op jit(solution)/shard_map/pallas_call | solution.py:262
  77.2 4.4 %collective-permute-done.10 = bf16[32,2,16,128]{3,2,1,0:T(8,128)(2,1)S(1)} collective-permute-done((bf16[32,2,16,128]{3,2,1,0:T(8,128)(2,1)S(1)}, bf16[32,2,16,128]{3,2,1,0:T(8,128)(2,1)S(1)}, u32[]{:S(2)}, u32[]{:S(2)}) %collective-permute-start.10) | collective-permute-done | bytes 262176 | tf_op jit(solution)/shard_map/ppermute | solution.py:362
  81.6 6.2 %collective-permute-done.11 = bf16[32,2,16,128]{3,2,1,0:T(8,128)(2,1)S(1)} collective-permute-done((bf16[32,2,16,128]{3,2,1,0:T(8,128)(2,1)S(1)}, bf16[32,2,16,128]{3,2,1,0:T(8,128)(2,1)S(1)}, u32[]{:S(2)}, u32[]{:S(2)}) %collective-permute-start.11) | collective-permute-done | bytes 262176 | tf_op jit(solution)/shard_map/ppermute | solution.py:362
  88.0 20.1 %all_to_all.10 = bf16[32,2,16,128]{3,2,1,0:T(8,128)(2,1)S(1)} all-to-all(bf16[32,2,16,128]{3,2,1,0:T(8,128)(2,1)S(1)} %fusion.12), channel_id=1, replica_groups=mesh['freq'=8,'aux'=32] {'aux'}, dimensions={0} | all-to-all | bytes 524288 | tf_op jit(solution)/shard_map/all_to_all | solution.py:367
  (69 shorter events, 12.2 us)
Async XLA Ops:
  0.0 6.0 %copy-start = (bf16[2,128,4096]{2,1,0:T(8,128)(2,1)S(1)}, bf16[2,128,4096]{2,1,0:T(8,128)(2,1)}, u32[]{:S(2)}) copy-start(bf16[2,128,4096]{2,1,0:T(8,128)(2,1)} %screened_ref) | copy-start | bytes 6291460
  2.1 18.0 %collective-permute-start.1 = (bf16[128,1024]{1,0:T(8,128)(2,1)}, bf16[128,1024]{1,0:T(8,128)(2,1)S(1)}, u32[]{:S(2)}, u32[]{:S(2)}) collective-permute-start(bf16[128,1024]{1,0:T(8,128)(2,1)} %get-tuple-element.29), channel_id=1, source_target_pairs={{16,0},{17,1},{18,2},{19,3},{20,4},{21,5},{22,6},{23,7},{24,8},{25... | collective-permute-start | bytes 786440 | tf_op jit(solution)/shard_map/ppermute | solution.py:306
  5.3 14.8 %collective-permute-start = (bf16[128,1024]{1,0:T(8,128)(2,1)S(1)}, bf16[128,1024]{1,0:T(8,128)(2,1)S(1)}, u32[]{:S(2)}, u32[]{:S(2)}) collective-permute-start(bf16[128,1024]{1,0:T(8,128)(2,1)S(1)} %get-tuple-element.50), channel_id=1, source_target_pairs={{0,0},{1,1},{2,2},{3,3},{4,4},{5,5},{6,6},{7,7},{8,8},{9,9},{10,10... | collective-permute-start | bytes 786440 | tf_op jit(solution)/shard_map/ppermute | solution.py:305
  7.4 11.6 %copy-start.4 = (f32[16,16]{1,0:T(8,128)S(1)}, f32[16,16]{1,0:T(8,128)}, u32[]{:S(2)}) copy-start(f32[16,16]{1,0:T(8,128)} %param.10) | copy-start | bytes 3076
  7.5 11.9 %copy-start.9 = (s32[32]{0:T(128)S(1)}, s32[32]{0:T(128)}, u32[]{:S(2)}) copy-start(s32[32]{0:T(128)} %param.15) | copy-start | bytes 388
  7.5 12.0 %copy-start.6 = (s32[2,8]{1,0:T(2,128)S(1)}, s32[2,8]{1,0:T(2,128)}, u32[]{:S(2)}) copy-start(s32[2,8]{1,0:T(2,128)} %param.13) | copy-start | bytes 196
  7.5 13.8 %copy-start.7 = (f32[16]{0:T(128)S(1)}, f32[16]{0:T(128)}, u32[]{:S(2)}) copy-start(f32[16]{0:T(128)} %param.9) | copy-start | bytes 196
  7.5 23.0 %copy-start.10 = (s32[2]{0:T(128)S(1)}, s32[2]{0:T(128)}, u32[]{:S(2)}) copy-start(s32[2]{0:T(128)} %param.14) | copy-start | bytes 28
  7.5 36.7 %copy-start.3 = (bf16[128,16,512]{2,1,0:T(8,128)(2,1)S(1)}, bf16[128,16,512]{2,1,0:T(8,128)(2,1)}, u32[]{:S(2)}) copy-start(bf16[128,16,512]{2,1,0:T(8,128)(2,1)} %param.12) | copy-start | bytes 6291460
  7.5 42.6 %all-to-all-start = ((bf16[8,2,128,512]{3,2,1,0:T(8,128)(2,1)}), bf16[8,2,128,512]{3,2,1,0:T(8,128)(2,1)}, u32[]{:S(2)}, u32[]{:S(2)}) async-start(bf16[8,2,128,512]{3,2,1,0:T(8,128)(2,1)} %shard_map.82), calls=%async_computation | async-start | bytes 4194304 | tf_op jit(solution)/shard_map/all_to_all | solution.py:331
  20.1 1.3 %copy-start.8 = (bf16[128,1024]{1,0:T(8,128)(2,1)}, bf16[128,1024]{1,0:T(8,128)(2,1)S(1)}, u32[]{:S(2)}) copy-start(bf16[128,1024]{1,0:T(8,128)(2,1)S(1)} %collective-permute-done.1) | copy-start | bytes 786436
  20.1 8.8 %collective-permute-start.2 = (bf16[128,1024]{1,0:T(8,128)(2,1)S(1)}, bf16[128,1024]{1,0:T(8,128)(2,1)S(1)}, u32[]{:S(2)}, u32[]{:S(2)}) collective-permute-start(bf16[128,1024]{1,0:T(8,128)(2,1)S(1)} %collective-permute-done.refs_4_), channel_id=1, source_target_pairs={{8,0},{9,1},{10,2},{11,3},{12,4},{13,5},{14,6},{15,7},{16,8},{17,9... | collective-permute-start | bytes 786440 | tf_op jit(solution)/shard_map/ppermute | solution.py:308
  21.6 23.8 %collective-permute-start.5 = (bf16[128,1024]{1,0:T(8,128)(2,1)S(1)}, bf16[128,1024]{1,0:T(8,128)(2,1)S(1)}, u32[]{:S(2)}, u32[]{:S(2)}) collective-permute-start(bf16[128,1024]{1,0:T(8,128)(2,1)S(1)} %collective-permute-done.refs_4_), channel_id=1, source_target_pairs={{24,0},{25,1},{26,2},{27,3},{28,4},{29,5},{30,6},{31,7},{0,8},{1,9... | collective-permute-start | bytes 786440 | tf_op jit(solution)/shard_map/ppermute | solution.py:308
  28.9 15.3 %collective-permute-start.3 = (bf16[128,1024]{1,0:T(8,128)(2,1)}, bf16[128,1024]{1,0:T(8,128)(2,1)S(1)}, u32[]{:S(2)}, u32[]{:S(2)}) collective-permute-start(bf16[128,1024]{1,0:T(8,128)(2,1)} %get-tuple-element.29), channel_id=1, source_target_pairs={{0,0},{1,1},{2,2},{3,3},{4,4},{5,5},{6,6},{7,7},{8,8},{9,9},{10,10... | collective-permute-start | bytes 786440 | tf_op jit(solution)/shard_map/ppermute | solution.py:310
  39.8 9.6 %collective-permute-start.4 = (bf16[128,1024]{1,0:T(8,128)(2,1)S(1)}, bf16[128,1024]{1,0:T(8,128)(2,1)S(1)}, u32[]{:S(2)}, u32[]{:S(2)}) collective-permute-start(bf16[128,1024]{1,0:T(8,128)(2,1)S(1)} %collective-permute-done.refs_4_), channel_id=1, source_target_pairs={{16,0},{17,1},{18,2},{19,3},{20,4},{21,5},{22,6},{23,7},{24,8},{25... | collective-permute-start | bytes 786440 | tf_op jit(solution)/shard_map/ppermute | solution.py:308
  40.6 20.7 %collective-permute-start.7 = (bf16[128,1024]{1,0:T(8,128)(2,1)}, bf16[128,1024]{1,0:T(8,128)(2,1)}, u32[]{:S(2)}, u32[]{:S(2)}) collective-permute-start(bf16[128,1024]{1,0:T(8,128)(2,1)} %copy-done.8), channel_id=1, source_target_pairs={{0,0},{1,1},{2,2},{3,3},{4,4},{5,5},{6,6},{7,7},{8,8},{9,9},{10,10... | collective-permute-start | bytes 786440 | tf_op jit(solution)/shard_map/ppermute | solution.py:311
  44.2 3.9 %copy-start.5 = (s32[512]{0:T(512)S(1)}, s32[512]{0:T(512)}, u32[]{:S(2)}) copy-start(s32[512]{0:T(512)} %add.202) | copy-start | bytes 6148
  45.4 15.9 %collective-permute-start.6 = (bf16[128,1024]{1,0:T(8,128)(2,1)S(1)}, bf16[128,1024]{1,0:T(8,128)(2,1)}, u32[]{:S(2)}, u32[]{:S(2)}) collective-permute-start(bf16[128,1024]{1,0:T(8,128)(2,1)S(1)} %collective-permute-done.3.refs_4_), channel_id=1, source_target_pairs={{8,0},{9,1},{10,2},{11,3},{12,4},{13,5},{14,6},{15,7},{16,8},{17,9... | collective-permute-start | bytes 786440 | tf_op jit(solution)/shard_map/ppermute | solution.py:315
  48.0 13.3 %collective-permute-start.8 = (bf16[128,1024]{1,0:T(8,128)(2,1)S(1)}, bf16[128,1024]{1,0:T(8,128)(2,1)}, u32[]{:S(2)}, u32[]{:S(2)}) collective-permute-start(bf16[128,1024]{1,0:T(8,128)(2,1)S(1)} %collective-permute-done.3.refs_4_), channel_id=1, source_target_pairs={{24,0},{25,1},{26,2},{27,3},{28,4},{29,5},{30,6},{31,7},{0,8},{1,9... | collective-permute-start | bytes 786440 | tf_op jit(solution)/shard_map/ppermute | solution.py:315
  50.1 1.0 copy-start.2
  65.8 6.1 %collective-permute-start.9 = (bf16[4,32,2,16,128]{4,3,2,1,0:T(8,128)(2,1)S(1)}, bf16[4,32,2,16,128]{4,3,2,1,0:T(8,128)(2,1)S(1)}, u32[]{:S(2)}, u32[]{:S(2)}) collective-permute-start(bf16[4,32,2,16,128]{4,3,2,1,0:T(8,128)(2,1)S(1)} %get-tuple-element.42), channel_id=1, source_target_pairs={{0,32},{32,0},{64,96},{96,64},{128,160},{160,128},{192,224},{224,1... | collective-permute-start | bytes 3145736 | tf_op jit(solution)/shard_map/ppermute | solution.py:352
  72.1 9.5 %collective-permute-start.10 = (bf16[32,2,16,128]{3,2,1,0:T(8,128)(2,1)S(1)}, bf16[32,2,16,128]{3,2,1,0:T(8,128)(2,1)S(1)}, u32[]{:S(2)}, u32[]{:S(2)}) collective-permute-start(bf16[32,2,16,128]{3,2,1,0:T(8,128)(2,1)S(1)} %get-tuple-element.44), channel_id=1, source_target_pairs={{0,64},{32,96},{64,128},{96,160},{128,192},{160,224},{192,0},{224,... | collective-permute-start | bytes 786440 | tf_op jit(solution)/shard_map/ppermute | solution.py:362
  72.6 15.2 %collective-permute-start.11 = (bf16[32,2,16,128]{3,2,1,0:T(8,128)(2,1)S(1)}, bf16[32,2,16,128]{3,2,1,0:T(8,128)(2,1)S(1)}, u32[]{:S(2)}, u32[]{:S(2)}) collective-permute-start(bf16[32,2,16,128]{3,2,1,0:T(8,128)(2,1)S(1)} %get-tuple-element.49), channel_id=1, source_target_pairs={{0,128},{32,160},{64,192},{96,224},{128,0},{160,32},{192,64},{224,... | collective-permute-start | bytes 786440 | tf_op jit(solution)/shard_map/ppermute | solution.py:362
  75.5 12.4 %collective-permute-start.12 = (bf16[32,2,16,128]{3,2,1,0:T(8,128)(2,1)S(1)}, bf16[32,2,16,128]{3,2,1,0:T(8,128)(2,1)S(1)}, u32[]{:S(2)}, u32[]{:S(2)}) collective-permute-start(bf16[32,2,16,128]{3,2,1,0:T(8,128)(2,1)S(1)} %get-tuple-element.48), channel_id=1, source_target_pairs={{0,192},{32,224},{64,0},{96,32},{128,64},{160,96},{192,128},{224,1... | collective-permute-start | bytes 786440 | tf_op jit(solution)/shard_map/ppermute | solution.py:362
  (1 other events, 0.7 us)

commit v8 on v7

--- a/solution.py
+++ b/solution.py
@@ -17,34 +17,69 @@
     return pltpu.CompilerParams(vmem_limit_bytes=mebibytes * 1024 * 1024)
 
 
-def pick_kernel(place_ref, screened_ref, out_ref, piece_ref, sems):
-    place = place_ref[0]
+def pick_kernel(place_ref, freq_ref, shifts_ref, screened_ref, *refs):
+    count = len(refs) - 2
+    outs, piece_ref, sems = refs[:count], refs[count], refs[count + 1]
+    place, freq = place_ref[0], freq_ref[0]
     row, column = place // DEPTH, place % DEPTH
-    odd = column % 2
-    slab = out_ref.shape[3] // 4
+    slab = outs[0].shape[2] // 4
     copies = []
-    for f in range(out_ref.shape[0]):
-        far = lax.rem(column + jnp.where(odd == 1, SHIFTS[1][f], SHIFTS[0][f]), DEPTH)
+    for r in range(count):
+        target = lax.rem(freq // 2 + r // 2, count // 2) * 2 + lax.rem(freq + r, 2)
+        far = lax.rem(column + shifts_ref[lax.rem(column, 2) * count + target], DEPTH)
         for i in range(4):
             start = (lax.rem(row + i, 4) * DEPTH + far) * slab
-            piece_ref[f, :, :, i * slab : (i + 1) * slab] = screened_ref[:, :, pl.ds(pl.multiple_of(start, slab), slab)]
-        copies.append(pltpu.make_async_copy(piece_ref.at[f], out_ref.at[f], sems.at[f]))
+            piece_ref[r, :, :, i * slab : (i + 1) * slab] = screened_ref[:, :, pl.ds(pl.multiple_of(start, slab), slab)]
+        copies.append(pltpu.make_async_copy(piece_ref.at[r], outs[r], sems.at[r]))
         copies[-1].start()
     for copy in copies:
         copy.wait()
 
 
-def pick(place, screened, freqs):
+def pick(place, freq, screened, freqs):
     local, rows, width = screened.shape
-    shape = (freqs, local, rows, width // freqs)
+    shape = (local, rows, width // freqs)
+    shifts = jnp.array(SHIFTS, dtype=jnp.int32).reshape(2 * freqs)
     return pl.pallas_call(
         pick_kernel,
-        out_shape=jax.ShapeDtypeStruct(shape, screened.dtype),
-        in_specs=[pl.BlockSpec(memory_space=pltpu.SMEM), WHOLE],
-        out_specs=pl.BlockSpec(memory_space=pl.ANY),
-        scratch_shapes=[pltpu.VMEM(shape, screened.dtype), pltpu.SemaphoreType.DMA((freqs,))],
+        out_shape=[jax.ShapeDtypeStruct(shape, screened.dtype)] * freqs,
+        in_specs=[pl.BlockSpec(memory_space=pltpu.SMEM)] * 3 + [WHOLE],
+        out_specs=[pl.BlockSpec(memory_space=pl.ANY)] * freqs,
+        scratch_shapes=[pltpu.VMEM((freqs, *shape), screened.dtype), pltpu.SemaphoreType.DMA((freqs,))],
         compiler_params=params(16),
-    )(place, screened)
+    )(place, freq, shifts, screened)
+
+
+def dense_kernel(owners_ref, ids_ref, counts_ref, values_ref, out_ref):
+    blocks, orbitals, _ = out_ref.shape
+    aux, slots = owners_ref.shape[0], ids_ref.shape[1]
+    inner, block_width = orbitals // aux, orbitals // slots
+    row = lax.broadcasted_iota(jnp.int32, (orbitals, 128), 0)
+    owned = jnp.zeros((orbitals, 128), jnp.int32)
+    for g in range(aux):
+        owned = jnp.where(row // inner == owners_ref[g], g, owned)
+    wanted = (owned * inner + row % inner)[:, :1]
+    lane = lax.broadcasted_iota(jnp.int32, (8, orbitals), 1)
+    for block in range(blocks):
+        listed = jnp.full((8, orbitals), -1, jnp.int32)
+        for s in range(slots):
+            used = (lane // block_width == s) & (s < counts_ref[block])
+            listed = jnp.where(used, ids_ref[block, s] * block_width + lane % block_width, listed)
+        choose = jnp.where(wanted == listed[:1], 1.0, 0.0).astype(jnp.bfloat16)
+        out_ref[block] = lax.dot_general(
+            choose, values_ref[block], (((1,), (1,)), ((), ())), preferred_element_type=jnp.float32
+        ).astype(jnp.bfloat16)
+
+
+def expand(owners, block_ids, block_counts, values):
+    blocks, rows, orbitals = values.shape
+    return pl.pallas_call(
+        dense_kernel,
+        out_shape=jax.ShapeDtypeStruct((blocks, orbitals, rows), jnp.bfloat16),
+        in_specs=[pl.BlockSpec(memory_space=pltpu.SMEM)] * 3 + [WHOLE],
+        out_specs=WHOLE,
+        compiler_params=params(16),
+    )(owners, block_ids, block_counts, values)
 
 
 def spread_kernel(table_ref, out_ref):
@@ -81,7 +116,8 @@
     mix = mix_ref[...].reshape(4 * tall, sources * local * BAND)
     for band in range(bands):
         if band % 2 == 0:
-            pieces_at[band // 2].wait()
+            for copy in pieces_at[band // 2]:
+                copy.wait()
         piece = pieces_ref[:, :, band * BAND : (band + 1) * BAND, :].reshape(sources * local * BAND, width)
         both = jnp.dot(mix, piece, preferred_element_type=jnp.float32)
         for half in range(2):
@@ -92,7 +128,7 @@
                 timed_ref[half, place, band * pair : (band + 1) * pair, :] = mixed[place * pair : (place + 1) * pair]
 
 
-def run_jobs(jobs, part, timed_ref, gains_ref, dense_ref, dense_at, state_ref, scaled_ref, totals, outs):
+def run_jobs(jobs, part, timed_ref, gains_ref, dense_ref, state_ref, scaled_ref, totals, outs):
     span = state_ref.shape[1]
     blocks = dense_ref.shape[0]
     deep = scaled_ref.shape[0] // blocks
@@ -103,7 +139,7 @@
     owners, inner, targets = outs[0].shape[1], outs[0].shape[3], outs[0].shape[4]
     pair = 2 * targets
 
-    for number, ((half, first, count), total_ref, out_ref) in enumerate(zip(jobs, totals, outs)):
+    for (half, first, count), total_ref, out_ref in zip(jobs, totals, outs):
         timed = timed_ref[half, first : first + count].reshape(count * tall, depth)
 
         def states(step, carry):
@@ -127,13 +163,11 @@
             return carry
 
         lax.fori_loop(0, span // pair, states, 0)
-        if number == 0:
-            dense_at.wait()
         for place in range(count):
             columns = slice(place * pair, (place + 1) * pair)
             value = sum(
                 jnp.dot(
-                    dense_ref[block],
+                    dense_ref[block, :, part * deep : (part + 1) * deep],
                     scaled_ref[block * deep : (block + 1) * deep, columns],
                     preferred_element_type=jnp.float32,
                 )
@@ -146,53 +180,43 @@
                 out_ref[place, :, time, :, :] = piece.astype(out_ref.dtype)
 
 
-def first_kernel(jobs, *refs):
-    pieces_in, mix_ref, gains_ref, dense_in = refs[:4]
-    slabs, refs = refs[4:8], refs[8:]
+def first_kernel(jobs, sources, *refs):
+    pieces, refs = refs[:sources], refs[sources:]
+    mix_ref, gains_ref, dense_ref = refs[:3]
+    slabs, refs = refs[3:7], refs[7:]
     timed_ref, outs = refs[0], refs[1 : 1 + len(jobs)]
-    pieces_ref, state_ref, scaled_ref, dense_ref, pieces_sem, slab_sem, dense_sem = refs[1 + len(jobs) :]
-    deep = dense_ref.shape[2]
+    pieces_ref, state_ref, scaled_ref, pieces_sem, slab_sem = refs[1 + len(jobs) :]
     pieces_at = []
     for i in range(pieces_sem.shape[0]):
         rows = pl.ds(i * 2 * BAND, 2 * BAND)
-        pieces_at.append(pltpu.make_async_copy(pieces_in.at[:, :, rows], pieces_ref.at[:, :, rows], pieces_sem.at[i]))
-        pieces_at[-1].start()
-    slabs_at = slab_copies(slabs, state_ref, slab_sem)
-    dense_at = pltpu.make_async_copy(dense_in.at[:, :, pl.ds(0, deep)], dense_ref, dense_sem.at[0])
-    dense_at.start()
+        copies = []
+        for r in range(sources):
+            copies.append(
+                pltpu.make_async_copy(pieces[r].at[:, rows], pieces_ref.at[r, :, rows], pieces_sem.at[i, r])
+            )
+            copies[-1].start()
+        pieces_at.append(copies)
+    slab = slabs[0].shape[0]
+    slabs_at = []
+    for i in range(4):
+        slabs_at.append(pltpu.make_async_copy(slabs[i], state_ref.at[pl.ds(i * slab, slab)], slab_sem.at[i]))
+        slabs_at[-1].start()
     mix_bands(pieces_ref, pieces_at, mix_ref, timed_ref)
     for copy in slabs_at:
         copy.wait()
-    run_jobs(
-        jobs, 0, timed_ref, gains_ref, dense_ref, dense_at, state_ref, scaled_ref, (None,) * len(jobs), outs
-    )
-
-
-def slab_copies(slabs, state_ref, slab_sem):
-    slab = slabs[0].shape[0]
-    copies = []
-    for i in range(4):
-        copies.append(pltpu.make_async_copy(slabs[i], state_ref.at[pl.ds(i * slab, slab)], slab_sem.at[i]))
-        copies[-1].start()
-    return copies
+    run_jobs(jobs, 0, timed_ref, gains_ref, dense_ref, state_ref, scaled_ref, (None,) * len(jobs), outs)
 
 
 def last_kernel(job, gather, *refs):
-    timed_ref, gains_ref, dense_in, total_ref = refs[:4]
+    timed_ref, gains_ref, dense_ref, total_ref = refs[:4]
     if gather:
-        slabs, (out_ref, state_ref, scaled_ref, dense_ref, dense_sem, slab_sem) = refs[4:8], refs[8:]
-        slabs_at = slab_copies(slabs, state_ref, slab_sem)
+        slabs, (out_ref, state_ref, scaled_ref) = refs[4:8], refs[8:]
+        slab = slabs[0].shape[0]
+        for i in range(4):
+            state_ref[i * slab : (i + 1) * slab, :] = slabs[i][...]
     else:
-        state_ref, out_ref, scaled_ref, dense_ref, dense_sem = refs[4:]
-    deep = dense_ref.shape[2]
-    dense_at = pltpu.make_async_copy(dense_in.at[:, :, pl.ds(deep, deep)], dense_ref, dense_sem.at[0])
-    dense_at.start()
-    if gather:
-        for copy in slabs_at:
-            copy.wait()
-    run_jobs(
-        (job,), 1, timed_ref, gains_ref, dense_ref, dense_at, state_ref, scaled_ref, (total_ref,), (out_ref,)
-    )
+        state_ref, out_ref, scaled_ref = refs[4:]
+    run_jobs((job,), 1, timed_ref, gains_ref, dense_ref, state_ref, scaled_ref, (total_ref,), (out_ref,))
 
 
 AWAY = pl.BlockSpec(memory_space=pl.ANY)
@@ -212,7 +236,7 @@
 
 
 def first_part(jobs, pieces, mix, gains, dense, slabs, owners):
-    sources, local, rows, width = pieces.shape
+    local, rows, width = pieces[0].shape
     slab, span = slabs[0].shape
     blocks = dense.shape[0]
     targets = gains.shape[2] // (blocks * dense.shape[2] // rows)
@@ -220,29 +244,27 @@
     depth = span // targets * rows
     wide = max(count for _, _, count in jobs)
     return pl.pallas_call(
-        functools.partial(first_kernel, jobs),
+        functools.partial(first_kernel, jobs, len(pieces)),
         out_shape=[jax.ShapeDtypeStruct((2, times // 2, 2 * rows, width), jnp.bfloat16)]
         + [sums_shape(count, dense, owners, targets, jnp.float32) for _, _, count in jobs],
-        in_specs=[AWAY, WHOLE, WHOLE, AWAY] + [AWAY] * 4,
+        in_specs=[AWAY] * len(pieces) + [WHOLE] * 3 + [AWAY] * 4,
         out_specs=[WHOLE] * (1 + len(jobs)),
         scratch_shapes=[
-            pltpu.VMEM(pieces.shape, jnp.bfloat16),
+            pltpu.VMEM((len(pieces), local, rows, width), jnp.bfloat16),
             pltpu.VMEM((4 * slab, span), jnp.bfloat16),
             pltpu.VMEM((depth, wide * 2 * targets), jnp.bfloat16),
-            pltpu.VMEM((blocks, dense.shape[1], depth // blocks), jnp.bfloat16),
-            pltpu.SemaphoreType.DMA((rows // (2 * BAND),)),
+            pltpu.SemaphoreType.DMA((rows // (2 * BAND), len(pieces))),
             pltpu.SemaphoreType.DMA((4,)),
-            pltpu.SemaphoreType.DMA((1,)),
         ],
         compiler_params=params(),
         cost_estimate=cost(sum(count for _, _, count in jobs), rows, 4 * slab, span, dense, targets),
-    )(pieces, mix, gains, dense, *slabs)
+    )(*pieces, mix, gains, dense, *slabs)
 
 
 def last_part(job, timed, gains, dense, state, total, dtype, owners):
     gather = isinstance(state, list)
-    slabs = state if gather else []
-    span = slabs[0].shape[1] if gather else state.shape[1]
+    slabs = state if gather else [state]
+    span = slabs[0].shape[1]
     depth_in = timed.shape[3]
     rows = timed.shape[2] // 2
     blocks = dense.shape[0]
@@ -250,21 +272,15 @@
     depth = span // targets * rows
     count = job[2]
     out_shape = [sums_shape(count, dense, owners, targets, dtype)]
-    scratch = [
-        pltpu.VMEM((depth, count * 2 * targets), jnp.bfloat16),
-        pltpu.VMEM((blocks, dense.shape[1], depth // blocks), jnp.bfloat16),
-        pltpu.SemaphoreType.DMA((1,)),
-    ]
     if gather:
         out_shape.append(jax.ShapeDtypeStruct((depth_in, span), jnp.bfloat16))
-        scratch.append(pltpu.SemaphoreType.DMA((4,)))
-    operands = [timed, gains, dense, total] + (slabs if gather else [state])
+    operands = [timed, gains, dense, total, *slabs]
     return pl.pallas_call(
         functools.partial(last_kernel, job, gather),
         out_shape=out_shape,
-        in_specs=[WHOLE, WHOLE, AWAY, WHOLE] + ([AWAY] * 4 if gather else [WHOLE]),
+        in_specs=[WHOLE] * len(operands),
         out_specs=[WHOLE] * len(out_shape),
-        scratch_shapes=scratch,
+        scratch_shapes=[pltpu.VMEM((depth, count * 2 * targets), jnp.bfloat16)],
         compiler_params=params(),
         cost_estimate=cost(count, rows, depth_in, span, dense, targets),
     )(*operands)
@@ -299,9 +315,9 @@
         for i in range(height)
     ]
     flat_state = three_state.reshape(rows, states * targets)
-    flat_state, screened = lax.optimization_barrier((flat_state, screened))
     span = states * targets // 2
     first, second = (flat_state[:, part * span : (part + 1) * span] for part in range(2))
+    first, second, screened = lax.optimization_barrier((first, second, screened))
     own = lax.ppermute(first, ("freq", "aux"), along)
     far = lax.ppermute(second, "aux", across[2])
     own, far = lax.optimization_barrier((own, far))
@@ -314,21 +330,16 @@
         ready, slabs[0][i] = lax.optimization_barrier((own, slabs[0][i]))
         slabs[1][i] = lax.ppermute(ready, "aux", across[i])
 
-    device = jnp.arange(aux_count, dtype=jnp.int32)
-    owned = jnp.sum(jnp.where(owners[None, :] == device[:, None], device[None, :], 0), axis=1)
-    inner = orbitals // aux_count
-    wanted = (owned[:, None] * inner + jnp.arange(inner, dtype=jnp.int32)[None, :]).reshape(orbitals)
-    slot = jnp.arange(slot_count, dtype=jnp.int32)
-    listed = block_ids[:, :, None] * block_width + jnp.arange(block_width, dtype=jnp.int32)
-    listed = jnp.where(slot[None, :, None] < block_counts[:, None, None], listed, -1).reshape(block_count, orbitals)
-    choose = (wanted[None, :, None] == listed[:, None, :]).astype(jnp.bfloat16)
     _, three_orbital = lax.optimization_barrier((slabs[0][1], three_orbital))
     values = three_orbital.reshape(block_count, row_block, states, orbitals)
     values = values.transpose(0, 2, 1, 3).reshape(block_count, states * row_block, orbitals)
-    dense = jnp.einsum("bns,brs->bnr", choose, values, preferred_element_type=jnp.float32).astype(jnp.bfloat16)
+    dense = expand(owners, block_ids, block_counts, values)
+
     place = lax.axis_index("aux").astype(jnp.int32).reshape(1)
-    pieces = pick(place, screened, freq_count)
-    pieces = lax.all_to_all(pieces, "freq", split_axis=0, concat_axis=0, tiled=True)
+    pieces = list(pick(place, freq.astype(jnp.int32).reshape(1), screened, freq_count))
+    for r in (2, 6, 4, 5, 3, 7, 1):
+        moves = [(f, (f // 2 + r // 2) % chips * 2 + (f + r) % 2) for f in range(freq_count)]
+        pieces[r] = lax.ppermute(pieces[r], "freq", moves)
 
     half = jnp.arange(2, dtype=jnp.int32)[:, None, None]
     other = jnp.arange(chips, dtype=jnp.int32)[None, :, None]
@@ -336,8 +347,11 @@
     time = ((chip + other) % chips) * 2 * local_times + ((core + 1 + half) % 2) * local_times + step
     time = time.reshape(2, chips * local_times)
     freqs = jnp.arange(total_times, dtype=jnp.int32)
-    lanes = jnp.arange(total_times * BAND, dtype=jnp.int32) // BAND
-    weights = jnp.repeat(grid_weights, BAND)
+    lane = jnp.arange(total_times * BAND, dtype=jnp.int32) // BAND
+    away = lane // local_times
+    source = (chip + chips - away // 2) % chips * 2 + (core + away) % 2
+    lanes = source * local_times + lane % local_times
+    weights = jnp.sum(jnp.where(lanes[:, None] == freqs, grid_weights, 0.0), axis=1)
     table = weights * jnp.cos(
         jnp.pi * (time[:, :, None].astype(jnp.float32) + 0.5) * lanes.astype(jnp.float32) / total_times
     )

time: 109 us -> 111 us (1.018)
  local copies, waits for them, and re-layouts: 13.4 us -> 6.05 us
  waiting for transfers between devices: 17 us -> 23.7 us
  starting transfers between devices: 32.6 us -> 37.5 us
  other arithmetic: 3.58 us -> 1.62 us
  Pallas kernels: 20.5 us -> 22.4 us
  matrix products: 1.3 us -> 0 us
    ppermute x0 -> x7, starting transfers between devices: none -> 17.7 us  [shards(): pieces[r] = lax.ppermute(pieces[r], 'freq', moves)]
    all_to_all x1 -> x0, starting transfers between devices: 11.1 us -> none  [shards(): lax.all_to_all(pieces, 'freq', split_axis=0, concat_axis=0, tiled=True)]
    ppermute x0 -> x7, waiting for transfers between devices: none -> 8.21 us  [shards(): pieces[r] = lax.ppermute(pieces[r], 'freq', moves)]
    add x5 -> x0, local copies, waits for them, and re-layouts: 5.25 us -> none  [the longest x4 4.59 us: shards(): block_ids[:, :, None] * block_width]
    pallas_call x2 -> x3, Pallas kernels: 11.7 us -> 15 us  [the longest x1 11 us: first_part(): pl.pallas_call(functools.partial(first_kernel, jobs, len(pieces)), out_sh...]
    ppermute x1, starting transfers between devices: 3.34 us -> 0.19 us  [shards(): taken = lax.ppermute(given, 'freq', swap)]
    reshape x0 -> x1, local copies, waits for them, and re-layouts: none -> 2.77 us  [shards(): values = three_orbital.reshape(block_count, row_block, states, orbitals)]
    broadcast_in_dim x3 -> x0, local copies, waits for them, and re-layouts: 2.73 us -> none  [the longest x2 2.66 us: shards(): jnp.where(slot[None, :, None] < block_counts[:, None, None], listed, -1)]
  transfers between devices with their start and end apart: 14 -> 20, of which waited for: 4 -> 6; matrix products, arithmetic and copies ran while one was open for 12% -> 3% of each run, Pallas kernels for 15% -> 17%
where the time goes in v8:
time: 111 us
  starting transfers between devices  37.5 us (34%)
  waiting for transfers between devices  23.7 us (21%)
  Pallas kernels  22.4 us (20%)
  blocking collectives  19.4 us (17%)
  local copies, waits for them, and re-layouts  6.05 us (5%)
  other arithmetic  1.62 us (1%)
    all_to_all x1, blocking collectives, shards(): lax.all_to_all(summed.astype(jnp.bfloat16), 'aux', split_axis=0, concat_a...  19.4 us
    ppermute x7, starting transfers between devices, shards(): pieces[r] = lax.ppermute(pieces[r], 'freq', moves)  17.7 us
    pallas_call x1, Pallas kernels, first_part(): pl.pallas_call(functools.partial(first_kernel, jobs, len(pieces)), out_sh...  11 us
    ppermute x3, waiting for transfers between devices, shards(): lax.ppermute(sent[i], 'freq', chip_shift(i + 1))  8.96 us
    ppermute x7, waiting for transfers between devices, shards(): pieces[r] = lax.ppermute(pieces[r], 'freq', moves)  8.21 us
    pallas_call x3, Pallas kernels, last_part(): pl.pallas_call(functools.partial(last_kernel, job, gather), out_shape=out...  7.36 us
    ppermute x3, waiting for transfers between devices, shards(): lax.ppermute(own, 'aux', across[i])  6.53 us
    ppermute x3, starting transfers between devices, shards(): lax.ppermute(sent[i], 'freq', chip_shift(i + 1))  5.87 us
  transfers between devices with their start and end apart: 20, of which 6 were waited for; matrix products, arithmetic and copies ran while one was open for 3% of the time, Pallas kernels for 17%

profile of v8, /device:TPU:32, one launch (start us, length us, event | category | flops | bytes accessed | tf_op | source)
XLA Modules:
  0.0 110.9 jit_solution(6266583358654270977)
XLA Ops:
  2.2 3.2 %collective-permute-start.8 = (bf16[128,1024]{1,0:T(8,128)(2,1)}, bf16[128,1024]{1,0:T(8,128)(2,1)}, u32[]{:S(2)}, u32[]{:S(2)}) collective-permute-start(bf16[128,1024]{1,0:T(8,128)(2,1)} %get-tuple-element.47), channel_id=1, source_target_pairs={{16,0},{17,1},{18,2},{19,3},{20,4},{21,5},{22,6},{23,7},{24,8},{25... | collective-permute-start | bytes 786440 | tf_op jit(solution)/shard_map/ppermute | solution.py:322
  5.4 1.6 %collective-permute-start.7 = (bf16[128,1024]{1,0:T(8,128)(2,1)}, bf16[128,1024]{1,0:T(8,128)(2,1)S(1)}, u32[]{:S(2)}, u32[]{:S(2)}) collective-permute-start(bf16[128,1024]{1,0:T(8,128)(2,1)} %get-tuple-element.44), channel_id=1, source_target_pairs={{0,0},{1,1},{2,2},{3,3},{4,4},{5,5},{6,6},{7,7},{8,8},{9,9},{10,10... | collective-permute-start | bytes 786440 | tf_op jit(solution)/shard_map/ppermute | solution.py:321
  7.0 1.7 %shard_map.91 = (bf16[2,128,512]{2,1,0:T(8,128)(2,1)S(1)}, bf16[2,128,512]{2,1,0:T(8,128)(2,1)}, bf16[2,128,512]{2,1,0:T(8,128)(2,1)}, bf16[2,128,512]{2,1,0:T(8...) custom-call(s32[1]{0:T(128)} %bitcast.place_ref, ...), custom_call_target="tpu_custom_call" | custom-call | tf_op jit(solution)/shard_map/pallas_call | solution.py:43
  9.4 5.9 %collective-permute-start = (bf16[2,128,512]{2,1,0:T(8,128)(2,1)}, bf16[2,128,512]{2,1,0:T(8,128)(2,1)S(1)}, u32[]{:S(2)}, u32[]{:S(2)}) collective-permute-start(bf16[2,128,512]{2,1,0:T(8,128)(2,1)} %get-tuple-element.36), channel_id=1, source_target_pairs={{0,32},{32,0},{64,96},{96,64},{128,160},{160,128},{192,224},{224,1... | collective-permute-start | bytes 786440 | tf_op jit(solution)/shard_map/ppermute | solution.py:342
  15.3 1.8 %collective-permute-start.1 = (bf16[2,128,512]{2,1,0:T(8,128)(2,1)}, bf16[2,128,512]{2,1,0:T(8,128)(2,1)S(1)}, u32[]{:S(2)}, u32[]{:S(2)}) collective-permute-start(bf16[2,128,512]{2,1,0:T(8,128)(2,1)} %get-tuple-element.37), channel_id=1, source_target_pairs={{0,64},{32,96},{64,128},{96,160},{128,192},{160,224},{192,0},{224,... | collective-permute-start | bytes 786440 | tf_op jit(solution)/shard_map/ppermute | solution.py:342
  20.8 6.5 %collective-permute-done.9.refs_12_ = bf16[128,1024]{1,0:T(8,128)(2,1)S(1)} collective-permute-done((bf16[128,1024]{1,0:T(8,128)(2,1)S(1)}, bf16[128,1024]{1,0:T(8,128)(2,1)S(1)}, u32[]{:S(2)}, u32[]{:S(2)}) %collective-permute-start.9) | collective-permute-done | bytes 262176 | tf_op jit(solution)/shard_map/ppermute | solution.py:324
  27.3 1.6 %collective-permute-start.10 = (bf16[128,1024]{1,0:T(8,128)(2,1)}, bf16[128,1024]{1,0:T(8,128)(2,1)S(1)}, u32[]{:S(2)}, u32[]{:S(2)}) collective-permute-start(bf16[128,1024]{1,0:T(8,128)(2,1)} %get-tuple-element.47), channel_id=1, source_target_pairs={{0,0},{1,1},{2,2},{3,3},{4,4},{5,5},{6,6},{7,7},{8,8},{9,9},{10,10... | collective-permute-start | bytes 786440 | tf_op jit(solution)/shard_map/ppermute | solution.py:326
  29.2 5.5 %collective-permute-start.3 = (bf16[2,128,512]{2,1,0:T(8,128)(2,1)}, bf16[2,128,512]{2,1,0:T(8,128)(2,1)S(1)}, u32[]{:S(2)}, u32[]{:S(2)}) collective-permute-start(bf16[2,128,512]{2,1,0:T(8,128)(2,1)} %copy-done.5), channel_id=1, source_target_pairs={{0,128},{32,160},{64,192},{96,224},{128,0},{160,32},{192,64},{224,... | collective-permute-start | bytes 786440 | tf_op jit(solution)/shard_map/ppermute | solution.py:342
  35.6 2.7 %collective-permute-start.5 = (bf16[2,128,512]{2,1,0:T(8,128)(2,1)S(1)}, bf16[2,128,512]{2,1,0:T(8,128)(2,1)S(1)}, u32[]{:S(2)}, u32[]{:S(2)}) collective-permute-start(bf16[2,128,512]{2,1,0:T(8,128)(2,1)S(1)} %get-tuple-element.41), channel_id=1, source_target_pairs={{0,192},{32,224},{64,0},{96,32},{128,64},{160,96},{192,128},{224,1... | collective-permute-start | bytes 786440 | tf_op jit(solution)/shard_map/ppermute | solution.py:342
  39.1 2.8 %copy.13 = bf16[2,64,16,512]{3,1,2,0:T(8,128)(2,1)S(1)} copy(bf16[2,64,16,512]{3,2,1,0:T(8,128)(2,1)} %bitcast.27) | data formatting | bytes 4194304 | tf_op jit(solution)/shard_map/reshape | solution.py:334
  41.9 2.3 %shard_map.93.refs_10_.refs_2_ = bf16[2,512,1024]{2,1,0:T(8,128)(2,1)S(1)} custom-call(s32[32]{0:T(128)S(1)} %copy-done.3, s32[2,8]{1,0:T(2,128)S(1)} %copy-done.1, s32[2]{0:T(128)S(1)} %copy-done.4, bf16[2,1024,512]{2,1,0:T(8,128)(2,1)S(1)} %bitcast.26), custom_call_target="tpu_custom_call" | custom-call | tf_op jit(solution)/shard_map/pallas_call | solution.py:76
  44.3 1.6 %collective-permute-start.14 = (bf16[128,1024]{1,0:T(8,128)(2,1)}, bf16[128,1024]{1,0:T(8,128)(2,1)S(1)}, u32[]{:S(2)}, u32[]{:S(2)}) collective-permute-start(bf16[128,1024]{1,0:T(8,128)(2,1)} %collective-permute-done.8), channel_id=1, source_target_pairs={{0,0},{1,1},{2,2},{3,3},{4,4},{5,5},{6,6},{7,7},{8,8},{9,9},{10,10... | collective-permute-start | bytes 786440 | tf_op jit(solution)/shard_map/ppermute | solution.py:327
  45.9 1.8 %collective-permute-done.4.refs_5_ = bf16[2,128,512]{2,1,0:T(8,128)(2,1)S(1)} collective-permute-done((bf16[2,128,512]{2,1,0:T(8,128)(2,1)S(1)}, bf16[2,128,512]{2,1,0:T(8,128)(2,1)S(1)}, u32[]{:S(2)}, u32[]{:S(2)}) %collective-permute-start.4) | collective-permute-done | bytes 262176 | tf_op jit(solution)/shard_map/ppermute | solution.py:342
  47.7 2.3 %collective-permute-start.13 = (bf16[128,1024]{1,0:T(8,128)(2,1)S(1)}, bf16[128,1024]{1,0:T(8,128)(2,1)S(1)}, u32[]{:S(2)}, u32[]{:S(2)}) collective-permute-start(bf16[128,1024]{1,0:T(8,128)(2,1)S(1)} %collective-permute-done.10.refs_4_), channel_id=1, source_target_pairs={{8,0},{9,1},{10,2},{11,3},{12,4},{13,5},{14,6},{15,7},{16,8},{17,9... | collective-permute-start | bytes 786440 | tf_op jit(solution)/shard_map/ppermute | solution.py:331
  52.1 4.9 %collective-permute-done.6.refs_7_ = bf16[2,128,512]{2,1,0:T(8,128)(2,1)S(1)} collective-permute-done((bf16[2,128,512]{2,1,0:T(8,128)(2,1)S(1)}, bf16[2,128,512]{2,1,0:T(8,128)(2,1)S(1)}, u32[]{:S(2)}, u32[]{:S(2)}) %collective-permute-start.6) | collective-permute-done | bytes 262176 | tf_op jit(solution)/shard_map/ppermute | solution.py:342
  57.0 11.0 %shard_map.94 = (bf16[2,4,256,512]{3,2,1,0:T(8,128)(2,1)S(1)}, f32[4,32,2,16,128]{4,3,2,1,0:T(8,128)S(1)}, f32[3,32,2,16,128]{4,3,2,1,0:T(8,128)S(1)}, f32[1,32,2,16,128]{4,3,2,1,0:T(8,128)S(1)}) custom-call(bf16[2,128,512]{2,1,0:T(8,128)(2,1)S(1)} %get-tuple-element.35.refs_0_, bf16[2,128,512]{2,1,0:T(8,128)(2,1)S(1)} %collective-permute-done.refs_1_, ...), custom_call_target="tpu_custom_call" | custom-call | flops 4294967296 | bytes 16777216 | tf_op jit(solution)/shard_map/pallas_call | solution.py:246
  68.1 3.3 %shard_map.95 = (bf16[4,32,2,16,128]{4,3,2,1,0:T(8,128)(2,1)S(1)}, bf16[512,1024]{1,0:T(8,128)(2,1)S(1)}) custom-call(bf16[2,4,256,512]{3,2,1,0:T(8,128)(2,1)S(1)} %get-tuple-element.52.refs_0_, f32[2,8,2048]{2,1,0:T(8,128)S(1)} %broadcast_bitcast_fusion.refs_9_.refs_1_, bf16[2,512,1024]{2,1,0:T(8,128)(2,1)S(1)} %shard_map.93.refs_10_.refs_2_, ...), custom_call_target="tpu_custom_call" | custom-call | flops 2147483648 | bytes 8388608 | tf_op jit(solution)/shard_map/pallas_call | solution.py:278
  71.6 2.6 %shard_map.96 = f32[3,32,2,16,128]{4,3,2,1,0:T(8,128)S(1)} custom-call(bf16[2,4,256,512]{3,2,1,0:T(8,128)(2,1)S(1)} %get-tuple-element.52.refs_0_, f32[2,8,2048]{2,1,0:T(8,128)S(1)} %broadcast_bitcast_fusion.refs_9_.refs_1_, bf16[2,512,1024]{2,1,0:T(8,128)(2,1)S(1)} %shard_map.93.refs_10_.refs_2_, f32[3,32,2,16,128]{4,3,2,1,0:T(8,128)S(1)} %get-tuple-element.54.refs_3_, ...), custom_call_target="tpu_custom_call" | custom-call | flops 1610612736 | bytes 6291456 | tf_op jit(solution)/shard_map/pallas_call | solution.py:278
  74.4 2.0 %collective-permute-start.17 = (bf16[32,2,16,128]{3,2,1,0:T(8,128)(2,1)S(1)}, bf16[32,2,16,128]{3,2,1,0:T(8,128)(2,1)S(1)}, u32[]{:S(2)}, u32[]{:S(2)}) collective-permute-start(bf16[32,2,16,128]{3,2,1,0:T(8,128)(2,1)S(1)} %get-tuple-element.62), channel_id=1, source_target_pairs={{0,64},{32,96},{64,128},{96,160},{128,192},{160,224},{192,0},{224,... | collective-permute-start | bytes 786440 | tf_op jit(solution)/shard_map/ppermute | solution.py:376
  76.4 2.2 %collective-permute-start.18 = (bf16[32,2,16,128]{3,2,1,0:T(8,128)(2,1)S(1)}, bf16[32,2,16,128]{3,2,1,0:T(8,128)(2,1)S(1)}, u32[]{:S(2)}, u32[]{:S(2)}) collective-permute-start(bf16[32,2,16,128]{3,2,1,0:T(8,128)(2,1)S(1)} %get-tuple-element.67), channel_id=1, source_target_pairs={{0,128},{32,160},{64,192},{96,224},{128,0},{160,32},{192,64},{224,... | collective-permute-start | bytes 786440 | tf_op jit(solution)/shard_map/ppermute | solution.py:376
  78.6 1.7 %collective-permute-start.19 = (bf16[32,2,16,128]{3,2,1,0:T(8,128)(2,1)S(1)}, bf16[32,2,16,128]{3,2,1,0:T(8,128)(2,1)S(1)}, u32[]{:S(2)}, u32[]{:S(2)}) collective-permute-start(bf16[32,2,16,128]{3,2,1,0:T(8,128)(2,1)S(1)} %get-tuple-element.66), channel_id=1, source_target_pairs={{0,192},{32,224},{64,0},{96,32},{128,64},{160,96},{192,128},{224,1... | collective-permute-start | bytes 786440 | tf_op jit(solution)/shard_map/ppermute | solution.py:376
  81.8 2.6 %collective-permute-done.17 = bf16[32,2,16,128]{3,2,1,0:T(8,128)(2,1)S(1)} collective-permute-done((bf16[32,2,16,128]{3,2,1,0:T(8,128)(2,1)S(1)}, bf16[32,2,16,128]{3,2,1,0:T(8,128)(2,1)S(1)}, u32[]{:S(2)}, u32[]{:S(2)}) %collective-permute-start.17) | collective-permute-done | bytes 262176 | tf_op jit(solution)/shard_map/ppermute | solution.py:376
  84.4 6.4 %collective-permute-done.18 = bf16[32,2,16,128]{3,2,1,0:T(8,128)(2,1)S(1)} collective-permute-done((bf16[32,2,16,128]{3,2,1,0:T(8,128)(2,1)S(1)}, bf16[32,2,16,128]{3,2,1,0:T(8,128)(2,1)S(1)}, u32[]{:S(2)}, u32[]{:S(2)}) %collective-permute-start.18) | collective-permute-done | bytes 262176 | tf_op jit(solution)/shard_map/ppermute | solution.py:376
  90.9 19.4 %all_to_all.5 = bf16[32,2,16,128]{3,2,1,0:T(8,128)(2,1)S(1)} all-to-all(bf16[32,2,16,128]{3,2,1,0:T(8,128)(2,1)S(1)} %fusion.5), channel_id=1, replica_groups=mesh['freq'=8,'aux'=32] {'aux'}, dimensions={0} | all-to-all | bytes 524288 | tf_op jit(solution)/shard_map/all_to_all | solution.py:381
  (61 shorter events, 13.4 us)
Async XLA Ops:
  0.0 7.0 %copy-start.2 = (s32[16]{0:T(128)S(1)}, s32[16]{0:T(128)}, u32[]{:S(2)}) copy-start(s32[16]{0:T(128)} %constant.129.shifts_ref) | copy-start | bytes 196
  0.0 7.0 %copy-start = (bf16[2,128,4096]{2,1,0:T(8,128)(2,1)S(1)}, bf16[2,128,4096]{2,1,0:T(8,128)(2,1)}, u32[]{:S(2)}) copy-start(bf16[2,128,4096]{2,1,0:T(8,128)(2,1)} %screened_ref) | copy-start | bytes 6291460
  0.0 19.5 %copy-start.7 = (f32[16]{0:T(128)S(1)}, f32[16]{0:T(128)}, u32[]{:S(2)}) copy-start(f32[16]{0:T(128)} %param.10) | copy-start | bytes 196
  0.0 29.0 %copy-start.6 = (f32[16,16]{1,0:T(8,128)S(1)}, f32[16,16]{1,0:T(8,128)}, u32[]{:S(2)}) copy-start(f32[16,16]{1,0:T(8,128)} %param.11) | copy-start | bytes 3076
  2.2 16.2 %collective-permute-start.8 = (bf16[128,1024]{1,0:T(8,128)(2,1)}, bf16[128,1024]{1,0:T(8,128)(2,1)}, u32[]{:S(2)}, u32[]{:S(2)}) collective-permute-start(bf16[128,1024]{1,0:T(8,128)(2,1)} %get-tuple-element.47), channel_id=1, source_target_pairs={{16,0},{17,1},{18,2},{19,3},{20,4},{21,5},{22,6},{23,7},{24,8},{25... | collective-permute-start | bytes 786440 | tf_op jit(solution)/shard_map/ppermute | solution.py:322
  5.4 13.0 %collective-permute-start.7 = (bf16[128,1024]{1,0:T(8,128)(2,1)}, bf16[128,1024]{1,0:T(8,128)(2,1)S(1)}, u32[]{:S(2)}, u32[]{:S(2)}) collective-permute-start(bf16[128,1024]{1,0:T(8,128)(2,1)} %get-tuple-element.44), channel_id=1, source_target_pairs={{0,0},{1,1},{2,2},{3,3},{4,4},{5,5},{6,6},{7,7},{8,8},{9,9},{10,10... | collective-permute-start | bytes 786440 | tf_op jit(solution)/shard_map/ppermute | solution.py:321
  9.4 19.8 %collective-permute-start = (bf16[2,128,512]{2,1,0:T(8,128)(2,1)}, bf16[2,128,512]{2,1,0:T(8,128)(2,1)S(1)}, u32[]{:S(2)}, u32[]{:S(2)}) collective-permute-start(bf16[2,128,512]{2,1,0:T(8,128)(2,1)} %get-tuple-element.36), channel_id=1, source_target_pairs={{0,32},{32,0},{64,96},{96,64},{128,160},{160,128},{192,224},{224,1... | collective-permute-start | bytes 786440 | tf_op jit(solution)/shard_map/ppermute | solution.py:342
  15.3 19.4 %collective-permute-start.1 = (bf16[2,128,512]{2,1,0:T(8,128)(2,1)}, bf16[2,128,512]{2,1,0:T(8,128)(2,1)S(1)}, u32[]{:S(2)}, u32[]{:S(2)}) collective-permute-start(bf16[2,128,512]{2,1,0:T(8,128)(2,1)} %get-tuple-element.37), channel_id=1, source_target_pairs={{0,64},{32,96},{64,128},{96,160},{128,192},{160,224},{192,0},{224,... | collective-permute-start | bytes 786440 | tf_op jit(solution)/shard_map/ppermute | solution.py:342
  17.1 18.5 %collective-permute-start.2 = (bf16[2,128,512]{2,1,0:T(8,128)(2,1)}, bf16[2,128,512]{2,1,0:T(8,128)(2,1)S(1)}, u32[]{:S(2)}, u32[]{:S(2)}) collective-permute-start(bf16[2,128,512]{2,1,0:T(8,128)(2,1)} %get-tuple-element.38), channel_id=1, source_target_pairs={{0,96},{32,64},{64,160},{96,128},{128,224},{160,192},{192,32},{224... | collective-permute-start | bytes 786440 | tf_op jit(solution)/shard_map/ppermute | solution.py:342
  18.3 9.0 %collective-permute-start.9 = (bf16[128,1024]{1,0:T(8,128)(2,1)S(1)}, bf16[128,1024]{1,0:T(8,128)(2,1)S(1)}, u32[]{:S(2)}, u32[]{:S(2)}) collective-permute-start(bf16[128,1024]{1,0:T(8,128)(2,1)S(1)} %collective-permute-done.7.refs_11_), channel_id=1, source_target_pairs={{8,0},{9,1},{10,2},{11,3},{12,4},{13,5},{14,6},{15,7},{16,8},{17,9... | collective-permute-start | bytes 786440 | tf_op jit(solution)/shard_map/ppermute | solution.py:324
  19.7 18.6 %collective-permute-start.12 = (bf16[128,1024]{1,0:T(8,128)(2,1)S(1)}, bf16[128,1024]{1,0:T(8,128)(2,1)S(1)}, u32[]{:S(2)}, u32[]{:S(2)}) collective-permute-start(bf16[128,1024]{1,0:T(8,128)(2,1)S(1)} %collective-permute-done.7.refs_11_), channel_id=1, source_target_pairs={{24,0},{25,1},{26,2},{27,3},{28,4},{29,5},{30,6},{31,7},{0,8},{1,9... | collective-permute-start | bytes 786440 | tf_op jit(solution)/shard_map/ppermute | solution.py:324
  27.3 11.0 %collective-permute-start.10 = (bf16[128,1024]{1,0:T(8,128)(2,1)}, bf16[128,1024]{1,0:T(8,128)(2,1)S(1)}, u32[]{:S(2)}, u32[]{:S(2)}) collective-permute-start(bf16[128,1024]{1,0:T(8,128)(2,1)} %get-tuple-element.47), channel_id=1, source_target_pairs={{0,0},{1,1},{2,2},{3,3},{4,4},{5,5},{6,6},{7,7},{8,8},{9,9},{10,10... | collective-permute-start | bytes 786440 | tf_op jit(solution)/shard_map/ppermute | solution.py:326
  29.2 15.1 %collective-permute-start.3 = (bf16[2,128,512]{2,1,0:T(8,128)(2,1)}, bf16[2,128,512]{2,1,0:T(8,128)(2,1)S(1)}, u32[]{:S(2)}, u32[]{:S(2)}) collective-permute-start(bf16[2,128,512]{2,1,0:T(8,128)(2,1)} %copy-done.5), channel_id=1, source_target_pairs={{0,128},{32,160},{64,192},{96,224},{128,0},{160,32},{192,64},{224,... | collective-permute-start | bytes 786440 | tf_op jit(solution)/shard_map/ppermute | solution.py:342
  34.7 13.0 %collective-permute-start.4 = (bf16[2,128,512]{2,1,0:T(8,128)(2,1)S(1)}, bf16[2,128,512]{2,1,0:T(8,128)(2,1)S(1)}, u32[]{:S(2)}, u32[]{:S(2)}) collective-permute-start(bf16[2,128,512]{2,1,0:T(8,128)(2,1)S(1)} %get-tuple-element.40), channel_id=1, source_target_pairs={{0,160},{32,128},{64,224},{96,192},{128,32},{160,0},{192,96},{224,... | collective-permute-start | bytes 786440 | tf_op jit(solution)/shard_map/ppermute | solution.py:342
  35.6 15.8 %collective-permute-start.5 = (bf16[2,128,512]{2,1,0:T(8,128)(2,1)S(1)}, bf16[2,128,512]{2,1,0:T(8,128)(2,1)S(1)}, u32[]{:S(2)}, u32[]{:S(2)}) collective-permute-start(bf16[2,128,512]{2,1,0:T(8,128)(2,1)S(1)} %get-tuple-element.41), channel_id=1, source_target_pairs={{0,192},{32,224},{64,0},{96,32},{128,64},{160,96},{192,128},{224,1... | collective-permute-start | bytes 786440 | tf_op jit(solution)/shard_map/ppermute | solution.py:342
  38.3 18.7 %collective-permute-start.6 = (bf16[2,128,512]{2,1,0:T(8,128)(2,1)S(1)}, bf16[2,128,512]{2,1,0:T(8,128)(2,1)S(1)}, u32[]{:S(2)}, u32[]{:S(2)}) collective-permute-start(bf16[2,128,512]{2,1,0:T(8,128)(2,1)S(1)} %get-tuple-element.42), channel_id=1, source_target_pairs={{0,224},{32,192},{64,32},{96,0},{128,96},{160,64},{192,160},{224,1... | collective-permute-start | bytes 786440 | tf_op jit(solution)/shard_map/ppermute | solution.py:342
  38.3 18.7 %collective-permute-start.11 = (bf16[128,1024]{1,0:T(8,128)(2,1)S(1)}, bf16[128,1024]{1,0:T(8,128)(2,1)S(1)}, u32[]{:S(2)}, u32[]{:S(2)}) collective-permute-start(bf16[128,1024]{1,0:T(8,128)(2,1)S(1)} %collective-permute-done.7.refs_11_), channel_id=1, source_target_pairs={{16,0},{17,1},{18,2},{19,3},{20,4},{21,5},{22,6},{23,7},{24,8},{25... | collective-permute-start | bytes 786440 | tf_op jit(solution)/shard_map/ppermute | solution.py:324
  44.3 23.8 %collective-permute-start.14 = (bf16[128,1024]{1,0:T(8,128)(2,1)}, bf16[128,1024]{1,0:T(8,128)(2,1)S(1)}, u32[]{:S(2)}, u32[]{:S(2)}) collective-permute-start(bf16[128,1024]{1,0:T(8,128)(2,1)} %collective-permute-done.8), channel_id=1, source_target_pairs={{0,0},{1,1},{2,2},{3,3},{4,4},{5,5},{6,6},{7,7},{8,8},{9,9},{10,10... | collective-permute-start | bytes 786440 | tf_op jit(solution)/shard_map/ppermute | solution.py:327
  47.7 20.4 %collective-permute-start.13 = (bf16[128,1024]{1,0:T(8,128)(2,1)S(1)}, bf16[128,1024]{1,0:T(8,128)(2,1)S(1)}, u32[]{:S(2)}, u32[]{:S(2)}) collective-permute-start(bf16[128,1024]{1,0:T(8,128)(2,1)S(1)} %collective-permute-done.10.refs_4_), channel_id=1, source_target_pairs={{8,0},{9,1},{10,2},{11,3},{12,4},{13,5},{14,6},{15,7},{16,8},{17,9... | collective-permute-start | bytes 786440 | tf_op jit(solution)/shard_map/ppermute | solution.py:331
  51.4 16.7 %collective-permute-start.15 = (bf16[128,1024]{1,0:T(8,128)(2,1)S(1)}, bf16[128,1024]{1,0:T(8,128)(2,1)S(1)}, u32[]{:S(2)}, u32[]{:S(2)}) collective-permute-start(bf16[128,1024]{1,0:T(8,128)(2,1)S(1)} %collective-permute-done.10.refs_4_), channel_id=1, source_target_pairs={{24,0},{25,1},{26,2},{27,3},{28,4},{29,5},{30,6},{31,7},{0,8},{1,9... | collective-permute-start | bytes 786440 | tf_op jit(solution)/shard_map/ppermute | solution.py:331
  71.4 2.8 %collective-permute-start.16 = (bf16[4,32,2,16,128]{4,3,2,1,0:T(8,128)(2,1)S(1)}, bf16[4,32,2,16,128]{4,3,2,1,0:T(8,128)(2,1)S(1)}, u32[]{:S(2)}, u32[]{:S(2)}) collective-permute-start(bf16[4,32,2,16,128]{4,3,2,1,0:T(8,128)(2,1)S(1)} %get-tuple-element.60), channel_id=1, source_target_pairs={{0,32},{32,0},{64,96},{96,64},{128,160},{160,128},{192,224},{224,1... | collective-permute-start | bytes 3145736 | tf_op jit(solution)/shard_map/ppermute | solution.py:366
  74.4 9.9 %collective-permute-start.17 = (bf16[32,2,16,128]{3,2,1,0:T(8,128)(2,1)S(1)}, bf16[32,2,16,128]{3,2,1,0:T(8,128)(2,1)S(1)}, u32[]{:S(2)}, u32[]{:S(2)}) collective-permute-start(bf16[32,2,16,128]{3,2,1,0:T(8,128)(2,1)S(1)} %get-tuple-element.62), channel_id=1, source_target_pairs={{0,64},{32,96},{64,128},{96,160},{128,192},{160,224},{192,0},{224,... | collective-permute-start | bytes 786440 | tf_op jit(solution)/shard_map/ppermute | solution.py:376
  76.4 14.3 %collective-permute-start.18 = (bf16[32,2,16,128]{3,2,1,0:T(8,128)(2,1)S(1)}, bf16[32,2,16,128]{3,2,1,0:T(8,128)(2,1)S(1)}, u32[]{:S(2)}, u32[]{:S(2)}) collective-permute-start(bf16[32,2,16,128]{3,2,1,0:T(8,128)(2,1)S(1)} %get-tuple-element.67), channel_id=1, source_target_pairs={{0,128},{32,160},{64,192},{96,224},{128,0},{160,32},{192,64},{224,... | collective-permute-start | bytes 786440 | tf_op jit(solution)/shard_map/ppermute | solution.py:376
  78.6 12.1 %collective-permute-start.19 = (bf16[32,2,16,128]{3,2,1,0:T(8,128)(2,1)S(1)}, bf16[32,2,16,128]{3,2,1,0:T(8,128)(2,1)S(1)}, u32[]{:S(2)}, u32[]{:S(2)}) collective-permute-start(bf16[32,2,16,128]{3,2,1,0:T(8,128)(2,1)S(1)} %get-tuple-element.66), channel_id=1, source_target_pairs={{0,192},{32,224},{64,0},{96,32},{128,64},{160,96},{192,128},{224,1... | collective-permute-start | bytes 786440 | tf_op jit(solution)/shard_map/ppermute | solution.py:376
  (4 other events, 9.1 us)

commit v9 on v4

--- a/solution.py
+++ b/solution.py
@@ -10,38 +10,41 @@
 BAND = 16
 DEPTH = 8
 SHIFTS = ((0, 4, 3, 5, 2, 6, 1, 7), (0, 4, 1, 7, 2, 6, 3, 5))
+ORDER = (0, 2, 1, 3)
 WHOLE = pl.BlockSpec(memory_space=pltpu.VMEM)
 
 
-def params():
-    return pltpu.CompilerParams(vmem_limit_bytes=32 * 1024 * 1024)
-
-
-def pick_kernel(place_ref, screened_ref, out_ref):
+def params(mebibytes=32):
+    return pltpu.CompilerParams(vmem_limit_bytes=mebibytes * 1024 * 1024)
+
+
+def pick_kernel(place_ref, screened_ref, out_ref, piece_ref, sems):
     place = place_ref[0]
     row, column = place // DEPTH, place % DEPTH
     odd = column % 2
     slab = out_ref.shape[3] // 4
+    copies = []
     for f in range(out_ref.shape[0]):
         far = lax.rem(column + jnp.where(odd == 1, SHIFTS[1][f], SHIFTS[0][f]), DEPTH)
         for i in range(4):
             start = (lax.rem(row + i, 4) * DEPTH + far) * slab
-            out_ref[f, :, :, i * slab : (i + 1) * slab] = screened_ref[:, :, pl.ds(pl.multiple_of(start, slab), slab)]
+            piece_ref[f, :, :, i * slab : (i + 1) * slab] = screened_ref[:, :, pl.ds(pl.multiple_of(start, slab), slab)]
+        copies.append(pltpu.make_async_copy(piece_ref.at[f], out_ref.at[f], sems.at[f]))
+        copies[-1].start()
+    for copy in copies:
+        copy.wait()
 
 
 def pick(place, screened, freqs):
     local, rows, width = screened.shape
-    tall = rows // 4
+    shape = (freqs, local, rows, width // freqs)
     return pl.pallas_call(
         pick_kernel,
-        out_shape=jax.ShapeDtypeStruct((freqs, local, rows, width // freqs), screened.dtype),
-        grid_spec=pltpu.PrefetchScalarGridSpec(
-            num_scalar_prefetch=1,
-            grid=(rows // tall,),
-            in_specs=[pl.BlockSpec((local, tall, width), lambda i, place: (0, i, 0))],
-            out_specs=pl.BlockSpec((freqs, local, tall, width // freqs), lambda i, place: (0, 0, i, 0)),
-        ),
-        compiler_params=params(),
+        out_shape=jax.ShapeDtypeStruct(shape, screened.dtype),
+        in_specs=[pl.BlockSpec(memory_space=pltpu.SMEM), WHOLE],
+        out_specs=pl.BlockSpec(memory_space=pl.ANY),
+        scratch_shapes=[pltpu.VMEM(shape, screened.dtype), pltpu.SemaphoreType.DMA((freqs,))],
+        compiler_params=params(16),
     )(place, screened)
 
 
@@ -76,11 +79,14 @@
     places = out_ref.shape[1]
     pair = 2 * BAND
     tall = places * pair
+    mix = mix_ref[...].reshape(4 * tall, freqs * BAND)
     for band in range(rows // BAND):
         piece = pieces_ref[:, :, band * BAND : (band + 1) * BAND, :].reshape(freqs * BAND, width)
+        both = jnp.dot(mix, piece, preferred_element_type=jnp.float32)
         for half in range(2):
-            mixed = jnp.dot(mix_ref[half], piece, preferred_element_type=jnp.float32)
-            mixed = (mixed[:tall] + mixed[tall:]).astype(jnp.bfloat16)
+            upper = both[2 * half * tall : (2 * half + 1) * tall]
+            lower = both[(2 * half + 1) * tall : (2 * half + 2) * tall]
+            mixed = (upper + lower).astype(jnp.bfloat16)
             for place in range(places):
                 out_ref[half, place, band * pair : (band + 1) * pair, :] = mixed[place * pair : (place + 1) * pair]
 
@@ -101,9 +107,9 @@
     timed_ref, gains_ref, dense_ref = refs[:3]
     slabs = refs[3:7]
     refs = refs[7:]
-    totals = [None] * len(jobs)
+    totals = ()
     if has_total:
-        totals, refs = refs[: len(jobs)], refs[len(jobs) :]
+        totals, refs = refs[:2], refs[2:]
     outs, (state_ref, scaled_ref) = refs[: len(jobs)], refs[len(jobs) :]
     slab = slabs[0].shape[0]
     for i in range(4):
@@ -118,7 +124,7 @@
     owners, inner, targets = outs[0].shape[1], outs[0].shape[3], outs[0].shape[4]
     pair = 2 * targets
 
-    for (half, first, count), total_ref, out_ref in zip(jobs, totals, outs):
+    for (half, first, count), out_ref in zip(jobs, outs):
         timed = timed_ref[half, first : first + count].reshape(count * tall, depth)
 
         def states(step, carry):
@@ -155,7 +161,7 @@
             for time in range(2):
                 piece = value[:, time * targets : (time + 1) * targets].reshape(owners, inner, targets)
                 if has_total:
-                    piece = piece + total_ref[place, :, time, :, :]
+                    piece = piece + totals[half][first + place, :, time, :, :]
                 out_ref[place, :, time, :, :] = piece.astype(out_ref.dtype)
 
 
@@ -235,7 +241,7 @@
     pieces = lax.all_to_all(pieces, "freq", split_axis=0, concat_axis=0, tiled=True)
 
     half = jnp.arange(2, dtype=jnp.int32)[:, None, None]
-    other = jnp.arange(chips, dtype=jnp.int32)[None, :, None]
+    other = jnp.array(ORDER, dtype=jnp.int32)[None, :, None]
     step = jnp.arange(local_times, dtype=jnp.int32)[None, None, :]
     time = ((chip + other) % chips) * 2 * local_times + ((core + 1 + half) % 2) * local_times + step
     time = time.reshape(2, chips * local_times)
@@ -265,22 +271,23 @@
     timed = transform(pieces, spread_table(table))
     run = functools.partial(contract, timed=timed, gains=gains, dense=dense, owners=aux_count)
     swap = [(f, f ^ 1) for f in range(freq_count)]
-    jobs = ((0, 0, chips), (1, 1, chips - 1), (1, 0, 1))
-    totals = list(run(jobs, 0, slabs=slabs[0], totals=[], dtypes=(jnp.float32,) * 3))
-    (given,) = run(jobs[:1], 1, slabs=slabs[1], totals=totals[:1], dtypes=(jnp.bfloat16,))
-    taken = lax.ppermute(given, "freq", swap)
-    (kept,) = run(jobs[1:2], 1, slabs=slabs[1], totals=totals[1:2], dtypes=(jnp.float32,))
-    sent = [
-        (kept[i - 1] + taken[i].astype(jnp.float32)).astype(jnp.bfloat16) for i in range(1, chips)
-    ]
-
-    def chip_shift(by):
-        return [(2 * x + c, 2 * ((x + by) % chips) + c) for x in range(chips) for c in range(2)]
-
-    totals[2], sent[0] = lax.optimization_barrier((totals[2], sent[0]))
-    arrived = [lax.ppermute(sent[i], "freq", chip_shift(i + 1)) for i in range(chips - 1)]
-    (kept,) = run(jobs[2:], 1, slabs=slabs[1], totals=totals[2:], dtypes=(jnp.float32,))
-    summed = kept[0] + taken[0].astype(jnp.float32)
+    totals = list(run(((0, 0, chips), (1, 0, chips)), 0, slabs=slabs[0], totals=[], dtypes=(jnp.float32,) * 2))
+
+    def last(first, count, totals):
+        jobs = ((0, first, count), (1, first, count))
+        given, kept = run(jobs, 1, slabs=slabs[1], totals=totals, dtypes=(jnp.bfloat16, jnp.float32))
+        taken = lax.ppermute(given, "freq", swap)
+        return [kept[i] + taken[i].astype(jnp.float32) for i in range(count)]
+
+    def send(value, by):
+        moves = [(2 * x + c, 2 * ((x + by) % chips) + c) for x in range(chips) for c in range(2)]
+        return lax.ppermute(value, "freq", moves)
+
+    far = last(1, 1, totals)[0].astype(jnp.bfloat16)
+    near = last(2, 2, totals)
+    totals[0], far = lax.optimization_barrier((totals[0], far))
+    arrived = [send(far, ORDER[1])] + [send(near[i].astype(jnp.bfloat16), ORDER[2 + i]) for i in range(2)]
+    summed = last(0, 1, totals)[0]
     for piece in arrived:
         summed = summed + piece.astype(jnp.float32)
     spread = lax.all_to_all(summed.astype(jnp.bfloat16), "aux", split_axis=0, concat_axis=0, tiled=True)

time: 98.5 us -> 99.8 us (1.013)
    ppermute x4 -> x6, starting transfers between devices: 4.5 us -> 7.28 us  [the longest x3 6.51 us: send(): return lax.ppermute(value, 'freq', moves)]
    ppermute x4 -> x6, waiting for transfers between devices: 10.8 us -> 8.75 us  [the longest x3 8.74 us: send(): return lax.ppermute(value, 'freq', moves)]
    pallas_call x4, Pallas kernels: 14.9 us -> 16.4 us  [contract(): pl.pallas_call(functools.partial(contract_kernel, jobs, part, bool(totals...]
    ppermute x3, waiting for transfers between devices: 6.01 us -> 7.3 us  [shards(): lax.ppermute(own, 'aux', across[i])]
    ppermute x3, starting transfers between devices: 5.9 us -> 4.69 us  [shards(): lax.ppermute(own, 'aux', across[i])]
    ppermute x3, starting transfers between devices: 5.04 us -> 3.84 us  [shards(): slabs[1].append(lax.ppermute(ready, 'aux', across[i]))]
    all_to_all x1, waiting for transfers between devices: 2.18 us -> 3.29 us  [shards(): lax.all_to_all(pieces, 'freq', split_axis=0, concat_axis=0, tiled=True)]
    unnamed x31 -> x33, local copies, waits for them, and re-layouts: 3.52 us -> 3.55 us
  transfers between devices with their start and end apart: 13 -> 15, of which waited for: 6 -> 6; matrix products, arithmetic and copies ran while one was open for 4% -> 4% of each run, Pallas kernels for 17% -> 18%
where the time goes in v9:
time: 99.8 us; the launch traced here: 99.6 us
  starting transfers between devices  29.2 us (29%)
  Pallas kernels  20.8 us (21%)
  blocking collectives  20.3 us (20%)
  waiting for transfers between devices  19.3 us (19%)
  local copies, waits for them, and re-layouts  6.51 us (7%)
  other arithmetic  1.77 us (2%)
  matrix products  1.3 us (1%)
    all_to_all x1, blocking collectives, shards(): lax.all_to_all(summed.astype(jnp.bfloat16), 'aux', split_axis=0, concat_a...  20.3 us
    pallas_call x4, Pallas kernels, contract(): pl.pallas_call(functools.partial(contract_kernel, jobs, part, bool(totals...  16.4 us
    all_to_all x1, starting transfers between devices, shards(): lax.all_to_all(pieces, 'freq', split_axis=0, concat_axis=0, tiled=True)  11.1 us
    ppermute x3, waiting for transfers between devices, send(): return lax.ppermute(value, 'freq', moves)  8.74 us
    ppermute x3, waiting for transfers between devices, shards(): lax.ppermute(own, 'aux', across[i])  7.3 us
    ppermute x3, starting transfers between devices, send(): return lax.ppermute(value, 'freq', moves)  6.51 us
    ppermute x3, starting transfers between devices, shards(): lax.ppermute(own, 'aux', across[i])  4.69 us
    ppermute x3, starting transfers between devices, shards(): slabs[1].append(lax.ppermute(ready, 'aux', across[i]))  3.84 us
  transfers between devices with their start and end apart: 15, of which 6 were waited for; matrix products, arithmetic and copies ran while one was open for 4% of the time, Pallas kernels for 18%

profile of v9, /device:TPU:32, one launch (start us, length us, event | category | flops | bytes accessed | tf_op | source)
XLA Modules:
  0.0 99.6 jit_solution(15850793754448811699)
XLA Ops:
  0.0 1.3 %copy.16 = bf16[16,8,16,128]{3,1,2,0:T(8,128)(2,1)S(1)} copy(bf16[16,8,16,128]{3,2,1,0:T(8,128)(2,1)} %bitcast.29) | data formatting | bytes 1048576
  1.3 0.8 fusion.18
  2.8 1.5 %shard_map.91 = bf16[8,2,128,512]{3,2,1,0:T(8,128)(2,1)} custom-call(s32[1]{0:T(128)} %bitcast.place_ref, bf16[2,128,4096]{2,1,0:T(8,128)(2,1)S(1)} %copy-done), custom_call_target="tpu_custom_call" | custom-call | tf_op jit(solution)/shard_map/pallas_call | solution.py:41
  4.3 11.1 %all-to-all-start = ((bf16[8,2,128,512]{3,2,1,0:T(8,128)(2,1)}), bf16[8,2,128,512]{3,2,1,0:T(8,128)(2,1)}, u32[]{:S(2)}, u32[]{:S(2)}) async-start(bf16[8,2,128,512]{3,2,1,0:T(8,128)(2,1)} %shard_map.91), calls=%async_computation | async-start | bytes 4194304 | tf_op jit(solution)/shard_map/all_to_all | solution.py:241
  17.3 1.6 %collective-permute-start.1 = (bf16[128,1024]{1,0:T(8,128)(2,1)}, bf16[128,1024]{1,0:T(8,128)(2,1)S(1)}, u32[]{:S(2)}, u32[]{:S(2)}) collective-permute-start(bf16[128,1024]{1,0:T(8,128)(2,1)} %get-tuple-element.29), channel_id=1, source_target_pairs={{0,0},{1,1},{2,2},{3,3},{4,4},{5,5},{6,6},{7,7},{8,8},{9,9},{10,10... | collective-permute-start | bytes 786440 | tf_op jit(solution)/shard_map/ppermute | solution.py:233
  18.9 1.2 %copy.13 = bf16[2,16,64,512]{3,2,1,0:T(8,128)(2,1)S(1)} copy(bf16[2,16,64,512]{3,1,2,0:T(8,128)(2,1)S(1)} %bitcast.26) | data formatting | bytes 4194304 | tf_op jit(solution)/shard_map/transpose | solution.py:267
  20.1 3.1 %collective-permute-start.2 = (bf16[128,1024]{1,0:T(8,128)(2,1)S(1)}, bf16[128,1024]{1,0:T(8,128)(2,1)S(1)}, u32[]{:S(2)}, u32[]{:S(2)}) collective-permute-start(bf16[128,1024]{1,0:T(8,128)(2,1)S(1)} %collective-permute-done.refs_3_), channel_id=1, source_target_pairs={{8,0},{9,1},{10,2},{11,3},{12,4},{13,5},{14,6},{15,7},{16,8},{17,9... | collective-permute-start | bytes 786440 | tf_op jit(solution)/shard_map/ppermute | solution.py:231
  23.8 1.0 collective-permute-start.6
  24.8 1.3 %fusion.2.refs_2_ = bf16[2,512,1024]{2,1,0:T(8,128)(2,1)S(1)} fusion(bf16[2,1024,512]{2,1,0:T(8,128)(2,1)S(1)} %bitcast.27, s32[2,512]{1,0:T(2,128)S(1)} %add_select_fusion, s32[512]{0:T(512)S(1)} %add.194), kind=kOutput, calls=%fused_computation.2 | convolution fusion | flops 1075314688 | bytes 4200448 | tf_op jit(solution)/shard_map/bns,brs->bnr/dot_general | solution.py:268
  26.1 4.4 %collective-permute-done.2.refs_4_ = bf16[128,1024]{1,0:T(8,128)(2,1)S(1)} collective-permute-done((bf16[128,1024]{1,0:T(8,128)(2,1)S(1)}, bf16[128,1024]{1,0:T(8,128)(2,1)S(1)}, u32[]{:S(2)}, u32[]{:S(2)}) %collective-permute-start.2) | collective-permute-done | bytes 262176 | tf_op jit(solution)/shard_map/ppermute | solution.py:231
  31.2 3.8 %collective-permute-start.3 = (bf16[128,1024]{1,0:T(8,128)(2,1)S(1)}, bf16[128,1024]{1,0:T(8,128)(2,1)S(1)}, u32[]{:S(2)}, u32[]{:S(2)}) collective-permute-start(bf16[128,1024]{1,0:T(8,128)(2,1)S(1)} %collective-permute-done.1.refs_3_), channel_id=1, source_target_pairs={{8,0},{9,1},{10,2},{11,3},{12,4},{13,5},{14,6},{15,7},{16,8},{17,9... | collective-permute-start | bytes 786440 | tf_op jit(solution)/shard_map/ppermute | solution.py:237
  35.7 2.9 %collective-permute-done.6.refs_6_ = bf16[128,1024]{1,0:T(8,128)(2,1)S(1)} collective-permute-done((bf16[128,1024]{1,0:T(8,128)(2,1)S(1)}, bf16[128,1024]{1,0:T(8,128)(2,1)S(1)}, u32[]{:S(2)}, u32[]{:S(2)}) %collective-permute-start.6) | collective-permute-done | bytes 262176 | tf_op jit(solution)/shard_map/ppermute | solution.py:231
  38.7 0.7 copy-done.7
  39.4 3.3 %all-to-all-done.pieces_ref = bf16[8,2,128,512]{3,2,1,0:T(8,128)(2,1)} async-done(((bf16[8,2,128,512]{3,2,1,0:T(8,128)(2,1)}), bf16[8,2,128,512]{3,2,1,0:T(8,128)(2,1)}, u32[]{:S(2)}, u32[]{:S(2)}) %all-to-all-start) | async-done | bytes 2097184 | tf_op jit(solution)/shard_map/all_to_all | solution.py:241
  42.7 2.9 %shard_map.93.refs_0_ = bf16[2,4,256,512]{3,2,1,0:T(8,128)(2,1)S(1)} custom-call(bf16[8,2,128,512]{3,2,1,0:T(8,128)(2,1)} %all-to-all-done.pieces_ref, bf16[2,256,256]{2,1,0:T(8,128)(2,1)S(1)} %shard_map.92.mix_ref), custom_call_target="tpu_custom_call" | custom-call | tf_op jit(solution)/shard_map/pallas_call | solution.py:97
  45.7 6.5 %shard_map.94 = (f32[4,32,2,16,128]{4,3,2,1,0:T(8,128)S(1)}, f32[4,32,2,16,128]{4,3,2,1,0:T(8,128)S(1)}) custom-call(bf16[2,4,256,512]{3,2,1,0:T(8,128)(2,1)S(1)} %shard_map.93.refs_0_, f32[2,8,2048]{2,1,0:T(8,128)S(1)} %broadcast_bitcast_fusion.refs_1_, bf16[2,512,1024]{2,1,0:T(8,128)(2,1)S(1)} %fusion.2.refs_2_, bf16[128,1024]{1,0:T(8,128)(2,1)S(1)} %copy-done.2, ...), custom_call_target="tpu_custom_call" | custom-call | flops 4294967296 | bytes 16777216 | tf_op jit(solution)/shard_map/pallas_call | solution.py:177
  52.3 2.9 %shard_map.95 = (bf16[1,32,2,16,128]{4,3,2,1,0:T(8,128)(2,1)S(1)}, f32[1,32,2,16,128]{4,3,2,1,0:T(8,128)S(1)}) custom-call(bf16[2,4,256,512]{3,2,1,0:T(8,128)(2,1)S(1)} %shard_map.93.refs_0_, f32[2,8,2048]{2,1,0:T(8,128)S(1)} %broadcast_bitcast_fusion.refs_1_, bf16[2,512,1024]{2,1,0:T(8,128)(2,1)S(1)} %fusion.2.refs_2_, ...), custom_call_target="tpu_custom_call" | custom-call | flops 1073741824 | bytes 4194304 | tf_op jit(solution)/shard_map/pallas_call | solution.py:177
  55.6 4.0 %shard_map.97 = (bf16[2,32,2,16,128]{4,3,2,1,0:T(8,128)(2,1)S(1)}, f32[2,32,2,16,128]{4,3,2,1,0:T(8,128)S(1)}) custom-call(bf16[2,4,256,512]{3,2,1,0:T(8,128)(2,1)S(1)} %shard_map.93.refs_0_, f32[2,8,2048]{2,1,0:T(8,128)S(1)} %broadcast_bitcast_fusion.refs_1_, bf16[2,512,1024]{2,1,0:T(8,128)(2,1)S(1)} %fusion.2.refs_2_, ...), custom_call_target="tpu_custom_call" | custom-call | flops 2147483648 | bytes 8388608 | tf_op jit(solution)/shard_map/pallas_call | solution.py:177
  60.0 3.9 %collective-permute-start.10 = (bf16[32,2,16,128]{3,2,1,0:T(8,128)(2,1)S(1)}, bf16[32,2,16,128]{3,2,1,0:T(8,128)(2,1)S(1)}, u32[]{:S(2)}, u32[]{:S(2)}) collective-permute-start(bf16[32,2,16,128]{3,2,1,0:T(8,128)(2,1)S(1)} %fusion.10), channel_id=1, source_target_pairs={{0,128},{32,160},{64,192},{96,224},{128,0},{160,32},{192,64},{224,... | collective-permute-start | bytes 786440 | tf_op jit(solution)/shard_map/ppermute | solution.py:284
  63.9 2.9 %shard_map.96 = (bf16[1,32,2,16,128]{4,3,2,1,0:T(8,128)(2,1)S(1)}, f32[1,32,2,16,128]{4,3,2,1,0:T(8,128)S(1)}) custom-call(bf16[2,4,256,512]{3,2,1,0:T(8,128)(2,1)S(1)} %shard_map.93.refs_0_, f32[2,8,2048]{2,1,0:T(8,128)S(1)} %broadcast_bitcast_fusion.refs_1_, bf16[2,512,1024]{2,1,0:T(8,128)(2,1)S(1)} %fusion.2.refs_2_, ...), custom_call_target="tpu_custom_call" | custom-call | flops 1073741824 | bytes 4194304 | tf_op jit(solution)/shard_map/pallas_call | solution.py:177
  67.1 1.7 %collective-permute-start.13 = (bf16[32,2,16,128]{3,2,1,0:T(8,128)(2,1)S(1)}, bf16[32,2,16,128]{3,2,1,0:T(8,128)(2,1)S(1)}, u32[]{:S(2)}, u32[]{:S(2)}) collective-permute-start(bf16[32,2,16,128]{3,2,1,0:T(8,128)(2,1)S(1)} %get-tuple-element.54), channel_id=1, source_target_pairs={{0,192},{32,224},{64,0},{96,32},{128,64},{160,96},{192,128},{224,1... | collective-permute-start | bytes 786440 | tf_op jit(solution)/shard_map/ppermute | solution.py:284
  68.8 0.9 collective-permute-start.12
  70.4 7.7 %collective-permute-done.13 = bf16[32,2,16,128]{3,2,1,0:T(8,128)(2,1)S(1)} collective-permute-done((bf16[32,2,16,128]{3,2,1,0:T(8,128)(2,1)S(1)}, bf16[32,2,16,128]{3,2,1,0:T(8,128)(2,1)S(1)}, u32[]{:S(2)}, u32[]{:S(2)}) %collective-permute-start.13) | collective-permute-done | bytes 262176 | tf_op jit(solution)/shard_map/ppermute | solution.py:284
  78.6 20.3 %all_to_all.10 = bf16[32,2,16,128]{3,2,1,0:T(8,128)(2,1)S(1)} all-to-all(bf16[32,2,16,128]{3,2,1,0:T(8,128)(2,1)S(1)} %fusion.9), channel_id=1, replica_groups=mesh['freq'=8,'aux'=32] {'aux'}, dimensions={0} | all-to-all | bytes 524288 | tf_op jit(solution)/shard_map/all_to_all | solution.py:293
  (83 shorter events, 7.4 us)
Async XLA Ops:
  2.1 15.2 %collective-permute-start = (bf16[128,1024]{1,0:T(8,128)(2,1)S(1)}, bf16[128,1024]{1,0:T(8,128)(2,1)S(1)}, u32[]{:S(2)}, u32[]{:S(2)}) collective-permute-start(bf16[128,1024]{1,0:T(8,128)(2,1)S(1)} %get-tuple-element.55), channel_id=1, source_target_pairs={{0,0},{1,1},{2,2},{3,3},{4,4},{5,5},{6,6},{7,7},{8,8},{9,9},{10,10... | collective-permute-start | bytes 786440 | tf_op jit(solution)/shard_map/ppermute | solution.py:230
  4.2 11.2 %copy-start.15 = (s32[4]{0:T(128)S(1)}, s32[4]{0:T(128)}, u32[]{:S(2)}) copy-start(s32[4]{0:T(128)} %constant.90.clone) | copy-start | bytes 52
  4.3 11.6 %copy-start.11 = (s32[2,8]{1,0:T(2,128)S(1)}, s32[2,8]{1,0:T(2,128)}, u32[]{:S(2)}) copy-start(s32[2,8]{1,0:T(2,128)} %param.14) | copy-start | bytes 196
  4.3 11.6 %copy-start.13 = (s32[32]{0:T(128)S(1)}, s32[32]{0:T(128)}, u32[]{:S(2)}) copy-start(s32[32]{0:T(128)} %param.16) | copy-start | bytes 388
  4.3 11.7 %copy-start.10 = (f32[16,16]{1,0:T(8,128)S(1)}, f32[16,16]{1,0:T(8,128)}, u32[]{:S(2)}) copy-start(f32[16,16]{1,0:T(8,128)} %param.11) | copy-start | bytes 3076
  4.3 11.8 %copy-start.12 = (f32[16]{0:T(128)S(1)}, f32[16]{0:T(128)}, u32[]{:S(2)}) copy-start(f32[16]{0:T(128)} %param.10) | copy-start | bytes 196
  4.3 12.4 %copy-start.14 = (s32[2]{0:T(128)S(1)}, s32[2]{0:T(128)}, u32[]{:S(2)}) copy-start(s32[2]{0:T(128)} %param.15) | copy-start | bytes 28
  4.3 14.6 %copy-start.9 = (bf16[128,16,512]{2,1,0:T(8,128)(2,1)S(1)}, bf16[128,16,512]{2,1,0:T(8,128)(2,1)}, u32[]{:S(2)}) copy-start(bf16[128,16,512]{2,1,0:T(8,128)(2,1)} %param.13) | copy-start | bytes 6291460
  4.3 38.4 %all-to-all-start = ((bf16[8,2,128,512]{3,2,1,0:T(8,128)(2,1)}), bf16[8,2,128,512]{3,2,1,0:T(8,128)(2,1)}, u32[]{:S(2)}, u32[]{:S(2)}) async-start(bf16[8,2,128,512]{3,2,1,0:T(8,128)(2,1)} %shard_map.91), calls=%async_computation | async-start | bytes 4194304 | tf_op jit(solution)/shard_map/all_to_all | solution.py:241
  17.3 6.5 %copy-start.1 = (bf16[128,1024]{1,0:T(8,128)(2,1)}, bf16[128,1024]{1,0:T(8,128)(2,1)S(1)}, u32[]{:S(2)}) copy-start(bf16[128,1024]{1,0:T(8,128)(2,1)S(1)} %collective-permute-done.refs_3_) | copy-start | bytes 786436
  17.3 8.8 %collective-permute-start.1 = (bf16[128,1024]{1,0:T(8,128)(2,1)}, bf16[128,1024]{1,0:T(8,128)(2,1)S(1)}, u32[]{:S(2)}, u32[]{:S(2)}) collective-permute-start(bf16[128,1024]{1,0:T(8,128)(2,1)} %get-tuple-element.29), channel_id=1, source_target_pairs={{0,0},{1,1},{2,2},{3,3},{4,4},{5,5},{6,6},{7,7},{8,8},{9,9},{10,10... | collective-permute-start | bytes 786440 | tf_op jit(solution)/shard_map/ppermute | solution.py:233
  20.1 10.4 %collective-permute-start.2 = (bf16[128,1024]{1,0:T(8,128)(2,1)S(1)}, bf16[128,1024]{1,0:T(8,128)(2,1)S(1)}, u32[]{:S(2)}, u32[]{:S(2)}) collective-permute-start(bf16[128,1024]{1,0:T(8,128)(2,1)S(1)} %collective-permute-done.refs_3_), channel_id=1, source_target_pairs={{8,0},{9,1},{10,2},{11,3},{12,4},{13,5},{14,6},{15,7},{16,8},{17,9... | collective-permute-start | bytes 786440 | tf_op jit(solution)/shard_map/ppermute | solution.py:231
  23.2 11.8 %collective-permute-start.4 = (bf16[128,1024]{1,0:T(8,128)(2,1)S(1)}, bf16[128,1024]{1,0:T(8,128)(2,1)S(1)}, u32[]{:S(2)}, u32[]{:S(2)}) collective-permute-start(bf16[128,1024]{1,0:T(8,128)(2,1)S(1)} %collective-permute-done.refs_3_), channel_id=1, source_target_pairs={{16,0},{17,1},{18,2},{19,3},{20,4},{21,5},{22,6},{23,7},{24,8},{25... | collective-permute-start | bytes 786440 | tf_op jit(solution)/shard_map/ppermute | solution.py:231
  23.8 14.9 %collective-permute-start.6 = (bf16[128,1024]{1,0:T(8,128)(2,1)S(1)}, bf16[128,1024]{1,0:T(8,128)(2,1)S(1)}, u32[]{:S(2)}, u32[]{:S(2)}) collective-permute-start(bf16[128,1024]{1,0:T(8,128)(2,1)S(1)} %collective-permute-done.refs_3_), channel_id=1, source_target_pairs={{24,0},{25,1},{26,2},{27,3},{28,4},{29,5},{30,6},{31,7},{0,8},{1,9... | collective-permute-start | bytes 786440 | tf_op jit(solution)/shard_map/ppermute | solution.py:231
  31.2 21.0 %collective-permute-start.3 = (bf16[128,1024]{1,0:T(8,128)(2,1)S(1)}, bf16[128,1024]{1,0:T(8,128)(2,1)S(1)}, u32[]{:S(2)}, u32[]{:S(2)}) collective-permute-start(bf16[128,1024]{1,0:T(8,128)(2,1)S(1)} %collective-permute-done.1.refs_3_), channel_id=1, source_target_pairs={{8,0},{9,1},{10,2},{11,3},{12,4},{13,5},{14,6},{15,7},{16,8},{17,9... | collective-permute-start | bytes 786440 | tf_op jit(solution)/shard_map/ppermute | solution.py:237
  35.7 16.5 %collective-permute-start.5 = (bf16[128,1024]{1,0:T(8,128)(2,1)S(1)}, bf16[128,1024]{1,0:T(8,128)(2,1)S(1)}, u32[]{:S(2)}, u32[]{:S(2)}) collective-permute-start(bf16[128,1024]{1,0:T(8,128)(2,1)S(1)} %collective-permute-done.1.refs_3_), channel_id=1, source_target_pairs={{16,0},{17,1},{18,2},{19,3},{20,4},{21,5},{22,6},{23,7},{24,8},{25... | collective-permute-start | bytes 786440 | tf_op jit(solution)/shard_map/ppermute | solution.py:237
  39.4 12.8 %collective-permute-start.7 = (bf16[128,1024]{1,0:T(8,128)(2,1)S(1)}, bf16[128,1024]{1,0:T(8,128)(2,1)S(1)}, u32[]{:S(2)}, u32[]{:S(2)}) collective-permute-start(bf16[128,1024]{1,0:T(8,128)(2,1)S(1)} %collective-permute-done.1.refs_3_), channel_id=1, source_target_pairs={{24,0},{25,1},{26,2},{27,3},{28,4},{29,5},{30,6},{31,7},{0,8},{1,9... | collective-permute-start | bytes 786440 | tf_op jit(solution)/shard_map/ppermute | solution.py:237
  42.7 3.0 %copy-start.8 = (bf16[128,1024]{1,0:T(8,128)(2,1)S(1)}, bf16[128,1024]{1,0:T(8,128)(2,1)}, u32[]{:S(2)}) copy-start(bf16[128,1024]{1,0:T(8,128)(2,1)} %copy-done.7) | copy-start | bytes 786436
  55.2 4.7 %collective-permute-start.8 = (bf16[1,32,2,16,128]{4,3,2,1,0:T(8,128)(2,1)S(1)}, bf16[1,32,2,16,128]{4,3,2,1,0:T(8,128)(2,1)S(1)}, u32[]{:S(2)}, u32[]{:S(2)}) collective-permute-start(bf16[1,32,2,16,128]{4,3,2,1,0:T(8,128)(2,1)S(1)} %get-tuple-element.44), channel_id=1, source_target_pairs={{0,32},{32,0},{64,96},{96,64},{128,160},{160,128},{192,224},{224,1... | collective-permute-start | bytes 786440 | tf_op jit(solution)/shard_map/ppermute | solution.py:279
  59.6 7.4 %collective-permute-start.11 = (bf16[2,32,2,16,128]{4,3,2,1,0:T(8,128)(2,1)S(1)}, bf16[2,32,2,16,128]{4,3,2,1,0:T(8,128)(2,1)S(1)}, u32[]{:S(2)}, u32[]{:S(2)}) collective-permute-start(bf16[2,32,2,16,128]{4,3,2,1,0:T(8,128)(2,1)S(1)} %get-tuple-element.50), channel_id=1, source_target_pairs={{0,32},{32,0},{64,96},{96,64},{128,160},{160,128},{192,224},{224,1... | collective-permute-start | bytes 1572872 | tf_op jit(solution)/shard_map/ppermute | solution.py:279
  60.0 10.4 %collective-permute-start.10 = (bf16[32,2,16,128]{3,2,1,0:T(8,128)(2,1)S(1)}, bf16[32,2,16,128]{3,2,1,0:T(8,128)(2,1)S(1)}, u32[]{:S(2)}, u32[]{:S(2)}) collective-permute-start(bf16[32,2,16,128]{3,2,1,0:T(8,128)(2,1)S(1)} %fusion.10), channel_id=1, source_target_pairs={{0,128},{32,160},{64,192},{96,224},{128,0},{160,32},{192,64},{224,... | collective-permute-start | bytes 786440 | tf_op jit(solution)/shard_map/ppermute | solution.py:284
  66.9 3.6 %collective-permute-start.9 = (bf16[1,32,2,16,128]{4,3,2,1,0:T(8,128)(2,1)S(1)}, bf16[1,32,2,16,128]{4,3,2,1,0:T(8,128)(2,1)S(1)}, u32[]{:S(2)}, u32[]{:S(2)}) collective-permute-start(bf16[1,32,2,16,128]{4,3,2,1,0:T(8,128)(2,1)S(1)} %get-tuple-element.47), channel_id=1, source_target_pairs={{0,32},{32,0},{64,96},{96,64},{128,160},{160,128},{192,224},{224,1... | collective-permute-start | bytes 786440 | tf_op jit(solution)/shard_map/ppermute | solution.py:279
  67.1 11.0 %collective-permute-start.13 = (bf16[32,2,16,128]{3,2,1,0:T(8,128)(2,1)S(1)}, bf16[32,2,16,128]{3,2,1,0:T(8,128)(2,1)S(1)}, u32[]{:S(2)}, u32[]{:S(2)}) collective-permute-start(bf16[32,2,16,128]{3,2,1,0:T(8,128)(2,1)S(1)} %get-tuple-element.54), channel_id=1, source_target_pairs={{0,192},{32,224},{64,0},{96,32},{128,64},{160,96},{192,128},{224,1... | collective-permute-start | bytes 786440 | tf_op jit(solution)/shard_map/ppermute | solution.py:284
  68.8 9.6 %collective-permute-start.12 = (bf16[32,2,16,128]{3,2,1,0:T(8,128)(2,1)S(1)}, bf16[32,2,16,128]{3,2,1,0:T(8,128)(2,1)S(1)}, u32[]{:S(2)}, u32[]{:S(2)}) collective-permute-start(bf16[32,2,16,128]{3,2,1,0:T(8,128)(2,1)S(1)} %get-tuple-element.53), channel_id=1, source_target_pairs={{0,64},{32,96},{64,128},{96,160},{128,192},{160,224},{192,0},{224,... | collective-permute-start | bytes 786440 | tf_op jit(solution)/shard_map/ppermute | solution.py:284
  (7 other events, 13.8 us)

commit v10 on v9

--- a/solution.py
+++ b/solution.py
@@ -10,7 +10,6 @@
 BAND = 16
 DEPTH = 8
 SHIFTS = ((0, 4, 3, 5, 2, 6, 1, 7), (0, 4, 1, 7, 2, 6, 3, 5))
-ORDER = (0, 2, 1, 3)
 WHOLE = pl.BlockSpec(memory_space=pltpu.VMEM)
 
 
@@ -73,14 +72,21 @@
     )(table)
 
 
-def mix_kernel(pieces_ref, mix_ref, out_ref):
+def mix_kernel(pieces_in, mix_ref, out_ref, pieces_ref, sems):
     sources, local, rows, width = pieces_ref.shape
+    copies = []
+    for i in range(rows // (2 * BAND)):
+        part = pl.ds(i * 2 * BAND, 2 * BAND)
+        copies.append(pltpu.make_async_copy(pieces_in.at[:, :, part], pieces_ref.at[:, :, part], sems.at[i]))
+        copies[-1].start()
     freqs = sources * local
     places = out_ref.shape[1]
     pair = 2 * BAND
     tall = places * pair
     mix = mix_ref[...].reshape(4 * tall, freqs * BAND)
     for band in range(rows // BAND):
+        if band % 2 == 0:
+            copies[band // 2].wait()
         piece = pieces_ref[:, :, band * BAND : (band + 1) * BAND, :].reshape(freqs * BAND, width)
         both = jnp.dot(mix, piece, preferred_element_type=jnp.float32)
         for half in range(2):
@@ -97,8 +103,9 @@
     return pl.pallas_call(
         mix_kernel,
         out_shape=jax.ShapeDtypeStruct((2, times // 2, 2 * rows, width), jnp.bfloat16),
-        in_specs=[WHOLE] * 2,
+        in_specs=[pl.BlockSpec(memory_space=pl.ANY), WHOLE],
         out_specs=WHOLE,
+        scratch_shapes=[pltpu.VMEM(pieces.shape, pieces.dtype), pltpu.SemaphoreType.DMA((rows // (2 * BAND),))],
         compiler_params=params(),
     )(pieces, mix)
 
@@ -109,7 +116,7 @@
     refs = refs[7:]
     totals = ()
     if has_total:
-        totals, refs = refs[:2], refs[2:]
+        totals, refs = refs[:1], refs[1:]
     outs, (state_ref, scaled_ref) = refs[: len(jobs)], refs[len(jobs) :]
     slab = slabs[0].shape[0]
     for i in range(4):
@@ -161,7 +168,7 @@
             for time in range(2):
                 piece = value[:, time * targets : (time + 1) * targets].reshape(owners, inner, targets)
                 if has_total:
-                    piece = piece + totals[half][first + place, :, time, :, :]
+                    piece = piece + totals[0][first + place, :, time, :, :]
                 out_ref[place, :, time, :, :] = piece.astype(out_ref.dtype)
 
 
@@ -241,7 +248,7 @@
     pieces = lax.all_to_all(pieces, "freq", split_axis=0, concat_axis=0, tiled=True)
 
     half = jnp.arange(2, dtype=jnp.int32)[:, None, None]
-    other = jnp.array(ORDER, dtype=jnp.int32)[None, :, None]
+    other = jnp.arange(chips, dtype=jnp.int32)[None, :, None]
     step = jnp.arange(local_times, dtype=jnp.int32)[None, None, :]
     time = ((chip + other) % chips) * 2 * local_times + ((core + 1 + half) % 2) * local_times + step
     time = time.reshape(2, chips * local_times)
@@ -262,7 +269,7 @@
     listed = block_ids[:, :, None] * block_width + jnp.arange(block_width, dtype=jnp.int32)
     listed = jnp.where(slot[None, :, None] < block_counts[:, None, None], listed, -1).reshape(block_count, orbitals)
     choose = (wanted[None, :, None] == listed[:, None, :]).astype(jnp.bfloat16)
-    _, three_orbital = lax.optimization_barrier((slabs[0][0], three_orbital))
+    _, three_orbital = lax.optimization_barrier((slabs[0][1], three_orbital))
     values = three_orbital.reshape(block_count, row_block, states, orbitals)
     values = values.transpose(0, 2, 1, 3).reshape(block_count, states * row_block, orbitals)
     dense = jnp.einsum("bns,brs->bnr", choose, values, preferred_element_type=jnp.float32).astype(jnp.bfloat16)
@@ -271,23 +278,20 @@
     timed = transform(pieces, spread_table(table))
     run = functools.partial(contract, timed=timed, gains=gains, dense=dense, owners=aux_count)
     swap = [(f, f ^ 1) for f in range(freq_count)]
-    totals = list(run(((0, 0, chips), (1, 0, chips)), 0, slabs=slabs[0], totals=[], dtypes=(jnp.float32,) * 2))
-
-    def last(first, count, totals):
-        jobs = ((0, first, count), (1, first, count))
-        given, kept = run(jobs, 1, slabs=slabs[1], totals=totals, dtypes=(jnp.bfloat16, jnp.float32))
-        taken = lax.ppermute(given, "freq", swap)
-        return [kept[i] + taken[i].astype(jnp.float32) for i in range(count)]
-
-    def send(value, by):
-        moves = [(2 * x + c, 2 * ((x + by) % chips) + c) for x in range(chips) for c in range(2)]
-        return lax.ppermute(value, "freq", moves)
-
-    far = last(1, 1, totals)[0].astype(jnp.bfloat16)
-    near = last(2, 2, totals)
-    totals[0], far = lax.optimization_barrier((totals[0], far))
-    arrived = [send(far, ORDER[1])] + [send(near[i].astype(jnp.bfloat16), ORDER[2 + i]) for i in range(2)]
-    summed = last(0, 1, totals)[0]
+    away = chips - 1
+    totals = run(((0, 0, chips), (1, 0, chips)), 0, slabs=slabs[0], totals=[], dtypes=(jnp.float32,) * 2)
+    (given,) = run(((0, 0, chips),), 1, slabs=slabs[1], totals=[totals[0]], dtypes=(jnp.bfloat16,))
+    taken = lax.ppermute(given, "freq", swap)
+    (kept,) = run(((1, 1, away),), 1, slabs=slabs[1], totals=[totals[1]], dtypes=(jnp.float32,))
+    sent = [(kept[i - 1] + taken[i].astype(jnp.float32)).astype(jnp.bfloat16) for i in range(1, chips)]
+
+    def chip_shift(by):
+        return [(2 * x + c, 2 * ((x + by) % chips) + c) for x in range(chips) for c in range(2)]
+
+    own, sent[0] = lax.optimization_barrier((totals[1], sent[0]))
+    arrived = [lax.ppermute(sent[i], "freq", chip_shift(i + 1)) for i in range(away)]
+    (kept,) = run(((1, 0, 1),), 1, slabs=slabs[1], totals=[own], dtypes=(jnp.float32,))
+    summed = kept[0] + taken[0].astype(jnp.float32)
     for piece in arrived:
         summed = summed + piece.astype(jnp.float32)
     spread = lax.all_to_all(summed.astype(jnp.bfloat16), "aux", split_axis=0, concat_axis=0, tiled=True)

time: 99.8 us -> 97.3 us (0.975)
  Pallas kernels: 20.8 us -> 18.4 us
  waiting for transfers between devices: 19.3 us -> 21.3 us
    all_to_all x1, waiting for transfers between devices: 3.29 us -> 6.89 us  [shards(): lax.all_to_all(pieces, 'freq', split_axis=0, concat_axis=0, tiled=True)]
    ppermute x3, waiting for transfers between devices: 7.3 us -> 4.32 us  [shards(): lax.ppermute(own, 'aux', across[i])]
    pallas_call x4, Pallas kernels: 16.4 us -> 14 us  [contract(): pl.pallas_call(functools.partial(contract_kernel, jobs, part, bool(totals...]
    transpose x1, local copies, waits for them, and re-layouts: 1.16 us -> 2.75 us  [shards(): values.transpose(0, 2, 1, 3)]
    unnamed x33 -> x29, local copies, waits for them, and re-layouts: 3.55 us -> 2.09 us
    ppermute x6 -> x4, waiting for transfers between devices: 8.75 us -> 10 us  [the longest x3 10 us: shards(): lax.ppermute(sent[i], 'freq', chip_shift(i + 1))]
    ppermute x3, starting transfers between devices: 4.69 us -> 5.9 us  [shards(): lax.ppermute(own, 'aux', across[i])]
    ppermute x3, starting transfers between devices: 3.84 us -> 2.77 us  [shards(): slabs[1].append(lax.ppermute(ready, 'aux', across[i]))]
  transfers between devices with their start and end apart: 15 -> 13, of which waited for: 6 -> 6; matrix products, arithmetic and copies ran while one was open for 4% -> 6% of each run, Pallas kernels for 18% -> 16%
where the time goes in v10:
time: 97.3 us; the launch traced here: 96.9 us
  starting transfers between devices  28.4 us (29%)
  waiting for transfers between devices  21.3 us (22%)
  blocking collectives  19.5 us (20%)
  Pallas kernels  18.4 us (19%)
  local copies, waits for them, and re-layouts  5.92 us (6%)
  other arithmetic  1.78 us (2%)
  matrix products  1.3 us (1%)
    all_to_all x1, blocking collectives, shards(): lax.all_to_all(summed.astype(jnp.bfloat16), 'aux', split_axis=0, concat_a...  19.5 us
    pallas_call x4, Pallas kernels, contract(): pl.pallas_call(functools.partial(contract_kernel, jobs, part, bool(totals...  14 us
    all_to_all x1, starting transfers between devices, shards(): lax.all_to_all(pieces, 'freq', split_axis=0, concat_axis=0, tiled=True)  11.1 us
    ppermute x3, waiting for transfers between devices, shards(): lax.ppermute(sent[i], 'freq', chip_shift(i + 1))  10 us
    all_to_all x1, waiting for transfers between devices, shards(): lax.all_to_all(pieces, 'freq', split_axis=0, concat_axis=0, tiled=True)  6.89 us
    ppermute x3, starting transfers between devices, shards(): lax.ppermute(own, 'aux', across[i])  5.9 us
    ppermute x3, waiting for transfers between devices, shards(): lax.ppermute(own, 'aux', across[i])  4.32 us
    ppermute x3, starting transfers between devices, shards(): lax.ppermute(sent[i], 'freq', chip_shift(i + 1))  4.26 us
  transfers between devices with their start and end apart: 13, of which 6 were waited for; matrix products, arithmetic and copies ran while one was open for 6% of the time, Pallas kernels for 16%

profile of v10, /device:TPU:32, one launch (start us, length us, event | category | flops | bytes accessed | tf_op | source)
XLA Modules:
  0.0 96.9 jit_solution(10575652826312903626)
XLA Ops:
  0.0 1.3 %copy.15 = bf16[16,8,16,128]{3,1,2,0:T(8,128)(2,1)S(1)} copy(bf16[16,8,16,128]{3,2,1,0:T(8,128)(2,1)} %bitcast.29) | data formatting | bytes 1048576
  2.1 1.5 %shard_map.82 = bf16[8,2,128,512]{3,2,1,0:T(8,128)(2,1)} custom-call(s32[1]{0:T(128)} %bitcast.place_ref, bf16[2,128,4096]{2,1,0:T(8,128)(2,1)S(1)} %copy-done), custom_call_target="tpu_custom_call" | custom-call | tf_op jit(solution)/shard_map/pallas_call | solution.py:40
  3.6 11.1 %all-to-all-start = ((bf16[8,2,128,512]{3,2,1,0:T(8,128)(2,1)}), bf16[8,2,128,512]{3,2,1,0:T(8,128)(2,1)}, u32[]{:S(2)}, u32[]{:S(2)}) async-start(bf16[8,2,128,512]{3,2,1,0:T(8,128)(2,1)} %shard_map.82), calls=%async_computation | async-start | bytes 4194304 | tf_op jit(solution)/shard_map/all_to_all | solution.py:248
  16.7 1.7 %collective-permute-start.6 = (bf16[128,1024]{1,0:T(8,128)(2,1)S(1)}, bf16[128,1024]{1,0:T(8,128)(2,1)S(1)}, u32[]{:S(2)}, u32[]{:S(2)}) collective-permute-start(bf16[128,1024]{1,0:T(8,128)(2,1)S(1)} %collective-permute-done.refs_3_), channel_id=1, source_target_pairs={{24,0},{25,1},{26,2},{27,3},{28,4},{29,5},{30,6},{31,7},{0,8},{1,9... | collective-permute-start | bytes 786440 | tf_op jit(solution)/shard_map/ppermute | solution.py:238
  18.3 2.9 %collective-permute-start.4 = (bf16[128,1024]{1,0:T(8,128)(2,1)S(1)}, bf16[128,1024]{1,0:T(8,128)(2,1)S(1)}, u32[]{:S(2)}, u32[]{:S(2)}) collective-permute-start(bf16[128,1024]{1,0:T(8,128)(2,1)S(1)} %collective-permute-done.refs_3_), channel_id=1, source_target_pairs={{16,0},{17,1},{18,2},{19,3},{20,4},{21,5},{22,6},{23,7},{24,8},{25... | collective-permute-start | bytes 786440 | tf_op jit(solution)/shard_map/ppermute | solution.py:238
  21.2 1.3 %collective-permute-start.2 = (bf16[128,1024]{1,0:T(8,128)(2,1)S(1)}, bf16[128,1024]{1,0:T(8,128)(2,1)S(1)}, u32[]{:S(2)}, u32[]{:S(2)}) collective-permute-start(bf16[128,1024]{1,0:T(8,128)(2,1)S(1)} %collective-permute-done.refs_3_), channel_id=1, source_target_pairs={{8,0},{9,1},{10,2},{11,3},{12,4},{13,5},{14,6},{15,7},{16,8},{17,9... | collective-permute-start | bytes 786440 | tf_op jit(solution)/shard_map/ppermute | solution.py:238
  23.2 1.1 %collective-permute-done.6.refs_6_ = bf16[128,1024]{1,0:T(8,128)(2,1)S(1)} collective-permute-done((bf16[128,1024]{1,0:T(8,128)(2,1)S(1)}, bf16[128,1024]{1,0:T(8,128)(2,1)S(1)}, u32[]{:S(2)}, u32[]{:S(2)}) %collective-permute-start.6) | collective-permute-done | bytes 262176 | tf_op jit(solution)/shard_map/ppermute | solution.py:238
  25.4 3.2 %collective-permute-done.4.refs_5_ = bf16[128,1024]{1,0:T(8,128)(2,1)S(1)} collective-permute-done((bf16[128,1024]{1,0:T(8,128)(2,1)S(1)}, bf16[128,1024]{1,0:T(8,128)(2,1)S(1)}, u32[]{:S(2)}, u32[]{:S(2)}) %collective-permute-start.4) | collective-permute-done | bytes 262176 | tf_op jit(solution)/shard_map/ppermute | solution.py:238
  29.4 1.6 %collective-permute-start.3 = (bf16[128,1024]{1,0:T(8,128)(2,1)S(1)}, bf16[128,1024]{1,0:T(8,128)(2,1)S(1)}, u32[]{:S(2)}, u32[]{:S(2)}) collective-permute-start(bf16[128,1024]{1,0:T(8,128)(2,1)S(1)} %collective-permute-done.1.refs_3_), channel_id=1, source_target_pairs={{8,0},{9,1},{10,2},{11,3},{12,4},{13,5},{14,6},{15,7},{16,8},{17,9... | collective-permute-start | bytes 786440 | tf_op jit(solution)/shard_map/ppermute | solution.py:244
  31.0 2.8 %copy.12 = bf16[2,16,64,512]{3,2,1,0:T(8,128)(2,1)S(1)} copy(bf16[2,16,64,512]{3,1,2,0:T(8,128)(2,1)} %bitcast.26) | data formatting | bytes 4194304 | tf_op jit(solution)/shard_map/transpose | solution.py:274
  33.8 1.3 %fusion.2.refs_2_ = bf16[2,512,1024]{2,1,0:T(8,128)(2,1)S(1)} fusion(bf16[2,1024,512]{2,1,0:T(8,128)(2,1)S(1)} %bitcast.27, s32[2,512]{1,0:T(2,128)S(1)} %add_select_fusion, s32[512]{0:T(512)S(1)} %add.202), kind=kOutput, calls=%fused_computation.2 | convolution fusion | flops 1075314688 | bytes 4200448 | tf_op jit(solution)/shard_map/bns,brs->bnr/dot_general | solution.py:275
  35.1 6.9 %all-to-all-done.pieces_in = bf16[8,2,128,512]{3,2,1,0:T(8,128)(2,1)} async-done(((bf16[8,2,128,512]{3,2,1,0:T(8,128)(2,1)}), bf16[8,2,128,512]{3,2,1,0:T(8,128)(2,1)}, u32[]{:S(2)}, u32[]{:S(2)}) %all-to-all-start) | async-done | bytes 2097184 | tf_op jit(solution)/shard_map/all_to_all | solution.py:248
  42.0 2.9 %shard_map.84.refs_0_ = bf16[2,4,256,512]{3,2,1,0:T(8,128)(2,1)S(1)} custom-call(bf16[8,2,128,512]{3,2,1,0:T(8,128)(2,1)} %all-to-all-done.pieces_in, bf16[2,256,256]{2,1,0:T(8,128)(2,1)S(1)} %shard_map.83.mix_ref), custom_call_target="tpu_custom_call" | custom-call | tf_op jit(solution)/shard_map/pallas_call | solution.py:103
  45.0 6.5 %shard_map.85 = (f32[4,32,2,16,128]{4,3,2,1,0:T(8,128)S(1)}, f32[4,32,2,16,128]{4,3,2,1,0:T(8,128)S(1)}) custom-call(bf16[2,4,256,512]{3,2,1,0:T(8,128)(2,1)S(1)} %shard_map.84.refs_0_, f32[2,8,2048]{2,1,0:T(8,128)S(1)} %broadcast_bitcast_fusion.refs_1_, bf16[2,512,1024]{2,1,0:T(8,128)(2,1)S(1)} %fusion.2.refs_2_, bf16[128,1024]{1,0:T(8,128)(2,1)S(1)} %copy-done.2, ...), custom_call_target="tpu_custom_call" | custom-call | flops 4294967296 | bytes 16777216 | tf_op jit(solution)/shard_map/pallas_call | solution.py:184
  51.5 3.3 %shard_map.87 = bf16[4,32,2,16,128]{4,3,2,1,0:T(8,128)(2,1)S(1)} custom-call(bf16[2,4,256,512]{3,2,1,0:T(8,128)(2,1)S(1)} %shard_map.84.refs_0_, f32[2,8,2048]{2,1,0:T(8,128)S(1)} %broadcast_bitcast_fusion.refs_1_, bf16[2,512,1024]{2,1,0:T(8,128)(2,1)S(1)} %fusion.2.refs_2_, bf16[128,1024]{1,0:T(8,128)(2,1)S(1)} %collective-permute-done.1.refs_3_, ...), custom_call_target="tpu_custom_call" | custom-call | flops 2147483648 | bytes 8388608 | tf_op jit(solution)/shard_map/pallas_call | solution.py:184
  54.9 3.0 %collective-permute-start.8 = (bf16[4,32,2,16,128]{4,3,2,1,0:T(8,128)(2,1)S(1)}, bf16[4,32,2,16,128]{4,3,2,1,0:T(8,128)(2,1)S(1)}, u32[]{:S(2)}, u32[]{:S(2)}) collective-permute-start(bf16[4,32,2,16,128]{4,3,2,1,0:T(8,128)(2,1)S(1)} %shard_map.87), channel_id=1, source_target_pairs={{0,32},{32,0},{64,96},{96,64},{128,160},{160,128},{192,224},{224,1... | collective-permute-start | bytes 3145736 | tf_op jit(solution)/shard_map/ppermute | solution.py:284
  57.9 2.6 %shard_map.86 = f32[3,32,2,16,128]{4,3,2,1,0:T(8,128)S(1)} custom-call(bf16[2,4,256,512]{3,2,1,0:T(8,128)(2,1)S(1)} %shard_map.84.refs_0_, f32[2,8,2048]{2,1,0:T(8,128)S(1)} %broadcast_bitcast_fusion.refs_1_, bf16[2,512,1024]{2,1,0:T(8,128)(2,1)S(1)} %fusion.2.refs_2_, bf16[128,1024]{1,0:T(8,128)(2,1)S(1)} %collective-permute-done.1.refs_3_, ...), custom_call_target="tpu_custom_call" | custom-call | flops 1610612736 | bytes 6291456 | tf_op jit(solution)/shard_map/pallas_call | solution.py:184
  60.8 1.0 collective-permute-start.9
  61.8 2.3 %collective-permute-start.11 = (bf16[32,2,16,128]{3,2,1,0:T(8,128)(2,1)S(1)}, bf16[32,2,16,128]{3,2,1,0:T(8,128)(2,1)S(1)}, u32[]{:S(2)}, u32[]{:S(2)}) collective-permute-start(bf16[32,2,16,128]{3,2,1,0:T(8,128)(2,1)S(1)} %get-tuple-element.42), channel_id=1, source_target_pairs={{0,192},{32,224},{64,0},{96,32},{128,64},{160,96},{192,128},{224,1... | collective-permute-start | bytes 786440 | tf_op jit(solution)/shard_map/ppermute | solution.py:292
  65.1 1.5 %shard_map.88 = f32[1,32,2,16,128]{4,3,2,1,0:T(8,128)S(1)} custom-call(bf16[2,4,256,512]{3,2,1,0:T(8,128)(2,1)S(1)} %shard_map.84.refs_0_, f32[2,8,2048]{2,1,0:T(8,128)S(1)} %broadcast_bitcast_fusion.refs_1_, bf16[2,512,1024]{2,1,0:T(8,128)(2,1)S(1)} %fusion.2.refs_2_, bf16[128,1024]{1,0:T(8,128)(2,1)S(1)} %collective-permute-done.1.refs_3_, ...), custom_call_target="tpu_custom_call" | custom-call | flops 536870912 | bytes 2097152 | tf_op jit(solution)/shard_map/pallas_call | solution.py:184
  66.6 3.7 %collective-permute-done.9 = bf16[32,2,16,128]{3,2,1,0:T(8,128)(2,1)S(1)} collective-permute-done((bf16[32,2,16,128]{3,2,1,0:T(8,128)(2,1)S(1)}, bf16[32,2,16,128]{3,2,1,0:T(8,128)(2,1)S(1)}, u32[]{:S(2)}, u32[]{:S(2)}) %collective-permute-start.9) | collective-permute-done | bytes 262176 | tf_op jit(solution)/shard_map/ppermute | solution.py:292
  70.3 4.9 %collective-permute-done.11 = bf16[32,2,16,128]{3,2,1,0:T(8,128)(2,1)S(1)} collective-permute-done((bf16[32,2,16,128]{3,2,1,0:T(8,128)(2,1)S(1)}, bf16[32,2,16,128]{3,2,1,0:T(8,128)(2,1)S(1)}, u32[]{:S(2)}, u32[]{:S(2)}) %collective-permute-start.11) | collective-permute-done | bytes 262176 | tf_op jit(solution)/shard_map/ppermute | solution.py:292
  75.2 1.4 %collective-permute-done.10 = bf16[32,2,16,128]{3,2,1,0:T(8,128)(2,1)S(1)} collective-permute-done((bf16[32,2,16,128]{3,2,1,0:T(8,128)(2,1)S(1)}, bf16[32,2,16,128]{3,2,1,0:T(8,128)(2,1)S(1)}, u32[]{:S(2)}, u32[]{:S(2)}) %collective-permute-start.10) | collective-permute-done | bytes 262176 | tf_op jit(solution)/shard_map/ppermute | solution.py:292
  76.8 19.5 %all_to_all.10 = bf16[32,2,16,128]{3,2,1,0:T(8,128)(2,1)S(1)} all-to-all(bf16[32,2,16,128]{3,2,1,0:T(8,128)(2,1)S(1)} %fusion.12), channel_id=1, replica_groups=mesh['freq'=8,'aux'=32] {'aux'}, dimensions={0} | all-to-all | bytes 524288 | tf_op jit(solution)/shard_map/all_to_all | solution.py:297
  (74 shorter events, 7.2 us)
Async XLA Ops:
  1.4 14.6 %collective-permute-start = (bf16[128,1024]{1,0:T(8,128)(2,1)S(1)}, bf16[128,1024]{1,0:T(8,128)(2,1)S(1)}, u32[]{:S(2)}, u32[]{:S(2)}) collective-permute-start(bf16[128,1024]{1,0:T(8,128)(2,1)S(1)} %get-tuple-element.44), channel_id=1, source_target_pairs={{0,0},{1,1},{2,2},{3,3},{4,4},{5,5},{6,6},{7,7},{8,8},{9,9},{10,10... | collective-permute-start | bytes 786440 | tf_op jit(solution)/shard_map/ppermute | solution.py:237
  3.5 11.2 %copy-start.12 = (s32[32]{0:T(128)S(1)}, s32[32]{0:T(128)}, u32[]{:S(2)}) copy-start(s32[32]{0:T(128)} %param.15) | copy-start | bytes 388
  3.5 11.3 %copy-start.10 = (s32[2,8]{1,0:T(2,128)S(1)}, s32[2,8]{1,0:T(2,128)}, u32[]{:S(2)}) copy-start(s32[2,8]{1,0:T(2,128)} %param.13) | copy-start | bytes 196
  3.6 11.7 %copy-start.9 = (f32[16,16]{1,0:T(8,128)S(1)}, f32[16,16]{1,0:T(8,128)}, u32[]{:S(2)}) copy-start(f32[16,16]{1,0:T(8,128)} %param.10) | copy-start | bytes 3076
  3.6 12.1 %copy-start.11 = (f32[16]{0:T(128)S(1)}, f32[16]{0:T(128)}, u32[]{:S(2)}) copy-start(f32[16]{0:T(128)} %param.9) | copy-start | bytes 196
  3.6 19.0 %copy-start.13 = (s32[2]{0:T(128)S(1)}, s32[2]{0:T(128)}, u32[]{:S(2)}) copy-start(s32[2]{0:T(128)} %param.14) | copy-start | bytes 28
  3.6 38.4 %all-to-all-start = ((bf16[8,2,128,512]{3,2,1,0:T(8,128)(2,1)}), bf16[8,2,128,512]{3,2,1,0:T(8,128)(2,1)}, u32[]{:S(2)}, u32[]{:S(2)}) async-start(bf16[8,2,128,512]{3,2,1,0:T(8,128)(2,1)} %shard_map.82), calls=%async_computation | async-start | bytes 4194304 | tf_op jit(solution)/shard_map/all_to_all | solution.py:248
  16.0 13.4 %copy-start.1 = (bf16[128,1024]{1,0:T(8,128)(2,1)}, bf16[128,1024]{1,0:T(8,128)(2,1)S(1)}, u32[]{:S(2)}) copy-start(bf16[128,1024]{1,0:T(8,128)(2,1)S(1)} %collective-permute-done.refs_3_) | copy-start | bytes 786436
  16.0 7.2 %collective-permute-start.1 = (bf16[128,1024]{1,0:T(8,128)(2,1)S(1)}, bf16[128,1024]{1,0:T(8,128)(2,1)S(1)}, u32[]{:S(2)}, u32[]{:S(2)}) collective-permute-start(bf16[128,1024]{1,0:T(8,128)(2,1)S(1)} %get-tuple-element.23), channel_id=1, source_target_pairs={{0,0},{1,1},{2,2},{3,3},{4,4},{5,5},{6,6},{7,7},{8,8},{9,9},{10,10... | collective-permute-start | bytes 786440 | tf_op jit(solution)/shard_map/ppermute | solution.py:240
  16.7 7.7 %collective-permute-start.6 = (bf16[128,1024]{1,0:T(8,128)(2,1)S(1)}, bf16[128,1024]{1,0:T(8,128)(2,1)S(1)}, u32[]{:S(2)}, u32[]{:S(2)}) collective-permute-start(bf16[128,1024]{1,0:T(8,128)(2,1)S(1)} %collective-permute-done.refs_3_), channel_id=1, source_target_pairs={{24,0},{25,1},{26,2},{27,3},{28,4},{29,5},{30,6},{31,7},{0,8},{1,9... | collective-permute-start | bytes 786440 | tf_op jit(solution)/shard_map/ppermute | solution.py:238
  18.3 10.3 %collective-permute-start.4 = (bf16[128,1024]{1,0:T(8,128)(2,1)S(1)}, bf16[128,1024]{1,0:T(8,128)(2,1)S(1)}, u32[]{:S(2)}, u32[]{:S(2)}) collective-permute-start(bf16[128,1024]{1,0:T(8,128)(2,1)S(1)} %collective-permute-done.refs_3_), channel_id=1, source_target_pairs={{16,0},{17,1},{18,2},{19,3},{20,4},{21,5},{22,6},{23,7},{24,8},{25... | collective-permute-start | bytes 786440 | tf_op jit(solution)/shard_map/ppermute | solution.py:238
  21.2 8.2 %collective-permute-start.2 = (bf16[128,1024]{1,0:T(8,128)(2,1)S(1)}, bf16[128,1024]{1,0:T(8,128)(2,1)S(1)}, u32[]{:S(2)}, u32[]{:S(2)}) collective-permute-start(bf16[128,1024]{1,0:T(8,128)(2,1)S(1)} %collective-permute-done.refs_3_), channel_id=1, source_target_pairs={{8,0},{9,1},{10,2},{11,3},{12,4},{13,5},{14,6},{15,7},{16,8},{17,9... | collective-permute-start | bytes 786440 | tf_op jit(solution)/shard_map/ppermute | solution.py:238
  25.0 26.5 %collective-permute-start.7 = (bf16[128,1024]{1,0:T(8,128)(2,1)S(1)}, bf16[128,1024]{1,0:T(8,128)(2,1)S(1)}, u32[]{:S(2)}, u32[]{:S(2)}) collective-permute-start(bf16[128,1024]{1,0:T(8,128)(2,1)S(1)} %collective-permute-done.1.refs_3_), channel_id=1, source_target_pairs={{24,0},{25,1},{26,2},{27,3},{28,4},{29,5},{30,6},{31,7},{0,8},{1,9... | collective-permute-start | bytes 786440 | tf_op jit(solution)/shard_map/ppermute | solution.py:244
  28.6 5.2 %copy-start.5 = (bf16[128,1024]{1,0:T(8,128)(2,1)}, bf16[128,1024]{1,0:T(8,128)(2,1)S(1)}, u32[]{:S(2)}) copy-start(bf16[128,1024]{1,0:T(8,128)(2,1)S(1)} %collective-permute-done.4.refs_5_) | copy-start | bytes 786436
  28.6 22.9 %collective-permute-start.5 = (bf16[128,1024]{1,0:T(8,128)(2,1)S(1)}, bf16[128,1024]{1,0:T(8,128)(2,1)S(1)}, u32[]{:S(2)}, u32[]{:S(2)}) collective-permute-start(bf16[128,1024]{1,0:T(8,128)(2,1)S(1)} %collective-permute-done.1.refs_3_), channel_id=1, source_target_pairs={{16,0},{17,1},{18,2},{19,3},{20,4},{21,5},{22,6},{23,7},{24,8},{25... | collective-permute-start | bytes 786440 | tf_op jit(solution)/shard_map/ppermute | solution.py:244
  29.4 4.4 %copy-start.7 = (bf16[128,1024]{1,0:T(8,128)(2,1)}, bf16[128,1024]{1,0:T(8,128)(2,1)S(1)}, u32[]{:S(2)}) copy-start(bf16[128,1024]{1,0:T(8,128)(2,1)S(1)} %collective-permute-done.2.refs_4_) | copy-start | bytes 786436
  29.4 22.1 %collective-permute-start.3 = (bf16[128,1024]{1,0:T(8,128)(2,1)S(1)}, bf16[128,1024]{1,0:T(8,128)(2,1)S(1)}, u32[]{:S(2)}, u32[]{:S(2)}) collective-permute-start(bf16[128,1024]{1,0:T(8,128)(2,1)S(1)} %collective-permute-done.1.refs_3_), channel_id=1, source_target_pairs={{8,0},{9,1},{10,2},{11,3},{12,4},{13,5},{14,6},{15,7},{16,8},{17,9... | collective-permute-start | bytes 786440 | tf_op jit(solution)/shard_map/ppermute | solution.py:244
  42.0 3.0 %copy-start.4 = (bf16[128,1024]{1,0:T(8,128)(2,1)S(1)}, bf16[128,1024]{1,0:T(8,128)(2,1)}, u32[]{:S(2)}) copy-start(bf16[128,1024]{1,0:T(8,128)(2,1)} %copy-done.3) | copy-start | bytes 786436
  42.0 3.0 %copy-start.6 = (bf16[128,1024]{1,0:T(8,128)(2,1)S(1)}, bf16[128,1024]{1,0:T(8,128)(2,1)}, u32[]{:S(2)}) copy-start(bf16[128,1024]{1,0:T(8,128)(2,1)} %copy-done.5) | copy-start | bytes 786436
  42.0 3.0 %copy-start.8 = (bf16[128,1024]{1,0:T(8,128)(2,1)S(1)}, bf16[128,1024]{1,0:T(8,128)(2,1)}, u32[]{:S(2)}) copy-start(bf16[128,1024]{1,0:T(8,128)(2,1)} %copy-done.7) | copy-start | bytes 786436
  54.9 5.7 %collective-permute-start.8 = (bf16[4,32,2,16,128]{4,3,2,1,0:T(8,128)(2,1)S(1)}, bf16[4,32,2,16,128]{4,3,2,1,0:T(8,128)(2,1)S(1)}, u32[]{:S(2)}, u32[]{:S(2)}) collective-permute-start(bf16[4,32,2,16,128]{4,3,2,1,0:T(8,128)(2,1)S(1)} %shard_map.87), channel_id=1, source_target_pairs={{0,32},{32,0},{64,96},{96,64},{128,160},{160,128},{192,224},{224,1... | collective-permute-start | bytes 3145736 | tf_op jit(solution)/shard_map/ppermute | solution.py:284
  60.8 9.5 %collective-permute-start.9 = (bf16[32,2,16,128]{3,2,1,0:T(8,128)(2,1)S(1)}, bf16[32,2,16,128]{3,2,1,0:T(8,128)(2,1)S(1)}, u32[]{:S(2)}, u32[]{:S(2)}) collective-permute-start(bf16[32,2,16,128]{3,2,1,0:T(8,128)(2,1)S(1)} %get-tuple-element.38), channel_id=1, source_target_pairs={{0,64},{32,96},{64,128},{96,160},{128,192},{160,224},{192,0},{224,... | collective-permute-start | bytes 786440 | tf_op jit(solution)/shard_map/ppermute | solution.py:292
  61.8 13.5 %collective-permute-start.11 = (bf16[32,2,16,128]{3,2,1,0:T(8,128)(2,1)S(1)}, bf16[32,2,16,128]{3,2,1,0:T(8,128)(2,1)S(1)}, u32[]{:S(2)}, u32[]{:S(2)}) collective-permute-start(bf16[32,2,16,128]{3,2,1,0:T(8,128)(2,1)S(1)} %get-tuple-element.42), channel_id=1, source_target_pairs={{0,192},{32,224},{64,0},{96,32},{128,64},{160,96},{192,128},{224,1... | collective-permute-start | bytes 786440 | tf_op jit(solution)/shard_map/ppermute | solution.py:292
  64.1 12.5 %collective-permute-start.10 = (bf16[32,2,16,128]{3,2,1,0:T(8,128)(2,1)S(1)}, bf16[32,2,16,128]{3,2,1,0:T(8,128)(2,1)S(1)}, u32[]{:S(2)}, u32[]{:S(2)}) collective-permute-start(bf16[32,2,16,128]{3,2,1,0:T(8,128)(2,1)S(1)} %get-tuple-element.43), channel_id=1, source_target_pairs={{0,128},{32,160},{64,192},{96,224},{128,0},{160,32},{192,64},{224,... | collective-permute-start | bytes 786440 | tf_op jit(solution)/shard_map/ppermute | solution.py:292
  (3 other events, 5.7 us)

commit v11 on v10

--- a/solution.py
+++ b/solution.py
@@ -13,7 +13,7 @@
 WHOLE = pl.BlockSpec(memory_space=pltpu.VMEM)
 
 
-def params(mebibytes=32):
+def params(mebibytes=24):
     return pltpu.CompilerParams(vmem_limit_bytes=mebibytes * 1024 * 1024)
 
 
@@ -43,7 +43,7 @@
         in_specs=[pl.BlockSpec(memory_space=pltpu.SMEM), WHOLE],
         out_specs=pl.BlockSpec(memory_space=pl.ANY),
         scratch_shapes=[pltpu.VMEM(shape, screened.dtype), pltpu.SemaphoreType.DMA((freqs,))],
-        compiler_params=params(16),
+        compiler_params=params(8),
     )(place, screened)
 
 
@@ -72,21 +72,14 @@
     )(table)
 
 
-def mix_kernel(pieces_in, mix_ref, out_ref, pieces_ref, sems):
+def mix_kernel(pieces_ref, mix_ref, out_ref):
     sources, local, rows, width = pieces_ref.shape
-    copies = []
-    for i in range(rows // (2 * BAND)):
-        part = pl.ds(i * 2 * BAND, 2 * BAND)
-        copies.append(pltpu.make_async_copy(pieces_in.at[:, :, part], pieces_ref.at[:, :, part], sems.at[i]))
-        copies[-1].start()
     freqs = sources * local
     places = out_ref.shape[1]
     pair = 2 * BAND
     tall = places * pair
     mix = mix_ref[...].reshape(4 * tall, freqs * BAND)
     for band in range(rows // BAND):
-        if band % 2 == 0:
-            copies[band // 2].wait()
         piece = pieces_ref[:, :, band * BAND : (band + 1) * BAND, :].reshape(freqs * BAND, width)
         both = jnp.dot(mix, piece, preferred_element_type=jnp.float32)
         for half in range(2):
@@ -103,9 +96,8 @@
     return pl.pallas_call(
         mix_kernel,
         out_shape=jax.ShapeDtypeStruct((2, times // 2, 2 * rows, width), jnp.bfloat16),
-        in_specs=[pl.BlockSpec(memory_space=pl.ANY), WHOLE],
+        in_specs=[WHOLE] * 2,
         out_specs=WHOLE,
-        scratch_shapes=[pltpu.VMEM(pieces.shape, pieces.dtype), pltpu.SemaphoreType.DMA((rows // (2 * BAND),))],
         compiler_params=params(),
     )(pieces, mix)
 
@@ -269,12 +261,11 @@
     listed = block_ids[:, :, None] * block_width + jnp.arange(block_width, dtype=jnp.int32)
     listed = jnp.where(slot[None, :, None] < block_counts[:, None, None], listed, -1).reshape(block_count, orbitals)
     choose = (wanted[None, :, None] == listed[:, None, :]).astype(jnp.bfloat16)
-    _, three_orbital = lax.optimization_barrier((slabs[0][1], three_orbital))
+    _, three_orbital = lax.optimization_barrier((slabs[0][0], three_orbital))
     values = three_orbital.reshape(block_count, row_block, states, orbitals)
     values = values.transpose(0, 2, 1, 3).reshape(block_count, states * row_block, orbitals)
     dense = jnp.einsum("bns,brs->bnr", choose, values, preferred_element_type=jnp.float32).astype(jnp.bfloat16)
 
-    slabs[0][1], pieces = lax.optimization_barrier((slabs[0][1], pieces))
     timed = transform(pieces, spread_table(table))
     run = functools.partial(contract, timed=timed, gains=gains, dense=dense, owners=aux_count)
     swap = [(f, f ^ 1) for f in range(freq_count)]

time: 97.3 us -> 96.7 us (level)
  waiting for transfers between devices: 21.3 us -> 19.1 us
    all_to_all x1, waiting for transfers between devices: 6.89 us -> 3.85 us  [shards(): lax.all_to_all(pieces, 'freq', split_axis=0, concat_axis=0, tiled=True)]
    ppermute x1, starting transfers between devices: 3.02 us -> 0.4 us  [shards(): taken = lax.ppermute(given, 'freq', swap)]
    transpose x1, local copies, waits for them, and re-layouts: 2.75 us -> 1.16 us  [shards(): values.transpose(0, 2, 1, 3)]
    unnamed x29 -> x31, local copies, waits for them, and re-layouts: 2.09 us -> 3.53 us
    ppermute x3, starting transfers between devices: 2.77 us -> 4.17 us  [shards(): slabs[1].append(lax.ppermute(ready, 'aux', across[i]))]
  transfers between devices with their start and end apart: 13 -> 13, of which waited for: 6 -> 6; matrix products, arithmetic and copies ran while one was open for 6% -> 4% of each run, Pallas kernels for 16% -> 16%
where the time goes in v11:
time: 96.7 us; the launch traced here: 96.5 us
  starting transfers between devices  28.7 us (30%)
  blocking collectives  20.3 us (21%)
  waiting for transfers between devices  19.1 us (20%)
  Pallas kernels  18.5 us (19%)
  local copies, waits for them, and re-layouts  6.49 us (7%)
  other arithmetic  1.79 us (2%)
  matrix products  1.3 us (1%)
    all_to_all x1, blocking collectives, shards(): lax.all_to_all(summed.astype(jnp.bfloat16), 'aux', split_axis=0, concat_a...  20.3 us
    pallas_call x4, Pallas kernels, contract(): pl.pallas_call(functools.partial(contract_kernel, jobs, part, bool(totals...  14 us
    all_to_all x1, starting transfers between devices, shards(): lax.all_to_all(pieces, 'freq', split_axis=0, concat_axis=0, tiled=True)  11.1 us
    ppermute x3, waiting for transfers between devices, shards(): lax.ppermute(sent[i], 'freq', chip_shift(i + 1))  9.98 us
    ppermute x3, starting transfers between devices, shards(): lax.ppermute(own, 'aux', across[i])  5.9 us
    ppermute x3, waiting for transfers between devices, shards(): lax.ppermute(own, 'aux', across[i])  5.22 us
    ppermute x3, starting transfers between devices, shards(): lax.ppermute(sent[i], 'freq', chip_shift(i + 1))  4.89 us
    ppermute x3, starting transfers between devices, shards(): slabs[1].append(lax.ppermute(ready, 'aux', across[i]))  4.17 us
  transfers between devices with their start and end apart: 13, of which 6 were waited for; matrix products, arithmetic and copies ran while one was open for 4% of the time, Pallas kernels for 16%

profile of v11, /device:TPU:32, one launch (start us, length us, event | category | flops | bytes accessed | tf_op | source)
XLA Modules:
  0.0 96.5 jit_solution(13700394352792598408)
XLA Ops:
  0.0 1.3 %copy.15 = bf16[16,8,16,128]{3,1,2,0:T(8,128)(2,1)S(1)} copy(bf16[16,8,16,128]{3,2,1,0:T(8,128)(2,1)} %bitcast.29) | data formatting | bytes 1048576
  2.8 1.5 %shard_map.82 = bf16[8,2,128,512]{3,2,1,0:T(8,128)(2,1)} custom-call(s32[1]{0:T(128)} %bitcast.place_ref, bf16[2,128,4096]{2,1,0:T(8,128)(2,1)S(1)} %copy-done), custom_call_target="tpu_custom_call" | custom-call | tf_op jit(solution)/shard_map/pallas_call | solution.py:40
  4.3 11.1 %all-to-all-start = ((bf16[8,2,128,512]{3,2,1,0:T(8,128)(2,1)}), bf16[8,2,128,512]{3,2,1,0:T(8,128)(2,1)}, u32[]{:S(2)}, u32[]{:S(2)}) async-start(bf16[8,2,128,512]{3,2,1,0:T(8,128)(2,1)} %shard_map.82), calls=%async_computation | async-start | bytes 4194304 | tf_op jit(solution)/shard_map/all_to_all | solution.py:240
  17.3 1.6 %collective-permute-start.1 = (bf16[128,1024]{1,0:T(8,128)(2,1)}, bf16[128,1024]{1,0:T(8,128)(2,1)S(1)}, u32[]{:S(2)}, u32[]{:S(2)}) collective-permute-start(bf16[128,1024]{1,0:T(8,128)(2,1)} %get-tuple-element.24), channel_id=1, source_target_pairs={{0,0},{1,1},{2,2},{3,3},{4,4},{5,5},{6,6},{7,7},{8,8},{9,9},{10,10... | collective-permute-start | bytes 786440 | tf_op jit(solution)/shard_map/ppermute | solution.py:232
  18.9 1.2 %copy.12 = bf16[2,16,64,512]{3,2,1,0:T(8,128)(2,1)S(1)} copy(bf16[2,16,64,512]{3,1,2,0:T(8,128)(2,1)S(1)} %bitcast.26) | data formatting | bytes 4194304 | tf_op jit(solution)/shard_map/transpose | solution.py:266
  20.1 1.7 %collective-permute-start.6 = (bf16[128,1024]{1,0:T(8,128)(2,1)S(1)}, bf16[128,1024]{1,0:T(8,128)(2,1)S(1)}, u32[]{:S(2)}, u32[]{:S(2)}) collective-permute-start(bf16[128,1024]{1,0:T(8,128)(2,1)S(1)} %collective-permute-done.refs_3_), channel_id=1, source_target_pairs={{24,0},{25,1},{26,2},{27,3},{28,4},{29,5},{30,6},{31,7},{0,8},{1,9... | collective-permute-start | bytes 786440 | tf_op jit(solution)/shard_map/ppermute | solution.py:230
  21.8 2.9 %collective-permute-start.4 = (bf16[128,1024]{1,0:T(8,128)(2,1)S(1)}, bf16[128,1024]{1,0:T(8,128)(2,1)S(1)}, u32[]{:S(2)}, u32[]{:S(2)}) collective-permute-start(bf16[128,1024]{1,0:T(8,128)(2,1)S(1)} %collective-permute-done.refs_3_), channel_id=1, source_target_pairs={{16,0},{17,1},{18,2},{19,3},{20,4},{21,5},{22,6},{23,7},{24,8},{25... | collective-permute-start | bytes 786440 | tf_op jit(solution)/shard_map/ppermute | solution.py:230
  24.7 1.3 %collective-permute-start.2 = (bf16[128,1024]{1,0:T(8,128)(2,1)S(1)}, bf16[128,1024]{1,0:T(8,128)(2,1)S(1)}, u32[]{:S(2)}, u32[]{:S(2)}) collective-permute-start(bf16[128,1024]{1,0:T(8,128)(2,1)S(1)} %collective-permute-done.refs_3_), channel_id=1, source_target_pairs={{8,0},{9,1},{10,2},{11,3},{12,4},{13,5},{14,6},{15,7},{16,8},{17,9... | collective-permute-start | bytes 786440 | tf_op jit(solution)/shard_map/ppermute | solution.py:230
  26.0 1.3 %fusion.2.refs_2_ = bf16[2,512,1024]{2,1,0:T(8,128)(2,1)S(1)} fusion(bf16[2,1024,512]{2,1,0:T(8,128)(2,1)S(1)} %bitcast.27, s32[2,512]{1,0:T(2,128)S(1)} %add_select_fusion, s32[512]{0:T(512)S(1)} %add.202), kind=kOutput, calls=%fused_computation.2 | convolution fusion | flops 1075314688 | bytes 4200448 | tf_op jit(solution)/shard_map/bns,brs->bnr/dot_general | solution.py:267
  28.9 4.8 %collective-permute-done.4.refs_5_ = bf16[128,1024]{1,0:T(8,128)(2,1)S(1)} collective-permute-done((bf16[128,1024]{1,0:T(8,128)(2,1)S(1)}, bf16[128,1024]{1,0:T(8,128)(2,1)S(1)}, u32[]{:S(2)}, u32[]{:S(2)}) %collective-permute-start.4) | collective-permute-done | bytes 262176 | tf_op jit(solution)/shard_map/ppermute | solution.py:230
  35.9 2.9 %collective-permute-start.3 = (bf16[128,1024]{1,0:T(8,128)(2,1)S(1)}, bf16[128,1024]{1,0:T(8,128)(2,1)S(1)}, u32[]{:S(2)}, u32[]{:S(2)}) collective-permute-start(bf16[128,1024]{1,0:T(8,128)(2,1)S(1)} %collective-permute-done.1.refs_3_), channel_id=1, source_target_pairs={{8,0},{9,1},{10,2},{11,3},{12,4},{13,5},{14,6},{15,7},{16,8},{17,9... | collective-permute-start | bytes 786440 | tf_op jit(solution)/shard_map/ppermute | solution.py:236
  38.9 3.9 %all-to-all-done.pieces_ref = bf16[8,2,128,512]{3,2,1,0:T(8,128)(2,1)} async-done(((bf16[8,2,128,512]{3,2,1,0:T(8,128)(2,1)}), bf16[8,2,128,512]{3,2,1,0:T(8,128)(2,1)}, u32[]{:S(2)}, u32[]{:S(2)}) %all-to-all-start) | async-done | bytes 2097184 | tf_op jit(solution)/shard_map/all_to_all | solution.py:240
  42.7 2.9 %shard_map.84.refs_0_ = bf16[2,4,256,512]{3,2,1,0:T(8,128)(2,1)S(1)} custom-call(bf16[8,2,128,512]{3,2,1,0:T(8,128)(2,1)} %all-to-all-done.pieces_ref, bf16[2,256,256]{2,1,0:T(8,128)(2,1)S(1)} %shard_map.83.mix_ref), custom_call_target="tpu_custom_call" | custom-call | tf_op jit(solution)/shard_map/pallas_call | solution.py:96
  45.7 6.5 %shard_map.85 = (f32[4,32,2,16,128]{4,3,2,1,0:T(8,128)S(1)}, f32[4,32,2,16,128]{4,3,2,1,0:T(8,128)S(1)}) custom-call(bf16[2,4,256,512]{3,2,1,0:T(8,128)(2,1)S(1)} %shard_map.84.refs_0_, f32[2,8,2048]{2,1,0:T(8,128)S(1)} %broadcast_bitcast_fusion.refs_1_, bf16[2,512,1024]{2,1,0:T(8,128)(2,1)S(1)} %fusion.2.refs_2_, bf16[128,1024]{1,0:T(8,128)(2,1)S(1)} %copy-done.2, ...), custom_call_target="tpu_custom_call" | custom-call | flops 4294967296 | bytes 16777216 | tf_op jit(solution)/shard_map/pallas_call | solution.py:176
  52.3 3.3 %shard_map.87 = bf16[4,32,2,16,128]{4,3,2,1,0:T(8,128)(2,1)S(1)} custom-call(bf16[2,4,256,512]{3,2,1,0:T(8,128)(2,1)S(1)} %shard_map.84.refs_0_, f32[2,8,2048]{2,1,0:T(8,128)S(1)} %broadcast_bitcast_fusion.refs_1_, bf16[2,512,1024]{2,1,0:T(8,128)(2,1)S(1)} %fusion.2.refs_2_, bf16[128,1024]{1,0:T(8,128)(2,1)S(1)} %collective-permute-done.1.refs_3_, ...), custom_call_target="tpu_custom_call" | custom-call | flops 2147483648 | bytes 8388608 | tf_op jit(solution)/shard_map/pallas_call | solution.py:176
  56.0 2.6 %shard_map.86 = f32[3,32,2,16,128]{4,3,2,1,0:T(8,128)S(1)} custom-call(bf16[2,4,256,512]{3,2,1,0:T(8,128)(2,1)S(1)} %shard_map.84.refs_0_, f32[2,8,2048]{2,1,0:T(8,128)S(1)} %broadcast_bitcast_fusion.refs_1_, bf16[2,512,1024]{2,1,0:T(8,128)(2,1)S(1)} %fusion.2.refs_2_, bf16[128,1024]{1,0:T(8,128)(2,1)S(1)} %collective-permute-done.1.refs_3_, ...), custom_call_target="tpu_custom_call" | custom-call | flops 1610612736 | bytes 6291456 | tf_op jit(solution)/shard_map/pallas_call | solution.py:176
  58.9 1.8 %collective-permute-start.9 = (bf16[32,2,16,128]{3,2,1,0:T(8,128)(2,1)S(1)}, bf16[32,2,16,128]{3,2,1,0:T(8,128)(2,1)S(1)}, u32[]{:S(2)}, u32[]{:S(2)}) collective-permute-start(bf16[32,2,16,128]{3,2,1,0:T(8,128)(2,1)S(1)} %get-tuple-element.34), channel_id=1, source_target_pairs={{0,64},{32,96},{64,128},{96,160},{128,192},{160,224},{192,0},{224,... | collective-permute-start | bytes 786440 | tf_op jit(solution)/shard_map/ppermute | solution.py:283
  60.7 1.5 %collective-permute-start.11 = (bf16[32,2,16,128]{3,2,1,0:T(8,128)(2,1)S(1)}, bf16[32,2,16,128]{3,2,1,0:T(8,128)(2,1)S(1)}, u32[]{:S(2)}, u32[]{:S(2)}) collective-permute-start(bf16[32,2,16,128]{3,2,1,0:T(8,128)(2,1)S(1)} %get-tuple-element.38), channel_id=1, source_target_pairs={{0,192},{32,224},{64,0},{96,32},{128,64},{160,96},{192,128},{224,1... | collective-permute-start | bytes 786440 | tf_op jit(solution)/shard_map/ppermute | solution.py:283
  62.2 1.6 %collective-permute-start.10 = (bf16[32,2,16,128]{3,2,1,0:T(8,128)(2,1)S(1)}, bf16[32,2,16,128]{3,2,1,0:T(8,128)(2,1)S(1)}, u32[]{:S(2)}, u32[]{:S(2)}) collective-permute-start(bf16[32,2,16,128]{3,2,1,0:T(8,128)(2,1)S(1)} %get-tuple-element.39), channel_id=1, source_target_pairs={{0,128},{32,160},{64,192},{96,224},{128,0},{160,32},{192,64},{224,... | collective-permute-start | bytes 786440 | tf_op jit(solution)/shard_map/ppermute | solution.py:283
  63.8 1.5 %shard_map.88 = f32[1,32,2,16,128]{4,3,2,1,0:T(8,128)S(1)} custom-call(bf16[2,4,256,512]{3,2,1,0:T(8,128)(2,1)S(1)} %shard_map.84.refs_0_, f32[2,8,2048]{2,1,0:T(8,128)S(1)} %broadcast_bitcast_fusion.refs_1_, bf16[2,512,1024]{2,1,0:T(8,128)(2,1)S(1)} %fusion.2.refs_2_, bf16[128,1024]{1,0:T(8,128)(2,1)S(1)} %collective-permute-done.1.refs_3_, ...), custom_call_target="tpu_custom_call" | custom-call | flops 536870912 | bytes 2097152 | tf_op jit(solution)/shard_map/pallas_call | solution.py:176
  65.3 3.3 %collective-permute-done.9 = bf16[32,2,16,128]{3,2,1,0:T(8,128)(2,1)S(1)} collective-permute-done((bf16[32,2,16,128]{3,2,1,0:T(8,128)(2,1)S(1)}, bf16[32,2,16,128]{3,2,1,0:T(8,128)(2,1)S(1)}, u32[]{:S(2)}, u32[]{:S(2)}) %collective-permute-start.9) | collective-permute-done | bytes 262176 | tf_op jit(solution)/shard_map/ppermute | solution.py:283
  68.6 1.2 %collective-permute-done.11 = bf16[32,2,16,128]{3,2,1,0:T(8,128)(2,1)S(1)} collective-permute-done((bf16[32,2,16,128]{3,2,1,0:T(8,128)(2,1)S(1)}, bf16[32,2,16,128]{3,2,1,0:T(8,128)(2,1)S(1)}, u32[]{:S(2)}, u32[]{:S(2)}) %collective-permute-start.11) | collective-permute-done | bytes 262176 | tf_op jit(solution)/shard_map/ppermute | solution.py:283
  69.8 5.5 %collective-permute-done.10 = bf16[32,2,16,128]{3,2,1,0:T(8,128)(2,1)S(1)} collective-permute-done((bf16[32,2,16,128]{3,2,1,0:T(8,128)(2,1)S(1)}, bf16[32,2,16,128]{3,2,1,0:T(8,128)(2,1)S(1)}, u32[]{:S(2)}, u32[]{:S(2)}) %collective-permute-start.10) | collective-permute-done | bytes 262176 | tf_op jit(solution)/shard_map/ppermute | solution.py:283
  75.5 20.3 %all_to_all.10 = bf16[32,2,16,128]{3,2,1,0:T(8,128)(2,1)S(1)} all-to-all(bf16[32,2,16,128]{3,2,1,0:T(8,128)(2,1)S(1)} %fusion.12), channel_id=1, replica_groups=mesh['freq'=8,'aux'=32] {'aux'}, dimensions={0} | all-to-all | bytes 524288 | tf_op jit(solution)/shard_map/all_to_all | solution.py:288
  (76 shorter events, 8.6 us)
Async XLA Ops:
  2.1 15.2 %collective-permute-start = (bf16[128,1024]{1,0:T(8,128)(2,1)S(1)}, bf16[128,1024]{1,0:T(8,128)(2,1)S(1)}, u32[]{:S(2)}, u32[]{:S(2)}) collective-permute-start(bf16[128,1024]{1,0:T(8,128)(2,1)S(1)} %get-tuple-element.40), channel_id=1, source_target_pairs={{0,0},{1,1},{2,2},{3,3},{4,4},{5,5},{6,6},{7,7},{8,8},{9,9},{10,10... | collective-permute-start | bytes 786440 | tf_op jit(solution)/shard_map/ppermute | solution.py:229
  4.3 11.2 %copy-start.13 = (s32[32]{0:T(128)S(1)}, s32[32]{0:T(128)}, u32[]{:S(2)}) copy-start(s32[32]{0:T(128)} %param.15) | copy-start | bytes 388
  4.3 11.3 %copy-start.11 = (s32[2,8]{1,0:T(2,128)S(1)}, s32[2,8]{1,0:T(2,128)}, u32[]{:S(2)}) copy-start(s32[2,8]{1,0:T(2,128)} %param.13) | copy-start | bytes 196
  4.3 11.7 %copy-start.10 = (f32[16,16]{1,0:T(8,128)S(1)}, f32[16,16]{1,0:T(8,128)}, u32[]{:S(2)}) copy-start(f32[16,16]{1,0:T(8,128)} %param.10) | copy-start | bytes 3076
  4.3 11.9 %copy-start.12 = (f32[16]{0:T(128)S(1)}, f32[16]{0:T(128)}, u32[]{:S(2)}) copy-start(f32[16]{0:T(128)} %param.9) | copy-start | bytes 196
  4.3 12.4 %copy-start.14 = (s32[2]{0:T(128)S(1)}, s32[2]{0:T(128)}, u32[]{:S(2)}) copy-start(s32[2]{0:T(128)} %param.14) | copy-start | bytes 28
  4.3 14.6 %copy-start.9 = (bf16[128,16,512]{2,1,0:T(8,128)(2,1)S(1)}, bf16[128,16,512]{2,1,0:T(8,128)(2,1)}, u32[]{:S(2)}) copy-start(bf16[128,16,512]{2,1,0:T(8,128)(2,1)} %param.12) | copy-start | bytes 6291460
  4.3 38.4 %all-to-all-start = ((bf16[8,2,128,512]{3,2,1,0:T(8,128)(2,1)}), bf16[8,2,128,512]{3,2,1,0:T(8,128)(2,1)}, u32[]{:S(2)}, u32[]{:S(2)}) async-start(bf16[8,2,128,512]{3,2,1,0:T(8,128)(2,1)} %shard_map.82), calls=%async_computation | async-start | bytes 4194304 | tf_op jit(solution)/shard_map/all_to_all | solution.py:240
  17.3 7.3 %copy-start.1 = (bf16[128,1024]{1,0:T(8,128)(2,1)}, bf16[128,1024]{1,0:T(8,128)(2,1)S(1)}, u32[]{:S(2)}) copy-start(bf16[128,1024]{1,0:T(8,128)(2,1)S(1)} %collective-permute-done.refs_3_) | copy-start | bytes 786436
  17.3 10.0 %collective-permute-start.1 = (bf16[128,1024]{1,0:T(8,128)(2,1)}, bf16[128,1024]{1,0:T(8,128)(2,1)S(1)}, u32[]{:S(2)}, u32[]{:S(2)}) collective-permute-start(bf16[128,1024]{1,0:T(8,128)(2,1)} %get-tuple-element.24), channel_id=1, source_target_pairs={{0,0},{1,1},{2,2},{3,3},{4,4},{5,5},{6,6},{7,7},{8,8},{9,9},{10,10... | collective-permute-start | bytes 786440 | tf_op jit(solution)/shard_map/ppermute | solution.py:232
  20.1 7.7 %collective-permute-start.6 = (bf16[128,1024]{1,0:T(8,128)(2,1)S(1)}, bf16[128,1024]{1,0:T(8,128)(2,1)S(1)}, u32[]{:S(2)}, u32[]{:S(2)}) collective-permute-start(bf16[128,1024]{1,0:T(8,128)(2,1)S(1)} %collective-permute-done.refs_3_), channel_id=1, source_target_pairs={{24,0},{25,1},{26,2},{27,3},{28,4},{29,5},{30,6},{31,7},{0,8},{1,9... | collective-permute-start | bytes 786440 | tf_op jit(solution)/shard_map/ppermute | solution.py:230
  21.8 11.9 %collective-permute-start.4 = (bf16[128,1024]{1,0:T(8,128)(2,1)S(1)}, bf16[128,1024]{1,0:T(8,128)(2,1)S(1)}, u32[]{:S(2)}, u32[]{:S(2)}) collective-permute-start(bf16[128,1024]{1,0:T(8,128)(2,1)S(1)} %collective-permute-done.refs_3_), channel_id=1, source_target_pairs={{16,0},{17,1},{18,2},{19,3},{20,4},{21,5},{22,6},{23,7},{24,8},{25... | collective-permute-start | bytes 786440 | tf_op jit(solution)/shard_map/ppermute | solution.py:230
  24.7 10.5 %collective-permute-start.2 = (bf16[128,1024]{1,0:T(8,128)(2,1)S(1)}, bf16[128,1024]{1,0:T(8,128)(2,1)S(1)}, u32[]{:S(2)}, u32[]{:S(2)}) collective-permute-start(bf16[128,1024]{1,0:T(8,128)(2,1)S(1)} %collective-permute-done.refs_3_), channel_id=1, source_target_pairs={{8,0},{9,1},{10,2},{11,3},{12,4},{13,5},{14,6},{15,7},{16,8},{17,9... | collective-permute-start | bytes 786440 | tf_op jit(solution)/shard_map/ppermute | solution.py:230
  28.5 23.7 %collective-permute-start.7 = (bf16[128,1024]{1,0:T(8,128)(2,1)S(1)}, bf16[128,1024]{1,0:T(8,128)(2,1)S(1)}, u32[]{:S(2)}, u32[]{:S(2)}) collective-permute-start(bf16[128,1024]{1,0:T(8,128)(2,1)S(1)} %collective-permute-done.1.refs_3_), channel_id=1, source_target_pairs={{24,0},{25,1},{26,2},{27,3},{28,4},{29,5},{30,6},{31,7},{0,8},{1,9... | collective-permute-start | bytes 786440 | tf_op jit(solution)/shard_map/ppermute | solution.py:236
  34.3 17.9 %collective-permute-start.5 = (bf16[128,1024]{1,0:T(8,128)(2,1)S(1)}, bf16[128,1024]{1,0:T(8,128)(2,1)S(1)}, u32[]{:S(2)}, u32[]{:S(2)}) collective-permute-start(bf16[128,1024]{1,0:T(8,128)(2,1)S(1)} %collective-permute-done.1.refs_3_), channel_id=1, source_target_pairs={{16,0},{17,1},{18,2},{19,3},{20,4},{21,5},{22,6},{23,7},{24,8},{25... | collective-permute-start | bytes 786440 | tf_op jit(solution)/shard_map/ppermute | solution.py:236
  35.9 16.3 %collective-permute-start.3 = (bf16[128,1024]{1,0:T(8,128)(2,1)S(1)}, bf16[128,1024]{1,0:T(8,128)(2,1)S(1)}, u32[]{:S(2)}, u32[]{:S(2)}) collective-permute-start(bf16[128,1024]{1,0:T(8,128)(2,1)S(1)} %collective-permute-done.1.refs_3_), channel_id=1, source_target_pairs={{8,0},{9,1},{10,2},{11,3},{12,4},{13,5},{14,6},{15,7},{16,8},{17,9... | collective-permute-start | bytes 786440 | tf_op jit(solution)/shard_map/ppermute | solution.py:236
  42.7 2.9 %copy-start.2 = (bf16[128,1024]{1,0:T(8,128)(2,1)S(1)}, bf16[128,1024]{1,0:T(8,128)(2,1)}, u32[]{:S(2)}) copy-start(bf16[128,1024]{1,0:T(8,128)(2,1)} %copy-done.1) | copy-start | bytes 786436
  42.7 3.0 %copy-start.4 = (bf16[128,1024]{1,0:T(8,128)(2,1)S(1)}, bf16[128,1024]{1,0:T(8,128)(2,1)}, u32[]{:S(2)}) copy-start(bf16[128,1024]{1,0:T(8,128)(2,1)} %copy-done.3) | copy-start | bytes 786436
  42.7 3.0 %copy-start.6 = (bf16[128,1024]{1,0:T(8,128)(2,1)S(1)}, bf16[128,1024]{1,0:T(8,128)(2,1)}, u32[]{:S(2)}) copy-start(bf16[128,1024]{1,0:T(8,128)(2,1)} %copy-done.5) | copy-start | bytes 786436
  42.7 3.0 %copy-start.8 = (bf16[128,1024]{1,0:T(8,128)(2,1)S(1)}, bf16[128,1024]{1,0:T(8,128)(2,1)}, u32[]{:S(2)}) copy-start(bf16[128,1024]{1,0:T(8,128)(2,1)} %copy-done.7) | copy-start | bytes 786436
  55.6 3.1 %collective-permute-start.8 = (bf16[4,32,2,16,128]{4,3,2,1,0:T(8,128)(2,1)S(1)}, bf16[4,32,2,16,128]{4,3,2,1,0:T(8,128)(2,1)S(1)}, u32[]{:S(2)}, u32[]{:S(2)}) collective-permute-start(bf16[4,32,2,16,128]{4,3,2,1,0:T(8,128)(2,1)S(1)} %shard_map.87), channel_id=1, source_target_pairs={{0,32},{32,0},{64,96},{96,64},{128,160},{160,128},{192,224},{224,1... | collective-permute-start | bytes 3145736 | tf_op jit(solution)/shard_map/ppermute | solution.py:275
  58.9 9.7 %collective-permute-start.9 = (bf16[32,2,16,128]{3,2,1,0:T(8,128)(2,1)S(1)}, bf16[32,2,16,128]{3,2,1,0:T(8,128)(2,1)S(1)}, u32[]{:S(2)}, u32[]{:S(2)}) collective-permute-start(bf16[32,2,16,128]{3,2,1,0:T(8,128)(2,1)S(1)} %get-tuple-element.34), channel_id=1, source_target_pairs={{0,64},{32,96},{64,128},{96,160},{128,192},{160,224},{192,0},{224,... | collective-permute-start | bytes 786440 | tf_op jit(solution)/shard_map/ppermute | solution.py:283
  60.7 9.1 %collective-permute-start.11 = (bf16[32,2,16,128]{3,2,1,0:T(8,128)(2,1)S(1)}, bf16[32,2,16,128]{3,2,1,0:T(8,128)(2,1)S(1)}, u32[]{:S(2)}, u32[]{:S(2)}) collective-permute-start(bf16[32,2,16,128]{3,2,1,0:T(8,128)(2,1)S(1)} %get-tuple-element.38), channel_id=1, source_target_pairs={{0,192},{32,224},{64,0},{96,32},{128,64},{160,96},{192,128},{224,1... | collective-permute-start | bytes 786440 | tf_op jit(solution)/shard_map/ppermute | solution.py:283
  62.2 13.1 %collective-permute-start.10 = (bf16[32,2,16,128]{3,2,1,0:T(8,128)(2,1)S(1)}, bf16[32,2,16,128]{3,2,1,0:T(8,128)(2,1)S(1)}, u32[]{:S(2)}, u32[]{:S(2)}) collective-permute-start(bf16[32,2,16,128]{3,2,1,0:T(8,128)(2,1)S(1)} %get-tuple-element.39), channel_id=1, source_target_pairs={{0,128},{32,160},{64,192},{96,224},{128,0},{160,32},{192,64},{224,... | collective-permute-start | bytes 786440 | tf_op jit(solution)/shard_map/ppermute | solution.py:283
  (4 other events, 4.9 us)

commit v12 on v11

--- a/solution.py
+++ b/solution.py
@@ -225,14 +225,11 @@
     flat_state = three_state.reshape(rows, states * targets)
     flat_state, screened = lax.optimization_barrier((flat_state, screened))
     span = states * targets // 2
-    parts = [flat_state[:, part * span : (part + 1) * span] for part in range(2)]
-    own = lax.ppermute(parts[0], ("freq", "aux"), along)
-    slabs = [[own] + [lax.ppermute(own, "aux", across[i]) for i in range(1, height)]]
-    parts[1], slabs[0][0] = lax.optimization_barrier((parts[1], slabs[0][0]))
-    own = lax.ppermute(parts[1], ("freq", "aux"), along)
-    slabs.append([own])
+    parts = jnp.stack([flat_state[:, part * span : (part + 1) * span] for part in range(2)])
+    own = lax.ppermute(parts, ("freq", "aux"), along)
+    slabs = [[own[0]] + [lax.ppermute(own[0], "aux", across[i]) for i in range(1, height)], [own[1]]]
     for i in range(1, height):
-        ready, slabs[0][i] = lax.optimization_barrier((own, slabs[0][i]))
+        ready, slabs[0][i] = lax.optimization_barrier((own[1], slabs[0][i]))
         slabs[1].append(lax.ppermute(ready, "aux", across[i]))
 
     place = lax.axis_index("aux").astype(jnp.int32).reshape(1)

time: 96.7 us -> 98.4 us (1.018)
  waiting for transfers between devices: 19.1 us -> 20.6 us
  blocking collectives: 20.3 us -> 21.4 us
  starting transfers between devices: 28.7 us -> 27.6 us
    all_to_all x1, waiting for transfers between devices: 3.85 us -> 7.15 us  [shards(): lax.all_to_all(pieces, 'freq', split_axis=0, concat_axis=0, tiled=True)]
    ppermute x5 -> x4, waiting for transfers between devices: 5.22 us -> 3.42 us  [the longest x3 3.42 us: shards(): lax.ppermute(own[0], 'aux', across[i])]
    all_to_all x1, blocking collectives: 20.3 us -> 21.4 us  [shards(): lax.all_to_all(summed.astype(jnp.bfloat16), 'aux', split_axis=0, concat_a...]
    all_to_all x1, starting transfers between devices: 11.1 us -> 10.1 us  [shards(): lax.all_to_all(pieces, 'freq', split_axis=0, concat_axis=0, tiled=True)]
    ppermute x5 -> x4, starting transfers between devices: 8.18 us -> 7.59 us  [the longest x3 5.9 us: shards(): lax.ppermute(own[0], 'aux', across[i])]
  transfers between devices with their start and end apart: 13 -> 12, of which waited for: 6 -> 5; matrix products, arithmetic and copies ran while one was open for 4% -> 4% of each run, Pallas kernels for 16% -> 15%
where the time goes in v12:
time: 98.4 us; the launch traced here: 98.2 us
  starting transfers between devices  27.6 us (28%)
  blocking collectives  21.4 us (22%)
  waiting for transfers between devices  20.6 us (21%)
  Pallas kernels  18.4 us (19%)
  local copies, waits for them, and re-layouts  5.79 us (6%)
  other arithmetic  2.63 us (3%)
  matrix products  1.3 us (1%)
    all_to_all x1, blocking collectives, shards(): lax.all_to_all(summed.astype(jnp.bfloat16), 'aux', split_axis=0, concat_a...  21.4 us
    pallas_call x4, Pallas kernels, contract(): pl.pallas_call(functools.partial(contract_kernel, jobs, part, bool(totals...  14 us
    all_to_all x1, starting transfers between devices, shards(): lax.all_to_all(pieces, 'freq', split_axis=0, concat_axis=0, tiled=True)  10.1 us
    ppermute x3, waiting for transfers between devices, shards(): lax.ppermute(sent[i], 'freq', chip_shift(i + 1))  10.1 us
    all_to_all x1, waiting for transfers between devices, shards(): lax.all_to_all(pieces, 'freq', split_axis=0, concat_axis=0, tiled=True)  7.15 us
    ppermute x3, starting transfers between devices, shards(): lax.ppermute(own[0], 'aux', across[i])  5.9 us
    ppermute x3, starting transfers between devices, shards(): lax.ppermute(sent[i], 'freq', chip_shift(i + 1))  5.56 us
    ppermute x3, starting transfers between devices, shards(): slabs[1].append(lax.ppermute(ready, 'aux', across[i]))  4.24 us
  transfers between devices with their start and end apart: 12, of which 5 were waited for; matrix products, arithmetic and copies ran while one was open for 4% of the time, Pallas kernels for 15%

profile of v12, /device:TPU:32, one launch (start us, length us, event | category | flops | bytes accessed | tf_op | source)
XLA Modules:
  0.0 98.2 jit_solution(2638973526694942422)
XLA Ops:
  0.0 1.3 %copy.15 = bf16[16,8,16,128]{3,1,2,0:T(8,128)(2,1)S(1)} copy(bf16[16,8,16,128]{3,2,1,0:T(8,128)(2,1)} %bitcast.37) | data formatting | bytes 1048576
  2.2 1.7 %collective-permute-start = (bf16[2,128,1024]{2,1,0:T(8,128)(2,1)}, bf16[2,128,1024]{2,1,0:T(8,128)(2,1)S(1)}, u32[]{:S(2)}, u32[]{:S(2)}) collective-permute-start(bf16[2,128,1024]{2,1,0:T(8,128)(2,1)} %pad_maximum_fusion), channel_id=1, source_target_pairs={{0,0},{1,1},{2,2},{3,3},{4,4},{5,5},{6,6},{7,7},{8,8},{9,9},{10,10... | collective-permute-start | bytes 1572872 | tf_op jit(solution)/shard_map/ppermute | solution.py:229
  3.9 1.4 %shard_map.82 = bf16[8,2,128,512]{3,2,1,0:T(8,128)(2,1)} custom-call(s32[1]{0:T(128)} %bitcast.place_ref, bf16[2,128,4096]{2,1,0:T(8,128)(2,1)S(1)} %copy-done), custom_call_target="tpu_custom_call" | custom-call | tf_op jit(solution)/shard_map/pallas_call | solution.py:40
  5.4 10.1 %all-to-all-start = ((bf16[8,2,128,512]{3,2,1,0:T(8,128)(2,1)}), bf16[8,2,128,512]{3,2,1,0:T(8,128)(2,1)}, u32[]{:S(2)}, u32[]{:S(2)}) async-start(bf16[8,2,128,512]{3,2,1,0:T(8,128)(2,1)} %shard_map.82), calls=%async_computation | async-start | bytes 4194304 | tf_op jit(solution)/shard_map/all_to_all | solution.py:237
  17.5 1.7 %collective-permute-start.5 = (bf16[128,1024]{1,0:T(8,128)(2,1)S(1)}, bf16[128,1024]{1,0:T(8,128)(2,1)S(1)}, u32[]{:S(2)}, u32[]{:S(2)}) collective-permute-start(bf16[128,1024]{1,0:T(8,128)(2,1)S(1)} %get-tuple-element.37.refs_3_), channel_id=1, source_target_pairs={{24,0},{25,1},{26,2},{27,3},{28,4},{29,5},{30,6},{31,7},{0,8},{1,9... | collective-permute-start | bytes 786440 | tf_op jit(solution)/shard_map/ppermute | solution.py:230
  19.1 2.9 %collective-permute-start.3 = (bf16[128,1024]{1,0:T(8,128)(2,1)S(1)}, bf16[128,1024]{1,0:T(8,128)(2,1)S(1)}, u32[]{:S(2)}, u32[]{:S(2)}) collective-permute-start(bf16[128,1024]{1,0:T(8,128)(2,1)S(1)} %get-tuple-element.37.refs_3_), channel_id=1, source_target_pairs={{16,0},{17,1},{18,2},{19,3},{20,4},{21,5},{22,6},{23,7},{24,8},{25... | collective-permute-start | bytes 786440 | tf_op jit(solution)/shard_map/ppermute | solution.py:230
  22.0 1.3 %collective-permute-start.1 = (bf16[128,1024]{1,0:T(8,128)(2,1)S(1)}, bf16[128,1024]{1,0:T(8,128)(2,1)S(1)}, u32[]{:S(2)}, u32[]{:S(2)}) collective-permute-start(bf16[128,1024]{1,0:T(8,128)(2,1)S(1)} %get-tuple-element.37.refs_3_), channel_id=1, source_target_pairs={{8,0},{9,1},{10,2},{11,3},{12,4},{13,5},{14,6},{15,7},{16,8},{17,9... | collective-permute-start | bytes 786440 | tf_op jit(solution)/shard_map/ppermute | solution.py:230
  23.4 1.2 %copy.12 = bf16[2,16,64,512]{3,2,1,0:T(8,128)(2,1)S(1)} copy(bf16[2,16,64,512]{3,1,2,0:T(8,128)(2,1)S(1)} %bitcast.34) | data formatting | bytes 4194304 | tf_op jit(solution)/shard_map/transpose | solution.py:263
  24.6 1.3 %fusion.2.refs_2_ = bf16[2,512,1024]{2,1,0:T(8,128)(2,1)S(1)} fusion(bf16[2,1024,512]{2,1,0:T(8,128)(2,1)S(1)} %bitcast.35, s32[2,512]{1,0:T(2,128)S(1)} %add_select_fusion, s32[512]{0:T(512)S(1)} %add.202), kind=kOutput, calls=%fused_computation.2 | convolution fusion | flops 1075314688 | bytes 4200448 | tf_op jit(solution)/shard_map/bns,brs->bnr/dot_general | solution.py:264
  27.3 3.4 %collective-permute-done.3.refs_5_ = bf16[128,1024]{1,0:T(8,128)(2,1)S(1)} collective-permute-done((bf16[128,1024]{1,0:T(8,128)(2,1)S(1)}, bf16[128,1024]{1,0:T(8,128)(2,1)S(1)}, u32[]{:S(2)}, u32[]{:S(2)}) %collective-permute-start.3) | collective-permute-done | bytes 262176 | tf_op jit(solution)/shard_map/ppermute | solution.py:230
  31.4 0.9 collective-permute-start.4
  33.0 2.7 %collective-permute-start.2 = (bf16[128,1024]{1,0:T(8,128)(2,1)S(1)}, bf16[128,1024]{1,0:T(8,128)(2,1)S(1)}, u32[]{:S(2)}, u32[]{:S(2)}) collective-permute-start(bf16[128,1024]{1,0:T(8,128)(2,1)S(1)} %get-tuple-element.23.refs_3_), channel_id=1, source_target_pairs={{8,0},{9,1},{10,2},{11,3},{12,4},{13,5},{14,6},{15,7},{16,8},{17,9... | collective-permute-start | bytes 786440 | tf_op jit(solution)/shard_map/ppermute | solution.py:233
  35.7 7.1 %all-to-all-done.pieces_ref = bf16[8,2,128,512]{3,2,1,0:T(8,128)(2,1)} async-done(((bf16[8,2,128,512]{3,2,1,0:T(8,128)(2,1)}), bf16[8,2,128,512]{3,2,1,0:T(8,128)(2,1)}, u32[]{:S(2)}, u32[]{:S(2)}) %all-to-all-start) | async-done | bytes 2097184 | tf_op jit(solution)/shard_map/all_to_all | solution.py:237
  42.9 2.9 %shard_map.84.refs_0_ = bf16[2,4,256,512]{3,2,1,0:T(8,128)(2,1)S(1)} custom-call(bf16[8,2,128,512]{3,2,1,0:T(8,128)(2,1)} %all-to-all-done.pieces_ref, bf16[2,256,256]{2,1,0:T(8,128)(2,1)S(1)} %shard_map.83.mix_ref), custom_call_target="tpu_custom_call" | custom-call | tf_op jit(solution)/shard_map/pallas_call | solution.py:96
  45.8 6.5 %shard_map.85 = (f32[4,32,2,16,128]{4,3,2,1,0:T(8,128)S(1)}, f32[4,32,2,16,128]{4,3,2,1,0:T(8,128)S(1)}) custom-call(bf16[2,4,256,512]{3,2,1,0:T(8,128)(2,1)S(1)} %shard_map.84.refs_0_, f32[2,8,2048]{2,1,0:T(8,128)S(1)} %broadcast_bitcast_fusion.refs_1_, bf16[2,512,1024]{2,1,0:T(8,128)(2,1)S(1)} %fusion.2.refs_2_, bf16[128,1024]{1,0:T(8,128)(2,1)S(1)} %copy-done.2, ...), custom_call_target="tpu_custom_call" | custom-call | flops 4294967296 | bytes 16777216 | tf_op jit(solution)/shard_map/pallas_call | solution.py:176
  52.4 3.3 %shard_map.87 = bf16[4,32,2,16,128]{4,3,2,1,0:T(8,128)(2,1)S(1)} custom-call(bf16[2,4,256,512]{3,2,1,0:T(8,128)(2,1)S(1)} %shard_map.84.refs_0_, f32[2,8,2048]{2,1,0:T(8,128)S(1)} %broadcast_bitcast_fusion.refs_1_, bf16[2,512,1024]{2,1,0:T(8,128)(2,1)S(1)} %fusion.2.refs_2_, bf16[128,1024]{1,0:T(8,128)(2,1)S(1)} %get-tuple-element.23.refs_3_, ...), custom_call_target="tpu_custom_call" | custom-call | flops 2147483648 | bytes 8388608 | tf_op jit(solution)/shard_map/pallas_call | solution.py:176
  55.8 2.6 %shard_map.86 = f32[3,32,2,16,128]{4,3,2,1,0:T(8,128)S(1)} custom-call(bf16[2,4,256,512]{3,2,1,0:T(8,128)(2,1)S(1)} %shard_map.84.refs_0_, f32[2,8,2048]{2,1,0:T(8,128)S(1)} %broadcast_bitcast_fusion.refs_1_, bf16[2,512,1024]{2,1,0:T(8,128)(2,1)S(1)} %fusion.2.refs_2_, bf16[128,1024]{1,0:T(8,128)(2,1)S(1)} %get-tuple-element.23.refs_3_, ...), custom_call_target="tpu_custom_call" | custom-call | flops 1610612736 | bytes 6291456 | tf_op jit(solution)/shard_map/pallas_call | solution.py:176
  59.4 2.8 %collective-permute-start.10 = (bf16[32,2,16,128]{3,2,1,0:T(8,128)(2,1)S(1)}, bf16[32,2,16,128]{3,2,1,0:T(8,128)(2,1)S(1)}, u32[]{:S(2)}, u32[]{:S(2)}) collective-permute-start(bf16[32,2,16,128]{3,2,1,0:T(8,128)(2,1)S(1)} %get-tuple-element.34), channel_id=1, source_target_pairs={{0,192},{32,224},{64,0},{96,32},{128,64},{160,96},{192,128},{224,1... | collective-permute-start | bytes 786440 | tf_op jit(solution)/shard_map/ppermute | solution.py:280
  62.2 2.1 %collective-permute-start.9 = (bf16[32,2,16,128]{3,2,1,0:T(8,128)(2,1)S(1)}, bf16[32,2,16,128]{3,2,1,0:T(8,128)(2,1)S(1)}, u32[]{:S(2)}, u32[]{:S(2)}) collective-permute-start(bf16[32,2,16,128]{3,2,1,0:T(8,128)(2,1)S(1)} %get-tuple-element.35), channel_id=1, source_target_pairs={{0,128},{32,160},{64,192},{96,224},{128,0},{160,32},{192,64},{224,... | collective-permute-start | bytes 786440 | tf_op jit(solution)/shard_map/ppermute | solution.py:280
  64.3 1.5 %shard_map.88 = f32[1,32,2,16,128]{4,3,2,1,0:T(8,128)S(1)} custom-call(bf16[2,4,256,512]{3,2,1,0:T(8,128)(2,1)S(1)} %shard_map.84.refs_0_, f32[2,8,2048]{2,1,0:T(8,128)S(1)} %broadcast_bitcast_fusion.refs_1_, bf16[2,512,1024]{2,1,0:T(8,128)(2,1)S(1)} %fusion.2.refs_2_, bf16[128,1024]{1,0:T(8,128)(2,1)S(1)} %get-tuple-element.23.refs_3_, ...), custom_call_target="tpu_custom_call" | custom-call | flops 536870912 | bytes 2097152 | tf_op jit(solution)/shard_map/pallas_call | solution.py:176
  65.8 3.3 %collective-permute-done.8 = bf16[32,2,16,128]{3,2,1,0:T(8,128)(2,1)S(1)} collective-permute-done((bf16[32,2,16,128]{3,2,1,0:T(8,128)(2,1)S(1)}, bf16[32,2,16,128]{3,2,1,0:T(8,128)(2,1)S(1)}, u32[]{:S(2)}, u32[]{:S(2)}) %collective-permute-start.8) | collective-permute-done | bytes 262176 | tf_op jit(solution)/shard_map/ppermute | solution.py:280
  69.1 5.0 %collective-permute-done.10 = bf16[32,2,16,128]{3,2,1,0:T(8,128)(2,1)S(1)} collective-permute-done((bf16[32,2,16,128]{3,2,1,0:T(8,128)(2,1)S(1)}, bf16[32,2,16,128]{3,2,1,0:T(8,128)(2,1)S(1)}, u32[]{:S(2)}, u32[]{:S(2)}) %collective-permute-start.10) | collective-permute-done | bytes 262176 | tf_op jit(solution)/shard_map/ppermute | solution.py:280
  74.1 1.8 %collective-permute-done.9 = bf16[32,2,16,128]{3,2,1,0:T(8,128)(2,1)S(1)} collective-permute-done((bf16[32,2,16,128]{3,2,1,0:T(8,128)(2,1)S(1)}, bf16[32,2,16,128]{3,2,1,0:T(8,128)(2,1)S(1)}, u32[]{:S(2)}, u32[]{:S(2)}) %collective-permute-start.9) | collective-permute-done | bytes 262176 | tf_op jit(solution)/shard_map/ppermute | solution.py:280
  76.1 21.4 %all_to_all.10 = bf16[32,2,16,128]{3,2,1,0:T(8,128)(2,1)S(1)} all-to-all(bf16[32,2,16,128]{3,2,1,0:T(8,128)(2,1)S(1)} %fusion.12), channel_id=1, replica_groups=mesh['freq'=8,'aux'=32] {'aux'}, dimensions={0} | all-to-all | bytes 524288 | tf_op jit(solution)/shard_map/all_to_all | solution.py:285
  (76 shorter events, 7.4 us)
Async XLA Ops:
  0.0 3.9 %copy-start = (bf16[2,128,4096]{2,1,0:T(8,128)(2,1)S(1)}, bf16[2,128,4096]{2,1,0:T(8,128)(2,1)}, u32[]{:S(2)}) copy-start(bf16[2,128,4096]{2,1,0:T(8,128)(2,1)} %screened_ref) | copy-start | bytes 6291460
  2.2 15.2 %collective-permute-start = (bf16[2,128,1024]{2,1,0:T(8,128)(2,1)}, bf16[2,128,1024]{2,1,0:T(8,128)(2,1)S(1)}, u32[]{:S(2)}, u32[]{:S(2)}) collective-permute-start(bf16[2,128,1024]{2,1,0:T(8,128)(2,1)} %pad_maximum_fusion), channel_id=1, source_target_pairs={{0,0},{1,1},{2,2},{3,3},{4,4},{5,5},{6,6},{7,7},{8,8},{9,9},{10,10... | collective-permute-start | bytes 1572872 | tf_op jit(solution)/shard_map/ppermute | solution.py:229
  5.4 10.2 %copy-start.13 = (s32[2]{0:T(128)S(1)}, s32[2]{0:T(128)}, u32[]{:S(2)}) copy-start(s32[2]{0:T(128)} %param.14) | copy-start | bytes 28
  5.4 10.3 %copy-start.14 = (s32[32]{0:T(128)S(1)}, s32[32]{0:T(128)}, u32[]{:S(2)}) copy-start(s32[32]{0:T(128)} %param.15) | copy-start | bytes 388
  5.4 10.4 %copy-start.11 = (s32[2,8]{1,0:T(2,128)S(1)}, s32[2,8]{1,0:T(2,128)}, u32[]{:S(2)}) copy-start(s32[2,8]{1,0:T(2,128)} %param.13) | copy-start | bytes 196
  5.4 11.2 %copy-start.12 = (f32[16]{0:T(128)S(1)}, f32[16]{0:T(128)}, u32[]{:S(2)}) copy-start(f32[16]{0:T(128)} %param.9) | copy-start | bytes 196
  5.4 11.6 %copy-start.10 = (f32[16,16]{1,0:T(8,128)S(1)}, f32[16,16]{1,0:T(8,128)}, u32[]{:S(2)}) copy-start(f32[16,16]{1,0:T(8,128)} %param.10) | copy-start | bytes 3076
  5.4 18.0 %copy-start.9 = (bf16[128,16,512]{2,1,0:T(8,128)(2,1)S(1)}, bf16[128,16,512]{2,1,0:T(8,128)(2,1)}, u32[]{:S(2)}) copy-start(bf16[128,16,512]{2,1,0:T(8,128)(2,1)} %param.12) | copy-start | bytes 6291460
  5.4 37.4 %all-to-all-start = ((bf16[8,2,128,512]{3,2,1,0:T(8,128)(2,1)}), bf16[8,2,128,512]{3,2,1,0:T(8,128)(2,1)}, u32[]{:S(2)}, u32[]{:S(2)}) async-start(bf16[8,2,128,512]{3,2,1,0:T(8,128)(2,1)} %shard_map.82), calls=%async_computation | async-start | bytes 4194304 | tf_op jit(solution)/shard_map/all_to_all | solution.py:237
  17.5 7.1 %copy-start.1 = (bf16[128,1024]{1,0:T(8,128)(2,1)}, bf16[128,1024]{1,0:T(8,128)(2,1)S(1)}, u32[]{:S(2)}) copy-start(bf16[128,1024]{1,0:T(8,128)(2,1)S(1)} %get-tuple-element.37.refs_3_) | copy-start | bytes 786436
  17.5 8.4 %collective-permute-start.5 = (bf16[128,1024]{1,0:T(8,128)(2,1)S(1)}, bf16[128,1024]{1,0:T(8,128)(2,1)S(1)}, u32[]{:S(2)}, u32[]{:S(2)}) collective-permute-start(bf16[128,1024]{1,0:T(8,128)(2,1)S(1)} %get-tuple-element.37.refs_3_), channel_id=1, source_target_pairs={{24,0},{25,1},{26,2},{27,3},{28,4},{29,5},{30,6},{31,7},{0,8},{1,9... | collective-permute-start | bytes 786440 | tf_op jit(solution)/shard_map/ppermute | solution.py:230
  19.1 11.6 %collective-permute-start.3 = (bf16[128,1024]{1,0:T(8,128)(2,1)S(1)}, bf16[128,1024]{1,0:T(8,128)(2,1)S(1)}, u32[]{:S(2)}, u32[]{:S(2)}) collective-permute-start(bf16[128,1024]{1,0:T(8,128)(2,1)S(1)} %get-tuple-element.37.refs_3_), channel_id=1, source_target_pairs={{16,0},{17,1},{18,2},{19,3},{20,4},{21,5},{22,6},{23,7},{24,8},{25... | collective-permute-start | bytes 786440 | tf_op jit(solution)/shard_map/ppermute | solution.py:230
  22.0 10.2 %collective-permute-start.1 = (bf16[128,1024]{1,0:T(8,128)(2,1)S(1)}, bf16[128,1024]{1,0:T(8,128)(2,1)S(1)}, u32[]{:S(2)}, u32[]{:S(2)}) collective-permute-start(bf16[128,1024]{1,0:T(8,128)(2,1)S(1)} %get-tuple-element.37.refs_3_), channel_id=1, source_target_pairs={{8,0},{9,1},{10,2},{11,3},{12,4},{13,5},{14,6},{15,7},{16,8},{17,9... | collective-permute-start | bytes 786440 | tf_op jit(solution)/shard_map/ppermute | solution.py:230
  26.6 25.7 %collective-permute-start.6 = (bf16[128,1024]{1,0:T(8,128)(2,1)S(1)}, bf16[128,1024]{1,0:T(8,128)(2,1)S(1)}, u32[]{:S(2)}, u32[]{:S(2)}) collective-permute-start(bf16[128,1024]{1,0:T(8,128)(2,1)S(1)} %get-tuple-element.23.refs_3_), channel_id=1, source_target_pairs={{24,0},{25,1},{26,2},{27,3},{28,4},{29,5},{30,6},{31,7},{0,8},{1,9... | collective-permute-start | bytes 786440 | tf_op jit(solution)/shard_map/ppermute | solution.py:233
  31.4 21.0 %collective-permute-start.4 = (bf16[128,1024]{1,0:T(8,128)(2,1)S(1)}, bf16[128,1024]{1,0:T(8,128)(2,1)S(1)}, u32[]{:S(2)}, u32[]{:S(2)}) collective-permute-start(bf16[128,1024]{1,0:T(8,128)(2,1)S(1)} %get-tuple-element.23.refs_3_), channel_id=1, source_target_pairs={{16,0},{17,1},{18,2},{19,3},{20,4},{21,5},{22,6},{23,7},{24,8},{25... | collective-permute-start | bytes 786440 | tf_op jit(solution)/shard_map/ppermute | solution.py:233
  33.0 19.4 %collective-permute-start.2 = (bf16[128,1024]{1,0:T(8,128)(2,1)S(1)}, bf16[128,1024]{1,0:T(8,128)(2,1)S(1)}, u32[]{:S(2)}, u32[]{:S(2)}) collective-permute-start(bf16[128,1024]{1,0:T(8,128)(2,1)S(1)} %get-tuple-element.23.refs_3_), channel_id=1, source_target_pairs={{8,0},{9,1},{10,2},{11,3},{12,4},{13,5},{14,6},{15,7},{16,8},{17,9... | collective-permute-start | bytes 786440 | tf_op jit(solution)/shard_map/ppermute | solution.py:233
  42.8 2.9 %copy-start.2 = (bf16[128,1024]{1,0:T(8,128)(2,1)S(1)}, bf16[128,1024]{1,0:T(8,128)(2,1)}, u32[]{:S(2)}) copy-start(bf16[128,1024]{1,0:T(8,128)(2,1)} %copy-done.1) | copy-start | bytes 786436
  42.8 3.0 %copy-start.4 = (bf16[128,1024]{1,0:T(8,128)(2,1)S(1)}, bf16[128,1024]{1,0:T(8,128)(2,1)}, u32[]{:S(2)}) copy-start(bf16[128,1024]{1,0:T(8,128)(2,1)} %copy-done.3) | copy-start | bytes 786436
  42.8 3.0 %copy-start.6 = (bf16[128,1024]{1,0:T(8,128)(2,1)S(1)}, bf16[128,1024]{1,0:T(8,128)(2,1)}, u32[]{:S(2)}) copy-start(bf16[128,1024]{1,0:T(8,128)(2,1)} %copy-done.5) | copy-start | bytes 786436
  42.8 3.0 %copy-start.8 = (bf16[128,1024]{1,0:T(8,128)(2,1)S(1)}, bf16[128,1024]{1,0:T(8,128)(2,1)}, u32[]{:S(2)}) copy-start(bf16[128,1024]{1,0:T(8,128)(2,1)} %copy-done.7) | copy-start | bytes 786436
  55.7 2.8 %collective-permute-start.7 = (bf16[4,32,2,16,128]{4,3,2,1,0:T(8,128)(2,1)S(1)}, bf16[4,32,2,16,128]{4,3,2,1,0:T(8,128)(2,1)S(1)}, u32[]{:S(2)}, u32[]{:S(2)}) collective-permute-start(bf16[4,32,2,16,128]{4,3,2,1,0:T(8,128)(2,1)S(1)} %shard_map.87), channel_id=1, source_target_pairs={{0,32},{32,0},{64,96},{96,64},{128,160},{160,128},{192,224},{224,1... | collective-permute-start | bytes 3145736 | tf_op jit(solution)/shard_map/ppermute | solution.py:272
  58.7 10.3 %collective-permute-start.8 = (bf16[32,2,16,128]{3,2,1,0:T(8,128)(2,1)S(1)}, bf16[32,2,16,128]{3,2,1,0:T(8,128)(2,1)S(1)}, u32[]{:S(2)}, u32[]{:S(2)}) collective-permute-start(bf16[32,2,16,128]{3,2,1,0:T(8,128)(2,1)S(1)} %get-tuple-element.30), channel_id=1, source_target_pairs={{0,64},{32,96},{64,128},{96,160},{128,192},{160,224},{192,0},{224,... | collective-permute-start | bytes 786440 | tf_op jit(solution)/shard_map/ppermute | solution.py:280
  59.4 14.7 %collective-permute-start.10 = (bf16[32,2,16,128]{3,2,1,0:T(8,128)(2,1)S(1)}, bf16[32,2,16,128]{3,2,1,0:T(8,128)(2,1)S(1)}, u32[]{:S(2)}, u32[]{:S(2)}) collective-permute-start(bf16[32,2,16,128]{3,2,1,0:T(8,128)(2,1)S(1)} %get-tuple-element.34), channel_id=1, source_target_pairs={{0,192},{32,224},{64,0},{96,32},{128,64},{160,96},{192,128},{224,1... | collective-permute-start | bytes 786440 | tf_op jit(solution)/shard_map/ppermute | solution.py:280
  62.2 13.7 %collective-permute-start.9 = (bf16[32,2,16,128]{3,2,1,0:T(8,128)(2,1)S(1)}, bf16[32,2,16,128]{3,2,1,0:T(8,128)(2,1)S(1)}, u32[]{:S(2)}, u32[]{:S(2)}) collective-permute-start(bf16[32,2,16,128]{3,2,1,0:T(8,128)(2,1)S(1)} %get-tuple-element.35), channel_id=1, source_target_pairs={{0,128},{32,160},{64,192},{96,224},{128,0},{160,32},{192,64},{224,... | collective-permute-start | bytes 786440 | tf_op jit(solution)/shard_map/ppermute | solution.py:280
  (3 other events, 2.1 us)

commit v13 on v12

--- a/solution.py
+++ b/solution.py
@@ -222,11 +222,9 @@
         [(((y + i) % height) * DEPTH + z, y * DEPTH + z) for y in range(height) for z in range(DEPTH)]
         for i in range(height)
     ]
-    flat_state = three_state.reshape(rows, states * targets)
-    flat_state, screened = lax.optimization_barrier((flat_state, screened))
     span = states * targets // 2
-    parts = jnp.stack([flat_state[:, part * span : (part + 1) * span] for part in range(2)])
-    own = lax.ppermute(parts, ("freq", "aux"), along)
+    moved = lax.ppermute(three_state, ("freq", "aux"), along).reshape(rows, states * targets)
+    own = [moved[:, part * span : (part + 1) * span] for part in range(2)]
     slabs = [[own[0]] + [lax.ppermute(own[0], "aux", across[i]) for i in range(1, height)], [own[1]]]
     for i in range(1, height):
         ready, slabs[0][i] = lax.optimization_barrier((own[1], slabs[0][i]))

time: 98.4 us -> 96.4 us (0.980)
    all_to_all x1, waiting for transfers between devices: 7.15 us -> 4.53 us  [shards(): lax.all_to_all(pieces, 'freq', split_axis=0, concat_axis=0, tiled=True)]
    ppermute x3, waiting for transfers between devices: 3.42 us -> 5.11 us  [shards(): lax.ppermute(own[0], 'aux', across[i])]
    ppermute x3, starting transfers between devices: 5.56 us -> 4.15 us  [shards(): lax.ppermute(sent[i], 'freq', chip_shift(i + 1))]
  transfers between devices with their start and end apart: 12 -> 12, of which waited for: 5 -> 5; matrix products, arithmetic and copies ran while one was open for 4% -> 5% of each run, Pallas kernels for 15% -> 16%
where the time goes in v13:
time: 96.4 us; the launch traced here: 96.1 us
  starting transfers between devices  26.9 us (28%)
  blocking collectives  21.4 us (22%)
  waiting for transfers between devices  19.7 us (20%)
  Pallas kernels  18.4 us (19%)
  local copies, waits for them, and re-layouts  6.13 us (6%)
  other arithmetic  1.78 us (2%)
  matrix products  1.3 us (1%)
    all_to_all x1, blocking collectives, shards(): lax.all_to_all(summed.astype(jnp.bfloat16), 'aux', split_axis=0, concat_a...  21.4 us
    pallas_call x4, Pallas kernels, contract(): pl.pallas_call(functools.partial(contract_kernel, jobs, part, bool(totals...  14 us
    ppermute x3, waiting for transfers between devices, shards(): lax.ppermute(sent[i], 'freq', chip_shift(i + 1))  10.1 us
    all_to_all x1, starting transfers between devices, shards(): lax.all_to_all(pieces, 'freq', split_axis=0, concat_axis=0, tiled=True)  10.1 us
    ppermute x3, starting transfers between devices, shards(): lax.ppermute(own[0], 'aux', across[i])  5.9 us
    ppermute x3, waiting for transfers between devices, shards(): lax.ppermute(own[0], 'aux', across[i])  5.11 us
    ppermute x3, starting transfers between devices, shards(): slabs[1].append(lax.ppermute(ready, 'aux', across[i]))  5.01 us
    all_to_all x1, waiting for transfers between devices, shards(): lax.all_to_all(pieces, 'freq', split_axis=0, concat_axis=0, tiled=True)  4.53 us
  transfers between devices with their start and end apart: 12, of which 5 were waited for; matrix products, arithmetic and copies ran while one was open for 5% of the time, Pallas kernels for 16%

profile of v13, /device:TPU:32, one launch (start us, length us, event | category | flops | bytes accessed | tf_op | source)
XLA Modules:
  0.0 96.1 jit_solution(12225092944932338456)
XLA Ops:
  0.0 1.7 %collective-permute-start = (bf16[128,16,128]{2,1,0:T(8,128)(2,1)}, bf16[128,16,128]{2,1,0:T(8,128)(2,1)S(1)}, u32[]{:S(2)}, u32[]{:S(2)}) collective-permute-start(bf16[128,16,128]{2,1,0:T(8,128)(2,1)} %param.11), channel_id=1, source_target_pairs={{0,0},{1,1},{2,2},{3,3},{4,4},{5,5},{6,6},{7,7},{8,8},{9,9},{10,10... | collective-permute-start | bytes 1572872 | tf_op jit(solution)/shard_map/ppermute | solution.py:226
  1.7 1.6 %copy-done = bf16[2,128,4096]{2,1,0:T(8,128)(2,1)S(1)} copy-done((bf16[2,128,4096]{2,1,0:T(8,128)(2,1)S(1)}, bf16[2,128,4096]{2,1,0:T(8,128)(2,1)}, u32[]{:S(2)}) %copy-start) | copy-done | bytes 2097176
  3.3 1.4 %shard_map.82 = bf16[8,2,128,512]{3,2,1,0:T(8,128)(2,1)} custom-call(s32[1]{0:T(128)} %bitcast.place_ref, bf16[2,128,4096]{2,1,0:T(8,128)(2,1)S(1)} %copy-done), custom_call_target="tpu_custom_call" | custom-call | tf_op jit(solution)/shard_map/pallas_call | solution.py:40
  4.8 10.1 %all-to-all-start = ((bf16[8,2,128,512]{3,2,1,0:T(8,128)(2,1)}), bf16[8,2,128,512]{3,2,1,0:T(8,128)(2,1)}, u32[]{:S(2)}, u32[]{:S(2)}) async-start(bf16[8,2,128,512]{3,2,1,0:T(8,128)(2,1)} %shard_map.82), calls=%async_computation | async-start | bytes 4194304 | tf_op jit(solution)/shard_map/all_to_all | solution.py:235
  17.0 1.7 %collective-permute-start.5 = (bf16[128,1024]{1,0:T(8,128)(2,1)S(1)}, bf16[128,1024]{1,0:T(8,128)(2,1)S(1)}, u32[]{:S(2)}, u32[]{:S(2)}) collective-permute-start(bf16[128,1024]{1,0:T(8,128)(2,1)S(1)} %get-tuple-element.33.refs_3_), channel_id=1, source_target_pairs={{24,0},{25,1},{26,2},{27,3},{28,4},{29,5},{30,6},{31,7},{0,8},{1,9... | collective-permute-start | bytes 786440 | tf_op jit(solution)/shard_map/ppermute | solution.py:228
  18.6 2.9 %collective-permute-start.3 = (bf16[128,1024]{1,0:T(8,128)(2,1)S(1)}, bf16[128,1024]{1,0:T(8,128)(2,1)S(1)}, u32[]{:S(2)}, u32[]{:S(2)}) collective-permute-start(bf16[128,1024]{1,0:T(8,128)(2,1)S(1)} %get-tuple-element.33.refs_3_), channel_id=1, source_target_pairs={{16,0},{17,1},{18,2},{19,3},{20,4},{21,5},{22,6},{23,7},{24,8},{25... | collective-permute-start | bytes 786440 | tf_op jit(solution)/shard_map/ppermute | solution.py:228
  21.5 1.3 %collective-permute-start.1 = (bf16[128,1024]{1,0:T(8,128)(2,1)S(1)}, bf16[128,1024]{1,0:T(8,128)(2,1)S(1)}, u32[]{:S(2)}, u32[]{:S(2)}) collective-permute-start(bf16[128,1024]{1,0:T(8,128)(2,1)S(1)} %get-tuple-element.33.refs_3_), channel_id=1, source_target_pairs={{8,0},{9,1},{10,2},{11,3},{12,4},{13,5},{14,6},{15,7},{16,8},{17,9... | collective-permute-start | bytes 786440 | tf_op jit(solution)/shard_map/ppermute | solution.py:228
  22.9 1.2 %copy.12 = bf16[2,16,64,512]{3,2,1,0:T(8,128)(2,1)S(1)} copy(bf16[2,16,64,512]{3,1,2,0:T(8,128)(2,1)S(1)} %bitcast.26) | data formatting | bytes 4194304 | tf_op jit(solution)/shard_map/transpose | solution.py:261
  24.1 1.3 %fusion.2.refs_2_ = bf16[2,512,1024]{2,1,0:T(8,128)(2,1)S(1)} fusion(bf16[2,1024,512]{2,1,0:T(8,128)(2,1)S(1)} %bitcast.27, s32[2,512]{1,0:T(2,128)S(1)} %add_select_fusion, s32[512]{0:T(512)S(1)} %add.202), kind=kOutput, calls=%fused_computation.2 | convolution fusion | flops 1075314688 | bytes 4200448 | tf_op jit(solution)/shard_map/bns,brs->bnr/dot_general | solution.py:262
  26.8 5.1 %collective-permute-done.3.refs_5_ = bf16[128,1024]{1,0:T(8,128)(2,1)S(1)} collective-permute-done((bf16[128,1024]{1,0:T(8,128)(2,1)S(1)}, bf16[128,1024]{1,0:T(8,128)(2,1)S(1)}, u32[]{:S(2)}, u32[]{:S(2)}) %collective-permute-start.3) | collective-permute-done | bytes 262176 | tf_op jit(solution)/shard_map/ppermute | solution.py:228
  33.2 0.7 copy-done.7
  33.9 3.7 %collective-permute-start.2 = (bf16[128,1024]{1,0:T(8,128)(2,1)S(1)}, bf16[128,1024]{1,0:T(8,128)(2,1)S(1)}, u32[]{:S(2)}, u32[]{:S(2)}) collective-permute-start(bf16[128,1024]{1,0:T(8,128)(2,1)S(1)} %get-tuple-element.19.refs_3_), channel_id=1, source_target_pairs={{8,0},{9,1},{10,2},{11,3},{12,4},{13,5},{14,6},{15,7},{16,8},{17,9... | collective-permute-start | bytes 786440 | tf_op jit(solution)/shard_map/ppermute | solution.py:231
  37.6 4.5 %all-to-all-done.pieces_ref = bf16[8,2,128,512]{3,2,1,0:T(8,128)(2,1)} async-done(((bf16[8,2,128,512]{3,2,1,0:T(8,128)(2,1)}), bf16[8,2,128,512]{3,2,1,0:T(8,128)(2,1)}, u32[]{:S(2)}, u32[]{:S(2)}) %all-to-all-start) | async-done | bytes 2097184 | tf_op jit(solution)/shard_map/all_to_all | solution.py:235
  42.2 2.9 %shard_map.84.refs_0_ = bf16[2,4,256,512]{3,2,1,0:T(8,128)(2,1)S(1)} custom-call(bf16[8,2,128,512]{3,2,1,0:T(8,128)(2,1)} %all-to-all-done.pieces_ref, bf16[2,256,256]{2,1,0:T(8,128)(2,1)S(1)} %shard_map.83.mix_ref), custom_call_target="tpu_custom_call" | custom-call | tf_op jit(solution)/shard_map/pallas_call | solution.py:96
  45.1 6.5 %shard_map.85 = (f32[4,32,2,16,128]{4,3,2,1,0:T(8,128)S(1)}, f32[4,32,2,16,128]{4,3,2,1,0:T(8,128)S(1)}) custom-call(bf16[2,4,256,512]{3,2,1,0:T(8,128)(2,1)S(1)} %shard_map.84.refs_0_, f32[2,8,2048]{2,1,0:T(8,128)S(1)} %broadcast_bitcast_fusion.refs_1_, bf16[2,512,1024]{2,1,0:T(8,128)(2,1)S(1)} %fusion.2.refs_2_, bf16[128,1024]{1,0:T(8,128)(2,1)S(1)} %copy-done.2, ...), custom_call_target="tpu_custom_call" | custom-call | flops 4294967296 | bytes 16777216 | tf_op jit(solution)/shard_map/pallas_call | solution.py:176
  51.7 3.3 %shard_map.87 = bf16[4,32,2,16,128]{4,3,2,1,0:T(8,128)(2,1)S(1)} custom-call(bf16[2,4,256,512]{3,2,1,0:T(8,128)(2,1)S(1)} %shard_map.84.refs_0_, f32[2,8,2048]{2,1,0:T(8,128)S(1)} %broadcast_bitcast_fusion.refs_1_, bf16[2,512,1024]{2,1,0:T(8,128)(2,1)S(1)} %fusion.2.refs_2_, bf16[128,1024]{1,0:T(8,128)(2,1)S(1)} %get-tuple-element.19.refs_3_, ...), custom_call_target="tpu_custom_call" | custom-call | flops 2147483648 | bytes 8388608 | tf_op jit(solution)/shard_map/pallas_call | solution.py:176
  55.1 2.6 %shard_map.86 = f32[3,32,2,16,128]{4,3,2,1,0:T(8,128)S(1)} custom-call(bf16[2,4,256,512]{3,2,1,0:T(8,128)(2,1)S(1)} %shard_map.84.refs_0_, f32[2,8,2048]{2,1,0:T(8,128)S(1)} %broadcast_bitcast_fusion.refs_1_, bf16[2,512,1024]{2,1,0:T(8,128)(2,1)S(1)} %fusion.2.refs_2_, bf16[128,1024]{1,0:T(8,128)(2,1)S(1)} %get-tuple-element.19.refs_3_, ...), custom_call_target="tpu_custom_call" | custom-call | flops 1610612736 | bytes 6291456 | tf_op jit(solution)/shard_map/pallas_call | solution.py:176
  58.7 2.7 %collective-permute-start.10 = (bf16[32,2,16,128]{3,2,1,0:T(8,128)(2,1)S(1)}, bf16[32,2,16,128]{3,2,1,0:T(8,128)(2,1)S(1)}, u32[]{:S(2)}, u32[]{:S(2)}) collective-permute-start(bf16[32,2,16,128]{3,2,1,0:T(8,128)(2,1)S(1)} %get-tuple-element.30), channel_id=1, source_target_pairs={{0,192},{32,224},{64,0},{96,32},{128,64},{160,96},{192,128},{224,1... | collective-permute-start | bytes 786440 | tf_op jit(solution)/shard_map/ppermute | solution.py:278
  61.4 0.8 collective-permute-start.9
  62.2 1.5 %shard_map.88 = f32[1,32,2,16,128]{4,3,2,1,0:T(8,128)S(1)} custom-call(bf16[2,4,256,512]{3,2,1,0:T(8,128)(2,1)S(1)} %shard_map.84.refs_0_, f32[2,8,2048]{2,1,0:T(8,128)S(1)} %broadcast_bitcast_fusion.refs_1_, bf16[2,512,1024]{2,1,0:T(8,128)(2,1)S(1)} %fusion.2.refs_2_, bf16[128,1024]{1,0:T(8,128)(2,1)S(1)} %get-tuple-element.19.refs_3_, ...), custom_call_target="tpu_custom_call" | custom-call | flops 536870912 | bytes 2097152 | tf_op jit(solution)/shard_map/pallas_call | solution.py:176
  63.7 4.5 %collective-permute-done.8 = bf16[32,2,16,128]{3,2,1,0:T(8,128)(2,1)S(1)} collective-permute-done((bf16[32,2,16,128]{3,2,1,0:T(8,128)(2,1)S(1)}, bf16[32,2,16,128]{3,2,1,0:T(8,128)(2,1)S(1)}, u32[]{:S(2)}, u32[]{:S(2)}) %collective-permute-start.8) | collective-permute-done | bytes 262176 | tf_op jit(solution)/shard_map/ppermute | solution.py:278
  68.3 4.7 %collective-permute-done.10 = bf16[32,2,16,128]{3,2,1,0:T(8,128)(2,1)S(1)} collective-permute-done((bf16[32,2,16,128]{3,2,1,0:T(8,128)(2,1)S(1)}, bf16[32,2,16,128]{3,2,1,0:T(8,128)(2,1)S(1)}, u32[]{:S(2)}, u32[]{:S(2)}) %collective-permute-start.10) | collective-permute-done | bytes 262176 | tf_op jit(solution)/shard_map/ppermute | solution.py:278
  73.0 0.9 collective-permute-done.9
  74.0 21.4 %all_to_all.10 = bf16[32,2,16,128]{3,2,1,0:T(8,128)(2,1)S(1)} all-to-all(bf16[32,2,16,128]{3,2,1,0:T(8,128)(2,1)S(1)} %fusion.12), channel_id=1, replica_groups=mesh['freq'=8,'aux'=32] {'aux'}, dimensions={0} | all-to-all | bytes 524288 | tf_op jit(solution)/shard_map/all_to_all | solution.py:283
  (74 shorter events, 6.5 us)
Async XLA Ops:
  0.0 16.8 %collective-permute-start = (bf16[128,16,128]{2,1,0:T(8,128)(2,1)}, bf16[128,16,128]{2,1,0:T(8,128)(2,1)S(1)}, u32[]{:S(2)}, u32[]{:S(2)}) collective-permute-start(bf16[128,16,128]{2,1,0:T(8,128)(2,1)} %param.11), channel_id=1, source_target_pairs={{0,0},{1,1},{2,2},{3,3},{4,4},{5,5},{6,6},{7,7},{8,8},{9,9},{10,10... | collective-permute-start | bytes 1572872 | tf_op jit(solution)/shard_map/ppermute | solution.py:226
  1.7 1.6 %copy-start = (bf16[2,128,4096]{2,1,0:T(8,128)(2,1)S(1)}, bf16[2,128,4096]{2,1,0:T(8,128)(2,1)}, u32[]{:S(2)}) copy-start(bf16[2,128,4096]{2,1,0:T(8,128)(2,1)} %screened_ref.1) | copy-start | bytes 6291460
  4.7 10.2 %copy-start.13 = (s32[2]{0:T(128)S(1)}, s32[2]{0:T(128)}, u32[]{:S(2)}) copy-start(s32[2]{0:T(128)} %param.14) | copy-start | bytes 28
  4.7 10.3 %copy-start.14 = (s32[32]{0:T(128)S(1)}, s32[32]{0:T(128)}, u32[]{:S(2)}) copy-start(s32[32]{0:T(128)} %param.15) | copy-start | bytes 388
  4.7 10.4 %copy-start.11 = (s32[2,8]{1,0:T(2,128)S(1)}, s32[2,8]{1,0:T(2,128)}, u32[]{:S(2)}) copy-start(s32[2,8]{1,0:T(2,128)} %param.13) | copy-start | bytes 196
  4.8 11.2 %copy-start.12 = (f32[16]{0:T(128)S(1)}, f32[16]{0:T(128)}, u32[]{:S(2)}) copy-start(f32[16]{0:T(128)} %param.9) | copy-start | bytes 196
  4.8 11.6 %copy-start.10 = (f32[16,16]{1,0:T(8,128)S(1)}, f32[16,16]{1,0:T(8,128)}, u32[]{:S(2)}) copy-start(f32[16,16]{1,0:T(8,128)} %param.10) | copy-start | bytes 3076
  4.8 37.4 %all-to-all-start = ((bf16[8,2,128,512]{3,2,1,0:T(8,128)(2,1)}), bf16[8,2,128,512]{3,2,1,0:T(8,128)(2,1)}, u32[]{:S(2)}, u32[]{:S(2)}) async-start(bf16[8,2,128,512]{3,2,1,0:T(8,128)(2,1)} %shard_map.82), calls=%async_computation | async-start | bytes 4194304 | tf_op jit(solution)/shard_map/all_to_all | solution.py:235
  14.9 8.0 %copy-start.9 = (bf16[128,16,512]{2,1,0:T(8,128)(2,1)S(1)}, bf16[128,16,512]{2,1,0:T(8,128)(2,1)}, u32[]{:S(2)}) copy-start(bf16[128,16,512]{2,1,0:T(8,128)(2,1)} %param.12) | copy-start | bytes 6291460
  17.0 7.1 %copy-start.1 = (bf16[128,1024]{1,0:T(8,128)(2,1)}, bf16[128,1024]{1,0:T(8,128)(2,1)S(1)}, u32[]{:S(2)}) copy-start(bf16[128,1024]{1,0:T(8,128)(2,1)S(1)} %get-tuple-element.33.refs_3_) | copy-start | bytes 786436
  17.0 8.4 %collective-permute-start.5 = (bf16[128,1024]{1,0:T(8,128)(2,1)S(1)}, bf16[128,1024]{1,0:T(8,128)(2,1)S(1)}, u32[]{:S(2)}, u32[]{:S(2)}) collective-permute-start(bf16[128,1024]{1,0:T(8,128)(2,1)S(1)} %get-tuple-element.33.refs_3_), channel_id=1, source_target_pairs={{24,0},{25,1},{26,2},{27,3},{28,4},{29,5},{30,6},{31,7},{0,8},{1,9... | collective-permute-start | bytes 786440 | tf_op jit(solution)/shard_map/ppermute | solution.py:228
  18.6 13.2 %collective-permute-start.3 = (bf16[128,1024]{1,0:T(8,128)(2,1)S(1)}, bf16[128,1024]{1,0:T(8,128)(2,1)S(1)}, u32[]{:S(2)}, u32[]{:S(2)}) collective-permute-start(bf16[128,1024]{1,0:T(8,128)(2,1)S(1)} %get-tuple-element.33.refs_3_), channel_id=1, source_target_pairs={{16,0},{17,1},{18,2},{19,3},{20,4},{21,5},{22,6},{23,7},{24,8},{25... | collective-permute-start | bytes 786440 | tf_op jit(solution)/shard_map/ppermute | solution.py:228
  21.5 11.7 %collective-permute-start.1 = (bf16[128,1024]{1,0:T(8,128)(2,1)S(1)}, bf16[128,1024]{1,0:T(8,128)(2,1)S(1)}, u32[]{:S(2)}, u32[]{:S(2)}) collective-permute-start(bf16[128,1024]{1,0:T(8,128)(2,1)S(1)} %get-tuple-element.33.refs_3_), channel_id=1, source_target_pairs={{8,0},{9,1},{10,2},{11,3},{12,4},{13,5},{14,6},{15,7},{16,8},{17,9... | collective-permute-start | bytes 786440 | tf_op jit(solution)/shard_map/ppermute | solution.py:228
  26.1 25.6 %collective-permute-start.6 = (bf16[128,1024]{1,0:T(8,128)(2,1)S(1)}, bf16[128,1024]{1,0:T(8,128)(2,1)S(1)}, u32[]{:S(2)}, u32[]{:S(2)}) collective-permute-start(bf16[128,1024]{1,0:T(8,128)(2,1)S(1)} %get-tuple-element.19.refs_3_), channel_id=1, source_target_pairs={{24,0},{25,1},{26,2},{27,3},{28,4},{29,5},{30,6},{31,7},{0,8},{1,9... | collective-permute-start | bytes 786440 | tf_op jit(solution)/shard_map/ppermute | solution.py:231
  32.6 19.1 %collective-permute-start.4 = (bf16[128,1024]{1,0:T(8,128)(2,1)S(1)}, bf16[128,1024]{1,0:T(8,128)(2,1)S(1)}, u32[]{:S(2)}, u32[]{:S(2)}) collective-permute-start(bf16[128,1024]{1,0:T(8,128)(2,1)S(1)} %get-tuple-element.19.refs_3_), channel_id=1, source_target_pairs={{16,0},{17,1},{18,2},{19,3},{20,4},{21,5},{22,6},{23,7},{24,8},{25... | collective-permute-start | bytes 786440 | tf_op jit(solution)/shard_map/ppermute | solution.py:231
  33.9 17.8 %collective-permute-start.2 = (bf16[128,1024]{1,0:T(8,128)(2,1)S(1)}, bf16[128,1024]{1,0:T(8,128)(2,1)S(1)}, u32[]{:S(2)}, u32[]{:S(2)}) collective-permute-start(bf16[128,1024]{1,0:T(8,128)(2,1)S(1)} %get-tuple-element.19.refs_3_), channel_id=1, source_target_pairs={{8,0},{9,1},{10,2},{11,3},{12,4},{13,5},{14,6},{15,7},{16,8},{17,9... | collective-permute-start | bytes 786440 | tf_op jit(solution)/shard_map/ppermute | solution.py:231
  42.2 2.9 %copy-start.2 = (bf16[128,1024]{1,0:T(8,128)(2,1)S(1)}, bf16[128,1024]{1,0:T(8,128)(2,1)}, u32[]{:S(2)}) copy-start(bf16[128,1024]{1,0:T(8,128)(2,1)} %copy-done.1) | copy-start | bytes 786436
  42.2 3.0 %copy-start.4 = (bf16[128,1024]{1,0:T(8,128)(2,1)S(1)}, bf16[128,1024]{1,0:T(8,128)(2,1)}, u32[]{:S(2)}) copy-start(bf16[128,1024]{1,0:T(8,128)(2,1)} %copy-done.3) | copy-start | bytes 786436
  42.2 3.0 %copy-start.6 = (bf16[128,1024]{1,0:T(8,128)(2,1)S(1)}, bf16[128,1024]{1,0:T(8,128)(2,1)}, u32[]{:S(2)}) copy-start(bf16[128,1024]{1,0:T(8,128)(2,1)} %copy-done.5) | copy-start | bytes 786436
  42.2 3.0 %copy-start.8 = (bf16[128,1024]{1,0:T(8,128)(2,1)S(1)}, bf16[128,1024]{1,0:T(8,128)(2,1)}, u32[]{:S(2)}) copy-start(bf16[128,1024]{1,0:T(8,128)(2,1)} %copy-done.7) | copy-start | bytes 786436
  55.0 2.8 %collective-permute-start.7 = (bf16[4,32,2,16,128]{4,3,2,1,0:T(8,128)(2,1)S(1)}, bf16[4,32,2,16,128]{4,3,2,1,0:T(8,128)(2,1)S(1)}, u32[]{:S(2)}, u32[]{:S(2)}) collective-permute-start(bf16[4,32,2,16,128]{4,3,2,1,0:T(8,128)(2,1)S(1)} %shard_map.87), channel_id=1, source_target_pairs={{0,32},{32,0},{64,96},{96,64},{128,160},{160,128},{192,224},{224,1... | collective-permute-start | bytes 3145736 | tf_op jit(solution)/shard_map/ppermute | solution.py:270
  58.1 10.2 %collective-permute-start.8 = (bf16[32,2,16,128]{3,2,1,0:T(8,128)(2,1)S(1)}, bf16[32,2,16,128]{3,2,1,0:T(8,128)(2,1)S(1)}, u32[]{:S(2)}, u32[]{:S(2)}) collective-permute-start(bf16[32,2,16,128]{3,2,1,0:T(8,128)(2,1)S(1)} %get-tuple-element.26), channel_id=1, source_target_pairs={{0,64},{32,96},{64,128},{96,160},{128,192},{160,224},{192,0},{224,... | collective-permute-start | bytes 786440 | tf_op jit(solution)/shard_map/ppermute | solution.py:278
  58.7 14.3 %collective-permute-start.10 = (bf16[32,2,16,128]{3,2,1,0:T(8,128)(2,1)S(1)}, bf16[32,2,16,128]{3,2,1,0:T(8,128)(2,1)S(1)}, u32[]{:S(2)}, u32[]{:S(2)}) collective-permute-start(bf16[32,2,16,128]{3,2,1,0:T(8,128)(2,1)S(1)} %get-tuple-element.30), channel_id=1, source_target_pairs={{0,192},{32,224},{64,0},{96,32},{128,64},{160,96},{192,128},{224,1... | collective-permute-start | bytes 786440 | tf_op jit(solution)/shard_map/ppermute | solution.py:278
  61.4 12.5 %collective-permute-start.9 = (bf16[32,2,16,128]{3,2,1,0:T(8,128)(2,1)S(1)}, bf16[32,2,16,128]{3,2,1,0:T(8,128)(2,1)S(1)}, u32[]{:S(2)}, u32[]{:S(2)}) collective-permute-start(bf16[32,2,16,128]{3,2,1,0:T(8,128)(2,1)S(1)} %get-tuple-element.31), channel_id=1, source_target_pairs={{0,128},{32,160},{64,192},{96,224},{128,0},{160,32},{192,64},{224,... | collective-permute-start | bytes 786440 | tf_op jit(solution)/shard_map/ppermute | solution.py:278
  (3 other events, 2.1 us)
